TPU v7x, 32 devices: a whole 2x2x4 slice. The times are simulated.
32 devices in a mesh: dp: 8 (over y, x, core), chan: 4 (over z).
Axes of the slice: x: 2, y: 2, z: 4, core: 2. Of those that a mesh axis runs over, the one named last changes fastest.
Arguments:
- slow_input: bfloat16 [24, 8, 14, 14, 1024], P('dp', None, None, None, 'chan'), may hold values from -6 to 6
- fast_input: bfloat16 [24, 32, 14, 14, 128], P('dp', None, None, None, 'chan'), may hold values from -6 to 6
- clip_counts: int32 [8], replicated, may hold values from 1 to 3, as said below
- frame_counts: int32 [24], replicated, may hold values from 1 to 8, as said below
- fast_reduce: float32 [3, 128, 32], replicated, may hold values from -0.3125 to 0.3125
- fast_spatial: float32 [3, 3, 32, 32], replicated, may hold values from -0.375 to 0.375
- fast_expand: float32 [32, 128], replicated, may hold values from -1 to 1
- lateral_kernel: float32 [5, 128, 256], P(None, None, 'chan'), may hold values from -0.25 to 0.25
- slow_reduce: float32 [3, 1024, 256], P(None, None, 'chan'), may hold values from -0.09375 to 0.09375
- lateral_reduce: float32 [3, 256, 256], P(None, None, 'chan'), may hold values from -0.09375 to 0.09375
- slow_spatial: float32 [3, 3, 256, 256], P(None, None, None, 'chan'), may hold values from -0.125 to 0.125
- slow_expand: float32 [256, 1024], P('chan'), may hold values from -0.375 to 0.375
- shortcut: float32 [1024, 1024], P('chan'), may hold values from -0.15625 to 0.15625
- lateral_shortcut: float32 [256, 1024], P('chan'), may hold values from -0.15625 to 0.15625
- fast_inner_norm: float32 [2, 2, 32], replicated, may hold values from 0.4 to 1.4
- fast_outer_norm: float32 [2, 128], replicated, may hold values from 0.4 to 1.4
- lateral_norm: float32 [2, 256], P(None, 'chan'), may hold values from 0.4 to 1.4
- slow_inner_norm: float32 [2, 2, 256], P(None, None, 'chan'), may hold values from 0.4 to 1.4
- slow_outer_norm: float32 [2, 2, 1024], P(None, None, 'chan'), may hold values from 0.4 to 1.4
- slow_cotangent: bfloat16 [24, 8, 14, 14, 1024], P('dp', None, None, None, 'chan'), may hold values from -6 to 6
- fast_cotangent: bfloat16 [24, 32, 14, 14, 128], P('dp', None, None, None, 'chan'), may hold values from -6 to 6
Outputs:
- slow_output: bfloat16 [24, 8, 14, 14, 1024], P('dp', None, None, None, 'chan')
- fast_output: bfloat16 [24, 32, 14, 14, 128], P('dp', None, None, None, 'chan')
- slow_input_grad: bfloat16 [24, 8, 14, 14, 1024], P('dp', None, None, None, 'chan')
- fast_input_grad: bfloat16 [24, 32, 14, 14, 128], P('dp', None, None, None, 'chan')
- fast_reduce_grad: float32 [3, 128, 32], replicated
- fast_spatial_grad: float32 [3, 3, 32, 32], replicated
- fast_expand_grad: float32 [32, 128], replicated
- lateral_kernel_grad: float32 [5, 128, 256], P(None, None, 'chan')
- slow_reduce_grad: float32 [3, 1024, 256], P(None, None, 'chan')
- lateral_reduce_grad: float32 [3, 256, 256], P(None, None, 'chan')
- slow_spatial_grad: float32 [3, 3, 256, 256], P(None, None, None, 'chan')
- slow_expand_grad: float32 [256, 1024], P('chan')
- shortcut_grad: float32 [1024, 1024], P('chan')
- lateral_shortcut_grad: float32 [256, 1024], P('chan')
- fast_inner_norm_grad: float32 [2, 2, 32], replicated
- fast_outer_norm_grad: float32 [2, 128], replicated
- lateral_norm_grad: float32 [2, 256], P(None, 'chan')
- slow_inner_norm_grad: float32 [2, 2, 256], P(None, None, 'chan')
- slow_outer_norm_grad: float32 [2, 2, 1024], P(None, None, 'chan')
Inputs may be any that keep to these rules, and one draw needn't show every extreme that they name: `clip_counts`: some index of dp holds 3 clips; the clips of an index are its first slots. `frame_counts`: the valid frames of a clip are its first ones; the first slot of every index of dp has 8.
All inputs are finite; a program needn't handle non-finite values.
Results may differ from a plain program's by a relative error of at most 0.024.
Values may be sent and summed in bfloat16 or wider, within the bound.
No kernel may reach another device: no remote copies, remote signals or barrier semaphores. Data moves between devices by JAX's collectives and lax.ppermute only.
A program may use at most 448 MiB of HBM per device.

v0:
```python
import jax
import jax.numpy as jnp
from jax import lax
from jax.sharding import PartitionSpec as P

EPSILON = 1e-05
CELLS = (0, 1, 2, 3)


def gelu_tanh(value):
    return jax.nn.gelu(value, approximate=True)


def gelu_slope(value, upstream):
    unused, pullback = jax.vjp(gelu_tanh, value)
    return pullback(upstream)[0]


def apply_mix(source, kernel):
    return jnp.einsum("cthwi,io->cthwo", source, kernel, preferred_element_type=jnp.float32)


def mix_back(upstream, kernel):
    return jnp.einsum("cthwo,io->cthwi", upstream, kernel, preferred_element_type=jnp.float32)


def mix_weight(source, upstream):
    return jnp.einsum("cthwi,cthwo->io", source, upstream, preferred_element_type=jnp.float32)


def temporal_apply(source, kernel):
    half_width = kernel.shape[0] // 2
    length = source.shape[1]
    padded = jnp.pad(source, ((0, 0), (half_width, half_width), (0, 0), (0, 0), (0, 0)))
    summed = apply_mix(padded[:, 0:length], kernel[0])
    for offset in range(1, kernel.shape[0]):
        summed = summed + apply_mix(padded[:, offset : offset + length], kernel[offset])
    return summed


def temporal_back(upstream, kernel):
    half_width = kernel.shape[0] // 2
    length = upstream.shape[1]
    padded = jnp.pad(upstream, ((0, 0), (half_width, half_width), (0, 0), (0, 0), (0, 0)))
    summed = mix_back(padded[:, 2 * half_width : 2 * half_width + length], kernel[0])
    for offset in range(1, kernel.shape[0]):
        begin = 2 * half_width - offset
        summed = summed + mix_back(padded[:, begin : begin + length], kernel[offset])
    return summed


def temporal_weight(source, upstream, kernel_taps):
    half_width = kernel_taps // 2
    length = source.shape[1]
    padded = jnp.pad(source, ((0, 0), (half_width, half_width), (0, 0), (0, 0), (0, 0)))
    return jnp.stack(
        [mix_weight(padded[:, offset : offset + length], upstream) for offset in range(kernel_taps)]
    )


def spatial_apply(source, kernel):
    height, across = (source.shape[2], source.shape[3])
    padded = jnp.pad(source, ((0, 0), (0, 0), (1, 1), (1, 1), (0, 0)))
    summed = apply_mix(padded[:, :, 0:height, 0:across], kernel[0, 0])
    for row_step in range(3):
        for col_step in range(3):
            if row_step + col_step > 0:
                summed = summed + apply_mix(
                    padded[:, :, row_step : row_step + height, col_step : col_step + across],
                    kernel[row_step, col_step],
                )
    return summed


def spatial_back(upstream, kernel):
    height, across = (upstream.shape[2], upstream.shape[3])
    padded = jnp.pad(upstream, ((0, 0), (0, 0), (1, 1), (1, 1), (0, 0)))
    summed = mix_back(padded[:, :, 2 : 2 + height, 2 : 2 + across], kernel[0, 0])
    for row_step in range(3):
        for col_step in range(3):
            if row_step + col_step > 0:
                summed = summed + mix_back(
                    padded[
                        :,
                        :,
                        2 - row_step : 2 - row_step + height,
                        2 - col_step : 2 - col_step + across,
                    ],
                    kernel[row_step, col_step],
                )
    return summed


def spatial_weight(source, upstream):
    height, across = (source.shape[2], source.shape[3])
    padded = jnp.pad(source, ((0, 0), (0, 0), (1, 1), (1, 1), (0, 0)))
    return jnp.stack(
        [
            jnp.stack(
                [
                    mix_weight(
                        padded[:, :, row_step : row_step + height, col_step : col_step + across],
                        upstream,
                    )
                    for col_step in range(3)
                ]
            )
            for row_step in range(3)
        ]
    )


def lateral_apply(source, kernel, step_ratio):
    frames = source.shape[1] // step_ratio
    padded = jnp.pad(source, ((0, 0), (2, 2), (0, 0), (0, 0), (0, 0)))
    summed = apply_mix(padded[:, 0 : step_ratio * frames : step_ratio], kernel[0])
    for offset in range(1, kernel.shape[0]):
        summed = summed + apply_mix(
            padded[:, offset : offset + step_ratio * frames : step_ratio], kernel[offset]
        )
    return summed


def lateral_weight(source, upstream, step_ratio, kernel_taps):
    frames = source.shape[1] // step_ratio
    padded = jnp.pad(source, ((0, 0), (2, 2), (0, 0), (0, 0), (0, 0)))
    return jnp.stack(
        [
            mix_weight(padded[:, offset : offset + step_ratio * frames : step_ratio], upstream)
            for offset in range(kernel_taps)
        ]
    )


def lateral_back(upstream, kernel, step_ratio):
    frames = upstream.shape[1]
    products = [mix_back(upstream, kernel[offset]) for offset in range(kernel.shape[0])]
    grid = jnp.stack(products[:step_ratio], axis=2)
    grid = jnp.pad(grid, ((0, 0), (0, 1), (0, 0), (0, 0), (0, 0), (0, 0)))
    spill = jnp.pad(products[step_ratio], ((0, 0), (1, 0), (0, 0), (0, 0), (0, 0)))
    grid = jnp.concatenate([(grid[:, :, 0] + spill)[:, :, None], grid[:, :, 1:]], axis=2)
    grid_shape = grid.shape
    flat = grid.reshape(
        grid_shape[0], grid_shape[1] * grid_shape[2], grid_shape[3], grid_shape[4], grid_shape[5]
    )
    return flat[:, 2 : 2 + step_ratio * frames]


def pooled_moments(layers):
    pieces = []
    for values, live_mask in layers:
        masked = values * live_mask
        pieces.append(jnp.sum(masked, axis=CELLS))
        pieces.append(jnp.sum(masked * values, axis=CELLS))
    joined = lax.psum(jnp.concatenate(pieces), "dp")
    result = []
    offset = 0
    for values, live_mask in layers:
        breadth = values.shape[-1]
        result.append(
            (joined[offset : offset + breadth], joined[offset + breadth : offset + 2 * breadth])
        )
        offset = offset + 2 * breadth
    return result


def pooled_slopes(layers):
    pieces = []
    for upstream, standard in layers:
        pieces.append(jnp.sum(upstream, axis=CELLS))
        pieces.append(jnp.sum(upstream * standard, axis=CELLS))
    joined = lax.psum(jnp.concatenate(pieces), "dp")
    result = []
    offset = 0
    for upstream, standard in layers:
        breadth = upstream.shape[-1]
        result.append(
            (joined[offset : offset + breadth], joined[offset + breadth : offset + 2 * breadth])
        )
        offset = offset + 2 * breadth
    return result


def normalize(values, sums, voxels, gain, bias):
    center = sums[0] / voxels
    spread = sums[1] / voxels - center * center
    inv_std = lax.rsqrt(spread + EPSILON)
    standard = (values - center) * inv_std
    return (standard, inv_std, standard * gain + bias)


def norm_back(upstream, standard, inv_std, gain, slopes, live_mask, voxels):
    bias_grad, gain_grad = slopes
    return inv_std * (
        upstream * gain - live_mask * (gain * bias_grad + standard * (gain * gain_grad)) / voxels
    )


def norm_pair(slopes):
    return jnp.stack([slopes[1], slopes[0]])


def local(
    slow_input,
    fast_input,
    clip_counts,
    frame_counts,
    fast_reduce,
    fast_spatial,
    fast_expand,
    lateral_kernel,
    slow_reduce,
    lateral_reduce,
    slow_spatial,
    slow_expand,
    shortcut,
    lateral_shortcut,
    fast_inner_norm,
    fast_outer_norm,
    lateral_norm,
    slow_inner_norm,
    slow_outer_norm,
    slow_cotangent,
    fast_cotangent,
):
    clips_here = slow_input.shape[0]
    slow_frames = slow_input.shape[1]
    cells = slow_input.shape[2] * slow_input.shape[3]
    fast_part = fast_input.shape[4]
    fast_whole, fast_cot_whole = (
        lax.all_gather(fast_input, "chan", axis=4, tiled=True),
        lax.all_gather(fast_cotangent, "chan", axis=4, tiled=True),
    )
    fast_frames = fast_whole.shape[1]
    step_ratio = fast_frames // slow_frames
    all_clips = frame_counts.shape[0]
    clip_ids = jnp.arange(all_clips, dtype=jnp.int32)
    held_all = jnp.repeat(clip_counts, clips_here)
    live_all = clip_ids % clips_here < held_all
    slow_all = live_all[:, None] & (
        jnp.arange(slow_frames, dtype=jnp.int32)[None, :] < frame_counts[:, None]
    )
    fast_all = live_all[:, None] & (
        (jnp.arange(fast_frames, dtype=jnp.int32) // step_ratio)[None, :] < frame_counts[:, None]
    )
    voxels_slow = jnp.sum(slow_all.astype(jnp.float32)) * cells
    voxels_fast = jnp.sum(fast_all.astype(jnp.float32)) * cells
    first_clip = lax.axis_index("dp") * clips_here
    mask_slow = lax.dynamic_slice_in_dim(slow_all, first_clip, clips_here, 0).astype(jnp.float32)[
        :, :, None, None, None
    ]
    mask_fast = lax.dynamic_slice_in_dim(fast_all, first_clip, clips_here, 0).astype(jnp.float32)[
        :, :, None, None, None
    ]
    chan_index = lax.axis_index("chan")
    fast_reduce_bf = fast_reduce.astype(jnp.bfloat16)
    fast_spatial_bf = fast_spatial.astype(jnp.bfloat16)
    fast_expand_bf = fast_expand.astype(jnp.bfloat16)
    lateral_bf = lateral_kernel.astype(jnp.bfloat16)
    slow_reduce_bf = slow_reduce.astype(jnp.bfloat16)
    lateral_reduce_bf = lateral_reduce.astype(jnp.bfloat16)
    slow_spatial_bf = slow_spatial.astype(jnp.bfloat16)
    slow_expand_bf = slow_expand.astype(jnp.bfloat16)
    shortcut_bf = shortcut.astype(jnp.bfloat16)
    lateral_shortcut_bf = lateral_shortcut.astype(jnp.bfloat16)
    fast_x = fast_whole * mask_fast.astype(jnp.bfloat16)
    slow_x = slow_input * mask_slow.astype(jnp.bfloat16)
    fast_residual = fast_x.astype(jnp.float32)
    lateral_raw = lateral_apply(fast_x, lateral_bf, step_ratio)
    (lateral_sums,) = pooled_moments([(lateral_raw, mask_slow)])
    fast_reduced = temporal_apply(fast_x, fast_reduce_bf)
    (reduced_sums,) = pooled_moments([(fast_reduced, mask_fast)])
    lateral_std, lateral_inv, lateral_shaped = normalize(
        lateral_raw, lateral_sums, voxels_slow, lateral_norm[0], lateral_norm[1]
    )
    lateral_hidden = (gelu_tanh(lateral_shaped) * mask_slow).astype(jnp.bfloat16)
    fast_std1, fast_inv1, fast_shaped1 = normalize(
        fast_reduced, reduced_sums, voxels_fast, fast_inner_norm[0, 0], fast_inner_norm[0, 1]
    )
    fast_hidden = (gelu_tanh(fast_shaped1) * mask_fast).astype(jnp.bfloat16)
    fast_spread = spatial_apply(fast_hidden, fast_spatial_bf)
    (spread_sums,) = pooled_moments([(fast_spread, mask_fast)])
    fast_std2, fast_inv2, fast_shaped2 = normalize(
        fast_spread, spread_sums, voxels_fast, fast_inner_norm[1, 0], fast_inner_norm[1, 1]
    )
    fast_second = (gelu_tanh(fast_shaped2) * mask_fast).astype(jnp.bfloat16)
    fast_widened = apply_mix(fast_second, fast_expand_bf)
    (widened_fast_sums,) = pooled_moments([(fast_widened, mask_fast)])
    fast_std3, fast_inv3, fast_shaped3 = normalize(
        fast_widened, widened_fast_sums, voxels_fast, fast_outer_norm[0], fast_outer_norm[1]
    )
    fast_total = fast_shaped3 + fast_residual
    fast_full_out = gelu_tanh(fast_total) * mask_fast
    fast_output = lax.dynamic_slice_in_dim(
        fast_full_out, chan_index * fast_part, fast_part, 4
    ).astype(jnp.bfloat16)
    slow_whole, lateral_whole = (
        lax.all_gather(slow_x, "chan", axis=4, tiled=True),
        lax.all_gather(lateral_hidden, "chan", axis=4, tiled=True),
    )
    slow_reduced = temporal_apply(slow_whole, slow_reduce_bf) + temporal_apply(
        lateral_whole, lateral_reduce_bf
    )
    (slow_sums1,) = pooled_moments([(slow_reduced, mask_slow)])
    slow_std1, slow_inv1, slow_shaped1 = normalize(
        slow_reduced, slow_sums1, voxels_slow, slow_inner_norm[0, 0], slow_inner_norm[0, 1]
    )
    slow_hidden = (gelu_tanh(slow_shaped1) * mask_slow).astype(jnp.bfloat16)
    hidden_whole = lax.all_gather(slow_hidden, "chan", axis=4, tiled=True)
    slow_spread = spatial_apply(hidden_whole, slow_spatial_bf)
    (slow_sums2,) = pooled_moments([(slow_spread, mask_slow)])
    slow_std2, slow_inv2, slow_shaped2 = normalize(
        slow_spread, slow_sums2, voxels_slow, slow_inner_norm[1, 0], slow_inner_norm[1, 1]
    )
    slow_second = (gelu_tanh(slow_shaped2) * mask_slow).astype(jnp.bfloat16)
    widened_part = apply_mix(slow_second, slow_expand_bf)
    bypass_part = apply_mix(slow_x, shortcut_bf) + apply_mix(lateral_hidden, lateral_shortcut_bf)
    slow_widened, slow_bypass = (
        lax.psum_scatter(
            widened_part.astype(jnp.bfloat16), "chan", scatter_dimension=4, tiled=True
        ).astype(jnp.float32),
        lax.psum_scatter(
            bypass_part.astype(jnp.bfloat16), "chan", scatter_dimension=4, tiled=True
        ).astype(jnp.float32),
    )
    widened_sums, bypass_sums = pooled_moments(
        [(slow_widened, mask_slow), (slow_bypass, mask_slow)]
    )
    widened_std, widened_inv, widened_shaped = normalize(
        slow_widened, widened_sums, voxels_slow, slow_outer_norm[0, 0], slow_outer_norm[0, 1]
    )
    bypass_std, bypass_inv, bypass_shaped = normalize(
        slow_bypass, bypass_sums, voxels_slow, slow_outer_norm[1, 0], slow_outer_norm[1, 1]
    )
    slow_total = widened_shaped + bypass_shaped
    slow_output = (gelu_tanh(slow_total) * mask_slow).astype(jnp.bfloat16)
    slow_up = gelu_slope(slow_total, slow_cotangent.astype(jnp.float32) * mask_slow)
    fast_up = gelu_slope(fast_total, fast_cot_whole.astype(jnp.float32) * mask_fast)
    widened_slopes, bypass_slopes = pooled_slopes([(slow_up, widened_std), (slow_up, bypass_std)])
    widened_grad = norm_back(
        slow_up,
        widened_std,
        widened_inv,
        slow_outer_norm[0, 0],
        widened_slopes,
        mask_slow,
        voxels_slow,
    ).astype(jnp.bfloat16)
    bypass_grad = norm_back(
        slow_up,
        bypass_std,
        bypass_inv,
        slow_outer_norm[1, 0],
        bypass_slopes,
        mask_slow,
        voxels_slow,
    ).astype(jnp.bfloat16)
    widened_whole, bypass_whole = (
        lax.all_gather(widened_grad, "chan", axis=4, tiled=True),
        lax.all_gather(bypass_grad, "chan", axis=4, tiled=True),
    )
    slow_expand_grad = mix_weight(slow_second, widened_whole)
    shortcut_grad = mix_weight(slow_x, bypass_whole)
    lateral_shortcut_grad = mix_weight(lateral_hidden, bypass_whole)
    second_up = mix_back(widened_whole, slow_expand_bf)
    slow_x_up = mix_back(bypass_whole, shortcut_bf)
    lateral_up = mix_back(bypass_whole, lateral_shortcut_bf)
    spread_up = gelu_slope(slow_shaped2, second_up * mask_slow)
    (spread_slopes,) = pooled_slopes([(spread_up, slow_std2)])
    spread_grad = norm_back(
        spread_up,
        slow_std2,
        slow_inv2,
        slow_inner_norm[1, 0],
        spread_slopes,
        mask_slow,
        voxels_slow,
    ).astype(jnp.bfloat16)
    slow_spatial_grad = spatial_weight(hidden_whole, spread_grad)
    hidden_part = spatial_back(spread_grad, slow_spatial_bf)
    hidden_up = lax.psum_scatter(
        hidden_part.astype(jnp.bfloat16), "chan", scatter_dimension=4, tiled=True
    ).astype(jnp.float32)
    reduce_up = gelu_slope(slow_shaped1, hidden_up * mask_slow)
    (reduce_slopes,) = pooled_slopes([(reduce_up, slow_std1)])
    reduce_grad = norm_back(
        reduce_up,
        slow_std1,
        slow_inv1,
        slow_inner_norm[0, 0],
        reduce_slopes,
        mask_slow,
        voxels_slow,
    ).astype(jnp.bfloat16)
    kernel_taps = slow_reduce.shape[0]
    slow_reduce_grad = temporal_weight(slow_whole, reduce_grad, kernel_taps)
    lateral_reduce_grad = temporal_weight(lateral_whole, reduce_grad, kernel_taps)
    slow_part = temporal_back(reduce_grad, slow_reduce_bf)
    lateral_part = temporal_back(reduce_grad, lateral_reduce_bf)
    slow_from_reduce, lateral_from_reduce = (
        lax.psum_scatter(
            slow_part.astype(jnp.bfloat16), "chan", scatter_dimension=4, tiled=True
        ).astype(jnp.float32),
        lax.psum_scatter(
            lateral_part.astype(jnp.bfloat16), "chan", scatter_dimension=4, tiled=True
        ).astype(jnp.float32),
    )
    slow_input_grad = ((slow_from_reduce + slow_x_up) * mask_slow).astype(jnp.bfloat16)
    lateral_pre_up = gelu_slope(lateral_shaped, (lateral_from_reduce + lateral_up) * mask_slow)
    (lateral_slopes,) = pooled_slopes([(lateral_pre_up, lateral_std)])
    lateral_grad = norm_back(
        lateral_pre_up,
        lateral_std,
        lateral_inv,
        lateral_norm[0],
        lateral_slopes,
        mask_slow,
        voxels_slow,
    ).astype(jnp.bfloat16)
    lateral_kernel_grad = lateral_weight(fast_x, lateral_grad, step_ratio, lateral_kernel.shape[0])
    lateral_fast_part = lateral_back(lateral_grad, lateral_bf, step_ratio)
    lateral_to_fast = lax.psum_scatter(
        lateral_fast_part.astype(jnp.bfloat16), "chan", scatter_dimension=4, tiled=True
    ).astype(jnp.float32)
    (fast_slopes3,) = pooled_slopes([(fast_up, fast_std3)])
    fast_widened_grad = norm_back(
        fast_up, fast_std3, fast_inv3, fast_outer_norm[0], fast_slopes3, mask_fast, voxels_fast
    ).astype(jnp.bfloat16)
    fast_expand_grad = mix_weight(fast_second, fast_widened_grad)
    fast_second_up = mix_back(fast_widened_grad, fast_expand_bf)
    fast_spread_up = gelu_slope(fast_shaped2, fast_second_up * mask_fast)
    (fast_slopes2,) = pooled_slopes([(fast_spread_up, fast_std2)])
    fast_spread_grad = norm_back(
        fast_spread_up,
        fast_std2,
        fast_inv2,
        fast_inner_norm[1, 0],
        fast_slopes2,
        mask_fast,
        voxels_fast,
    ).astype(jnp.bfloat16)
    fast_spatial_grad = spatial_weight(fast_hidden, fast_spread_grad)
    fast_hidden_up = spatial_back(fast_spread_grad, fast_spatial_bf)
    fast_reduce_up = gelu_slope(fast_shaped1, fast_hidden_up * mask_fast)
    (fast_slopes1,) = pooled_slopes([(fast_reduce_up, fast_std1)])
    fast_reduce_grad_bf = norm_back(
        fast_reduce_up,
        fast_std1,
        fast_inv1,
        fast_inner_norm[0, 0],
        fast_slopes1,
        mask_fast,
        voxels_fast,
    ).astype(jnp.bfloat16)
    fast_reduce_grad = temporal_weight(fast_x, fast_reduce_grad_bf, fast_reduce.shape[0])
    fast_x_up = fast_up + temporal_back(fast_reduce_grad_bf, fast_reduce_bf)
    own_fast = lax.dynamic_slice_in_dim(fast_x_up, chan_index * fast_part, fast_part, 4)
    fast_input_grad = ((own_fast + lateral_to_fast) * mask_fast).astype(jnp.bfloat16)
    summed = (
        lax.psum(fast_reduce_grad.astype(jnp.bfloat16), "dp").astype(jnp.float32),
        lax.psum(fast_spatial_grad.astype(jnp.bfloat16), "dp").astype(jnp.float32),
        lax.psum(fast_expand_grad.astype(jnp.bfloat16), "dp").astype(jnp.float32),
        lax.psum(lateral_kernel_grad.astype(jnp.bfloat16), "dp").astype(jnp.float32),
        lax.psum(slow_reduce_grad.astype(jnp.bfloat16), "dp").astype(jnp.float32),
        lax.psum(lateral_reduce_grad.astype(jnp.bfloat16), "dp").astype(jnp.float32),
        lax.psum(slow_spatial_grad.astype(jnp.bfloat16), "dp").astype(jnp.float32),
        lax.psum(slow_expand_grad.astype(jnp.bfloat16), "dp").astype(jnp.float32),
        lax.psum(shortcut_grad.astype(jnp.bfloat16), "dp").astype(jnp.float32),
        lax.psum(lateral_shortcut_grad.astype(jnp.bfloat16), "dp").astype(jnp.float32),
    )
    fast_inner_norm_grad = jnp.stack([norm_pair(fast_slopes1), norm_pair(fast_slopes2)])
    fast_outer_norm_grad = norm_pair(fast_slopes3)
    lateral_norm_grad = norm_pair(lateral_slopes)
    slow_inner_norm_grad = jnp.stack([norm_pair(reduce_slopes), norm_pair(spread_slopes)])
    slow_outer_norm_grad = jnp.stack([norm_pair(widened_slopes), norm_pair(bypass_slopes)])
    return (
        slow_output,
        fast_output,
        slow_input_grad,
        fast_input_grad,
        summed[0],
        summed[1],
        summed[2],
        summed[3],
        summed[4],
        summed[5],
        summed[6],
        summed[7],
        summed[8],
        summed[9],
        fast_inner_norm_grad,
        fast_outer_norm_grad,
        lateral_norm_grad,
        slow_inner_norm_grad,
        slow_outer_norm_grad,
    )


def solution(mesh):
    return jax.shard_map(
        local,
        mesh=mesh,
        in_specs=(
            P("dp", None, None, None, "chan"),
            P("dp", None, None, None, "chan"),
            P(),
            P(),
            P(),
            P(),
            P(),
            P(None, None, "chan"),
            P(None, None, "chan"),
            P(None, None, "chan"),
            P(None, None, None, "chan"),
            P("chan", None),
            P("chan", None),
            P("chan", None),
            P(),
            P(),
            P(None, "chan"),
            P(None, None, "chan"),
            P(None, None, "chan"),
            P("dp", None, None, None, "chan"),
            P("dp", None, None, None, "chan"),
        ),
        out_specs=(
            P("dp", None, None, None, "chan"),
            P("dp", None, None, None, "chan"),
            P("dp", None, None, None, "chan"),
            P("dp", None, None, None, "chan"),
            P(),
            P(),
            P(),
            P(None, None, "chan"),
            P(None, None, "chan"),
            P(None, None, "chan"),
            P(None, None, None, "chan"),
            P("chan", None),
            P("chan", None),
            P("chan", None),
            P(),
            P(),
            P(None, "chan"),
            P(None, None, "chan"),
            P(None, None, "chan"),
        ),
        check_vma=False,
    )
```

profile of v0, /device:TPU:0, one launch (start us, length us, event | category | flops | bytes accessed | tf_op | source)
XLA Modules:
  0.0 3448.1 jit_solution(7700564020138846667)
XLA Ops:
  21.0 373.7 %all-gather.10.cloned.1.call-done = bf16[3,32,14,14,128]{1,3,2,0,4:T(8,128)(2,1)} async-done(((bf16[3,32,14,14,32]{1,3,2,0,4:T(8,128)(2,1)}), bf16[3,32,14,14,128]{1,3,2,0,4:T(8,128)(2,1)}) %all-gather.10.cloned.1.call-update) | async-done | bytes 4816912 | tf_op jit(solution)/shard_map/all_gather | solution.py:231
  394.7 25.4 copy.598
  429.4 22.9 slice.489
  452.3 20.0 slice.487
  472.3 20.3 slice.485
  492.7 22.7 slice.483
  515.4 22.5 slice.481
  571.0 365.3 %all-gather.12.cloned.1.call-done = bf16[3,8,14,14,256]{3,1,2,0,4:T(8,128)(2,1)} async-done(((bf16[3,8,14,14,64]{3,1,2,0,4:T(8,128)(2,1)}), bf16[3,8,14,14,256]{3,1,2,0,4:T(8,128)(2,1)}) %all-gather.12.cloned.1.call-update) | async-done | bytes 2408464 | tf_op jit(solution)/shard_map/all_gather | solution.py:299
  936.3 22.5 copy.605
  963.6 164.7 %all-gather.8.cloned.1.call-done = bf16[3,8,14,14,1024]{4,3,2,1,0:T(8,128)(2,1)} async-done(((bf16[3,8,14,14,256]{4,3,2,1,0:T(8,128)(2,1)}), bf16[3,8,14,14,1024]{4,3,2,1,0:T(8,128)(2,1)}) %all-gather.8.cloned.1.call-update) | async-done | bytes 9633808 | tf_op jit(solution)/shard_map/all_gather | solution.py:298
  1221.4 315.8 %all-gather.14.cloned.1.call-done = bf16[3,8,14,14,256]{3,1,2,0,4:T(8,128)(2,1)} async-done(((bf16[3,8,14,14,64]{3,1,2,0,4:T(8,128)(2,1)}), bf16[3,8,14,14,256]{3,1,2,0,4:T(8,128)(2,1)}) %all-gather.14.cloned.1.call-update) | async-done | bytes 2408464 | tf_op jit(solution)/shard_map/all_gather | solution.py:309
  1537.2 22.2 copy.608
  1650.1 30.2 multiply_reduce_fusion.1
  1680.4 43.9 %reduce-scatter.15.cloned.1.call-done = bf16[3,8,14,14,256]{4,3,2,1,0:T(8,128)(2,1)} async-done(((bf16[3,8,14,14,1024]{4,3,2,1,0:T(8,128)(2,1)}), bf16[3,8,14,14,256]{4,3,2,1,0:T(8,128)(2,1)}) %reduce-scatter.15.cloned.1.call-update) | async-done | bytes 2408464 | tf_op jit(solution)/shard_map/reduce_scatter | solution.py:322
  1724.3 189.8 %reduce-scatter.13.cloned.1.call-done = bf16[3,8,14,14,256]{4,3,2,1,0:T(8,128)(2,1)} async-done(((bf16[3,8,14,14,1024]{4,3,2,1,0:T(8,128)(2,1)}), bf16[3,8,14,14,256]{4,3,2,1,0:T(8,128)(2,1)}) %reduce-scatter.13.cloned.1.call-update) | async-done | bytes 2408464 | tf_op jit(solution)/shard_map/reduce_scatter | solution.py:319
  1979.1 311.7 %all-gather.20.cloned.1.call-done = bf16[3,32,14,14,128]{1,3,2,0,4:T(8,128)(2,1)} async-done(((bf16[3,32,14,14,32]{1,3,2,0,4:T(8,128)(2,1)}), bf16[3,32,14,14,128]{1,3,2,0,4:T(8,128)(2,1)}) %all-gather.20.cloned.1.call-update) | async-done | bytes 4816912 | tf_op jit(solution)/shard_map/all_gather | solution.py:232
  2290.7 26.0 copy.615
  2347.0 19.8 fusion.465
  2366.8 116.0 %all-gather.16.cloned.1.call-done = bf16[3,8,14,14,1024]{4,3,2,1,0:T(8,128)(2,1)} async-done(((bf16[3,8,14,14,256]{4,3,2,1,0:T(8,128)(2,1)}), bf16[3,8,14,14,1024]{4,3,2,1,0:T(8,128)(2,1)}) %all-gather.16.cloned.1.call-update) | async-done | bytes 9633808 | tf_op jit(solution)/shard_map/all_gather | solution.py:359
  2555.4 36.8 %copy.801 = bf16[3,8,14,14,256]{3,2,1,0,4:T(8,128)(2,1)} copy(bf16[3,8,14,14,256]{4,3,2,1,0:T(8,128)(2,1)} %add_convert_fusion.3) | data formatting | bytes 4816896
  2592.2 25.2 reshape.201
  2687.1 36.8 %reduce-scatter.19.cloned.1.call-done = bf16[64,4704]{1,0:T(8,128)(2,1)} async-done(((bf16[256,4704]{1,0:T(8,128)(2,1)}), bf16[64,4704]{1,0:T(8,128)(2,1)}) %reduce-scatter.19.cloned.1.call-update) | async-done | bytes 602128
  2816.3 36.9 %copy.803 = bf16[3,8,14,14,256]{3,2,1,0,4:T(8,128)(2,1)} copy(bf16[3,8,14,14,256]{4,3,2,1,0:T(8,128)(2,1)} %add_convert_fusion.2) | data formatting | bytes 4816896
  2853.2 24.9 reshape.203
  2878.3 35.9 %fusion.463 = (f32[32]{0:T(128)S(1)}, f32[32]{0:T(128)S(1)}, f32[3,32,14,14,32]{4,1,3,2,0:T(8,128)}) fusion(f32[32]{0:T(128)S(1)} %copy-done.65, f32[3,32,14,14,32]{4,1,3,2,0:T(8,128)} %get-tuple-element.283, f32[32]{0:T(128)S(1)} %copy-done.68, f32[32]{0:T(128)S(1)} %copy-done.75, f32[32]{0:T(128)S(1)} %copy-done.71, f32[3,32]{1,0:T(4,128)S(1)} %get-tuple-element.226, ...), kind=kOutput, calls=%fused_computation.615 | convolution fusion | flops 54300608 | bytes 25301248 | tf_op jit(solution)/shard_map/cthwo,io->cthwi/dot_general | solution.py:24
  3033.2 75.3 %copy.805 = bf16[3,32,14,14,128]{3,2,1,0,4:T(8,128)(2,1)} copy(bf16[3,32,14,14,128]{4,1,3,2,0:T(8,128)(2,1)} %slice.640) | data formatting | bytes 9633792
  3108.5 46.4 %reshape.205 = bf16[128,18816]{1,0:T(8,128)(2,1)} reshape(bf16[128,3,32,14,14]{4,3,2,1,0:T(8,128)(2,1)} %bitcast.877) | data formatting | bytes 9633792
  3174.3 19.5 add_convert_fusion
  3241.9 24.4 all-reduce.18
  3315.9 18.4 copy.627
  3334.3 29.0 fusion.39
  3363.3 65.8 %reduce-scatter.17.cloned.1.call-done = bf16[3,8,14,14,256]{4,3,2,1,0:T(8,128)(2,1)} async-done(((bf16[3,8,14,14,1024]{4,3,2,1,0:T(8,128)(2,1)}), bf16[3,8,14,14,256]{4,3,2,1,0:T(8,128)(2,1)}) %reduce-scatter.17.cloned.1.call-update) | async-done | bytes 2408464 | tf_op jit(solution)/shard_map/reduce_scatter | solution.py:401
  (579 shorter events, 819.6 us)
Async XLA Ops:
  7.2 387.5 %all-gather.10.cloned.1.call-start = ((), (), s32[]{:S(2)}) async-start(), calls=%async_computation.7 | async-start | bytes 27525120 | tf_op jit(solution)/shard_map/all_gather | solution.py:231
  17.8 918.4 %all-gather.12.cloned.1.call-start = ((), (), s32[]{:S(2)}) async-start(), calls=%async_computation.8 | async-start | bytes 27525120 | tf_op jit(solution)/shard_map/all_gather | solution.py:299
  18.8 522.6 %copy-start.48 = (bf16[5,128,64]{1,2,0:T(8,128)(2,1)}, bf16[5,128,64]{1,2,0:T(8,128)(2,1)S(1)}, u32[]{:S(2)}) copy-start(bf16[5,128,64]{1,2,0:T(8,128)(2,1)S(1)} %convert_element_type.227) | copy-start | bytes 245764
  20.2 1146.6 %copy-start.62 = (bf16[3,8]{1,0:T(4,128)(2,1)}, bf16[3,8]{1,0:T(4,128)(2,1)S(1)}, u32[]{:S(2)}) copy-start(bf16[3,8]{1,0:T(4,128)(2,1)S(1)} %get-tuple-element.228) | copy-start | bytes 148
  20.2 2959.8 %copy-start.42 = (f32[3,8]{1,0:T(4,128)}, f32[3,8]{1,0:T(4,128)S(1)}, u32[]{:S(2)}) copy-start(f32[3,8]{1,0:T(4,128)S(1)} %get-tuple-element.229) | copy-start | bytes 292
  20.9 399.1 %copy-start.76 = (bf16[3,32]{1,0:T(4,128)(2,1)}, bf16[3,32]{1,0:T(4,128)(2,1)S(1)}, u32[]{:S(2)}) copy-start(bf16[3,32]{1,0:T(4,128)(2,1)S(1)} %get-tuple-element.227) | copy-start | bytes 580
  21.0 2857.3 %copy-start.46 = (f32[3,32]{1,0:T(4,128)}, f32[3,32]{1,0:T(4,128)S(1)}, u32[]{:S(2)}) copy-start(f32[3,32]{1,0:T(4,128)S(1)} %get-tuple-element.226) | copy-start | bytes 1156
  21.0 535.9 %copy-start.88 = (f32[64]{0:T(128)}, f32[64]{0:T(128)S(1)}, u32[]{:S(2)}) copy-start(f32[64]{0:T(128)S(1)} %get-tuple-element.258) | copy-start | bytes 772
  21.0 535.9 %copy-start.103 = (f32[64]{0:T(128)}, f32[64]{0:T(128)S(1)}, u32[]{:S(2)}) copy-start(f32[64]{0:T(128)S(1)} %get-tuple-element.259) | copy-start | bytes 772
  472.3 68.6 %copy-start.15 = (bf16[3,8,14,14,128]{4,1,3,2,0:T(8,128)(2,1)}, bf16[3,8,14,14,128]{4,1,3,2,0:T(8,128)(2,1)S(1)}, u32[]{:S(2)}) copy-start(bf16[3,8,14,14,128]{4,1,3,2,0:T(8,128)(2,1)S(1)} %slice.487) | copy-start | bytes 3612676
  492.7 47.7 %copy-start.17 = (bf16[3,8,14,14,128]{4,1,3,2,0:T(8,128)(2,1)}, bf16[3,8,14,14,128]{4,1,3,2,0:T(8,128)(2,1)S(1)}, u32[]{:S(2)}) copy-start(bf16[3,8,14,14,128]{4,1,3,2,0:T(8,128)(2,1)S(1)} %slice.485) | copy-start | bytes 3612676
  565.5 562.8 %all-gather.8.cloned.1.call-start = ((), (), s32[]{:S(2)}) async-start(), calls=%async_computation.6 | async-start | bytes 13762560 | tf_op jit(solution)/shard_map/all_gather | solution.py:298
  569.3 967.9 %all-gather.14.cloned.1.call-start = ((), (), s32[]{:S(2)}) async-start(), calls=%async_computation.9 | async-start | bytes 27525120 | tf_op jit(solution)/shard_map/all_gather | solution.py:309
  569.6 571.7 %copy-start.44 = (bf16[3,256,64]{1,2,0:T(8,128)(2,1)}, bf16[3,256,64]{1,2,0:T(8,128)(2,1)S(1)}, u32[]{:S(2)}) copy-start(bf16[3,256,64]{1,2,0:T(8,128)(2,1)S(1)} %convert_element_type.230) | copy-start | bytes 294916
  571.0 567.3 %copy-start.28 = (bf16[3,1024,64]{1,2,0:T(8,128)(2,1)}, bf16[3,1024,64]{1,2,0:T(8,128)(2,1)S(1)}, u32[]{:S(2)}) copy-start(bf16[3,1024,64]{1,2,0:T(8,128)(2,1)S(1)} %convert_element_type.224) | copy-start | bytes 1179652
  571.0 587.3 %copy-start.82 = (f32[64]{0:T(128)}, f32[64]{0:T(128)S(1)}, u32[]{:S(2)}) copy-start(f32[64]{0:T(128)S(1)} %get-tuple-element.248) | copy-start | bytes 772
  571.0 587.3 %copy-start.90 = (f32[64]{0:T(128)}, f32[64]{0:T(128)S(1)}, u32[]{:S(2)}) copy-start(f32[64]{0:T(128)S(1)} %get-tuple-element.247) | copy-start | bytes 772
  958.8 182.6 %copy-start.5 = (bf16[3,8,14,14,256]{4,3,2,1,0:T(8,128)(2,1)}, bf16[3,8,14,14,256]{4,3,2,1,0:T(8,128)(2,1)S(1)}, u32[]{:S(2)}) copy-start(bf16[3,8,14,14,256]{4,3,2,1,0:T(8,128)(2,1)S(1)} %copy.605) | copy-start | bytes 7225348
  1166.8 557.6 %reduce-scatter.15.cloned.1.call-start = ((), (), s32[]{:S(2)}) async-start(), calls=%async_computation.11 | async-start | bytes 13762560 | tf_op jit(solution)/shard_map/reduce_scatter | solution.py:322
  1195.4 718.7 %reduce-scatter.13.cloned.1.call-start = ((), (), s32[]{:S(2)}) async-start(), calls=%async_computation.10 | async-start | bytes 13762560 | tf_op jit(solution)/shard_map/reduce_scatter | solution.py:319
  1593.3 697.4 %all-gather.20.cloned.1.call-start = ((), (), s32[]{:S(2)}) async-start(), calls=%async_computation.15 | async-start | bytes 27525120 | tf_op jit(solution)/shard_map/all_gather | solution.py:232
  1603.9 878.9 %all-gather.16.cloned.1.call-start = ((), (), s32[]{:S(2)}) async-start(), calls=%async_computation.12 | async-start | bytes 13762560 | tf_op jit(solution)/shard_map/all_gather | solution.py:359
  1979.0 695.6 %all-gather.18.cloned.1.call-start = ((), (), s32[]{:S(2)}) async-start(), calls=%async_computation.14 | async-start | bytes 13762560 | tf_op jit(solution)/shard_map/all_gather | solution.py:360
  2346.7 377.3 %reduce-scatter.19.cloned.1.call-start = ((), (), s32[]{:S(2)}) async-start(), calls=%async_computation.16 | async-start | bytes 3031040
  2347.0 135.8 %copy-start.8 = (f32[3,8,14,14,64]{4,3,2,1,0:T(8,128)S(1)}, f32[3,8,14,14,64]{4,3,2,1,0:T(8,128)}, u32[]{:S(2)}) copy-start(f32[3,8,14,14,64]{4,3,2,1,0:T(8,128)} %get-tuple-element.282) | copy-start | bytes 3612676
  2366.8 141.7 %copy-start.93 = (f32[2,2,64]{2,1,0:T(2,128)S(1)}, f32[2,2,64]{2,1,0:T(2,128)}, u32[]{:S(2)}) copy-start(f32[2,2,64]{2,1,0:T(2,128)} %param.38) | copy-start | bytes 3076
  2649.5 288.5 %reduce-scatter.21.cloned.1.call-start = ((), (), s32[]{:S(2)}) async-start(), calls=%async_computation.17 | async-start | bytes 3031040
  2878.2 408.5 %all-reduce.22.cloned.1.call-start = ((), (), s32[]{:S(2)}) async-start(), calls=%async_computation.19 | async-start | bytes 3309568 | tf_op jit(solution)/shard_map/psum | solution.py:463
  2997.4 301.6 %reduce-scatter.23.cloned.1.call-start = ((), (), s32[]{:S(2)}) async-start(), calls=%async_computation.18 | async-start | bytes 6021120
  3155.0 274.1 %reduce-scatter.17.cloned.1.call-start = ((), (), s32[]{:S(2)}) async-start(), calls=%async_computation.13 | async-start | bytes 13762560 | tf_op jit(solution)/shard_map/reduce_scatter | solution.py:401
  3334.3 94.8 %copy-start.41 = (f32[256,1024]{1,0:T(8,128)S(1)}, f32[256,1024]{1,0:T(8,128)}, u32[]{:S(2)}) copy-start(f32[256,1024]{1,0:T(8,128)} %param.33) | copy-start | bytes 3145732
  3334.3 94.8 %copy-start.43 = (f32[3,8]{1,0:T(4,128)S(1)}, f32[3,8]{1,0:T(4,128)}, u32[]{:S(2)}) copy-start(f32[3,8]{1,0:T(4,128)} %copy-done.42) | copy-start | bytes 292
  (135 other events, 1159.0 us)
Sparse Core Ops, SparseCore 0:
  18.0 376.6 all-gather.9
  565.6 370.6 all-gather.11
  937.9 190.4 all-gather.7
  1166.9 370.2 all-gather.13
  1539.4 184.8 reduce-scatter.14
  1726.6 187.5 reduce-scatter.12
  1915.7 374.9 all-gather.19
  2292.3 190.4 all-gather.15
  2484.3 190.1 all-gather.17
  2676.7 47.2 reduce-scatter.18
  2878.3 46.9 reduce-scatter.20
  2997.6 59.1 all-reduce.21
  3155.1 84.7 reduce-scatter.22
  3242.1 186.9 reduce-scatter.16
where the time goes:
time: 3460 us; the launch traced here: 3450 us
  waiting for transfers between devices  1990 us (58%)
  local copies, waits for them, and re-layouts  644 us (19%)
  matrix products  475 us (14%)
  other arithmetic  177 us (5%)
  blocking collectives  133 us (4%)
    all_gather x1, waiting for transfers between devices, local(): lax.all_gather(fast_input, 'chan', axis=4, tiled=True)  374 us
    all_gather x1, waiting for transfers between devices, local(): lax.all_gather(lateral_hidden, 'chan', axis=4, tiled=True)  365 us
    unnamed x321, local copies, waits for them, and re-layouts  349 us
    all_gather x1, waiting for transfers between devices, local(): hidden_whole = lax.all_gather(slow_hidden, 'chan', axis=4, tiled=True)  316 us
    all_gather x1, waiting for transfers between devices, local(): lax.all_gather(fast_cotangent, 'chan', axis=4, tiled=True)  312 us
    dot_general x35, matrix products, mix_back(): jnp.einsum('cthwo,io->cthwi', upstream, kernel, preferred_element_type=jn...  226 us
    reduce_scatter x1, waiting for transfers between devices, local(): lax.psum_scatter(widened_part.astype(jnp.bfloat16), 'chan', scatter_dimen...  190 us
    all_gather x1, waiting for transfers between devices, local(): lax.all_gather(slow_x, 'chan', axis=4, tiled=True)  165 us
  transfers between devices with their start and end apart: 14, of which 11 were waited for; matrix products, arithmetic and copies ran while one was open for 26% of the time, Pallas kernels for 0%

commit v1 on v0

v1 whole, which is shorter than its diff:
```python
import functools

import jax
import jax.numpy as jnp
from jax import lax
from jax.experimental import pallas as pl
from jax.experimental.pallas import tpu as pltpu
from jax.sharding import PartitionSpec as P

F32 = jnp.float32
BF16 = jnp.bfloat16
EPSILON = 1e-05
ROOT = 0.7978845608028654
CUBIC = 0.044715
BIG = 49
SMALL = 7


def gelu(v):
    return 0.5 * v * (1.0 + jnp.tanh(ROOT * (v * (1.0 + CUBIC * (v * v)))))


def gelu_slope(v):
    square = v * v
    th = jnp.tanh(ROOT * (v * (1.0 + CUBIC * square)))
    half = 0.5 * (1.0 + th)
    return half + (0.5 * ROOT) * v * (1.0 - th * th) * (1.0 + 3.0 * CUBIC * square)


def gelu_pair(v):
    square = v * v
    th = jnp.tanh(ROOT * (v * (1.0 + CUBIC * square)))
    half = 0.5 * (1.0 + th)
    slope = half + (0.5 * ROOT) * v * (1.0 - th * th) * (1.0 + 3.0 * CUBIC * square)
    return v * half, slope


def rows(v):
    return v.reshape(v.shape[0] * v.shape[1], v.shape[2])


def cells(v):
    return v.reshape(v.shape[0] // 8, 8, v.shape[1])


def rows_bf(v):
    return rows(v.astype(F32)).astype(BF16)


def wide(mask, width):
    repeats = width // 128
    return mask if repeats == 1 else jnp.concatenate([mask] * repeats, axis=-1)


def nn(a, b):
    return jnp.dot(a, b, preferred_element_type=F32)


def nt(a, b):
    return lax.dot_general(a, b, (((1,), (1,)), ((), ())), preferred_element_type=F32)


def later(v):
    rolled = pltpu.roll(v, 1, 1)
    return jnp.where(lax.broadcasted_iota(jnp.int32, v.shape, 1) == 0, 0.0, rolled)


def sooner(v):
    rolled = pltpu.roll(v, 7, 1)
    return jnp.where(lax.broadcasted_iota(jnp.int32, v.shape, 1) == 7, 0.0, rolled)


def folded(v):
    out = []
    for block in range(v.shape[-1] // 128):
        part = v[:, 128 * block : 128 * block + 128]
        part = part + pltpu.roll(part, 64, 1)
        out.append(part + pltpu.roll(part, 32, 1))
    return out[0] if len(out) == 1 else jnp.concatenate(out, axis=-1)


def scale_of(sums, gains, inv_n):
    center = sums[0:1] * inv_n
    spread = sums[1:2] * inv_n - center * center
    inv_std = lax.rsqrt(spread + EPSILON)
    factor = gains[0:1] * inv_std
    return factor, gains[1:2] - center * factor, center, inv_std


def slope_of(slopes, factor, center, inv_std, inv_n):
    k1 = factor * slopes[1:2] * inv_n * inv_std
    k0 = factor * slopes[0:1] * inv_n - k1 * center
    return k0, k1


def down(v):
    return jnp.sum(v, axis=0)


def flat(v):
    return jnp.sum(v, axis=0, keepdims=True)


def steps(count, step, body, carry):
    return lax.fori_loop(0, count // step, lambda i, c: body(i * step, c), carry)


def call(kernel, outs, args, scratch=(), smem=0, flops=0, name=None):
    count = len(args)
    specs = [
        pl.BlockSpec(memory_space=pltpu.SMEM if i < smem else pltpu.VMEM) for i in range(count)
    ]
    total = sum(a.size * a.dtype.itemsize for a in args)
    total += sum(o.size * o.dtype.itemsize for o in outs)
    return pl.pallas_call(
        kernel,
        out_shape=tuple(outs),
        in_specs=specs,
        out_specs=tuple(pl.BlockSpec(memory_space=pltpu.VMEM) for _ in outs),
        scratch_shapes=list(scratch),
        compiler_params=pltpu.CompilerParams(vmem_limit_bytes=56 * 1024 * 1024),
        cost_estimate=pl.CostEstimate(flops=flops, bytes_accessed=total, transcendentals=0),
        name=name,
    )(*args)


def shape(dims, dtype=F32):
    return jax.ShapeDtypeStruct(dims, dtype)


def pack_kernel(per_clip, chunk, x_ref, mask_ref, out_ref, tmp_ref):
    def body(i, carry):
        begin = i * chunk
        tmp_ref[...] = x_ref[pl.ds(begin, chunk)].astype(F32).reshape(chunk * 32, 32)
        parts = [tmp_ref[pl.ds(r, chunk * 8, stride=4), :] for r in range(4)]
        joined = cells(jnp.concatenate(parts, axis=1))
        out_ref[pl.ds(begin, chunk)] = (joined * mask_ref[i // per_clip][None]).astype(BF16)
        return carry

    lax.fori_loop(0, x_ref.shape[0] // chunk, body, 0)


def unpack_kernel(chunk, x_ref, out_ref, tmp_ref):
    def body(i, carry):
        begin = i * chunk
        joined = rows(x_ref[pl.ds(begin, chunk)].astype(F32))
        for r in range(4):
            tmp_ref[pl.ds(r, chunk * 8, stride=4), :] = joined[:, 32 * r : 32 * r + 32]
        out_ref[pl.ds(begin, chunk)] = tmp_ref[...].reshape(chunk, 32, 32).astype(BF16)
        return carry

    lax.fori_loop(0, x_ref.shape[0] // chunk, body, 0)


def fast_first_kernel(fx_ref, mask_ref, w_ref, fa_ref, lp_ref, sums_ref):
    def body(p, carry):
        x = jnp.concatenate([rows_bf(fx_ref[z, pl.ds(p, BIG)]) for z in range(4)], axis=1)
        acc = cells(nn(x, w_ref[...]))
        fa = acc[:, :, 0:128] + later(acc[:, :, 128:256]) + sooner(acc[:, :, 256:384])
        lp = acc[:, :, 384:640] + later(acc[:, :, 640:896])
        fa_ref[pl.ds(p, BIG)] = fa
        lp_ref[pl.ds(p, BIG)] = lp
        mask = mask_ref[pl.ds(p, BIG)]
        fm, lm = fa * mask, lp * wide(mask, 256)
        return tuple(c + down(v) for c, v in zip(carry, (fm, fm * fa, lm, lm * lp)))

    zero = (jnp.zeros((8, 128), F32),) * 2 + (jnp.zeros((8, 256), F32),) * 2
    a, b, c, d = steps(fa_ref.shape[0], BIG, body, zero)
    sums_ref[0:1, 0:128], sums_ref[1:2, 0:128] = flat(a), flat(b)
    sums_ref[0:1, 128:384], sums_ref[1:2, 128:384] = flat(c), flat(d)


def fill_padded(y_refs, masks_ref, out_ref, value, halo, size):
    for (lo_ref, begin, count, step) in (
        (y_refs[0], 0, halo, 5),
        (y_refs[1], halo, size, SMALL),
        (y_refs[2], halo + size, halo, 5),
    ):
        def body(p, carry, lo_ref=lo_ref, begin=begin, step=step):
            v = value(lo_ref, p, step)
            for k in range(3):
                mask = wide(masks_ref[k, pl.ds(begin + p, step)], v.shape[-1])
                out_ref[k, pl.ds(begin + p, step)] = v * mask
            return carry

        steps(count, step, body, 0)


def conv_rows(pad_ref, edge_ref, weight, p, halo, row_len, dot):
    total = None
    for i in range(3):
        begin = p + halo + row_len * (i - 1)
        taps = [rows(pad_ref[j, pl.ds(begin + j - 1, BIG)]).astype(BF16) for j in range(3)]
        acc = None
        for j in range(3):
            part = dot(taps[j], weight(i, j))
            acc = part if acc is None else acc + part
        acc = cells(acc)
        if i != 1:
            acc = acc * wide(edge_ref[i // 2, pl.ds(p, BIG)], acc.shape[-1])
        total = acc if total is None else total + acc
    return total


def conv_kernel(halo, row_len, off, fold, n_ref, sums_ref, gains_ref, lo_ref, y_ref, hi_ref, masks_ref,
                edge_ref, w_ref, act_ref, out_ref, osums_ref, pad_ref):
    size, width = y_ref.shape[0], y_ref.shape[2]
    sums = sums_ref[:, off : off + width]
    sums = folded(sums) if fold else sums
    factor, shift, _, _ = scale_of(sums, gains_ref[...], n_ref[0])

    def value(ref, p, step):
        return gelu(ref[pl.ds(p, step)] * factor[None] + shift[None]).astype(BF16).astype(F32)

    fill_padded((lo_ref, y_ref, hi_ref), masks_ref, pad_ref, value, halo, size)

    def copy(p, carry):
        for k in range(3):
            act_ref[k, pl.ds(p, 3)] = pad_ref[k, pl.ds(p, 3)].astype(BF16)
        return carry

    steps(size + 2 * halo, 3, copy, 0)

    def body(p, carry):
        total = conv_rows(pad_ref, edge_ref, lambda i, j: w_ref[3 * i + j], p, halo, row_len, nn if fold else nt)
        out_ref[pl.ds(p, BIG)] = total
        masked = total * wide(masks_ref[1, pl.ds(halo + p, BIG)], width)
        return carry[0] + down(masked), carry[1] + down(masked * total)

    a, b = steps(size, BIG, body, (jnp.zeros((8, width), F32),) * 2)
    osums_ref[0:1], osums_ref[1:2] = flat(a), flat(b)


def slow_first_kernel(n_ref, xs_ref, lp_ref, lsums_ref, gains_ref, mask_ref, w_ref, wl_ref,
                      x_ref, lat_ref, sa_ref, sums_ref):
    size = lp_ref.shape[0]
    factor, shift, _, _ = scale_of(lsums_ref[:, 128:384], gains_ref[...], n_ref[0])

    def fill(p, carry):
        mask = wide(mask_ref[pl.ds(p, SMALL)], 256)
        lat_ref[pl.ds(p, SMALL)] = (gelu(lp_ref[pl.ds(p, SMALL)] * factor[None] + shift[None]) * mask).astype(BF16)
        for z in range(4):
            v = xs_ref[z, pl.ds(p, SMALL)].astype(F32) * mask
            x_ref[pl.ds(p, SMALL), :, 256 * z : 256 * z + 256] = v.astype(BF16)
        return carry

    steps(size, SMALL, fill, 0)

    def body(p, carry):
        acc = nt(rows_bf(x_ref[pl.ds(p, BIG)]), w_ref[...]) + nt(rows_bf(lat_ref[pl.ds(p, BIG)]), wl_ref[...])
        acc = cells(acc)
        sa = later(acc[:, :, 0:256]) + acc[:, :, 256:512] + sooner(acc[:, :, 512:768])
        sa_ref[pl.ds(p, BIG)] = sa
        masked = sa * wide(mask_ref[pl.ds(p, BIG)], 256)
        return carry[0] + down(masked), carry[1] + down(masked * sa)

    a, b = steps(size, BIG, body, (jnp.zeros((8, 256), F32),) * 2)
    sums_ref[0:1], sums_ref[1:2] = flat(a), flat(b)


def bypass_kernel(x_ref, lat_ref, mask_ref, w_ref, wl_ref, sp_ref, sums_ref):
    def body(p, carry):
        sp = cells(nn(rows_bf(x_ref[pl.ds(p, BIG)]), w_ref[...]) + nn(rows_bf(lat_ref[pl.ds(p, BIG)]), wl_ref[...]))
        sp_ref[pl.ds(p, BIG)] = sp
        masked = sp * wide(mask_ref[pl.ds(p, BIG)], sp.shape[-1])
        return carry[0] + down(masked), carry[1] + down(masked * sp)

    a, b = steps(sp_ref.shape[0], BIG, body, (jnp.zeros((8, sp_ref.shape[2]), F32),) * 2)
    sums_ref[0:1], sums_ref[1:2] = flat(a), flat(b)


def expand_kernel(fold, n_ref, y_ref, sums_ref, gains_ref, mask_ref, w_ref, h_ref, out_ref, osums_ref):
    size, width = y_ref.shape[0], y_ref.shape[2]
    sums = folded(sums_ref[...]) if fold else sums_ref[...]
    factor, shift, _, _ = scale_of(sums, gains_ref[...], n_ref[0])

    def fill(p, carry):
        mask = wide(mask_ref[pl.ds(p, SMALL)], width)
        h_ref[pl.ds(p, SMALL)] = (gelu(y_ref[pl.ds(p, SMALL)] * factor[None] + shift[None]) * mask).astype(BF16)
        return carry

    steps(size, SMALL, fill, 0)

    def body(p, carry):
        out = cells(nn(rows_bf(h_ref[pl.ds(p, BIG)]), w_ref[...]))
        out_ref[pl.ds(p, BIG)] = out
        masked = out * wide(mask_ref[pl.ds(p, BIG)], out.shape[-1])
        return carry[0] + down(masked), carry[1] + down(masked * out)

    a, b = steps(size, BIG, body, (jnp.zeros((8, out_ref.shape[2]), F32),) * 2)
    osums_ref[0:1], osums_ref[1:2] = flat(a), flat(b)


def fast_out_kernel(n_ref, fc_ref, sums_ref, gains_ref, mask_ref, fx_ref, cot_ref, out_ref, up_ref, slopes_ref):
    size = fc_ref.shape[0]
    factor, shift, center, inv_std = scale_of(folded(sums_ref[...]), gains_ref[...], n_ref[0])
    for z in range(4):
        lanes = slice(128 * z, 128 * z + 128)
        fz, sz, cz, rz = (v[:, lanes][None] for v in (factor, shift, center, inv_std))

        def body(p, carry, z=z, lanes=lanes, fz=fz, sz=sz, cz=cz, rz=rz):
            y = fc_ref[pl.ds(p, SMALL), :, lanes]
            mask = mask_ref[pl.ds(p, SMALL)]
            total = y * fz + sz + fx_ref[z, pl.ds(p, SMALL)].astype(F32)
            value, slope = gelu_pair(total)
            out_ref[z, pl.ds(p, SMALL)] = (value * mask).astype(BF16)
            up = slope * (cot_ref[z, pl.ds(p, SMALL)].astype(F32) * mask)
            up_ref[pl.ds(p, SMALL), :, lanes] = up
            return carry[0] + down(up), carry[1] + down(up * ((y - cz) * rz))

        a, b = steps(size, SMALL, body, (jnp.zeros((8, 128), F32),) * 2)
        slopes_ref[0:1, lanes], slopes_ref[1:2, lanes] = flat(a), flat(b)


def slow_out_kernel(n_ref, sc_ref, sp_ref, csums_ref, psums_ref, gains_ref, mask_ref, cot_ref, out_ref, up_ref, slopes_ref):
    size = sc_ref.shape[0]
    cf, cs, cc, cr = scale_of(csums_ref[...], gains_ref[0], n_ref[0])
    pf, ps, pc, pr = scale_of(psums_ref[...], gains_ref[1], n_ref[0])
    for z in range(4):
        lanes = slice(256 * z, 256 * z + 256)
        vecs = [v[:, lanes][None] for v in (cf, cs + ps, cc, cr, pf, pc, pr)]

        def body(p, carry, z=z, lanes=lanes, vecs=vecs):
            cf, shift, cc, cr, pf, pc, pr = vecs
            yc, yp = sc_ref[pl.ds(p, SMALL), :, lanes], sp_ref[pl.ds(p, SMALL), :, lanes]
            mask = wide(mask_ref[pl.ds(p, SMALL)], 256)
            value, slope = gelu_pair(yc * cf + yp * pf + shift)
            out_ref[z, pl.ds(p, SMALL)] = (value * mask).astype(BF16)
            up = slope * (cot_ref[z, pl.ds(p, SMALL)].astype(F32) * mask)
            up_ref[pl.ds(p, SMALL), :, lanes] = up
            return (carry[0] + down(up), carry[1] + down(up * ((yc - cc) * cr)), carry[2] + down(up * ((yp - pc) * pr)))

        a, b, c = steps(size, SMALL, body, (jnp.zeros((8, 256), F32),) * 3)
        slopes_ref[0:1, lanes], slopes_ref[1:2, lanes], slopes_ref[2:3, lanes] = flat(a), flat(b), flat(c)


def expand_back_kernel(fold, n_ref, up_ref, y_ref, sums_ref, gains_ref, slopes_ref, z_ref, zsums_ref, zgains_ref, mask_ref,
                       w_ref, dy_ref, dz_ref, oslopes_ref):
    size, width, inner = y_ref.shape[0], y_ref.shape[2], z_ref.shape[2]
    fix = folded if fold else (lambda v: v)
    factor, shift, center, inv_std = scale_of(fix(sums_ref[...]), gains_ref[...], n_ref[0])
    k0, k1 = slope_of(fix(slopes_ref[...]), factor, center, inv_std, n_ref[0])

    def fill(p, carry):
        mask = mask_ref[pl.ds(p, SMALL)]
        for q in range(width // 128):
            lanes = slice(128 * q, 128 * q + 128)
            y = y_ref[pl.ds(p, SMALL), :, lanes]
            dy = up_ref[pl.ds(p, SMALL), :, lanes] * factor[:, lanes][None]
            dy = dy - mask * (k0[:, lanes][None] + k1[:, lanes][None] * y)
            dy_ref[pl.ds(p, SMALL), :, lanes] = dy.astype(BF16)
        return carry

    steps(size, SMALL, fill, 0)
    zf, zs, zc, zr = scale_of(fix(zsums_ref[...]), zgains_ref[...], n_ref[0])

    def body(p, carry):
        dh = cells(nt(rows_bf(dy_ref[pl.ds(p, BIG)]), w_ref[...]))
        z = z_ref[pl.ds(p, BIG)]
        dz = gelu_slope(z * zf[None] + zs[None]) * dh * wide(mask_ref[pl.ds(p, BIG)], inner)
        dz_ref[pl.ds(p, BIG)] = dz
        return carry[0] + down(dz), carry[1] + down(dz * ((z - zc[None]) * zr[None]))

    a, b = steps(size, BIG, body, (jnp.zeros((8, inner), F32),) * 2)
    oslopes_ref[0:1], oslopes_ref[1:2] = flat(a), flat(b)


def bypass_back_kernel(n_ref, up_ref, y_ref, sums_ref, gains_ref, slopes_ref, mask_ref, w_ref, wl_ref, dy_ref, dx_ref, dl_ref):
    size, width = y_ref.shape[0], y_ref.shape[2]
    factor, shift, center, inv_std = scale_of(sums_ref[...], gains_ref[...], n_ref[0])
    k0, k1 = slope_of(slopes_ref[...], factor, center, inv_std, n_ref[0])

    def fill(p, carry):
        mask = mask_ref[pl.ds(p, SMALL)]
        for q in range(width // 128):
            lanes = slice(128 * q, 128 * q + 128)
            y = y_ref[pl.ds(p, SMALL), :, lanes]
            dy = up_ref[pl.ds(p, SMALL), :, lanes] * factor[:, lanes][None]
            dy = dy - mask * (k0[:, lanes][None] + k1[:, lanes][None] * y)
            dy_ref[pl.ds(p, SMALL), :, lanes] = dy.astype(BF16)
        return carry

    steps(size, SMALL, fill, 0)

    def body(p, carry):
        dy = rows_bf(dy_ref[pl.ds(p, BIG)])
        dx_ref[pl.ds(p, BIG)] = cells(nt(dy, w_ref[...]))
        dl_ref[pl.ds(p, BIG)] = cells(nt(dy, wl_ref[...]))
        return carry

    steps(size, BIG, body, 0)


def conv_back_kernel(halo, row_len, off, fold, n_ref, ysums_ref, ygains_ref, slopes_ref, ylo_ref, y_ref, yhi_ref, dlo_ref, d_ref,
                     dhi_ref, masks_ref, edge_ref, w_ref, z_ref, zsums_ref, zgains_ref, dy_ref, dz_ref, oslopes_ref, pad_ref):
    size, width = y_ref.shape[0], y_ref.shape[2]
    fix = folded if fold else (lambda v: v)
    factor, shift, center, inv_std = scale_of(fix(ysums_ref[...]), ygains_ref[...], n_ref[0])
    k0, k1 = slope_of(fix(slopes_ref[...]), factor, center, inv_std, n_ref[0])
    uppers = {id(ylo_ref): dlo_ref, id(y_ref): d_ref, id(yhi_ref): dhi_ref}

    def value(ref, p, step):
        dy = uppers[id(ref)][pl.ds(p, step)] * factor[None] - (k0[None] + k1[None] * ref[pl.ds(p, step)])
        return dy.astype(BF16).astype(F32)

    fill_padded((ylo_ref, y_ref, yhi_ref), masks_ref, pad_ref, value, halo, size)

    def copy(p, carry):
        dy = pad_ref[1, pl.ds(halo + p, SMALL)]
        dy_ref[1, pl.ds(p, SMALL)] = dy.astype(BF16)
        for k in (0, 1):
            dy_ref[2 * k, pl.ds(p, SMALL)] = (dy * wide(edge_ref[k, pl.ds(p, SMALL)], width)).astype(BF16)
        return carry

    steps(size, SMALL, copy, 0)
    zf, zs, zc, zr = scale_of(fix(zsums_ref[:, off : off + width]), zgains_ref[...], n_ref[0])

    def body(p, carry):
        dh = conv_rows(pad_ref, edge_ref, lambda i, j: w_ref[8 - 3 * i - j], p, halo, row_len, nt if fold else nn)
        z = z_ref[pl.ds(p, BIG)]
        dz = gelu_slope(z * zf[None] + zs[None]) * dh * wide(masks_ref[1, pl.ds(halo + p, BIG)], width)
        dz_ref[pl.ds(p, BIG)] = dz
        return carry[0] + down(dz), carry[1] + down(dz * ((z - zc[None]) * zr[None]))

    a, b = steps(size, BIG, body, (jnp.zeros((8, width), F32),) * 2)
    oslopes_ref[0:1], oslopes_ref[1:2] = flat(a), flat(b)


def slow_back_kernel(n_ref, dz_ref, y_ref, sums_ref, gains_ref, slopes_ref, mask_ref, w_ref, wl_ref, dx_ref, dl_ref,
                     lp_ref, lsums_ref, lgains_ref, taps_ref, out_ref, dzl_ref, oslopes_ref):
    size = y_ref.shape[0]
    factor, shift, center, inv_std = scale_of(sums_ref[...], gains_ref[...], n_ref[0])
    k0, k1 = slope_of(slopes_ref[...], factor, center, inv_std, n_ref[0])

    def fill(p, carry):
        mask = wide(mask_ref[pl.ds(p, SMALL)], 256)
        dy = dz_ref[pl.ds(p, SMALL)] * factor[None]
        dy = dy - mask * (k0[None] + k1[None] * y_ref[pl.ds(p, SMALL)])
        taps_ref[pl.ds(p, SMALL), :, 0:256] = sooner(dy).astype(BF16)
        taps_ref[pl.ds(p, SMALL), :, 256:512] = dy.astype(BF16)
        taps_ref[pl.ds(p, SMALL), :, 512:768] = later(dy).astype(BF16)
        return carry

    steps(size, SMALL, fill, 0)
    lf, ls, lc, lr = scale_of(lsums_ref[:, 128:384], lgains_ref[...], n_ref[0])

    def body(p, carry):
        taps = rows_bf(taps_ref[pl.ds(p, BIG)])
        mask = wide(mask_ref[pl.ds(p, BIG)], 256)
        for z in range(4):
            lanes = slice(256 * z, 256 * z + 256)
            dx = cells(nn(taps, w_ref[:, lanes])) + dx_ref[pl.ds(p, BIG), :, lanes]
            out_ref[z, pl.ds(p, BIG)] = (dx * mask).astype(BF16)
        dl = cells(nn(taps, wl_ref[...])) + dl_ref[pl.ds(p, BIG)]
        y = lp_ref[pl.ds(p, BIG)]
        dz = gelu_slope(y * lf[None] + ls[None]) * dl * mask
        dzl_ref[pl.ds(p, BIG)] = dz
        return carry[0] + down(dz), carry[1] + down(dz * ((y - lc[None]) * lr[None]))

    a, b = steps(size, BIG, body, (jnp.zeros((8, 256), F32),) * 2)
    oslopes_ref[0:1], oslopes_ref[1:2] = flat(a), flat(b)


def fast_back_kernel(n_ref, sums_ref, fgains_ref, lgains_ref, fslopes_ref, lslopes_ref, dzf_ref, fa_ref, dzl_ref, lp_ref, up_ref,
                     mask_ref, w_ref, taps_ref, out_ref):
    size = fa_ref.shape[0]
    ff, fs, fc, fr = scale_of(folded(sums_ref[:, 0:128]), fgains_ref[...], n_ref[1])
    f0, f1 = slope_of(folded(fslopes_ref[...]), ff, fc, fr, n_ref[1])
    lf, ls, lc, lr = scale_of(sums_ref[:, 128:384], lgains_ref[...], n_ref[0])
    l0, l1 = slope_of(lslopes_ref[...], lf, lc, lr, n_ref[0])

    def fill(p, carry):
        mask = mask_ref[pl.ds(p, SMALL)]
        dy = dzf_ref[pl.ds(p, SMALL)] * ff[None] - mask * (f0[None] + f1[None] * fa_ref[pl.ds(p, SMALL)])
        taps_ref[pl.ds(p, SMALL), :, 0:128] = dy.astype(BF16)
        taps_ref[pl.ds(p, SMALL), :, 128:256] = sooner(dy).astype(BF16)
        taps_ref[pl.ds(p, SMALL), :, 256:384] = later(dy).astype(BF16)
        mask = wide(mask, 256)
        dy = dzl_ref[pl.ds(p, SMALL)] * lf[None] - mask * (l0[None] + l1[None] * lp_ref[pl.ds(p, SMALL)])
        taps_ref[pl.ds(p, SMALL), :, 384:640] = dy.astype(BF16)
        taps_ref[pl.ds(p, SMALL), :, 640:896] = sooner(dy).astype(BF16)
        return carry

    steps(size, SMALL, fill, 0)

    def body(p, carry):
        dx = cells(nt(rows_bf(taps_ref[pl.ds(p, BIG)]), w_ref[...]))
        mask = mask_ref[pl.ds(p, BIG)]
        for z in range(4):
            lanes = slice(128 * z, 128 * z + 128)
            out_ref[z, pl.ds(p, BIG)] = ((dx[:, :, lanes] + up_ref[pl.ds(p, BIG), :, lanes]) * mask).astype(BF16)
        return carry

    steps(size, BIG, body, 0)


def swap(tree, axis, size, distance):
    pairs = [(i, i ^ distance) for i in range(size)]
    return jax.tree.map(lambda v: lax.ppermute(v, axis, pairs), tree)


def add(a, b):
    return jax.tree.map(jnp.add, a, b)


def stages(size, first_alone):
    bits = [1 << i for i in range(size.bit_length() - 1)]
    out = []
    if first_alone and bits:
        out.append(bits[:1])
        bits = bits[1:]
    while bits:
        out.append(bits[:2])
        bits = bits[2:]
    return out


def everywhere(tree, sizes):
    for axis, size in sizes.items():
        if size & (size - 1):
            tree = jax.tree.map(lambda v: lax.psum(v, axis), tree)
            continue
        for bits in stages(size, axis == "dp"):
            if len(bits) == 1:
                tree = add(tree, swap(tree, axis, size, bits[0]))
            else:
                a, b = bits
                near, far, both = (swap(tree, axis, size, k) for k in (a, b, a + b))
                tree = add(add(tree, near), add(far, both))
    return tree


def halos(v, halo, count):
    low = lax.ppermute(v[-halo:], "chan", [(i, i + 1) for i in range(count - 1)])
    high = lax.ppermute(v[:halo], "chan", [(i + 1, i) for i in range(count - 1)])
    return low, high


def share(parts, sizes):
    ways, blocks = sizes["dp"], sizes["chan"]
    me = lax.axis_index("dp")
    pieces = []
    for part in parts:
        lead, count, width = part.shape
        piece = lax.dynamic_slice_in_dim(part, me * (count // ways), count // ways, 1)
        pieces.append(piece.astype(BF16).reshape(-1))
    packed = jnp.concatenate(pieces)
    length = packed.shape[0]
    packed = jnp.pad(packed, (0, -length % 1024))
    whole = lax.all_gather(packed.reshape(-1, 1024), "chan", axis=0, tiled=False)
    whole = lax.all_gather(whole, "dp", axis=0, tiled=False).reshape(ways, blocks, -1)
    out, offset = [], 0
    for part in parts:
        lead, count, width = part.shape
        amount = lead * (count // ways) * width
        piece = whole[:, :, offset : offset + amount].reshape(ways, blocks, lead, count // ways, width)
        out.append(piece.transpose(2, 1, 0, 3, 4).reshape(lead, blocks * count, width))
        offset += amount
    return out


def collect(parts, sizes):
    ways, blocks = sizes["dp"], sizes["chan"]
    pieces = []
    for part in parts:
        lead, count, width = part.shape
        piece = part.astype(BF16).reshape(lead, blocks, ways, count // (blocks * ways), width)
        pieces.append(piece.transpose(2, 1, 0, 3, 4).reshape(ways, blocks, -1))
    packed = jnp.concatenate(pieces, axis=2)
    length = packed.shape[2]
    packed = jnp.pad(packed, ((0, 0), (0, 0), (0, -length % 1024)))
    mine = lax.psum_scatter(packed.reshape(ways, blocks, -1, 1024), "dp", scatter_dimension=0, tiled=False)
    mine = lax.psum_scatter(mine, "chan", scatter_dimension=0, tiled=False)
    whole = lax.all_gather(mine, "dp", axis=0, tiled=False).reshape(ways, -1)
    out, offset = [], 0
    for part in parts:
        lead, count, width = part.shape
        per = count // (blocks * ways)
        piece = whole[:, offset : offset + lead * per * width].reshape(ways, lead, per, width)
        out.append(piece.transpose(1, 0, 2, 3).reshape(lead, ways * per, width).astype(F32))
        offset += lead * per * width
    return out


def resplit(v):
    return lax.all_to_all(v, "chan", 0, 0, tiled=True)


def weight_sum(a, b):
    return jnp.einsum("pti,pto->io", a, b, preferred_element_type=F32)


def local(
    sizes,
    slow_input,
    fast_input,
    clip_counts,
    frame_counts,
    fast_reduce,
    fast_spatial,
    fast_expand,
    lateral_kernel,
    slow_reduce,
    lateral_reduce,
    slow_spatial,
    slow_expand,
    shortcut,
    lateral_shortcut,
    fast_inner_norm,
    fast_outer_norm,
    lateral_norm,
    slow_inner_norm,
    slow_outer_norm,
    slow_cotangent,
    fast_cotangent,
):
    ways = sizes["chan"]
    clips, slow_t, height, across, slow_part = slow_input.shape
    fast_t, fast_part = fast_input.shape[1], fast_input.shape[4]
    ratio = fast_t // slow_t
    area = height * across
    places = clips * area
    mine = places // ways
    halo = across + 1
    me = lax.axis_index("chan")
    wide_in = ways * slow_part

    all_clips = frame_counts.shape[0]
    live = (jnp.arange(all_clips, dtype=jnp.int32) % clips) < jnp.repeat(clip_counts, clips)
    valid = jnp.where(live, frame_counts, 0)
    count = jnp.sum(valid).astype(F32) * area
    inv_n = jnp.stack([1.0 / count, 1.0 / (count * ratio)])
    inv_slow, inv_fast = inv_n[0:1], inv_n[1:2]
    here = lax.dynamic_slice_in_dim(valid, lax.axis_index("dp") * clips, clips, 0)
    clip_mask = jnp.broadcast_to(
        (jnp.arange(slow_t)[None, :] < here[:, None]).astype(F32)[:, :, None], (clips, slow_t, 128)
    )
    place = me * mine - halo + jnp.arange(mine + 2 * halo)
    there = (place >= 0) & (place < places)
    frames = jnp.where(there, here[jnp.clip(place // area, 0, clips - 1)], 0)
    column = jnp.mod(place, across)
    row = jnp.mod(place // across, height)
    base = jnp.arange(slow_t)[None, :] < frames[:, None]
    masks = jnp.stack([base & (column != across - 1)[:, None], base, base & (column != 0)[:, None]])
    masks = jnp.broadcast_to(masks.astype(F32)[..., None], (3, mine + 2 * halo, slow_t, 128))
    own_row = row[halo : halo + mine]
    edges = jnp.stack([own_row != 0, own_row != height - 1]).astype(F32)
    edges = jnp.broadcast_to(edges[:, :, None, None], (2, mine, slow_t, 128))
    mask = masks[1, halo : halo + mine]

    chunk = 28

    def packed(v):
        v = v.transpose(0, 2, 3, 1, 4).reshape(places, fast_t, fast_part)
        (out,) = call(
            functools.partial(pack_kernel, area // chunk, chunk),
            [shape((places, slow_t, 128), BF16)],
            [v, clip_mask],
            [pltpu.VMEM((chunk * fast_t, fast_part), F32)],
            name="fast_pack",
        )
        return out.reshape(ways, mine, slow_t, 128)

    def unpacked(v):
        (out,) = call(
            functools.partial(unpack_kernel, chunk),
            [shape((places, fast_t, fast_part), BF16)],
            [v.reshape(places, slow_t, 128)],
            [pltpu.VMEM((chunk * fast_t, fast_part), F32)],
            name="fast_unpack",
        )
        return out.reshape(clips, height, across, fast_t, fast_part).transpose(0, 3, 1, 2, 4)

    def split(v):
        return v.transpose(0, 2, 3, 1, 4).reshape(ways, mine, slow_t, slow_part)

    def joined(v):
        return v.reshape(clips, height, across, slow_t, slow_part).transpose(0, 3, 1, 2, 4)

    fx = resplit(packed(fast_input))
    xs = resplit(split(slow_input))

    lat_t, red_t, lred_t = (v.transpose(0, 2, 1) for v in (lateral_kernel, slow_reduce, lateral_reduce))
    spatial_t = slow_spatial.reshape(9, slow_spatial.shape[2], -1).transpose(0, 2, 1)
    lat_w, red_w, lred_w = share([lat_t, red_t, lred_t], sizes)
    spat_w, exp_w, short_w, lshort_w = share([spatial_t, slow_expand[None], shortcut[None], lateral_shortcut[None]], sizes)
    red_w, lred_w = red_w.reshape(-1, red_w.shape[2]), lred_w.reshape(-1, lred_w.shape[2])
    exp_w, short_w, lshort_w = exp_w[0], short_w[0], lshort_w[0]

    norms = jnp.concatenate(
        [lateral_norm.reshape(-1), slow_inner_norm.reshape(-1), slow_outer_norm.reshape(-1)]
    )
    norms = lax.all_gather(norms, "chan", axis=0, tiled=False)
    lw, sw, ow = lateral_norm.shape[1], slow_inner_norm.shape[2], slow_outer_norm.shape[2]
    lat_g = norms[:, : 2 * lw].reshape(ways, 2, lw).transpose(1, 0, 2).reshape(2, -1)
    in_g = norms[:, 2 * lw : 2 * lw + 4 * sw].reshape(ways, 2, 2, sw).transpose(1, 2, 0, 3).reshape(2, 2, -1)
    out_g = norms[:, 2 * lw + 4 * sw :].reshape(ways, 2, 2, ow).transpose(1, 2, 0, 3).reshape(2, 2, -1)
    fin_g = jnp.concatenate([fast_inner_norm] * ratio, axis=2)
    fout_g = jnp.broadcast_to(fast_outer_norm.reshape(2, ways, 1, fast_part), (2, ways, ratio, fast_part)).reshape(2, -1)

    def in_blocks(w, frames_in, frames_out):
        width = next(v for line in w for v in line if v is not None).shape[1]
        blank = jnp.zeros((ways, fast_part, width), BF16)
        lines = []
        for r in range(frames_in):
            line = [blank if w[r][q] is None else w[r][q].reshape(ways, fast_part, width) for q in range(frames_out)]
            lines.append(jnp.concatenate(line, axis=2))
        return jnp.stack(lines, axis=1).reshape(ways * frames_in * fast_part, -1)

    fr = fast_reduce.astype(BF16)
    none = [None] * ratio
    main = [[fr[r - q + 1] if abs(r - q) <= 1 else None for q in range(ratio)] for r in range(ratio)]
    prev = [none] * (ratio - 1) + [[fr[0]] + none[1:]]
    after = [none[1:] + [fr[2]]] + [none] * (ratio - 1)
    taps = lat_w.transpose(0, 2, 1)
    lat_main = [[taps[2]], [taps[3]], [taps[4]], [None]]
    lat_prev = [[None], [None], [taps[0]], [taps[1]]]
    w_first = jnp.concatenate([in_blocks(v, ratio, len(v[0])) for v in (main, prev, after, lat_main, lat_prev)], axis=1)
    same = jnp.eye(ratio, dtype=BF16)
    fsp = fast_spatial.astype(BF16).reshape(9, fast_spatial.shape[2], -1)
    w_fsp = jnp.einsum("rq,kio->kriqo", same, fsp).reshape(9, 128, 128)
    fex = fast_expand.astype(BF16).reshape(-1, ways, fast_part)
    w_fex = jnp.einsum("rq,izc->rizqc", same, fex).reshape(128, -1)

    ext = mine + 2 * halo
    wide_f = ways * 128
    mid = 256
    fa, lp, sums1 = call(
        fast_first_kernel,
        [shape((mine, 8, 128)), shape((mine, 8, mid)), shape((2, 384))],
        [fx, mask, w_first],
        name="fast_first",
    )
    fa_lo, fa_hi = halos(fa, halo, ways)
    sums1 = everywhere(sums1, sizes)
    pad = [pltpu.VMEM((3, ext, 8, 128), F32)]
    h1, fb, fb_sums = call(
        functools.partial(conv_kernel, halo, across, 0, True),
        [shape((3, ext, 8, 128), BF16), shape((mine, 8, 128)), shape((2, 128))],
        [inv_fast, sums1, fin_g[0], fa_lo, fa, fa_hi, masks, edges, w_fsp],
        pad,
        smem=1,
        name="fast_second",
    )
    x, lat, sa, sa_sums = call(
        slow_first_kernel,
        [shape((mine, 8, wide_in), BF16), shape((mine, 8, mid), BF16), shape((mine, 8, mid)), shape((2, mid))],
        [inv_slow, xs, lp, sums1, lat_g, mask, red_w, lred_w],
        smem=1,
        name="slow_first",
    )
    sa_lo, sa_hi = halos(sa, halo, ways)
    sa_sums, fb_sums = everywhere((sa_sums, fb_sums), sizes)
    sp, sp_sums = call(
        bypass_kernel,
        [shape((mine, 8, wide_in)), shape((2, wide_in))],
        [x, lat, mask, short_w, lshort_w],
        name="bypass",
    )
    ha, sb, sb_sums = call(
        functools.partial(conv_kernel, halo, across, 0, False),
        [shape((3, ext, 8, mid), BF16), shape((mine, 8, mid)), shape((2, mid))],
        [inv_slow, sa_sums, in_g[0], sa_lo, sa, sa_hi, masks, edges, spat_w],
        [pltpu.VMEM((3, ext, 8, mid), F32)],
        smem=1,
        name="slow_second",
    )
    h2, fc, fc_sums = call(
        functools.partial(expand_kernel, True),
        [shape((mine, 8, 128), BF16), shape((mine, 8, wide_f)), shape((2, wide_f))],
        [inv_fast, fb, fb_sums, fin_g[1], mask, w_fex],
        smem=1,
        name="fast_third",
    )
    sb_lo, sb_hi = halos(sb, halo, ways)
    fb_lo, fb_hi = halos(fb, halo, ways)
    sb_sums, fc_sums = everywhere((sb_sums, fc_sums), sizes)
    cot = resplit(split(slow_cotangent))
    fcot = resplit(packed(fast_cotangent))
    hb, sc, sc_sums = call(
        functools.partial(expand_kernel, False),
        [shape((mine, 8, mid), BF16), shape((mine, 8, wide_in)), shape((2, wide_in))],
        [inv_slow, sb, sb_sums, in_g[1], mask, exp_w],
        smem=1,
        name="slow_third",
    )
    fast_out, dfs, fc_slopes = call(
        fast_out_kernel,
        [shape((ways, mine, 8, 128), BF16), shape((mine, 8, wide_f)), shape((2, wide_f))],
        [inv_fast, fc, fc_sums, fout_g, mask, fx, fcot],
        smem=1,
        name="fast_out",
    )
    sc_sums, sp_sums, fc_slopes = everywhere((sc_sums, sp_sums, fc_slopes), sizes)
    slow_out, dss, out_slopes = call(
        slow_out_kernel,
        [shape((ways, mine, 8, mid), BF16), shape((mine, 8, wide_in)), shape((3, wide_in))],
        [inv_slow, sc, sp, sc_sums, sp_sums, out_g, mask, cot],
        smem=1,
        name="slow_out",
    )

    dfc, dzfb, fb_slopes = call(
        functools.partial(expand_back_kernel, True),
        [shape((mine, 8, wide_f), BF16), shape((mine, 8, 128)), shape((2, 128))],
        [inv_fast, dfs, fc, fc_sums, fout_g, fc_slopes, fb, fb_sums, fin_g[1], mask, w_fex],
        smem=1,
        name="fast_third_back",
    )
    dzfb_lo, dzfb_hi = halos(dzfb, halo, ways)
    out_slopes, fb_slopes = everywhere((out_slopes, fb_slopes), sizes)
    sc_slopes = out_slopes[0:2]
    sp_slopes = jnp.concatenate([out_slopes[0:1], out_slopes[2:3]])
    dsc, dzsb, sb_slopes = call(
        functools.partial(expand_back_kernel, False),
        [shape((mine, 8, wide_in), BF16), shape((mine, 8, mid)), shape((2, mid))],
        [inv_slow, dss, sc, sc_sums, out_g[0], sc_slopes, sb, sb_sums, in_g[1], mask, exp_w],
        smem=1,
        name="slow_third_back",
    )
    dzsb_lo, dzsb_hi = halos(dzsb, halo, ways)
    dfb, dzfa, fa_slopes = call(
        functools.partial(conv_back_kernel, halo, across, 0, True),
        [shape((3, mine, 8, 128), BF16), shape((mine, 8, 128)), shape((2, 128))],
        [inv_fast, fb_sums, fin_g[1], fb_slopes, fb_lo, fb, fb_hi, dzfb_lo, dzfb, dzfb_hi, masks, edges, w_fsp, fa, sums1, fin_g[0]],
        pad,
        smem=1,
        name="fast_second_back",
    )
    sb_slopes, fa_slopes = everywhere((sb_slopes, fa_slopes), sizes)
    dsp, dx, dl = call(
        bypass_back_kernel,
        [shape((mine, 8, wide_in), BF16), shape((mine, 8, wide_in)), shape((mine, 8, mid))],
        [inv_slow, dss, sp, sp_sums, out_g[1], sp_slopes, mask, short_w, lshort_w],
        smem=1,
        name="bypass_back",
    )
    dsb, dzsa, sa_slopes = call(
        functools.partial(conv_back_kernel, halo, across, 0, False),
        [shape((3, mine, 8, mid), BF16), shape((mine, 8, mid)), shape((2, mid))],
        [inv_slow, sb_sums, in_g[1], sb_slopes, sb_lo, sb, sb_hi, dzsb_lo, dzsb, dzsb_hi, masks, edges, spat_w, sa, sa_sums, in_g[0]],
        [pltpu.VMEM((3, ext, 8, mid), F32)],
        smem=1,
        name="slow_second_back",
    )
    sa_slopes = everywhere(sa_slopes, sizes)
    dsa, dslow, dzlp, lp_slopes = call(
        slow_back_kernel,
        [shape((mine, 8, 3 * mid), BF16), shape((ways, mine, 8, mid), BF16), shape((mine, 8, mid)), shape((2, mid))],
        [inv_slow, dzsa, sa, sa_sums, in_g[0], sa_slopes, mask, red_w, lred_w, dx, dl, lp, sums1, lat_g],
        smem=1,
        name="slow_first_back",
    )
    lp_slopes = everywhere(lp_slopes, sizes)
    dfirst, dfast = call(
        fast_back_kernel,
        [shape((mine, 8, 896), BF16), shape((ways, mine, 8, 128), BF16)],
        [inv_n, sums1, fin_g[0], lat_g, fa_slopes, lp_slopes, dzfa, fa, dzlp, lp, dfs, mask, w_first],
        smem=1,
        name="fast_first_back",
    )

    slow_output = joined(resplit(slow_out))
    fast_output = unpacked(resplit(fast_out))
    slow_input_grad = joined(resplit(dslow))
    fast_input_grad = unpacked(resplit(dfast))

    def conv_weight(act, dy):
        taps = []
        for i in range(3):
            for j in range(3):
                begin = halo + across * (i - 1) + j - 1
                taps.append(weight_sum(dy[i], act[j, begin : begin + mine]))
        return jnp.stack(taps)

    g_exp = weight_sum(hb, dsc)
    g_short = weight_sum(x, dsp)
    g_lshort = weight_sum(lat, dsp)
    g_exp, g_short, g_lshort = collect([g_exp[None], g_short[None], g_lshort[None]], sizes)
    (g_spat,) = collect([conv_weight(ha, dsb)], sizes)
    g_red = weight_sum(dsa, x).reshape(3, mid, wide_in)
    g_lred = weight_sum(dsa, lat).reshape(3, mid, mid)
    g_red, g_lred = collect([g_red, g_lred], sizes)
    fx_whole = jnp.concatenate([fx[z] for z in range(ways)], axis=2)
    g_first = weight_sum(fx_whole, dfirst).reshape(ways, ratio, fast_part, 896)
    g_lat_main = g_first[:, :, :, 384:640].transpose(1, 3, 0, 2).reshape(ratio, mid, -1)
    g_lat_prev = g_first[:, :, :, 640:896].transpose(1, 3, 0, 2).reshape(ratio, mid, -1)
    g_lat = jnp.stack([g_lat_prev[2], g_lat_prev[3], g_lat_main[0], g_lat_main[1], g_lat_main[2]])
    (g_lat,) = collect([g_lat], sizes)
    g_main = g_first[:, :, :, 0:128].reshape(ways, ratio, fast_part, ratio, -1)
    inner = g_main.shape[-1]
    g_prev, g_after = g_first[:, :, :, 128:256], g_first[:, :, :, 256:384]
    g_fred = []
    for j in range(3):
        total = sum(g_main[:, q + j - 1, :, q] for q in range(ratio) if 0 <= q + j - 1 < ratio)
        if j == 0:
            total = total + g_prev[:, ratio - 1, :, 0:inner]
        if j == 2:
            total = total + g_after[:, 0, :, 128 - inner :]
        g_fred.append(total.reshape(-1, inner))
    g_fred = jnp.stack(g_fred)
    g_fsp = conv_weight(h1, dfb).reshape(9, ratio, inner, ratio, inner)
    g_fsp = sum(g_fsp[:, r, :, r] for r in range(ratio)).transpose(0, 2, 1).reshape(3, 3, inner, inner)
    g_fex = weight_sum(h2, dfc).reshape(ratio, inner, ways, ratio, fast_part)
    g_fex = sum(g_fex[r, :, :, r] for r in range(ratio)).reshape(inner, -1)
    g_fred, g_fsp, g_fex = jax.tree.map(
        lambda v: v.astype(F32), everywhere(jax.tree.map(lambda v: v.astype(BF16), (g_fred, g_fsp, g_fex)), sizes)
    )

    def pair(slopes):
        return slopes[::-1]

    def own(v, width):
        return lax.dynamic_slice_in_dim(v, me * width, width, v.ndim - 1)

    def fold_in(slopes):
        return jnp.sum(slopes.reshape(2, ratio, inner), axis=1)

    fast_inner_grad = jnp.stack([pair(fold_in(fa_slopes)), pair(fold_in(fb_slopes))])
    fast_outer_grad = pair(jnp.sum(fc_slopes.reshape(2, ways, ratio, fast_part), axis=2).reshape(2, -1))
    lateral_grad = pair(own(lp_slopes, lw))
    slow_inner_grad = own(jnp.stack([pair(sa_slopes), pair(sb_slopes)]), sw)
    slow_outer_grad = own(jnp.stack([pair(sc_slopes), pair(sp_slopes)]), ow)
    return (
        slow_output,
        fast_output,
        slow_input_grad,
        fast_input_grad,
        g_fred,
        g_fsp,
        g_fex,
        g_lat.transpose(0, 2, 1),
        g_red.transpose(0, 2, 1),
        g_lred.transpose(0, 2, 1),
        g_spat.transpose(0, 2, 1).reshape(slow_spatial.shape),
        g_exp[0],
        g_short[0],
        g_lshort[0],
        fast_inner_grad,
        fast_outer_grad,
        lateral_grad,
        slow_inner_grad,
        slow_outer_grad,
    )


def solution(mesh):
    sizes = {"dp": mesh.shape["dp"], "chan": mesh.shape["chan"]}
    big = P("dp", None, None, None, "chan")
    last2, last3, last4 = P(None, "chan"), P(None, None, "chan"), P(None, None, None, "chan")
    first = P("chan", None)
    return jax.shard_map(
        functools.partial(local, sizes),
        mesh=mesh,
        in_specs=(
            big, big, P(), P(), P(), P(), P(), last3, last3, last3, last4, first, first, first,
            P(), P(), last2, last3, last3, big, big,
        ),
        out_specs=(
            big, big, big, big, P(), P(), P(), last3, last3, last3, last4, first, first, first,
            P(), P(), last2, last3, last3,
        ),
        check_vma=False,
    )
```

time: 3460 us -> 1040 us (0.30)
  waiting for transfers between devices: 1990 us -> 211 us
  local copies, waits for them, and re-layouts: 644 us -> 190 us
  matrix products: 475 us -> 71.5 us
  starting transfers between devices: 9.67 us -> 206 us
  Pallas kernels: 0 us -> 154 us
  other arithmetic: 177 us -> 38.9 us
    all_gather x7 -> x2, waiting for transfers between devices: 1650 us -> 0.01 us  [share(): lax.all_gather(whole, 'dp', axis=0, tiled=False).reshape(ways, blocks, -1)]
    dot_general x107 -> x25, matrix products: 475 us -> 71.5 us  [weight_sum(): return jnp.einsum('pti,pto->io', a, b, preferred_element_type=F32)]
    unnamed x321 -> x211, local copies, waits for them, and re-layouts: 349 us -> 23.9 us
    reduce_scatter x3 -> x6, waiting for transfers between devices: 299 us -> 16.7 us  [the longest x4 16.6 us: collect(): mine = lax.psum_scatter(mine, 'chan', scatter_dimension=0, tiled=False)]
    ppermute x0 -> x131, starting transfers between devices: none -> 168 us  [the longest x119 139 us: swap(): return jax.tree.map(lambda v: lax.ppermute(v, axis, pairs), tree)]
    pallas_call x0 -> x20, Pallas kernels: none -> 154 us  [call(): pl.pallas_call(kernel, out_shape=tuple(outs), in_specs=specs, out_specs=t...]
    all_gather x0 -> x7, blocking collectives: none -> 146 us  [the longest x1 55.2 us: local(): norms = lax.all_gather(norms, 'chan', axis=0, tiled=False)]
    psum x9 -> x0, blocking collectives: 133 us -> none  [the longest x5 68.9 us: pooled_moments(): joined = lax.psum(jnp.concatenate(pieces), 'dp')]
  transfers between devices with their start and end apart: 14 -> 148, of which waited for: 11 -> 36; matrix products, arithmetic and copies ran while one was open for 26% -> 27% of each run, Pallas kernels for 0% -> 15%
where the time goes in v1:
time: 1040 us
  waiting for transfers between devices  211 us (20%)
  starting transfers between devices  206 us (20%)
  local copies, waits for them, and re-layouts  190 us (18%)
  Pallas kernels  154 us (15%)
  blocking collectives  146 us (14%)
  matrix products  71.5 us (7%)
  other arithmetic  38.9 us (4%)
  between operations  17.1 us (2%)
    pallas_call x20, Pallas kernels, call(): pl.pallas_call(kernel, out_shape=tuple(outs), in_specs=specs, out_specs=t...  154 us
    ppermute x119, starting transfers between devices, swap(): return jax.tree.map(lambda v: lax.ppermute(v, axis, pairs), tree)  139 us
    ppermute x119, waiting for transfers between devices, swap(): return jax.tree.map(lambda v: lax.ppermute(v, axis, pairs), tree)  98.4 us
    dot_general x25, matrix products, weight_sum(): return jnp.einsum('pti,pto->io', a, b, preferred_element_type=F32)  71.5 us
    all_gather x1, blocking collectives, local(): norms = lax.all_gather(norms, 'chan', axis=0, tiled=False)  55.2 us
    all_gather x2, blocking collectives, share(): lax.all_gather(packed.reshape(-1, 1024), 'chan', axis=0, tiled=False)  52.3 us
    unnamed x10, waiting for transfers between devices  47.3 us
    all_to_all x8, waiting for transfers between devices, resplit(): return lax.all_to_all(v, 'chan', 0, 0, tiled=True)  40.8 us
  transfers between devices with their start and end apart: 148, of which 36 were waited for; matrix products, arithmetic and copies ran while one was open for 27% of the time, Pallas kernels for 15%

profile of v1, /device:TPU:0, one launch (start us, length us, event | category | flops | bytes accessed | tf_op | source)
XLA Modules:
  0.0 1035.0 jit_solution(11911263125418190489)
XLA Ops:
  9.8 16.4 %all_gather.36 = bf16[4,35,1024]{2,1,0:T(8,128)(2,1)} all-gather(bf16[1,35,1024]{2,1,0:T(8,128)(2,1)S(1)} %all_gather_reshape.6), channel_id=1, replica_groups=mesh['dp'=8,'chan'=4] {'chan'}, dimensions={0}, use_global_device_ids=true | all-gather | bytes 358400 | tf_op jit(solution)/shard_map/all_gather | solution.py:550
  29.2 7.1 fast_pack.2
  43.9 35.9 %all_gather.41 = bf16[4,66,1024]{2,1,0:T(8,128)(2,1)} all-gather(bf16[1,66,1024]{2,1,0:T(8,128)(2,1)S(1)} %all_gather_reshape.7), channel_id=1, replica_groups=mesh['dp'=8,'chan'=4] {'chan'}, dimensions={0}, use_global_device_ids=true | all-gather | bytes 675840 | tf_op jit(solution)/shard_map/all_gather | solution.py:550
  90.5 55.2 %all-gather.3 = f32[4,1,1408]{2,1,0:T(1,128)S(1)} all-gather(f32[1,1,1408]{2,1,0:T(1,128)S(1)} %reshape.1005), channel_id=3, replica_groups=mesh['dp'=8,'chan'=4] {'chan'}, dimensions={0}, use_global_device_ids=true | all-gather | bytes 28160 | tf_op jit(solution)/shard_map/all_gather | solution.py:693
  178.6 7.1 fast_pack.3
  233.8 10.2 collective-permute-done.44
  257.2 8.1 slow_first.1
  289.3 7.9 fast_out.1
  326.7 16.1 %collective-permute-done.83 = f32[2,512]{1,0:T(2,128)S(1)} collective-permute-done((f32[2,512]{1,0:T(2,128)S(1)}, f32[2,512]{1,0:T(2,128)S(1)}, u32[]{:S(2)}, u32[]{:S(2)}) %collective-permute-start.83) | collective-permute-done | bytes 4128 | tf_op jit(solution)/shard_map/ppermute | solution.py:499
  388.2 7.7 reshape.911
  399.9 7.7 slow_second.1
  434.8 8.7 bypass.1
  482.3 14.2 %slow_out.1 = (bf16[4,147,8,256]{3,2,1,0:T(8,128)(2,1)}, f32[147,8,1024]{2,1,0:T(8,128)}, f32[3,1024]{1,0:T(4,128)}) custom-call(f32[1]{0:T(128)} %bitcast.n_ref, f32[147,8,1024]{2,1,0:T(8,128)} %get-tuple-element.73.sc_ref.y_ref, f32[147,8,1024]{2,1,0:T(8,128)} %get-tuple-element.76.sp_ref.y_ref, f32[2,1024]{1,0:T(2,128)} %add_add_fusion.7.csums_ref.sums_ref, ...), custom_call_target="tpu_custom_call" | custom-call | bytes 19914756 | tf_op jit(solution)/shard_map/slow_out/pallas_call | solution.py:115
  515.4 12.5 %bypass_back.1 = (bf16[147,8,1024]{2,1,0:T(8,128)(2,1)}, f32[147,8,1024]{2,1,0:T(8,128)}, f32[147,8,256]{2,1,0:T(8,128)}) custom-call(f32[1]{0:T(128)} %bitcast.n_ref, f32[147,8,1024]{2,1,0:T(8,128)} %get-tuple-element.86.up_ref, f32[147,8,1024]{2,1,0:T(8,128)} %get-tuple-element.76.sp_ref.y_ref, f32[2,1024]{1,0:T(2,128)} %add_add_fusion.5.psums_ref.sums_ref, ...), custom_call_target="tpu_custom_call" | custom-call | bytes 21311492 | tf_op jit(solution)/shard_map/bypass_back/pallas_call | solution.py:115
  533.7 8.9 slow_third_back.1
  579.4 8.3 slow_second_back.1
  590.3 7.9 copy.684
  611.6 8.3 copy.688
  640.6 7.9 copy.692
  649.1 10.8 %slow_first_back.1 = (bf16[147,8,768]{2,1,0:T(8,128)(2,1)}, bf16[4,147,8,256]{3,2,1,0:T(8,128)(2,1)}, f32[147,8,256]{2,1,0:T(8,128)}, f32[2,256]{1,0:T(2,128)}) custom-call(f32[1]{0:T(128)} %bitcast.n_ref, f32[147,8,256]{2,1,0:T(8,128)} %get-tuple-element.90.dz_ref, f32[147,8,256]{2,1,0:T(8,128)} %get-tuple-element.70.y_ref.z_ref, ...), custom_call_target="tpu_custom_call" | custom-call | bytes 17634308 | tf_op jit(solution)/shard_map/slow_first_back/pallas_call | solution.py:115
  684.0 7.2 fast_first_back.1
  712.9 47.2 %all-reduce.7.cloned.1.call-done = (bf16[8,4,5,1024]{3,1,2,0:T(4,128)(2,1)}, bf16[8,4,30,1024]{3,1,2,0:T(4,128)(2,1)}) async-done(((bf16[8,4,5,1024]{3,1,2,0:T(4,128)(2,1)}, bf16[8,4,30,1024]{3,1,2,0:T(4,128)(2,1)}), (bf16[8,4,5,1024]{3,1,2,0:T(4,128)(2,1)}, bf16[8,4,30,1024]{3,1,2,0:T(4,128)(2,1)})) %all-reduce.7.cloned.1.call-update) | async-done | bytes 2293776
  783.1 7.1 reshape.956
  798.3 12.0 %all-to-all-done.7 = bf16[4,147,8,128]{3,2,1,0:T(8,128)(2,1)} async-done(((bf16[4,147,8,128]{3,2,1,0:T(8,128)(2,1)}), bf16[4,147,8,128]{3,2,1,0:T(8,128)(2,1)}, u32[]{:S(2)}, u32[]{:S(2)}) %all-to-all-start.7) | async-done | bytes 1204256 | tf_op jit(solution)/shard_map/all_to_all | solution.py:586
  823.8 28.9 %collective-permute-done.128 = bf16[32,128]{1,0:T(8,128)(2,1)S(1)} collective-permute-done((bf16[32,128]{1,0:T(8,128)(2,1)S(1)}, bf16[32,128]{1,0:T(8,128)(2,1)S(1)}, u32[]{:S(2)}, u32[]{:S(2)}) %collective-permute-start.128) | collective-permute-done | bytes 8224 | tf_op jit(solution)/shard_map/ppermute | solution.py:499
  854.5 14.5 %collective-permute-done.129 = bf16[32,128]{1,0:T(8,128)(2,1)S(1)} collective-permute-done((bf16[32,128]{1,0:T(8,128)(2,1)S(1)}, bf16[32,128]{1,0:T(8,128)(2,1)S(1)}, u32[]{:S(2)}, u32[]{:S(2)}) %collective-permute-start.129) | collective-permute-done | bytes 8224 | tf_op jit(solution)/shard_map/ppermute | solution.py:499
  915.3 8.7 all_gather.44
  924.8 9.3 all_gather.45
  950.5 12.4 %reduce-scatter.13.cloned.1.call-done = bf16[1,18,1024]{2,1,0:T(8,128)(2,1)} async-done(((bf16[4,18,1024]{2,1,0:T(8,128)(2,1)}), bf16[1,18,1024]{2,1,0:T(8,128)(2,1)}) %reduce-scatter.13.cloned.1.call-update) | async-done | bytes 36880 | tf_op jit(solution)/shard_map/reduce_scatter | solution.py:573
  962.9 9.7 all_gather.46
  973.7 28.8 %all-to-all-done.6 = bf16[4,147,8,256]{3,2,1,0:T(8,128)(2,1)} async-done(((bf16[4,147,8,256]{3,2,1,0:T(8,128)(2,1)}), bf16[4,147,8,256]{3,2,1,0:T(8,128)(2,1)}, u32[]{:S(2)}, u32[]{:S(2)}) %all-to-all-start.6) | async-done | bytes 2408480 | tf_op jit(solution)/shard_map/all_to_all | solution.py:586
  1006.8 10.7 %all_gather.47 = bf16[8,48,1024]{2,1,0:T(8,128)(2,1)S(1)} all-gather(bf16[1,48,1024]{2,1,0:T(8,128)(2,1)} %reduce-scatter.17.cloned.1.call-done), channel_id=1, replica_groups=mesh['dp'=8,'chan'=4] {'dp'}, dimensions={0}, use_global_device_ids=true | all-gather | bytes 884736 | tf_op jit(solution)/shard_map/all_gather | solution.py:574
  (807 shorter events, 554.6 us)
Async XLA Ops:
  7.2 143.3 %all-gather.7.cloned.1.call-start = ((), (), s32[]{:S(2)}) async-start(), calls=%async_computation.20 | async-start | bytes 2949120 | tf_op jit(solution)/shard_map/all_gather | solution.py:551
  36.3 46.4 %all-to-all-start.1 = ((bf16[4,147,8,128]{3,2,1,0:T(8,128)(2,1)}), bf16[4,147,8,128]{3,2,1,0:T(8,128)(2,1)S(1)}, u32[]{:S(2)}, u32[]{:S(2)}) async-start(bf16[4,147,8,128]{3,2,1,0:T(8,128)(2,1)} %bitcast.692), calls=%async_computation.1 | async-start | bytes 2408448 | tf_op jit(solution)/shard_map/all_to_all | solution.py:586
  42.0 346.3 %all-gather.9.cloned.1.call-start = ((), (), s32[]{:S(2)}) async-start(), calls=%async_computation.21 | async-start | bytes 5308416 | tf_op jit(solution)/shard_map/all_gather | solution.py:551
  84.3 124.3 %all-to-all-start = ((bf16[4,147,8,256]{3,2,1,0:T(8,128)(2,1)}), bf16[4,147,8,256]{3,2,1,0:T(8,128)(2,1)}, u32[]{:S(2)}, u32[]{:S(2)}) async-start(bf16[4,147,8,256]{3,2,1,0:T(8,128)(2,1)} %bitcast.713), calls=%async_computation | async-start | bytes 4816896 | tf_op jit(solution)/shard_map/all_to_all | solution.py:586
  208.6 76.1 %all-to-all-start.4 = ((bf16[4,147,8,128]{3,2,1,0:T(8,128)(2,1)}), bf16[4,147,8,128]{3,2,1,0:T(8,128)(2,1)}, u32[]{:S(2)}, u32[]{:S(2)}) async-start(bf16[4,147,8,128]{3,2,1,0:T(8,128)(2,1)} %bitcast.73), calls=%async_computation.4 | async-start | bytes 2408448 | tf_op jit(solution)/shard_map/all_to_all | solution.py:586
  284.7 193.1 %all-to-all-start.2 = ((bf16[4,147,8,256]{3,2,1,0:T(8,128)(2,1)}), bf16[4,147,8,256]{3,2,1,0:T(8,128)(2,1)}, u32[]{:S(2)}, u32[]{:S(2)}) async-start(bf16[4,147,8,256]{3,2,1,0:T(8,128)(2,1)} %bitcast.62), calls=%async_computation.2 | async-start | bytes 4816896 | tf_op jit(solution)/shard_map/all_to_all | solution.py:586
  304.2 69.6 %collective-permute-start.92 = (f32[15,8,128]{2,1,0:T(8,128)S(1)}, f32[15,8,128]{2,1,0:T(8,128)S(1)}, u32[]{:S(2)}, u32[]{:S(2)}) collective-permute-start(f32[15,8,128]{2,1,0:T(8,128)S(1)} %get-tuple-element.167), channel_id=1, source_target_pairs={{0,1},{1,2},{2,3},{4,5},{5,6},{6,7},{8,9},{9,10},{10,11},{12,13},{... | collective-permute-start | bytes 184328 | tf_op jit(solution)/shard_map/ppermute | solution.py:534
  308.1 68.1 %collective-permute-start.93 = (f32[15,8,128]{2,1,0:T(8,128)}, f32[15,8,128]{2,1,0:T(8,128)}, u32[]{:S(2)}, u32[]{:S(2)}) collective-permute-start(f32[15,8,128]{2,1,0:T(8,128)} %get-tuple-element.166), channel_id=1, source_target_pairs={{1,0},{2,1},{3,2},{5,4},{6,5},{7,6},{9,8},{10,9},{11,10},{13,12},{... | collective-permute-start | bytes 184328 | tf_op jit(solution)/shard_map/ppermute | solution.py:535
  368.7 30.6 %collective-permute-start.14 = (f32[15,8,256]{2,1,0:T(8,128)}, f32[15,8,256]{2,1,0:T(8,128)S(1)}, u32[]{:S(2)}, u32[]{:S(2)}) collective-permute-start(f32[15,8,256]{2,1,0:T(8,128)} %get-tuple-element.137), channel_id=1, source_target_pairs={{0,1},{1,2},{2,3},{4,5},{5,6},{6,7},{8,9},{9,10},{10,11},{12,13},{... | collective-permute-start | bytes 368648 | tf_op jit(solution)/shard_map/ppermute | solution.py:534
  376.2 439.2 %collective-permute-start.125 = (bf16[32,128]{1,0:T(8,128)(2,1)}, bf16[32,128]{1,0:T(8,128)(2,1)}, u32[]{:S(2)}, u32[]{:S(2)}) collective-permute-start(bf16[32,128]{1,0:T(8,128)(2,1)} %add.742), channel_id=1, source_target_pairs={{0,8},{4,12},{8,0},{12,4},{16,24},{20,28},{24,16},{28,20},{1,9},{5... | collective-permute-start | bytes 24584 | tf_op jit(solution)/shard_map/ppermute | solution.py:499
  384.5 31.6 %collective-permute-start.96 = (f32[2,128]{1,0:T(2,128)}, f32[2,128]{1,0:T(2,128)S(1)}, u32[]{:S(2)}, u32[]{:S(2)}) collective-permute-start(f32[2,128]{1,0:T(2,128)} %get-tuple-element.99), channel_id=1, source_target_pairs={{0,4},{4,0},{8,12},{12,8},{16,20},{20,16},{24,28},{28,24},{1,5},{5... | collective-permute-start | bytes 3080 | tf_op jit(solution)/shard_map/ppermute | solution.py:499
  416.2 36.3 %collective-permute-start.97 = (f32[2,128]{1,0:T(2,128)S(1)}, f32[2,128]{1,0:T(2,128)S(1)}, u32[]{:S(2)}, u32[]{:S(2)}) collective-permute-start(f32[2,128]{1,0:T(2,128)S(1)} %add.696), channel_id=1, source_target_pairs={{0,8},{4,12},{8,0},{12,4},{16,24},{20,28},{24,16},{28,20},{1,9},{5... | collective-permute-start | bytes 3080 | tf_op jit(solution)/shard_map/ppermute | solution.py:499
  456.1 43.1 %collective-permute-start.100 = (f32[2,128]{1,0:T(2,128)S(1)}, f32[2,128]{1,0:T(2,128)S(1)}, u32[]{:S(2)}, u32[]{:S(2)}) collective-permute-start(f32[2,128]{1,0:T(2,128)S(1)} %add_add_fusion.26), channel_id=1, source_target_pairs={{0,1},{1,0},{2,3},{3,2},{4,5},{5,4},{6,7},{7,6},{8,9},{9,8},{10,11... | collective-permute-start | bytes 3080 | tf_op jit(solution)/shard_map/ppermute | solution.py:499
  477.8 294.8 %all-to-all-start.5 = ((bf16[4,147,8,128]{3,2,1,0:T(8,128)(2,1)}), bf16[4,147,8,128]{3,2,1,0:T(8,128)(2,1)}, u32[]{:S(2)}, u32[]{:S(2)}) async-start(bf16[4,147,8,128]{3,2,1,0:T(8,128)(2,1)} %get-tuple-element.85), calls=%async_computation.5 | async-start | bytes 2408448 | tf_op jit(solution)/shard_map/all_to_all | solution.py:586
  482.1 278.0 %all-reduce.7.cloned.1.call-start = ((), (), s32[]{:S(2)}) async-start(), calls=%async_computation.22 | async-start | bytes 4587520
  510.4 63.7 %collective-permute-start.67 = (f32[15,8,256]{2,1,0:T(8,128)}, f32[15,8,256]{2,1,0:T(8,128)}, u32[]{:S(2)}, u32[]{:S(2)}) collective-permute-start(f32[15,8,256]{2,1,0:T(8,128)} %get-tuple-element.135), channel_id=1, source_target_pairs={{0,1},{1,2},{2,3},{4,5},{5,6},{6,7},{8,9},{9,10},{10,11},{12,13},{... | collective-permute-start | bytes 368648 | tf_op jit(solution)/shard_map/ppermute | solution.py:534
  574.1 241.3 %collective-permute-start.126 = (bf16[32,128]{1,0:T(8,128)(2,1)}, bf16[32,128]{1,0:T(8,128)(2,1)}, u32[]{:S(2)}, u32[]{:S(2)}) collective-permute-start(bf16[32,128]{1,0:T(8,128)(2,1)} %add.742), channel_id=1, source_target_pairs={{0,16},{4,20},{8,24},{12,28},{16,0},{20,4},{24,8},{28,12},{1,17},{... | collective-permute-start | bytes 24584 | tf_op jit(solution)/shard_map/ppermute | solution.py:499
  682.0 133.5 %collective-permute-start.127 = (bf16[32,128]{1,0:T(8,128)(2,1)}, bf16[32,128]{1,0:T(8,128)(2,1)S(1)}, u32[]{:S(2)}, u32[]{:S(2)}) collective-permute-start(bf16[32,128]{1,0:T(8,128)(2,1)} %add.742), channel_id=1, source_target_pairs={{0,24},{4,28},{8,16},{12,20},{16,8},{20,12},{24,0},{28,4},{1,25},{... | collective-permute-start | bytes 24584 | tf_op jit(solution)/shard_map/ppermute | solution.py:499
  699.5 215.8 %reduce-scatter.7.cloned.1.call-start = ((), (), s32[]{:S(2)}) async-start(), calls=%async_computation.14 | async-start | bytes 81920 | tf_op jit(solution)/shard_map/reduce_scatter | solution.py:573
  762.1 162.7 %reduce-scatter.9.cloned.1.call-start = ((), (), s32[]{:S(2)}) async-start(), calls=%async_computation.15 | async-start | bytes 327680 | tf_op jit(solution)/shard_map/reduce_scatter | solution.py:573
  764.5 170.6 %reduce-scatter.11.cloned.1.call-start = ((), (), s32[]{:S(2)}) async-start(), calls=%async_computation.16 | async-start | bytes 1769472 | tf_op jit(solution)/shard_map/reduce_scatter | solution.py:572
  772.6 37.6 %all-to-all-start.7 = ((bf16[4,147,8,128]{3,2,1,0:T(8,128)(2,1)}), bf16[4,147,8,128]{3,2,1,0:T(8,128)(2,1)}, u32[]{:S(2)}, u32[]{:S(2)}) async-start(bf16[4,147,8,128]{3,2,1,0:T(8,128)(2,1)} %get-tuple-element.103), calls=%async_computation.7 | async-start | bytes 2408448 | tf_op jit(solution)/shard_map/all_to_all | solution.py:586
  777.5 163.4 %reduce-scatter.15.cloned.1.call-start = ((), (), s32[]{:S(2)}) async-start(), calls=%async_computation.18 | async-start | bytes 3538944 | tf_op jit(solution)/shard_map/reduce_scatter | solution.py:572
  810.2 124.9 %all-to-all-start.3 = ((bf16[4,147,8,256]{3,2,1,0:T(8,128)(2,1)}), bf16[4,147,8,256]{3,2,1,0:T(8,128)(2,1)S(1)}, u32[]{:S(2)}, u32[]{:S(2)}) async-start(bf16[4,147,8,256]{3,2,1,0:T(8,128)(2,1)} %get-tuple-element.79), calls=%async_computation.3 | async-start | bytes 4816896 | tf_op jit(solution)/shard_map/all_to_all | solution.py:586
  814.0 148.9 %reduce-scatter.13.cloned.1.call-start = ((), (), s32[]{:S(2)}) async-start(), calls=%async_computation.17 | async-start | bytes 245760 | tf_op jit(solution)/shard_map/reduce_scatter | solution.py:573
  816.2 36.5 %collective-permute-start.128 = (bf16[32,128]{1,0:T(8,128)(2,1)S(1)}, bf16[32,128]{1,0:T(8,128)(2,1)S(1)}, u32[]{:S(2)}, u32[]{:S(2)}) collective-permute-start(bf16[32,128]{1,0:T(8,128)(2,1)S(1)} %add_add_fusion.4), channel_id=1, source_target_pairs={{0,1},{1,0},{2,3},{3,2},{4,5},{5,4},{6,7},{7,6},{8,9},{9,8},{10,11... | collective-permute-start | bytes 24584 | tf_op jit(solution)/shard_map/ppermute | solution.py:499
  818.1 50.8 %collective-permute-start.129 = (bf16[32,128]{1,0:T(8,128)(2,1)S(1)}, bf16[32,128]{1,0:T(8,128)(2,1)S(1)}, u32[]{:S(2)}, u32[]{:S(2)}) collective-permute-start(bf16[32,128]{1,0:T(8,128)(2,1)S(1)} %add_add_fusion.4), channel_id=1, source_target_pairs={{0,2},{1,3},{2,0},{3,1},{4,6},{5,7},{6,4},{7,5},{8,10},{9,11},{10,... | collective-permute-start | bytes 24584 | tf_op jit(solution)/shard_map/ppermute | solution.py:499
  820.5 48.4 %collective-permute-start.130 = (bf16[32,128]{1,0:T(8,128)(2,1)S(1)}, bf16[32,128]{1,0:T(8,128)(2,1)S(1)}, u32[]{:S(2)}, u32[]{:S(2)}) collective-permute-start(bf16[32,128]{1,0:T(8,128)(2,1)S(1)} %add_add_fusion.4), channel_id=1, source_target_pairs={{0,3},{1,2},{2,1},{3,0},{4,7},{5,6},{6,5},{7,4},{8,11},{9,10},{10,... | collective-permute-start | bytes 24584 | tf_op jit(solution)/shard_map/ppermute | solution.py:499
  821.6 48.1 %collective-permute-start.118 = (bf16[3,3,32,32]{3,2,1,0:T(8,128)(2,1)S(1)}, bf16[3,3,32,32]{3,2,1,0:T(8,128)(2,1)S(1)}, u32[]{:S(2)}, u32[]{:S(2)}) collective-permute-start(bf16[3,3,32,32]{3,2,1,0:T(8,128)(2,1)S(1)} %add.732), channel_id=1, source_target_pairs={{0,8},{4,12},{8,0},{12,4},{16,24},{20,28},{24,16},{28,20},{1,9},{5... | collective-permute-start | bytes 55304 | tf_op jit(solution)/shard_map/ppermute | solution.py:499
  822.9 46.8 %collective-permute-start.119 = (bf16[3,3,32,32]{3,2,1,0:T(8,128)(2,1)S(1)}, bf16[3,3,32,32]{3,2,1,0:T(8,128)(2,1)S(1)}, u32[]{:S(2)}, u32[]{:S(2)}) collective-permute-start(bf16[3,3,32,32]{3,2,1,0:T(8,128)(2,1)S(1)} %add.732), channel_id=1, source_target_pairs={{0,16},{4,20},{8,24},{12,28},{16,0},{20,4},{24,8},{28,12},{1,17},{... | collective-permute-start | bytes 55304 | tf_op jit(solution)/shard_map/ppermute | solution.py:499
  935.2 67.3 %all-to-all-start.6 = ((bf16[4,147,8,256]{3,2,1,0:T(8,128)(2,1)}), bf16[4,147,8,256]{3,2,1,0:T(8,128)(2,1)}, u32[]{:S(2)}, u32[]{:S(2)}) async-start(bf16[4,147,8,256]{3,2,1,0:T(8,128)(2,1)} %get-tuple-element.94), calls=%async_computation.6 | async-start | bytes 4816896 | tf_op jit(solution)/shard_map/all_to_all | solution.py:586
  939.7 67.1 %reduce-scatter.17.cloned.1.call-start = ((), (), s32[]{:S(2)}) async-start(), calls=%async_computation.19 | async-start | bytes 491520 | tf_op jit(solution)/shard_map/reduce_scatter | solution.py:573
  (209 other events, 2084.4 us)
Sparse Core Ops, SparseCore 0:
  26.4 31.9 all-gather.6
  79.9 39.8 all-gather.8
  699.6 60.4 all-reduce.6
  762.8 18.4 reduce-scatter.6
  784.0 27.2 reduce-scatter.8
  814.8 35.8 reduce-scatter.10
  854.4 46.2 reduce-scatter.14
  935.3 27.5 reduce-scatter.12
  965.3 41.4 reduce-scatter.16

commit v2 on v1

v2 whole, which is shorter than its diff:
```python
import functools

import jax
import jax.numpy as jnp
from jax import lax
from jax.experimental import pallas as pl
from jax.experimental.pallas import tpu as pltpu
from jax.sharding import PartitionSpec as P

F32 = jnp.float32
BF16 = jnp.bfloat16
EPSILON = 1e-05
ROOT = 0.7978845608028654
CUBIC = 0.044715
BIG = 49
SMALL = 7


def gelu(v):
    return 0.5 * v * (1.0 + jnp.tanh(ROOT * (v * (1.0 + CUBIC * (v * v)))))


def gelu_slope(v):
    square = v * v
    th = jnp.tanh(ROOT * (v * (1.0 + CUBIC * square)))
    half = 0.5 * (1.0 + th)
    return half + (0.5 * ROOT) * v * (1.0 - th * th) * (1.0 + 3.0 * CUBIC * square)


def gelu_pair(v):
    square = v * v
    th = jnp.tanh(ROOT * (v * (1.0 + CUBIC * square)))
    half = 0.5 * (1.0 + th)
    slope = half + (0.5 * ROOT) * v * (1.0 - th * th) * (1.0 + 3.0 * CUBIC * square)
    return v * half, slope


def rows(v):
    return v.reshape(v.shape[0] * v.shape[1], v.shape[2])


def cells(v):
    return v.reshape(v.shape[0] // 8, 8, v.shape[1])


def rows_bf(v):
    return rows(v.astype(F32)).astype(BF16)


def wide(mask, width):
    repeats = width // 128
    return mask if repeats == 1 else jnp.concatenate([mask] * repeats, axis=-1)


def nn(a, b):
    return jnp.dot(a, b, preferred_element_type=F32)


def nt(a, b):
    return lax.dot_general(a, b, (((1,), (1,)), ((), ())), preferred_element_type=F32)


def later(v):
    rolled = pltpu.roll(v, 1, 1)
    return jnp.where(lax.broadcasted_iota(jnp.int32, v.shape, 1) == 0, 0.0, rolled)


def sooner(v):
    rolled = pltpu.roll(v, 7, 1)
    return jnp.where(lax.broadcasted_iota(jnp.int32, v.shape, 1) == 7, 0.0, rolled)


def folded(v):
    out = []
    for block in range(v.shape[-1] // 128):
        part = v[:, 128 * block : 128 * block + 128]
        part = part + pltpu.roll(part, 64, 1)
        out.append(part + pltpu.roll(part, 32, 1))
    return out[0] if len(out) == 1 else jnp.concatenate(out, axis=-1)


def scale_of(sums, gains, inv_n):
    center = sums[0:1] * inv_n
    spread = sums[1:2] * inv_n - center * center
    inv_std = lax.rsqrt(spread + EPSILON)
    factor = gains[0:1] * inv_std
    return factor, gains[1:2] - center * factor, center, inv_std


def slope_of(slopes, factor, center, inv_std, inv_n):
    k1 = factor * slopes[1:2] * inv_n * inv_std
    k0 = factor * slopes[0:1] * inv_n - k1 * center
    return k0, k1


def down(v):
    return jnp.sum(v, axis=0)


def flat(v):
    return jnp.sum(v, axis=0, keepdims=True)


def steps(count, step, body, carry):
    return lax.fori_loop(0, count // step, lambda i, c: body(i * step, c), carry)


def call(kernel, outs, args, scratch=(), smem=0, flops=0, name=None):
    specs = [pl.BlockSpec(memory_space=pltpu.SMEM if i < smem else pltpu.VMEM) for i in range(len(args))]
    total = sum(a.size * a.dtype.itemsize for a in args)
    total += sum(o.size * o.dtype.itemsize for o in outs)
    def padded(v):
        dims = list(v.shape)
        if len(dims) < 2:
            return 4096
        dims[-1] = -(-dims[-1] // 128) * 128
        dims[-2] = -(-dims[-2] // 8) * 8
        amount = v.dtype.itemsize
        for d in dims:
            amount *= d
        return amount

    room = sum(padded(v) for v in (*args, *outs, *scratch)) + 6 * 1024 * 1024
    return pl.pallas_call(
        kernel,
        out_shape=tuple(outs),
        in_specs=specs,
        out_specs=tuple(pl.BlockSpec(memory_space=pltpu.VMEM) for _ in outs),
        scratch_shapes=list(scratch),
        compiler_params=pltpu.CompilerParams(vmem_limit_bytes=room),
        cost_estimate=pl.CostEstimate(flops=flops, bytes_accessed=total, transcendentals=0),
        name=name,
    )(*args)


def shape(dims, dtype=F32):
    return jax.ShapeDtypeStruct(dims, dtype)


def tile_mask(frames, width):
    tile = (lax.broadcasted_iota(jnp.int32, (8, 128), 0) < frames).astype(F32)
    return wide(tile, width)[None]


def sweep(table_ref, size, step, body, carry=0):
    def run(i, kept):
        p = i * step
        return body(p, table_ref[1 + p // BIG], kept)

    return lax.fori_loop(0, size // step, run, carry)


def lane_group(v, group):
    return jnp.where(lax.broadcasted_iota(jnp.int32, v.shape, v.ndim - 1) // 32 == group, v, 0.0)


def moved(v, shift):
    shift = shift % 128
    return v if shift == 0 else pltpu.roll(v, shift, v.ndim - 1)


def pack_kernel(per_clip, clips, ids_ref, counts_ref, frames_ref, x_ref, out_ref, tmp_ref):
    clip, dp = pl.program_id(0) // per_clip, ids_ref[0]
    chunk = x_ref.shape[0]
    frames = jnp.where(clip < counts_ref[dp], frames_ref[dp * clips + clip], 0)
    tmp_ref[...] = x_ref[...].astype(F32).reshape(chunk * 32, 32)
    parts = [tmp_ref[pl.ds(r, chunk * 8, stride=4), :] for r in range(4)]
    out_ref[...] = (cells(jnp.concatenate(parts, axis=1)) * tile_mask(frames, 128)).astype(BF16)


def unpack_kernel(ids_ref, *refs):
    pieces, out_ref, tmp_ref = refs[:4], refs[4], refs[5]
    size = pieces[0].shape[0]
    for k in range(4):
        begin = (ids_ref[1] ^ k) * size

        def body(p, carry, k=k, begin=begin):
            joined = rows(pieces[k][pl.ds(p, BIG)].astype(F32))
            for r in range(4):
                tmp_ref[pl.ds(r, BIG * 8, stride=4), :] = joined[:, 32 * r : 32 * r + 32]
            out_ref[pl.ds(begin + p, BIG)] = tmp_ref[...].reshape(BIG, 32, 32).astype(BF16)
            return carry

        steps(size, BIG, body, 0)


def place_kernel(ids_ref, *refs):
    pieces, out_ref = refs[:4], refs[4]
    for k in range(4):

        def body(p, carry, k=k):
            out_ref[ids_ref[1] ^ k, pl.ds(p, SMALL)] = pieces[k][pl.ds(p, SMALL)]
            return carry

        steps(pieces[0].shape[0], SMALL, body, 0)


def first_weights_kernel(ids_ref, *refs):
    shares, lat_shares = refs[0:8], refs[8:16]
    fr_ref, fsp_ref, fex_ref, fin_ref, fout_ref = refs[16:21]
    red_ref, lred_ref, first_ref, wsp_ref, wex_ref, gin_ref, gout_ref, lat_ref = refs[21:]
    for kd in range(8):
        d = ids_ref[2] ^ kd
        for kz in range(4):
            z = ids_ref[1] ^ kz
            for j in range(3):
                red_ref[j, z, d] = shares[kd][kz, j, :, 0:1024]
                lred_ref[j, z, d] = shares[kd][kz, j, :, 1024:1280]
            for j in range(5):
                lat_ref[j, z, d] = lat_shares[kd][kz, j].astype(F32)
    first_ref[...] = jnp.zeros_like(first_ref)
    wsp_ref[...] = jnp.zeros_like(wsp_ref)
    for z in range(4):
        lanes = slice(128 * z, 128 * z + 128)

        def put(v, r, z=z):
            return lane_group(moved(v, 32 * r - 32 * z), r)

        for q in range(4):
            total = sum(put(fr_ref[r - q + 1], r) for r in range(4) if abs(r - q) <= 1)
            first_ref[32 * q : 32 * q + 32, lanes] = total.astype(BF16)
        first_ref[128:160, lanes] = put(fr_ref[0], 3).astype(BF16)
        first_ref[352:384, lanes] = put(fr_ref[2], 0).astype(BF16)
        taps = [lat_ref[j].reshape(256, 128) for j in range(5)]
        first_ref[384:640, lanes] = sum(put(taps[2 + r], r) for r in range(3)).astype(BF16)
        first_ref[640:896, lanes] = (put(taps[0], 2) + put(taps[1], 3)).astype(BF16)
        for r in range(4):
            wex_ref[32 * r : 32 * r + 32, lanes] = put(fex_ref[...], r).astype(BF16)
        gout_ref[:, lanes] = sum(put(fout_ref[...], r) for r in range(4))
    blank = jnp.zeros((32, 96), F32)
    for k in range(9):
        tap = jnp.concatenate([fsp_ref[k], blank], axis=1)
        for r in range(4):
            wsp_ref[k, 32 * r : 32 * r + 32, :] = moved(tap, 32 * r).astype(BF16)
    gin_ref[...] = jnp.concatenate([fin_ref[...]] * 4, axis=1)


def second_weights_kernel(ids_ref, *refs):
    shares, sp_shares = refs[0:8], refs[8:16]
    exp_ref, short_ref, lshort_ref, sp_ref = refs[16:]
    for kd in range(8):
        d = ids_ref[2] ^ kd
        for kz in range(4):
            z = ids_ref[1] ^ kz
            exp_ref[z, d] = shares[kd][kz, 0]
            lshort_ref[z, d] = shares[kd][kz, 5]
            for a in range(4):
                short_ref[z, d, a] = shares[kd][kz, 1 + a]
            for k in range(9):
                sp_ref[k, z, d] = sp_shares[kd][kz, k]


def first_grads_kernel(ids_ref, *refs):
    shares, sp_shares = refs[0:8], refs[8:16]
    exp_ref, short_ref, lshort_ref, sp_ref = refs[16:]
    for kd in range(8):
        d = ids_ref[2] ^ kd
        exp_ref[d] = shares[kd][0].astype(F32)
        lshort_ref[d] = shares[kd][5].astype(F32)
        for a in range(4):
            short_ref[d, a] = shares[kd][1 + a].astype(F32)
        for k in range(9):
            sp_ref[k, d] = sp_shares[kd][k].astype(F32)


def second_grads_kernel(ids_ref, *refs):
    shares, lat_shares = refs[0:8], refs[8:16]
    red_ref, lred_ref, lat_ref = refs[16:]
    for kd in range(8):
        d = ids_ref[2] ^ kd
        for j in range(3):
            red_ref[j, d] = shares[kd][j, :, 0:1024].astype(F32)
            lred_ref[j, d] = shares[kd][j, :, 1024:1280].astype(F32)
        for j in range(5):
            lat_ref[j, d] = lat_shares[kd][j].astype(F32)


def lanes_at(block, width):
    return pl.ds(pl.multiple_of(block * width, width), width)


def fast_first_kernel(table_ref, f0_ref, f1_ref, f2_ref, f3_ref, w_ref, fx_ref, fa_ref, lp_ref, sums_ref, first_ref, last_ref):
    size = fa_ref.shape[0]
    for k, ref in enumerate((f0_ref, f1_ref, f2_ref, f3_ref)):

        def fill(p, carry, ref=ref, lanes=lanes_at(table_ref[5] ^ k, 128)):
            fx_ref[pl.ds(p, SMALL), :, lanes] = ref[pl.ds(p, SMALL)]
            return carry

        steps(size, SMALL, fill, 0)

    def body(p, frames, carry):
        acc = cells(nt(rows_bf(fx_ref[pl.ds(p, BIG)]), w_ref[...]))
        fa = acc[:, :, 0:128] + later(acc[:, :, 128:256]) + sooner(acc[:, :, 256:384])
        lp = acc[:, :, 384:640] + later(acc[:, :, 640:896])
        fa_ref[pl.ds(p, BIG)] = fa
        lp_ref[pl.ds(p, BIG)] = lp
        fm, lm = fa * tile_mask(frames, 128), lp * tile_mask(frames, 256)
        return tuple(c + down(v) for c, v in zip(carry, (fm, fm * fa, lm, lm * lp)))

    zero = (jnp.zeros((8, 128), F32),) * 2 + (jnp.zeros((8, 256), F32),) * 2
    a, b, c, d = sweep(table_ref, size, BIG, body, zero)
    sums_ref[0:1, 0:128], sums_ref[1:2, 0:128] = flat(a), flat(b)
    sums_ref[0:1, 128:384], sums_ref[1:2, 128:384] = flat(c), flat(d)
    halo = first_ref.shape[0]
    first_ref[...], last_ref[...] = fa_ref[0:halo], fa_ref[size - halo : size]


def fill_padded(table_ref, refs, offset, out_ref, value, halo, size):
    low, middle, high = refs
    phase = table_ref[5] * (size // SMALL)

    def put(v, at, part, count, step=SMALL):
        even = ((phase + part + 2 * count) % 2 == 0).astype(F32)
        out_ref[1, pl.ds(at, step)] = v
        if step == 1:
            out_ref[0, pl.ds(at, 1)] = v * even
            out_ref[2, pl.ds(at, 1)] = v * (1.0 - even)
            return
        out_ref[0, pl.ds(at, step)] = v
        out_ref[2, pl.ds(at, step)] = v
        out_ref[0, pl.ds(at + step - 1, 1)] = v[step - 1 : step] * even
        out_ref[2, pl.ds(at, 1)] = v[0:1] * (1.0 - even)

    width = out_ref.shape[-1]
    lo_mask, hi_mask = tile_mask(table_ref[0], width), tile_mask(table_ref[4], width)
    put(value(low, 0, 1) * lo_mask, 0, -3, 4, 1)
    put(value(low, 1, SMALL) * lo_mask, 1, -2, 4)
    put(value(low, 1 + SMALL, SMALL) * lo_mask, 1 + SMALL, -1, 4)
    parts = size // SMALL
    put(value(high, 0, SMALL) * hi_mask, halo + size, parts, 0)
    put(value(high, SMALL, SMALL) * hi_mask, halo + size + SMALL, parts + 1, 0)
    put(value(high, 2 * SMALL, 1) * hi_mask, halo + size + 2 * SMALL, parts + 2, 0, 1)

    def body(p, frames, carry):
        put(value(middle, p, SMALL) * tile_mask(frames, width), halo + p, p // SMALL, 0)
        return carry

    sweep(table_ref, size, SMALL, body)


def edge_scales(table_ref, p, per_clip):
    part = table_ref[5] * table_ref[6] + p // BIG
    return (part % per_clip != 0).astype(F32), ((part + 1) % per_clip != 0).astype(F32)


def conv_rows(table_ref, per_clip, pad_ref, weight, p, halo, row_len, dot):
    top, bottom = edge_scales(table_ref, p, per_clip)
    total = None
    for i in (1, 0, 2):
        begin = p + halo + row_len * (i - 1)
        acc = None
        for j in range(3):
            tap = rows(pad_ref[j, pl.ds(begin + j - 1, BIG)]).astype(BF16)
            part = dot(tap, weight(i, j))
            acc = part if acc is None else acc + part
        acc = cells(acc)
        if i == 0:
            acc = jnp.concatenate([acc[0:row_len] * top, acc[row_len:]], axis=0)
        if i == 2:
            acc = jnp.concatenate([acc[: BIG - row_len], acc[BIG - row_len :] * bottom], axis=0)
        total = acc if total is None else total + acc
    return total


def conv_kernel(halo, row_len, per_clip, fold, offsets, table_ref, n_ref, sums_ref, gains_ref, lo_ref, y_ref, hi_ref, w_ref, *refs):
    if fold:
        act_ref, out_ref, osums_ref, pad_ref = refs
    else:
        more_ref, act_ref, out_ref, osums_ref, pad_ref = refs
    size, width = y_ref.shape[0], y_ref.shape[2]
    sums = sums_ref[:, offsets[0] : offsets[0] + width]
    sums = folded(sums) if fold else sums
    factor, shift, _, _ = scale_of(sums, gains_ref[...], n_ref[1 if fold else 0])
    lanes = slice(offsets[1], offsets[1] + width)

    def value(ref, p, step):
        y = ref[pl.ds(p, step)] if ref is y_ref else ref[pl.ds(p, step), :, lanes]
        return gelu(y * factor[None] + shift[None]).astype(BF16).astype(F32)

    fill_padded(table_ref, (lo_ref, y_ref, hi_ref), 0, pad_ref, value, halo, size)

    def copy(p, carry):
        act_ref[pl.ds(p, 3)] = pad_ref[1, pl.ds(p, 3)].astype(BF16)
        return carry

    steps(size + 2 * halo, 3, copy, 0)

    def body(p, frames, carry):
        total = conv_rows(table_ref, per_clip, pad_ref, lambda i, j: w_ref[3 * i + j], p, halo, row_len, nn if fold else nt)
        out_ref[pl.ds(p, BIG)] = total
        masked = total * tile_mask(frames, width)
        return carry[0] + down(masked), carry[1] + down(masked * total)

    a, b = sweep(table_ref, size, BIG, body, (jnp.zeros((8, width), F32),) * 2)
    osums_ref[0:1, 0:width], osums_ref[1:2, 0:width] = flat(a), flat(b)
    if not fold:
        osums_ref[:, width:] = more_ref[...]


def slow_first_kernel(table_ref, n_ref, x0_ref, x1_ref, x2_ref, x3_ref, lp_ref, lsums_ref, gains_ref, w_ref, wl_ref, fb_ref, more_ref,
                      x_ref, lat_ref, sa_ref, sums_ref, first_ref, last_ref):
    size = lp_ref.shape[0]
    factor, shift, _, _ = scale_of(lsums_ref[:, 128:384], gains_ref[...], n_ref[0])

    def fill(p, frames, carry):
        mask = tile_mask(frames, 256)
        lat_ref[pl.ds(p, SMALL)] = (gelu(lp_ref[pl.ds(p, SMALL)] * factor[None] + shift[None]) * mask).astype(BF16)
        for k, ref in enumerate((x0_ref, x1_ref, x2_ref, x3_ref)):
            v = ref[pl.ds(p, SMALL)].astype(F32) * mask
            x_ref[pl.ds(p, SMALL), :, lanes_at(table_ref[5] ^ k, 256)] = v.astype(BF16)
        return carry

    sweep(table_ref, size, SMALL, fill)

    def body(p, frames, carry):
        acc = nt(rows_bf(x_ref[pl.ds(p, BIG)]), w_ref[...]) + nt(rows_bf(lat_ref[pl.ds(p, BIG)]), wl_ref[...])
        acc = cells(acc)
        sa = later(acc[:, :, 0:256]) + acc[:, :, 256:512] + sooner(acc[:, :, 512:768])
        sa_ref[pl.ds(p, BIG)] = sa
        masked = sa * tile_mask(frames, 256)
        return carry[0] + down(masked), carry[1] + down(masked * sa)

    a, b = sweep(table_ref, size, BIG, body, (jnp.zeros((8, 256), F32),) * 2)
    sums_ref[0:1, 0:256], sums_ref[1:2, 0:256] = flat(a), flat(b)
    sums_ref[:, 256:] = more_ref[...]
    halo = first_ref.shape[0]
    first_ref[:, :, 0:256], last_ref[:, :, 0:256] = sa_ref[0:halo], sa_ref[size - halo : size]
    first_ref[:, :, 256:], last_ref[:, :, 256:] = fb_ref[0:halo], fb_ref[size - halo : size]


def bypass_kernel(table_ref, x_ref, lat_ref, w_ref, wl_ref, sp_ref, sums_ref):
    def body(p, frames, carry):
        sp = cells(nn(rows_bf(x_ref[pl.ds(p, BIG)]), w_ref[...]) + nn(rows_bf(lat_ref[pl.ds(p, BIG)]), wl_ref[...]))
        sp_ref[pl.ds(p, BIG)] = sp.astype(BF16)
        masked = sp * tile_mask(frames, sp.shape[-1])
        return carry[0] + down(masked), carry[1] + down(masked * sp)

    a, b = sweep(table_ref, sp_ref.shape[0], BIG, body, (jnp.zeros((8, sp_ref.shape[2]), F32),) * 2)
    sums_ref[0:1], sums_ref[1:2] = flat(a), flat(b)


def expand_kernel(fold, offset, table_ref, n_ref, y_ref, sums_ref, gains_ref, w_ref, *refs):
    more, (h_ref, out_ref, osums_ref) = refs[:-3], refs[-3:]
    size, width = y_ref.shape[0], y_ref.shape[2]
    sums = sums_ref[:, offset : offset + width]
    sums = folded(sums) if fold else sums
    factor, shift, _, _ = scale_of(sums, gains_ref[...], n_ref[1 if fold else 0])

    def fill(p, frames, carry):
        v = gelu(y_ref[pl.ds(p, SMALL)] * factor[None] + shift[None])
        h_ref[pl.ds(p, SMALL)] = (v * tile_mask(frames, width)).astype(BF16)
        return carry

    sweep(table_ref, size, SMALL, fill)

    def body(p, frames, carry):
        out = cells(nn(rows_bf(h_ref[pl.ds(p, BIG)]), w_ref[...]))
        out_ref[pl.ds(p, BIG)] = out.astype(BF16)
        masked = out * tile_mask(frames, out.shape[-1])
        return carry[0] + down(masked), carry[1] + down(masked * out)

    wide_out = out_ref.shape[2]
    a, b = sweep(table_ref, size, BIG, body, (jnp.zeros((8, wide_out), F32),) * 2)
    osums_ref[0:1, 0:wide_out], osums_ref[1:2, 0:wide_out] = flat(a), flat(b)
    for ref in more:
        osums_ref[:, wide_out : wide_out + ref.shape[1]] = ref[...]
        wide_out += ref.shape[1]


def fast_out_kernel(offset, table_ref, n_ref, fc_ref, sums_ref, gains_ref, fx_ref, cot_ref, out_ref, up_ref, slopes_ref):
    size, width = fc_ref.shape[0], fc_ref.shape[2]
    factor, shift, center, inv_std = scale_of(folded(sums_ref[:, offset : offset + width]), gains_ref[...], n_ref[1])
    for z in range(4):
        lanes = slice(128 * z, 128 * z + 128)
        vecs = [v[:, lanes][None] for v in (factor, shift, center, inv_std)]

        def body(p, frames, carry, z=z, lanes=lanes, vecs=vecs):
            fz, sz, cz, rz = vecs
            y = fc_ref[pl.ds(p, SMALL), :, lanes].astype(F32)
            mask = tile_mask(frames, 128)
            total = y * fz + sz + fx_ref[pl.ds(p, SMALL), :, lanes].astype(F32)
            value, slope = gelu_pair(total)
            out_ref[z ^ table_ref[5], pl.ds(p, SMALL)] = (value * mask).astype(BF16)
            up = slope * (cot_ref[z ^ table_ref[5], pl.ds(p, SMALL)].astype(F32) * mask)
            up_ref[pl.ds(p, SMALL), :, lanes] = up.astype(BF16)
            return carry[0] + down(up), carry[1] + down(up * ((y - cz) * rz))

        a, b = sweep(table_ref, size, SMALL, body, (jnp.zeros((8, 128), F32),) * 2)
        slopes_ref[0:1, lanes], slopes_ref[1:2, lanes] = flat(a), flat(b)


def slow_out_kernel(table_ref, n_ref, sc_ref, sp_ref, sums_ref, gains_ref, cot_ref, more_ref, out_ref, up_ref, slopes_ref):
    size, width = sc_ref.shape[0], sc_ref.shape[2]
    cf, cs, cc, cr = scale_of(sums_ref[:, 0:width], gains_ref[0:2], n_ref[0])
    pf, ps, pc, pr = scale_of(sums_ref[:, width : 2 * width], gains_ref[2:4], n_ref[0])
    for z in range(4):
        lanes = slice(256 * z, 256 * z + 256)
        vecs = [v[:, lanes][None] for v in (cf, cs + ps, cc, cr, pf, pc, pr)]

        def body(p, frames, carry, z=z, lanes=lanes, vecs=vecs):
            cf, shift, cc, cr, pf, pc, pr = vecs
            yc, yp = (ref[pl.ds(p, SMALL), :, lanes].astype(F32) for ref in (sc_ref, sp_ref))
            mask = tile_mask(frames, 256)
            value, slope = gelu_pair(yc * cf + yp * pf + shift)
            out_ref[z ^ table_ref[5], pl.ds(p, SMALL)] = (value * mask).astype(BF16)
            up = slope * (cot_ref[z ^ table_ref[5], pl.ds(p, SMALL)].astype(F32) * mask)
            up_ref[pl.ds(p, SMALL), :, lanes] = up.astype(BF16)
            return (carry[0] + down(up), carry[1] + down(up * ((yc - cc) * cr)), carry[2] + down(up * ((yp - pc) * pr)))

        a, b, c = sweep(table_ref, size, SMALL, body, (jnp.zeros((8, 256), F32),) * 3)
        own, other = lanes, slice(width + 256 * z, width + 256 * z + 256)
        slopes_ref[0:1, own], slopes_ref[1:2, own] = flat(a), flat(b)
        slopes_ref[0:1, other], slopes_ref[1:2, other] = flat(a), flat(c)
    slopes_ref[:, 2 * width :] = more_ref[...]


def norm_back_fill(table_ref, up_ref, y_ref, dy_ref, factor, k0, k1):
    def fill(p, frames, carry):
        mask = tile_mask(frames, 128)
        for q in range(y_ref.shape[2] // 128):
            lanes = slice(128 * q, 128 * q + 128)
            y = y_ref[pl.ds(p, SMALL), :, lanes].astype(F32)
            dy = up_ref[pl.ds(p, SMALL), :, lanes].astype(F32) * factor[:, lanes][None]
            dy = dy - mask * (k0[:, lanes][None] + k1[:, lanes][None] * y)
            dy_ref[pl.ds(p, SMALL), :, lanes] = dy.astype(BF16)
        return carry

    sweep(table_ref, y_ref.shape[0], SMALL, fill)


def expand_back_kernel(fold, offsets, table_ref, n_ref, up_ref, y_ref, sums_ref, gains_ref, slopes_ref, z_ref, zsums_ref, zgains_ref,
                       w_ref, other_ref, dy_ref, dz_ref, oslopes_ref, first_ref, last_ref):
    size, width, inner = y_ref.shape[0], y_ref.shape[2], z_ref.shape[2]
    fix = folded if fold else (lambda v: v)
    inv_n = n_ref[1 if fold else 0]
    at_y, at_s, at_z = offsets
    factor, shift, center, inv_std = scale_of(fix(sums_ref[:, at_y : at_y + width]), gains_ref[...], inv_n)
    k0, k1 = slope_of(fix(slopes_ref[:, at_s : at_s + width]), factor, center, inv_std, inv_n)
    norm_back_fill(table_ref, up_ref, y_ref, dy_ref, factor, k0, k1)
    zf, zs, zc, zr = scale_of(fix(zsums_ref[:, at_z : at_z + inner]), zgains_ref[...], inv_n)

    def body(p, frames, carry):
        dh = cells(nt(rows_bf(dy_ref[pl.ds(p, BIG)]), w_ref[...]))
        z = z_ref[pl.ds(p, BIG)]
        dz = gelu_slope(z * zf[None] + zs[None]) * dh * tile_mask(frames, inner)
        dz_ref[pl.ds(p, BIG)] = dz
        return carry[0] + down(dz), carry[1] + down(dz * ((z - zc[None]) * zr[None]))

    a, b = sweep(table_ref, size, BIG, body, (jnp.zeros((8, inner), F32),) * 2)
    oslopes_ref[0:1, 0:inner], oslopes_ref[1:2, 0:inner] = flat(a), flat(b)
    halo = first_ref.shape[0]
    first_ref[:, :, 0:inner], last_ref[:, :, 0:inner] = dz_ref[0:halo], dz_ref[size - halo : size]
    if fold:
        first_ref[:, :, inner:], last_ref[:, :, inner:] = other_ref[0:halo], other_ref[size - halo : size]
    else:
        oslopes_ref[:, inner:] = other_ref[...]


def bypass_back_kernel(table_ref, n_ref, up_ref, y_ref, sums_ref, gains_ref, slopes_ref, w_ref, wl_ref, dy_ref, dx_ref, dl_ref):
    size, width = y_ref.shape[0], y_ref.shape[2]
    factor, shift, center, inv_std = scale_of(sums_ref[:, width : 2 * width], gains_ref[...], n_ref[0])
    k0, k1 = slope_of(slopes_ref[:, width : 2 * width], factor, center, inv_std, n_ref[0])
    norm_back_fill(table_ref, up_ref, y_ref, dy_ref, factor, k0, k1)

    def body(p, carry):
        dy = rows_bf(dy_ref[pl.ds(p, BIG)])
        dx_ref[pl.ds(p, BIG)] = cells(nt(dy, w_ref[...])).astype(BF16)
        dl_ref[pl.ds(p, BIG)] = cells(nt(dy, wl_ref[...]))
        return carry

    steps(size, BIG, body, 0)


def conv_back_kernel(halo, row_len, per_clip, fold, offsets, table_ref, n_ref, ysums_ref, ygains_ref, slopes_ref, ylo_ref, y_ref, yhi_ref,
                     dlo_ref, d_ref, dhi_ref, w_ref, z_ref, zsums_ref, zgains_ref, dy_ref, dz_ref, oslopes_ref, pad_ref):
    size, width = y_ref.shape[0], y_ref.shape[2]
    fix = folded if fold else (lambda v: v)
    inv_n = n_ref[1 if fold else 0]
    at_y, at_s, at_z, at_yhalo, at_dhalo = offsets
    factor, shift, center, inv_std = scale_of(fix(ysums_ref[:, at_y : at_y + width]), ygains_ref[...], inv_n)
    k0, k1 = slope_of(fix(slopes_ref[:, at_s : at_s + width]), factor, center, inv_std, inv_n)

    def value(refs, p, step):
        y_of, d_of = refs
        if y_of is y_ref:
            y, d = y_of[pl.ds(p, step)], d_of[pl.ds(p, step)]
        else:
            y, d = y_of[pl.ds(p, step), :, at_yhalo : at_yhalo + width], d_of[pl.ds(p, step), :, at_dhalo : at_dhalo + width]
        return (d * factor[None] - (k0[None] + k1[None] * y)).astype(BF16).astype(F32)

    fill_padded(table_ref, ((ylo_ref, dlo_ref), (y_ref, d_ref), (yhi_ref, dhi_ref)), 0, pad_ref, value, halo, size)

    def copy(p, carry):
        dy_ref[pl.ds(p, SMALL)] = pad_ref[1, pl.ds(halo + p, SMALL)].astype(BF16)
        return carry

    steps(size, SMALL, copy, 0)
    zf, zs, zc, zr = scale_of(fix(zsums_ref[:, at_z : at_z + width]), zgains_ref[...], inv_n)

    def body(p, frames, carry):
        dh = conv_rows(table_ref, per_clip, pad_ref, lambda i, j: w_ref[8 - 3 * i - j], p, halo, row_len, nt if fold else nn)
        z = z_ref[pl.ds(p, BIG)]
        dz = gelu_slope(z * zf[None] + zs[None]) * dh * tile_mask(frames, width)
        dz_ref[pl.ds(p, BIG)] = dz
        return carry[0] + down(dz), carry[1] + down(dz * ((z - zc[None]) * zr[None]))

    a, b = sweep(table_ref, size, BIG, body, (jnp.zeros((8, width), F32),) * 2)
    oslopes_ref[0:1], oslopes_ref[1:2] = flat(a), flat(b)


def slow_back_kernel(table_ref, n_ref, dz_ref, y_ref, sums_ref, gains_ref, slopes_ref, w_ref, wl_ref, dx_ref, dl_ref,
                     lp_ref, lsums_ref, lgains_ref, taps_ref, out_ref, dzl_ref, oslopes_ref):
    size = y_ref.shape[0]
    factor, shift, center, inv_std = scale_of(sums_ref[:, 0:256], gains_ref[...], n_ref[0])
    k0, k1 = slope_of(slopes_ref[...], factor, center, inv_std, n_ref[0])

    def fill(p, frames, carry):
        dy = dz_ref[pl.ds(p, SMALL)] * factor[None]
        dy = dy - tile_mask(frames, 256) * (k0[None] + k1[None] * y_ref[pl.ds(p, SMALL)])
        taps_ref[pl.ds(p, SMALL), :, 0:256] = sooner(dy).astype(BF16)
        taps_ref[pl.ds(p, SMALL), :, 256:512] = dy.astype(BF16)
        taps_ref[pl.ds(p, SMALL), :, 512:768] = later(dy).astype(BF16)
        return carry

    sweep(table_ref, size, SMALL, fill)
    lf, ls, lc, lr = scale_of(lsums_ref[:, 128:384], lgains_ref[...], n_ref[0])

    def body(p, frames, carry):
        taps = rows_bf(taps_ref[pl.ds(p, BIG)])
        mask = tile_mask(frames, 256)
        for z in range(4):
            lanes = slice(256 * z, 256 * z + 256)
            dx = cells(nn(taps, w_ref[:, lanes])) + dx_ref[pl.ds(p, BIG), :, lanes].astype(F32)
            out_ref[z ^ table_ref[5], pl.ds(p, BIG)] = (dx * mask).astype(BF16)
        dl = cells(nn(taps, wl_ref[...])) + dl_ref[pl.ds(p, BIG)]
        y = lp_ref[pl.ds(p, BIG)]
        dz = gelu_slope(y * lf[None] + ls[None]) * dl * mask
        dzl_ref[pl.ds(p, BIG)] = dz
        return carry[0] + down(dz), carry[1] + down(dz * ((y - lc[None]) * lr[None]))

    a, b = sweep(table_ref, size, BIG, body, (jnp.zeros((8, 256), F32),) * 2)
    oslopes_ref[0:1], oslopes_ref[1:2] = flat(a), flat(b)


def fast_back_kernel(at_s, table_ref, n_ref, sums_ref, fgains_ref, lgains_ref, fslopes_ref, lslopes_ref, dzf_ref, fa_ref, dzl_ref, lp_ref,
                     up_ref, w_ref, taps_ref, out_ref):
    size = fa_ref.shape[0]
    ff, fs, fc, fr = scale_of(folded(sums_ref[:, 0:128]), fgains_ref[...], n_ref[1])
    f0, f1 = slope_of(folded(fslopes_ref[:, at_s : at_s + 128]), ff, fc, fr, n_ref[1])
    lf, ls, lc, lr = scale_of(sums_ref[:, 128:384], lgains_ref[...], n_ref[0])
    l0, l1 = slope_of(lslopes_ref[...], lf, lc, lr, n_ref[0])

    def fill(p, frames, carry):
        dy = dzf_ref[pl.ds(p, SMALL)] * ff[None]
        dy = dy - tile_mask(frames, 128) * (f0[None] + f1[None] * fa_ref[pl.ds(p, SMALL)])
        taps_ref[pl.ds(p, SMALL), :, 0:128] = dy.astype(BF16)
        taps_ref[pl.ds(p, SMALL), :, 128:256] = sooner(dy).astype(BF16)
        taps_ref[pl.ds(p, SMALL), :, 256:384] = later(dy).astype(BF16)
        dy = dzl_ref[pl.ds(p, SMALL)] * lf[None]
        dy = dy - tile_mask(frames, 256) * (l0[None] + l1[None] * lp_ref[pl.ds(p, SMALL)])
        taps_ref[pl.ds(p, SMALL), :, 384:640] = dy.astype(BF16)
        taps_ref[pl.ds(p, SMALL), :, 640:896] = sooner(dy).astype(BF16)
        return carry

    sweep(table_ref, size, SMALL, fill)

    def body(p, frames, carry):
        dx = cells(nn(rows_bf(taps_ref[pl.ds(p, BIG)]), w_ref[...]))
        mask = tile_mask(frames, 128)
        for z in range(4):
            lanes = slice(128 * z, 128 * z + 128)
            up = up_ref[pl.ds(p, BIG), :, lanes].astype(F32)
            out_ref[z ^ table_ref[5], pl.ds(p, BIG)] = ((dx[:, :, lanes] + up) * mask).astype(BF16)
        return carry

    sweep(table_ref, size, BIG, body)


def tn(a, b):
    return lax.dot_general(a, b, (((0,), (0,)), ((), ())), preferred_element_type=F32)


def conv_weight_kernel(halo, row_len, per_clip, fold, table_ref, act_ref, dy_ref, out_ref, pad_ref, acc_ref):
    size, width = dy_ref.shape[0], dy_ref.shape[2]
    phase = table_ref[5] * (size // SMALL)

    def copy(p, carry):
        v = act_ref[pl.ds(p, 3)].astype(F32)
        for k in range(3):
            pad_ref[k, pl.ds(p, 3)] = v
        return carry

    steps(size + 2 * halo, 3, copy, 0)
    parts = size // SMALL

    def clear(i, carry):
        even = ((phase + i) % 2 == 0).astype(F32)
        at = halo + (i - 2) * SMALL
        pad_ref[0, pl.ds(at + SMALL - 1, 1)] = pad_ref[0, pl.ds(at + SMALL - 1, 1)] * even
        pad_ref[2, pl.ds(at, 1)] = pad_ref[2, pl.ds(at, 1)] * (1.0 - even)
        return carry

    lax.fori_loop(0, parts + 4, clear, 0)
    low_even = ((phase + 1) % 2 == 0).astype(F32)
    pad_ref[0, 0:1] = pad_ref[0, 0:1] * low_even
    high_even = ((phase + parts) % 2 == 0).astype(F32)
    end = size + 2 * halo
    pad_ref[2, end - 1 : end] = pad_ref[2, end - 1 : end] * (1.0 - high_even)

    for c in range(size // BIG):
        p = c * BIG
        top, bottom = edge_scales(table_ref, p, per_clip)
        dy = rows_bf(dy_ref[p : p + BIG])
        for i in range(3):
            begin = p + halo + row_len * (i - 1)
            taps = []
            for j in range(3):
                v = pad_ref[j, begin + j - 1 : begin + j - 1 + BIG]
                if i == 0:
                    v = jnp.concatenate([v[0:row_len] * top, v[row_len:]], axis=0)
                if i == 2:
                    v = jnp.concatenate([v[: BIG - row_len], v[BIG - row_len :] * bottom], axis=0)
                taps.append(rows(v).astype(BF16))
            taps = jnp.concatenate(taps, axis=1)
            part = tn(taps, dy) if fold else tn(dy, taps)
            acc_ref[i] = part if c == 0 else acc_ref[i] + part
    if fold:
        out_ref[...] = acc_ref[...]
        return
    for i in range(3):
        for j in range(3):
            v = acc_ref[i, :, width * j : width * j + width].reshape(4, 8, 8, width)
            out_ref[:, :, 3 * i + j] = v.astype(BF16)


def fast_grads_kernel(first_ref, sp_ref, ex_ref, lat_ref, out_ref):
    def pick(at, count, r, ref=first_ref):
        return sum(lane_group(moved(ref[at : at + count, 128 * z : 128 * z + 128], 32 * z - 32 * r), z) for z in range(4))

    taps = [pick(640, 256, 2), pick(640, 256, 3), pick(384, 256, 0), pick(384, 256, 1), pick(384, 256, 2)]
    for j in range(5):
        lat_ref[:, :, j] = taps[j].reshape(4, 8, 8, 128).astype(BF16)
    for j in range(3):
        total = sum(pick(32 * q, 32, q + j - 1) for q in range(4) if 0 <= q + j - 1 < 4)
        if j == 0:
            total = total + pick(128, 32, 3)
        if j == 2:
            total = total + pick(352, 32, 0)
        out_ref[4 * j : 4 * j + 4] = total.reshape(4, 8, 128).astype(BF16)
    total = sum(pick(32 * r, 32, r, ex_ref) for r in range(4))
    out_ref[12:16] = total.reshape(4, 8, 128).astype(BF16)
    for i in range(3):
        total = None
        for j in range(3):
            tap = sum(
                lane_group(moved(sp_ref[i, 128 * j + 32 * r : 128 * j + 32 * r + 32, :], 32 * j - 32 * r), j) for r in range(4)
            )
            total = tap if total is None else total + tap
        out_ref[16 + 4 * i : 20 + 4 * i] = total.reshape(4, 8, 128).astype(BF16)


def swap(tree, axis, size, distance):
    pairs = [(i, i ^ distance) for i in range(size)]
    return jax.tree.map(lambda v: lax.ppermute(v, axis, pairs), tree)


def add(*trees):
    def total(*vs):
        wide_vs = [v.astype(F32) for v in vs]
        out = wide_vs[0] + wide_vs[1]
        if len(vs) == 4:
            out = out + (wide_vs[2] + wide_vs[3])
        return out.astype(vs[0].dtype)

    return jax.tree.map(total, *trees)


def stages(size, first_alone):
    bits = [1 << i for i in range(size.bit_length() - 1)]
    out = []
    if first_alone and bits:
        out.append(bits[:1])
        bits = bits[1:]
    while bits:
        out.append(bits[:2])
        bits = bits[2:]
    return out


def butterfly(tree, axis, size, bits):
    if len(bits) == 1:
        return add(tree, swap(tree, axis, size, bits[0]))
    near, far, both = (swap(tree, axis, size, k) for k in (bits[0], bits[1], bits[0] + bits[1]))
    return add(tree, near, far, both)


def everywhere(tree, sizes):
    for axis, size in sizes.items():
        for bits in stages(size, axis == "dp"):
            tree = butterfly(tree, axis, size, bits)
    return tree


def halos(first, last, count):
    low = lax.ppermute(last, "chan", [(i, i + 1) for i in range(count - 1)])
    high = lax.ppermute(first, "chan", [(i + 1, i) for i in range(count - 1)])
    return low, high


def gather_group(tree, sizes):
    dp = sizes["dp"]
    by_chip = [tree] + [swap(tree, "dp", dp, 2 * k) for k in (1, 2, 3)]
    out = []
    for piece in by_chip:
        out += [piece, swap(piece, "dp", dp, 1)]
    return out


def pick(v, index, axis):
    return lax.dynamic_index_in_dim(v, index, axis, keepdims=False)


def scatter_sum(tree, sizes, group, chan):
    dp = sizes["dp"]
    core, chip = group % 2, group // 2
    tree = jax.tree.map(lambda v: v.reshape(v.shape[0], 4, 2, *v.shape[2:]), tree)
    sent = jax.tree.map(lambda v: pick(v, 1 - core, 2), tree)
    kept = jax.tree.map(lambda v: pick(v, core, 2), tree)
    tree = add(kept, swap(sent, "dp", dp, 1))
    got = [swap(jax.tree.map(lambda v: pick(v, chip ^ k, 1), tree), "dp", dp, 2 * k) for k in (1, 2, 3)]
    tree = add(jax.tree.map(lambda v: pick(v, chip, 1), tree), *got)
    size = sizes["chan"]
    got = [swap(jax.tree.map(lambda v: pick(v, chan ^ k, 0), tree), "chan", size, k) for k in (1, 2, 3)]
    tree = add(jax.tree.map(lambda v: pick(v, chan, 0), tree), *got)
    bits = [1 << i for i in range(3, dp.bit_length() - 1)]
    while bits:
        tree = butterfly(tree, "dp", dp, bits[:2])
        bits = bits[2:]
    return tree


def send_blocks(blocks, size):
    return [blocks[0]] + [swap(blocks[k], "chan", size, k) for k in range(1, size)]


def weight_sum(a, b, dtype=BF16):
    return jnp.einsum("pti,pto->io", a, b, preferred_element_type=F32).astype(dtype)


def local(
    sizes,
    slow_input,
    fast_input,
    clip_counts,
    frame_counts,
    fast_reduce,
    fast_spatial,
    fast_expand,
    lateral_kernel,
    slow_reduce,
    lateral_reduce,
    slow_spatial,
    slow_expand,
    shortcut,
    lateral_shortcut,
    fast_inner_norm,
    fast_outer_norm,
    lateral_norm,
    slow_inner_norm,
    slow_outer_norm,
    slow_cotangent,
    fast_cotangent,
):
    ways = sizes["chan"]
    clips, slow_t, height, across, slow_part = slow_input.shape
    fast_t, fast_part = fast_input.shape[1], fast_input.shape[4]
    ratio = fast_t // slow_t
    area = height * across
    places = clips * area
    mine = places // ways
    halo = across + 1
    chan, dp = lax.axis_index("chan"), lax.axis_index("dp")
    group = dp % 8
    ids = jnp.stack([dp, chan, group]).astype(jnp.int32)
    wide_in = ways * slow_part
    wide_f = ways * 128
    mid = 256
    ext = mine + 2 * halo
    per_clip = area // BIG
    chunk = 98

    def packed(v):
        v = v.transpose(0, 2, 3, 1, 4).reshape(places, fast_t, fast_part)
        return pl.pallas_call(
            functools.partial(pack_kernel, area // chunk, clips),
            grid=(places // chunk,),
            out_shape=shape((places, slow_t, 128), BF16),
            in_specs=[pl.BlockSpec(memory_space=pltpu.SMEM)] * 3
            + [pl.BlockSpec((chunk, fast_t, fast_part), lambda i: (i, 0, 0))],
            out_specs=pl.BlockSpec((chunk, slow_t, 128), lambda i: (i, 0, 0)),
            scratch_shapes=[pltpu.VMEM((chunk * fast_t, fast_part), F32)],
            compiler_params=pltpu.CompilerParams(vmem_limit_bytes=12 * 1024 * 1024),
            name="fast_pack",
        )(ids, clip_counts, frame_counts, v).reshape(ways, mine, slow_t, 128)

    def unpacked(pieces):
        (out,) = call(
            unpack_kernel,
            [shape((places, fast_t, fast_part), BF16)],
            [ids, *pieces],
            [pltpu.VMEM((BIG * fast_t, fast_part), F32)],
            smem=1,
            name="fast_unpack",
        )
        return out.reshape(clips, height, across, fast_t, fast_part).transpose(0, 3, 1, 2, 4)

    def split(v):
        return v.transpose(0, 2, 3, 1, 4).reshape(ways, mine, slow_t, slow_part)

    def joined(pieces):
        (v,) = call(
            place_kernel, [shape((ways, mine, slow_t, slow_part), BF16)], [ids, *pieces], smem=1, name="slow_place"
        )
        return v.reshape(clips, height, across, slow_t, slow_part).transpose(0, 3, 1, 2, 4)

    def exchanged(v):
        return send_blocks([pick(v, chan ^ k, 0) for k in range(ways)], ways)

    def returned(v):
        return send_blocks([v[k] for k in range(ways)], ways)

    fx_pieces = exchanged(packed(fast_input))
    x_pieces = exchanged(split(slow_input))

    all_clips = frame_counts.shape[0]
    live = (jnp.arange(all_clips, dtype=jnp.int32) % clips) < jnp.repeat(clip_counts, clips)
    valid = jnp.where(live, frame_counts, 0)
    count = jnp.sum(valid).astype(F32) * area
    inv_n = jnp.stack([1.0 / count, 1.0 / (count * ratio)])
    parts = mine // BIG
    clip = (chan * parts + jnp.arange(-1, parts + 1)) // per_clip
    clip = jnp.clip(clip, 0, clips - 1) + dp * clips
    around = jnp.sum(jnp.where(clip[:, None] == jnp.arange(all_clips)[None, :], valid[None, :], 0), axis=1)
    table = jnp.concatenate([around, jnp.stack([chan, jnp.full_like(chan, parts)])]).astype(jnp.int32)

    def share_of(v, axis):
        amount = v.shape[axis] // 8
        return lax.dynamic_slice_in_dim(v, group * amount, amount, axis).astype(BF16)

    def over_chan(tree):
        pieces = [tree] + [swap(tree, "chan", ways, k) for k in (1, 2, 3)]
        return jax.tree.map(lambda *vs: jnp.stack(vs), *pieces)

    lat_t, red_t, lred_t = (v.transpose(0, 2, 1) for v in (lateral_kernel, slow_reduce, lateral_reduce))
    tree = (jnp.concatenate([share_of(red_t, 1), share_of(lred_t, 1)], axis=2), share_of(lat_t, 1))

    def blocks_of(v):
        width = v.shape[-1]
        tiled = jnp.concatenate([v] * ways, axis=1)
        return jnp.where(jnp.arange(ways * width)[None, :] // width == chan, tiled, 0.0)

    mid_g = blocks_of(jnp.concatenate([lateral_norm, slow_inner_norm.reshape(4, -1)]))
    out_g = blocks_of(slow_outer_norm.reshape(4, -1))
    mid_g, out_g = butterfly((mid_g, out_g), "chan", ways, (1, 2))
    lat_g, in_g = mid_g[0:2], (mid_g[2:4], mid_g[4:6])
    pieces = gather_group(over_chan(tree), sizes)
    fr_t = fast_reduce.transpose(0, 2, 1)
    red_w, lred_w, w_first, w_fsp, w_fex, fin_g, fout_g = call(
        first_weights_kernel,
        [
            shape((3, ways, 8, 8, wide_in), BF16),
            shape((3, ways, 8, 8, mid), BF16),
            shape((896, wide_f), BF16),
            shape((9, 128, 128), BF16),
            shape((128, wide_f), BF16),
            shape((4, 128)),
            shape((2, wide_f)),
        ],
        [ids, *(p[0] for p in pieces), *(p[1] for p in pieces), fr_t, fast_spatial.reshape(9, *fast_spatial.shape[2:]), fast_expand,
         fast_inner_norm.reshape(4, -1), fast_outer_norm],
        [pltpu.VMEM((5, ways, 8, 8, 128), F32)],
        smem=1,
        name="first_weights",
    )
    red_w, lred_w = red_w.reshape(-1, wide_in), lred_w.reshape(-1, mid)
    fin_g = (fin_g[0:2], fin_g[2:4])
    spatial_t = slow_spatial.reshape(9, slow_spatial.shape[2], -1).transpose(0, 2, 1)
    tree = (
        jnp.concatenate([share_of(v, 0).reshape(-1, 8, wide_in) for v in (slow_expand, shortcut, lateral_shortcut)]),
        share_of(spatial_t, 1),
    )
    pieces = gather_group(over_chan(tree), sizes)
    exp_w, short_w, lshort_w, spat_w = call(
        second_weights_kernel,
        [
            shape((ways, 8, 8, wide_in), BF16),
            shape((ways, 8, 4, 8, wide_in), BF16),
            shape((ways, 8, 8, wide_in), BF16),
            shape((9, ways, 8, 8, mid), BF16),
        ],
        [ids, *(p[0] for p in pieces), *(p[1] for p in pieces)],
        smem=1,
        name="second_weights",
    )
    exp_w, short_w, lshort_w = (v.reshape(-1, wide_in) for v in (exp_w, short_w, lshort_w))
    spat_w = spat_w.reshape(9, mid, mid)

    edge = [shape((halo, 8, 128))] * 2
    edges = [shape((halo, 8, 384))] * 2
    narrow, middle = shape((mine, 8, 128)), shape((mine, 8, mid))
    fx, fa, lp, sums1, first, last = call(
        fast_first_kernel,
        [shape((mine, 8, wide_f), BF16), narrow, middle, shape((2, 384)), *edge],
        [table, *fx_pieces, w_first],
        smem=1,
        name="fast_first",
    )
    sums1, fast_cotangent, slow_cotangent = lax.optimization_barrier((sums1, fast_cotangent, slow_cotangent))
    fa_lo, fa_hi = halos(first, last, ways)
    sums1 = everywhere(sums1, sizes)
    fast_pad = [pltpu.VMEM((3, ext, 8, 128), F32)]
    slow_pad = [pltpu.VMEM((3, ext, 8, mid), F32)]
    h1, fb, fb_sums = call(
        functools.partial(conv_kernel, halo, across, per_clip, True, (0, 0)),
        [shape((ext, 8, 128), BF16), narrow, shape((2, 128))],
        [table, inv_n, sums1, fin_g[0], fa_lo, fa, fa_hi, w_fsp],
        fast_pad,
        smem=2,
        name="fast_second",
    )
    x, lat, sa, sums2, first, last = call(
        slow_first_kernel,
        [shape((mine, 8, wide_in), BF16), shape((mine, 8, mid), BF16), middle, shape((2, mid + 128)), *edges],
        [table, inv_n, *x_pieces, lp, sums1, lat_g, red_w, lred_w, fb, fb_sums],
        smem=2,
        name="slow_first",
    )
    sa_lo, sa_hi = halos(first, last, ways)
    sums2 = everywhere(sums2, sizes)
    h2, fc, fc_sums = call(
        functools.partial(expand_kernel, True, mid),
        [shape((mine, 8, 128), BF16), shape((mine, 8, wide_f), BF16), shape((2, wide_f))],
        [table, inv_n, fb, sums2, fin_g[1], w_fex],
        smem=2,
        name="fast_third",
    )
    ha, sb, sums3 = call(
        functools.partial(conv_kernel, halo, across, per_clip, False, (0, 0)),
        [shape((ext, 8, mid), BF16), middle, shape((2, mid + wide_f))],
        [table, inv_n, sums2, in_g[0], sa_lo, sa, sa_hi, spat_w, fc_sums],
        slow_pad,
        smem=2,
        name="slow_second",
    )
    sums3 = everywhere(sums3, sizes)
    sp, sp_sums = call(
        bypass_kernel,
        [shape((mine, 8, wide_in), BF16), shape((2, wide_in))],
        [table, x, lat, short_w, lshort_w],
        smem=1,
        name="bypass",
    )
    fcot = jnp.stack(exchanged(packed(fast_cotangent)))
    cot = jnp.stack(exchanged(split(slow_cotangent)))
    fast_out, dfs, fc_slopes = call(
        functools.partial(fast_out_kernel, mid),
        [shape((ways, mine, 8, 128), BF16), shape((mine, 8, wide_f), BF16), shape((2, wide_f))],
        [table, inv_n, fc, sums3, fout_g, fx, fcot],
        smem=2,
        name="fast_out",
    )
    hb, sc, sums4 = call(
        functools.partial(expand_kernel, False, 0),
        [shape((mine, 8, mid), BF16), shape((mine, 8, wide_in), BF16), shape((2, 2 * wide_in + wide_f))],
        [table, inv_n, sb, sums3, in_g[1], exp_w, sp_sums, fc_slopes],
        smem=2,
        name="slow_third",
    )
    sums4 = everywhere(sums4, sizes)
    dfc, dzfb, fb_slopes, first, last = call(
        functools.partial(expand_back_kernel, True, (mid, 2 * wide_in, mid)),
        [shape((mine, 8, wide_f), BF16), narrow, shape((2, 128)), *edges],
        [table, inv_n, dfs, fc, sums3, fout_g, sums4, fb, sums2, fin_g[1], w_fex, sb],
        smem=2,
        name="fast_third_back",
    )
    slow_out, dss, sums5 = call(
        slow_out_kernel,
        [shape((ways, mine, 8, mid), BF16), shape((mine, 8, wide_in), BF16), shape((2, 2 * wide_in + 128))],
        [table, inv_n, sc, sp, sums4, out_g, cot, fb_slopes],
        smem=2,
        name="slow_out",
    )

    low5, high5 = halos(first, last, ways)
    sums5 = everywhere(sums5, sizes)
    dfb, dzfa, fa_slopes = call(
        functools.partial(conv_back_kernel, halo, across, per_clip, True, (mid, 2 * wide_in, 0, mid, 0)),
        [shape((mine, 8, 128), BF16), narrow, shape((2, 128))],
        [table, inv_n, sums2, fin_g[1], sums5, sa_lo, fb, sa_hi, low5, dzfb, high5, w_fsp, fa, sums1, fin_g[0]],
        fast_pad,
        smem=2,
        name="fast_second_back",
    )
    dsc, dzsb, sums6, first, last = call(
        functools.partial(expand_back_kernel, False, (0, 0, 0)),
        [shape((mine, 8, wide_in), BF16), middle, shape((2, mid + 128)), *[shape((halo, 8, mid))] * 2],
        [table, inv_n, dss, sc, sums4, out_g[0:2], sums5, sb, sums3, in_g[1], exp_w, fa_slopes],
        smem=2,
        name="slow_third_back",
    )
    low6, high6 = halos(first, last, ways)
    sums6 = everywhere(sums6, sizes)
    fast_output = unpacked(returned(fast_out))
    dzsb, fast_output = lax.optimization_barrier((dzsb, fast_output))
    dsp, dx, dl = call(
        bypass_back_kernel,
        [shape((mine, 8, wide_in), BF16), shape((mine, 8, wide_in), BF16), middle],
        [table, inv_n, dss, sp, sums4, out_g[2:4], sums5, short_w, lshort_w],
        smem=2,
        name="bypass_back",
    )
    dsb, dzsa, sums7 = call(
        functools.partial(conv_back_kernel, halo, across, per_clip, False, (0, 0, 0, 128, 0)),
        [shape((mine, 8, mid), BF16), middle, shape((2, mid))],
        [table, inv_n, sums3, in_g[1], sums6, low5, sb, high5, low6, dzsb, high6, spat_w, sa, sums2, in_g[0]],
        slow_pad,
        smem=2,
        name="slow_second_back",
    )
    sums7 = everywhere(sums7, sizes)
    slow_output = joined(returned(slow_out))
    dzsa, slow_output = lax.optimization_barrier((dzsa, slow_output))
    dsa, dslow, dzlp, sums8 = call(
        slow_back_kernel,
        [shape((mine, 8, 3 * mid), BF16), shape((ways, mine, 8, mid), BF16), middle, shape((2, mid))],
        [table, inv_n, dzsa, sa, sums2, in_g[0], sums7, red_w, lred_w, dx, dl, lp, sums1, lat_g],
        smem=2,
        name="slow_first_back",
    )
    slow_input_grad = joined(returned(dslow))
    sums8 = everywhere(sums8, sizes)
    dfirst, dfast = call(
        functools.partial(fast_back_kernel, mid),
        [shape((mine, 8, 896), BF16), shape((ways, mine, 8, 128), BF16)],
        [table, inv_n, sums1, fin_g[0], lat_g, sums6, sums8, dzfa, fa, dzlp, lp, dfs, w_first],
        smem=2,
        name="fast_first_back",
    )

    fast_input_grad = unpacked(returned(dfast))

    def shares(v, lead):
        return v.reshape(ways, 8, lead, 8, v.shape[-1])

    g_wide = jnp.concatenate(
        [shares(weight_sum(hb, dsc), 1), shares(weight_sum(x, dsp), 4), shares(weight_sum(lat, dsp), 1)], axis=2
    )
    (g_spat,) = call(
        functools.partial(conv_weight_kernel, halo, across, per_clip, False),
        [shape((ways, 8, 9, 8, mid), BF16)],
        [table, ha, dsb],
        [*slow_pad, pltpu.VMEM((3, mid, 3 * mid), F32)],
        smem=1,
        name="slow_spatial_grad",
    )
    pieces = gather_group(scatter_sum((g_wide, g_spat), sizes, group, chan), sizes)
    g_exp, g_short, g_lshort, g_spat = call(
        first_grads_kernel,
        [shape((8, 8, wide_in)), shape((8, 4, 8, wide_in)), shape((8, 8, wide_in)), shape((9, 8, 8, mid))],
        [ids, *(p[0] for p in pieces), *(p[1] for p in pieces)],
        smem=1,
        name="first_grads",
    )
    (g_fsp,) = call(
        functools.partial(conv_weight_kernel, halo, across, per_clip, True),
        [shape((3, 384, 128))],
        [table, h1, dfb],
        [*fast_pad, pltpu.VMEM((3, 384, 128), F32)],
        smem=1,
        name="fast_spatial_grad",
    )
    g_fex = weight_sum(h2, dfc, F32)
    g_lat, g_fast = call(
        fast_grads_kernel,
        [shape((ways, 8, 5, 8, 128), BF16), shape((28, 8, 128), BF16)],
        [weight_sum(dfirst, fx, F32), g_fsp, g_fex],
        name="fast_grads",
    )
    g_red = weight_sum(dsa, jnp.concatenate([x, lat], axis=2)).reshape(3, ways, 8, 8, wide_in + mid).transpose(1, 2, 0, 3, 4)
    g_fast = everywhere(g_fast, sizes)
    pieces = gather_group(scatter_sum((g_red, g_lat), sizes, group, chan), sizes)
    g_red, g_lred, g_lat = call(
        second_grads_kernel,
        [shape((3, 8, 8, wide_in)), shape((3, 8, 8, mid)), shape((5, 8, 8, 128))],
        [ids, *(p[0] for p in pieces), *(p[1] for p in pieces)],
        smem=1,
        name="second_grads",
    )
    g_fast = g_fast.astype(F32)
    g_fred = g_fast[0:12].reshape(3, 32, 128).transpose(0, 2, 1)
    g_fex = g_fast[12:16].reshape(32, 128)
    g_fsp = g_fast[16:28].reshape(3, 32, 128)[:, :, 0:96].reshape(3, 32, 3, 32).transpose(0, 2, 1, 3)

    def pair(slopes):
        return slopes[::-1]

    def own(v, width):
        return lax.dynamic_slice_in_dim(v, chan * width, width, v.ndim - 1)

    def fold_in(slopes):
        return jnp.sum(slopes.reshape(2, ratio, 128 // ratio), axis=1)

    lw, sw, ow = lateral_norm.shape[1], slow_inner_norm.shape[2], slow_outer_norm.shape[2]
    fast_inner_grad = jnp.stack([pair(fold_in(sums6[:, mid:])), pair(fold_in(sums5[:, 2 * wide_in :]))])
    fc_slopes = sums4[:, 2 * wide_in :].reshape(2, ways, ratio, fast_part)
    fast_outer_grad = pair(jnp.sum(fc_slopes, axis=2).reshape(2, -1))
    lateral_grad = pair(own(sums8, lw))
    slow_inner_grad = own(jnp.stack([pair(sums7), pair(sums6[:, 0:mid])]), sw)
    slow_outer_grad = own(jnp.stack([pair(sums5[:, 0:wide_in]), pair(sums5[:, wide_in : 2 * wide_in])]), ow)
    return (
        slow_output,
        fast_output,
        slow_input_grad,
        fast_input_grad,
        g_fred,
        g_fsp,
        g_fex,
        g_lat.reshape(5, -1, 128).transpose(0, 2, 1),
        g_red.reshape(3, -1, wide_in).transpose(0, 2, 1),
        g_lred.reshape(3, -1, mid).transpose(0, 2, 1),
        g_spat.reshape(9, -1, mid).transpose(0, 2, 1).reshape(slow_spatial.shape),
        g_exp.reshape(-1, wide_in),
        g_short.reshape(-1, wide_in),
        g_lshort.reshape(-1, wide_in),
        fast_inner_grad,
        fast_outer_grad,
        lateral_grad,
        slow_inner_grad,
        slow_outer_grad,
    )


def solution(mesh):
    sizes = {"dp": mesh.shape["dp"], "chan": mesh.shape["chan"]}
    big = P("dp", None, None, None, "chan")
    last2, last3, last4 = P(None, "chan"), P(None, None, "chan"), P(None, None, None, "chan")
    first = P("chan", None)
    return jax.shard_map(
        functools.partial(local, sizes),
        mesh=mesh,
        in_specs=(
            big, big, P(), P(), P(), P(), P(), last3, last3, last3, last4, first, first, first,
            P(), P(), last2, last3, last3, big, big,
        ),
        out_specs=(
            big, big, big, big, P(), P(), P(), last3, last3, last3, last4, first, first, first,
            P(), P(), last2, last3, last3,
        ),
        check_vma=False,
    )
```

time: 1040 us -> 707 us (0.68)
  blocking collectives: 146 us -> 0 us
  local copies, waits for them, and re-layouts: 190 us -> 103 us
  starting transfers between devices: 206 us -> 284 us
  matrix products: 71.5 us -> 10.2 us
  Pallas kernels: 154 us -> 103 us
  waiting for transfers between devices: 211 us -> 175 us
  other arithmetic: 38.9 us -> 17.1 us
  between operations: 17.1 us -> 4.83 us
    all_gather x7 -> x0, blocking collectives: 146 us -> none  [the longest x1 55.2 us: local(): norms = lax.all_gather(norms, 'chan', axis=0, tiled=False)]
    ppermute x119 -> x189, starting transfers between devices: 139 us -> 250 us  [swap(): return jax.tree.map(lambda v: lax.ppermute(v, axis, pairs), tree)]
    ppermute x119 -> x189, waiting for transfers between devices: 98.4 us -> 165 us  [swap(): return jax.tree.map(lambda v: lax.ppermute(v, axis, pairs), tree)]
    dot_general x25 -> x6, matrix products: 71.5 us -> 10.2 us  [weight_sum(): jnp.einsum('pti,pto->io', a, b, preferred_element_type=F32).astype(dtype)]
    pallas_call x20 -> x27, Pallas kernels: 154 us -> 96.9 us  [call(): pl.pallas_call(kernel, out_shape=tuple(outs), in_specs=specs, out_specs=t...]
    reshape x45 -> x10, local copies, waits for them, and re-layouts: 59.9 us -> 5.37 us  [the longest x1 1.61 us: local(): g_fast[16:28].reshape(3, 32, 128)[:, :, 0:96].reshape(3, 32, 3, 32)]
    unnamed x211 -> x495, local copies, waits for them, and re-layouts: 23.9 us -> 73.8 us
    unnamed x10 -> x0, waiting for transfers between devices: 47.3 us -> none
  transfers between devices with their start and end apart: 148 -> 197, of which waited for: 36 -> 67; matrix products, arithmetic and copies ran while one was open for 27% -> 8% of each run, Pallas kernels for 15% -> 13%
where the time goes in v2:
time: 707 us; the launch traced here: 697 us
  starting transfers between devices  284 us (40%)
  waiting for transfers between devices  175 us (25%)
  local copies, waits for them, and re-layouts  103 us (15%)
  Pallas kernels  103 us (15%)
  other arithmetic  17.1 us (2%)
  matrix products  10.2 us (1%)
    ppermute x189, starting transfers between devices, swap(): return jax.tree.map(lambda v: lax.ppermute(v, axis, pairs), tree)  250 us
    ppermute x189, waiting for transfers between devices, swap(): return jax.tree.map(lambda v: lax.ppermute(v, axis, pairs), tree)  165 us
    pallas_call x27, Pallas kernels, call(): pl.pallas_call(kernel, out_shape=tuple(outs), in_specs=specs, out_specs=t...  96.9 us
    unnamed x495, local copies, waits for them, and re-layouts  73.8 us
    ppermute x4, starting transfers between devices, halos(): low = lax.ppermute(last, 'chan', [(i, i + 1) for i in range(count - 1)])  28 us
  transfers between devices with their start and end apart: 197, of which 67 were waited for; matrix products, arithmetic and copies ran while one was open for 8% of the time, Pallas kernels for 13%

profile of v2, /device:TPU:0, one launch (start us, length us, event | category | flops | bytes accessed | tf_op | source)
XLA Modules:
  0.0 696.7 jit_solution(16179076906875924520)
XLA Ops:
  2.1 4.0 collective-permute-start.17
  10.4 3.9 collective-permute-start.8
  104.7 25.3 %collective-permute-start = (bf16[147,8,256]{2,1,0:T(8,128)(2,1)}, bf16[147,8,256]{2,1,0:T(8,128)(2,1)S(1)}, u32[]{:S(2)}, u32[]{:S(2)}) collective-permute-start(bf16[147,8,256]{2,1,0:T(8,128)(2,1)} %get-tuple-element.241), channel_id=1, source_target_pairs={{0,1},{1,0},{2,3},{3,2},{4,5},{5,4},{6,7},{7,6},{8,9},{9,8},{10,11... | collective-permute-start | bytes 1806344 | tf_op jit(solution)/shard_map/ppermute | solution.py:765
  145.2 12.0 %collective-permute-start.30 = (f32[2,384]{1,0:T(2,128)S(1)}, f32[2,384]{1,0:T(2,128)S(1)}, u32[]{:S(2)}, u32[]{:S(2)}) collective-permute-start(f32[2,384]{1,0:T(2,128)S(1)} %add_add_fusion.13), channel_id=1, source_target_pairs={{0,1},{1,0},{2,3},{3,2},{4,5},{5,4},{6,7},{7,6},{8,9},{9,8},{10,11... | collective-permute-start | bytes 9224 | tf_op jit(solution)/shard_map/ppermute | solution.py:765
  161.3 3.9 collective-permute-start.36
  167.4 4.2 collective-permute-done.37.hi_ref
  179.1 5.1 slow_first.1
  199.6 3.7 collective-permute-start.45
  210.8 4.7 slow_second.1
  245.1 16.1 %collective-permute-done.75 = bf16[147,8,128]{2,1,0:T(8,128)(2,1)} collective-permute-done((bf16[147,8,128]{2,1,0:T(8,128)(2,1)}, bf16[147,8,128]{2,1,0:T(8,128)(2,1)}, u32[]{:S(2)}, u32[]{:S(2)}) %collective-permute-start.75) | collective-permute-done | bytes 301088 | tf_op jit(solution)/shard_map/ppermute | solution.py:765
  269.4 4.4 bypass.1
  274.0 4.0 fast_out.1
  298.0 8.1 %collective-permute-done.81 = f32[2,2560]{1,0:T(2,128)S(1)} collective-permute-done((f32[2,2560]{1,0:T(2,128)S(1)}, f32[2,2560]{1,0:T(2,128)S(1)}, u32[]{:S(2)}, u32[]{:S(2)}) %collective-permute-start.81) | collective-permute-done | bytes 20512 | tf_op jit(solution)/shard_map/ppermute | solution.py:765
  312.0 34.6 %collective-permute-done.88 = bf16[147,8,256]{2,1,0:T(8,128)(2,1)S(1)} collective-permute-done((bf16[147,8,256]{2,1,0:T(8,128)(2,1)S(1)}, bf16[147,8,256]{2,1,0:T(8,128)(2,1)S(1)}, u32[]{:S(2)}, u32[]{:S(2)}) %collective-permute-start.88) | collective-permute-done | bytes 602144 | tf_op jit(solution)/shard_map/ppermute | solution.py:765
  346.9 7.6 %slow_out.1 = (bf16[4,147,8,256]{3,2,1,0:T(8,128)(2,1)S(1)}, bf16[147,8,1024]{2,1,0:T(8,128)(2,1)S(1)}, f32[2,2176]{1,0:T(2,128)S(1)}) custom-call(s32[7]{0:T(128)S(1)} %copy-done.110, f32[2]{0:T(128)S(1)} %copy-done.126, bf16[147,8,1024]{2,1,0:T(8,128)(2,1)S(1)} %get-tuple-element.136.sc_ref.y_ref, ...), custom_call_target="tpu_custom_call" | custom-call | bytes 12097572 | tf_op jit(solution)/shard_map/slow_out/pallas_call | solution.py:124
  369.1 9.5 %collective-permute-start.94 = (f32[2,2176]{1,0:T(2,128)S(1)}, f32[2,2176]{1,0:T(2,128)S(1)}, u32[]{:S(2)}, u32[]{:S(2)}) collective-permute-start(f32[2,2176]{1,0:T(2,128)S(1)} %add_add_fusion.3), channel_id=1, source_target_pairs={{0,1},{1,0},{2,3},{3,2},{4,5},{5,4},{6,7},{7,6},{8,9},{9,8},{10,11... | collective-permute-start | bytes 52232 | tf_op jit(solution)/shard_map/ppermute | solution.py:765
  390.0 5.4 fast_unpack.2
  395.4 5.4 collective-permute-start.113
  400.9 5.9 bypass_back.1
  418.1 3.9 slow_third_back.1
  434.9 18.8 %collective-permute-start.106 = (f32[15,8,256]{2,1,0:T(8,128)S(1)}, f32[15,8,256]{2,1,0:T(8,128)S(1)}, u32[]{:S(2)}, u32[]{:S(2)}) collective-permute-start(f32[15,8,256]{2,1,0:T(8,128)S(1)} %get-tuple-element.149), channel_id=1, source_target_pairs={{0,1},{1,2},{2,3},{4,5},{5,6},{6,7},{8,9},{9,10},{10,11},{12,13},{... | collective-permute-start | bytes 368648 | tf_op jit(solution)/shard_map/ppermute | solution.py:806
  456.1 4.4 collective-permute-done.110.dhi_ref
  460.5 4.0 slow_second_back.1
  484.7 7.3 %collective-permute-done.120 = f32[2,256]{1,0:T(2,128)S(1)} collective-permute-done((f32[2,256]{1,0:T(2,128)S(1)}, f32[2,256]{1,0:T(2,128)S(1)}, u32[]{:S(2)}, u32[]{:S(2)}) %collective-permute-start.120) | collective-permute-done | bytes 2080 | tf_op jit(solution)/shard_map/ppermute | solution.py:765
  496.5 3.8 slow_place.2
  503.3 4.9 slow_first_back.1
  590.6 7.7 %collective-permute-start.145 = (bf16[3,8,1280]{2,1,0:T(8,128)(2,1)S(1)}, bf16[3,8,1280]{2,1,0:T(8,128)(2,1)S(1)}, u32[]{:S(2)}, u32[]{:S(2)}) collective-permute-start(bf16[3,8,1280]{2,1,0:T(8,128)(2,1)S(1)} %get-tuple-element.277), channel_id=1, source_target_pairs={{0,1},{1,0},{2,3},{3,2},{4,5},{5,4},{6,7},{7,6},{8,9},{9,8},{10,11... | collective-permute-start | bytes 184328 | tf_op jit(solution)/shard_map/ppermute | solution.py:765
  611.7 23.2 %collective-permute-done.146 = bf16[3,8,1280]{2,1,0:T(8,128)(2,1)S(1)} collective-permute-done((bf16[3,8,1280]{2,1,0:T(8,128)(2,1)S(1)}, bf16[3,8,1280]{2,1,0:T(8,128)(2,1)S(1)}, u32[]{:S(2)}, u32[]{:S(2)}) %collective-permute-start.146) | collective-permute-done | bytes 61472 | tf_op jit(solution)/shard_map/ppermute | solution.py:765
  637.5 5.2 collective-permute-done.171
  646.2 5.2 collective-permute-start.173
  652.3 10.4 %collective-permute-done.122.refs_2_ = bf16[147,8,256]{2,1,0:T(8,128)(2,1)S(1)} collective-permute-done((bf16[147,8,256]{2,1,0:T(8,128)(2,1)S(1)}, bf16[147,8,256]{2,1,0:T(8,128)(2,1)S(1)}, u32[]{:S(2)}, u32[]{:S(2)}) %collective-permute-start.122) | collective-permute-done | bytes 602144 | tf_op jit(solution)/shard_map/ppermute | solution.py:765
  683.4 5.4 fast_unpack.3
  (1015 shorter events, 420.1 us)
Async XLA Ops:
  2.1 29.9 %collective-permute-start.17 = (bf16[5,8,128]{2,1,0:T(8,128)(2,1)}, bf16[5,8,128]{2,1,0:T(8,128)(2,1)}, u32[]{:S(2)}, u32[]{:S(2)}) collective-permute-start(bf16[5,8,128]{2,1,0:T(8,128)(2,1)} %get-tuple-element.284), channel_id=1, source_target_pairs={{0,2},{1,3},{2,0},{3,1},{4,6},{5,7},{6,4},{7,5},{8,10},{9,11},{10,... | collective-permute-start | bytes 30728 | tf_op jit(solution)/shard_map/ppermute | solution.py:765
  50.3 30.4 %collective-permute-start.5 = (bf16[147,8,128]{2,1,0:T(8,128)(2,1)}, bf16[147,8,128]{2,1,0:T(8,128)(2,1)S(1)}, u32[]{:S(2)}, u32[]{:S(2)}) collective-permute-start(bf16[147,8,128]{2,1,0:T(8,128)(2,1)} %get-tuple-element.258), channel_id=1, source_target_pairs={{0,3},{1,2},{2,1},{3,0},{4,7},{5,6},{6,5},{7,4},{8,11},{9,10},{10,... | collective-permute-start | bytes 903176 | tf_op jit(solution)/shard_map/ppermute | solution.py:765
  53.7 28.3 %collective-permute-start.4 = (bf16[147,8,128]{2,1,0:T(8,128)(2,1)}, bf16[147,8,128]{2,1,0:T(8,128)(2,1)}, u32[]{:S(2)}, u32[]{:S(2)}) collective-permute-start(bf16[147,8,128]{2,1,0:T(8,128)(2,1)} %get-tuple-element.259), channel_id=1, source_target_pairs={{0,2},{1,3},{2,0},{3,1},{4,6},{5,7},{6,4},{7,5},{8,10},{9,11},{10,... | collective-permute-start | bytes 903176 | tf_op jit(solution)/shard_map/ppermute | solution.py:765
  53.7 29.3 %collective-permute-start.3 = (bf16[147,8,128]{2,1,0:T(8,128)(2,1)}, bf16[147,8,128]{2,1,0:T(8,128)(2,1)}, u32[]{:S(2)}, u32[]{:S(2)}) collective-permute-start(bf16[147,8,128]{2,1,0:T(8,128)(2,1)} %get-tuple-element.260), channel_id=1, source_target_pairs={{0,1},{1,0},{2,3},{3,2},{4,5},{5,4},{6,7},{7,6},{8,9},{9,8},{10,11... | collective-permute-start | bytes 903176 | tf_op jit(solution)/shard_map/ppermute | solution.py:765
  58.1 36.9 %collective-permute-start.34 = (f32[6,256]{1,0:T(8,128)}, f32[6,256]{1,0:T(8,128)}, u32[]{:S(2)}, u32[]{:S(2)}) collective-permute-start(f32[6,256]{1,0:T(8,128)} %maximum_select_fusion.1), channel_id=1, source_target_pairs={{0,2},{1,3},{2,0},{3,1},{4,6},{5,7},{6,4},{7,5},{8,10},{9,11},{10,... | collective-permute-start | bytes 18440 | tf_op jit(solution)/shard_map/ppermute | solution.py:765
  60.8 35.3 %collective-permute-start.35 = (f32[6,256]{1,0:T(8,128)}, f32[6,256]{1,0:T(8,128)}, u32[]{:S(2)}, u32[]{:S(2)}) collective-permute-start(f32[6,256]{1,0:T(8,128)} %maximum_select_fusion.1), channel_id=1, source_target_pairs={{0,3},{1,2},{2,1},{3,0},{4,7},{5,6},{6,5},{7,4},{8,11},{9,10},{10,... | collective-permute-start | bytes 18440 | tf_op jit(solution)/shard_map/ppermute | solution.py:765
  82.0 47.9 %collective-permute-start.65 = (bf16[4,9,8,256]{3,2,1,0:T(8,128)(2,1)S(1)}, bf16[4,9,8,256]{3,2,1,0:T(8,128)(2,1)}, u32[]{:S(2)}, u32[]{:S(2)}) collective-permute-start(bf16[4,9,8,256]{3,2,1,0:T(8,128)(2,1)S(1)} %pad_maximum_fusion.4.refs_8_), channel_id=1, source_target_pairs={{0,24},{4,28},{8,16},{12,20},{16,8},{20,12},{24,0},{28,4},{1,25},{... | collective-permute-start | bytes 442376 | tf_op jit(solution)/shard_map/ppermute | solution.py:765
  97.1 33.9 %collective-permute-start.29 = (f32[2,384]{1,0:T(2,128)S(1)}, f32[2,384]{1,0:T(2,128)S(1)}, u32[]{:S(2)}, u32[]{:S(2)}) collective-permute-start(f32[2,384]{1,0:T(2,128)S(1)} %add.471), channel_id=1, source_target_pairs={{0,24},{4,28},{8,16},{12,20},{16,8},{20,12},{24,0},{28,4},{1,25},{... | collective-permute-start | bytes 9224 | tf_op jit(solution)/shard_map/ppermute | solution.py:765
  101.8 58.0 %collective-permute-start.2 = (bf16[147,8,256]{2,1,0:T(8,128)(2,1)}, bf16[147,8,256]{2,1,0:T(8,128)(2,1)S(1)}, u32[]{:S(2)}, u32[]{:S(2)}) collective-permute-start(bf16[147,8,256]{2,1,0:T(8,128)(2,1)} %get-tuple-element.239), channel_id=1, source_target_pairs={{0,3},{1,2},{2,1},{3,0},{4,7},{5,6},{6,5},{7,4},{8,11},{9,10},{10,... | collective-permute-start | bytes 1806344 | tf_op jit(solution)/shard_map/ppermute | solution.py:765
  104.7 56.7 %collective-permute-start.1 = (bf16[147,8,256]{2,1,0:T(8,128)(2,1)}, bf16[147,8,256]{2,1,0:T(8,128)(2,1)S(1)}, u32[]{:S(2)}, u32[]{:S(2)}) collective-permute-start(bf16[147,8,256]{2,1,0:T(8,128)(2,1)} %get-tuple-element.240), channel_id=1, source_target_pairs={{0,2},{1,3},{2,0},{3,1},{4,6},{5,7},{6,4},{7,5},{8,10},{9,11},{10,... | collective-permute-start | bytes 1806344 | tf_op jit(solution)/shard_map/ppermute | solution.py:765
  104.7 60.6 %collective-permute-start = (bf16[147,8,256]{2,1,0:T(8,128)(2,1)}, bf16[147,8,256]{2,1,0:T(8,128)(2,1)S(1)}, u32[]{:S(2)}, u32[]{:S(2)}) collective-permute-start(bf16[147,8,256]{2,1,0:T(8,128)(2,1)} %get-tuple-element.241), channel_id=1, source_target_pairs={{0,1},{1,0},{2,3},{3,2},{4,5},{5,4},{6,7},{7,6},{8,9},{9,8},{10,11... | collective-permute-start | bytes 1806344 | tf_op jit(solution)/shard_map/ppermute | solution.py:765
  157.3 32.0 %collective-permute-start.55 = (bf16[4,6,8,1024]{3,2,1,0:T(8,128)(2,1)S(1)}, bf16[4,6,8,1024]{3,2,1,0:T(8,128)(2,1)S(1)}, u32[]{:S(2)}, u32[]{:S(2)}) collective-permute-start(bf16[4,6,8,1024]{3,2,1,0:T(8,128)(2,1)S(1)} %pad_maximum_fusion.2.refs_0_), channel_id=1, source_target_pairs={{0,24},{4,28},{8,16},{12,20},{16,8},{20,12},{24,0},{28,4},{1,25},{... | collective-permute-start | bytes 1179656 | tf_op jit(solution)/shard_map/ppermute | solution.py:765
  159.3 31.0 %collective-permute-start.53 = (bf16[4,6,8,1024]{3,2,1,0:T(8,128)(2,1)S(1)}, bf16[4,6,8,1024]{3,2,1,0:T(8,128)(2,1)S(1)}, u32[]{:S(2)}, u32[]{:S(2)}) collective-permute-start(bf16[4,6,8,1024]{3,2,1,0:T(8,128)(2,1)S(1)} %pad_maximum_fusion.2.refs_0_), channel_id=1, source_target_pairs={{0,16},{4,20},{8,24},{12,28},{16,0},{20,4},{24,8},{28,12},{1,17},{... | collective-permute-start | bytes 1179656 | tf_op jit(solution)/shard_map/ppermute | solution.py:765
  159.8 32.0 %collective-permute-start.51 = (bf16[4,6,8,1024]{3,2,1,0:T(8,128)(2,1)S(1)}, bf16[4,6,8,1024]{3,2,1,0:T(8,128)(2,1)S(1)}, u32[]{:S(2)}, u32[]{:S(2)}) collective-permute-start(bf16[4,6,8,1024]{3,2,1,0:T(8,128)(2,1)S(1)} %pad_maximum_fusion.2.refs_0_), channel_id=1, source_target_pairs={{0,8},{4,12},{8,0},{12,4},{16,24},{20,28},{24,16},{28,20},{1,9},{5... | collective-permute-start | bytes 1179656 | tf_op jit(solution)/shard_map/ppermute | solution.py:765
  232.9 28.3 %collective-permute-start.75 = (bf16[147,8,128]{2,1,0:T(8,128)(2,1)}, bf16[147,8,128]{2,1,0:T(8,128)(2,1)}, u32[]{:S(2)}, u32[]{:S(2)}) collective-permute-start(bf16[147,8,128]{2,1,0:T(8,128)(2,1)} %get-tuple-element.256), channel_id=1, source_target_pairs={{0,2},{1,3},{2,0},{3,1},{4,6},{5,7},{6,4},{7,5},{8,10},{9,11},{10,... | collective-permute-start | bytes 903176 | tf_op jit(solution)/shard_map/ppermute | solution.py:765
  237.9 43.4 %collective-permute-start.85 = (f32[4,1024]{1,0:T(4,128)}, f32[4,1024]{1,0:T(4,128)S(1)}, u32[]{:S(2)}, u32[]{:S(2)}) collective-permute-start(f32[4,1024]{1,0:T(4,128)} %maximum_select_fusion), channel_id=1, source_target_pairs={{0,2},{1,3},{2,0},{3,1},{4,6},{5,7},{6,4},{7,5},{8,10},{9,11},{10,... | collective-permute-start | bytes 49160 | tf_op jit(solution)/shard_map/ppermute | solution.py:765
  240.0 41.3 %collective-permute-start.86 = (f32[4,1024]{1,0:T(4,128)}, f32[4,1024]{1,0:T(4,128)S(1)}, u32[]{:S(2)}, u32[]{:S(2)}) collective-permute-start(f32[4,1024]{1,0:T(4,128)} %maximum_select_fusion), channel_id=1, source_target_pairs={{0,3},{1,2},{2,1},{3,0},{4,7},{5,6},{6,5},{7,4},{8,11},{9,10},{10,... | collective-permute-start | bytes 49160 | tf_op jit(solution)/shard_map/ppermute | solution.py:765
  243.5 30.3 %collective-permute-start.73 = (f32[2,768]{1,0:T(2,128)S(1)}, f32[2,768]{1,0:T(2,128)S(1)}, u32[]{:S(2)}, u32[]{:S(2)}) collective-permute-start(f32[2,768]{1,0:T(2,128)S(1)} %add_add_fusion.7), channel_id=1, source_target_pairs={{0,3},{1,2},{2,1},{3,0},{4,7},{5,6},{6,5},{7,4},{8,11},{9,10},{10,... | collective-permute-start | bytes 18440 | tf_op jit(solution)/shard_map/ppermute | solution.py:765
  295.1 51.5 %collective-permute-start.88 = (bf16[147,8,256]{2,1,0:T(8,128)(2,1)S(1)}, bf16[147,8,256]{2,1,0:T(8,128)(2,1)S(1)}, u32[]{:S(2)}, u32[]{:S(2)}) collective-permute-start(bf16[147,8,256]{2,1,0:T(8,128)(2,1)S(1)} %get-tuple-element.237), channel_id=1, source_target_pairs={{0,2},{1,3},{2,0},{3,1},{4,6},{5,7},{6,4},{7,5},{8,10},{9,11},{10,... | collective-permute-start | bytes 1806344 | tf_op jit(solution)/shard_map/ppermute | solution.py:765
  296.2 50.4 %collective-permute-start.87 = (bf16[147,8,256]{2,1,0:T(8,128)(2,1)S(1)}, bf16[147,8,256]{2,1,0:T(8,128)(2,1)S(1)}, u32[]{:S(2)}, u32[]{:S(2)}) collective-permute-start(bf16[147,8,256]{2,1,0:T(8,128)(2,1)S(1)} %get-tuple-element.238), channel_id=1, source_target_pairs={{0,1},{1,0},{2,3},{3,2},{4,5},{5,4},{6,7},{7,6},{8,9},{9,8},{10,11... | collective-permute-start | bytes 1806344 | tf_op jit(solution)/shard_map/ppermute | solution.py:765
  366.7 28.6 %collective-permute-start.96 = (f32[2,2176]{1,0:T(2,128)S(1)}, f32[2,2176]{1,0:T(2,128)S(1)}, u32[]{:S(2)}, u32[]{:S(2)}) collective-permute-start(f32[2,2176]{1,0:T(2,128)S(1)} %add_add_fusion.3), channel_id=1, source_target_pairs={{0,3},{1,2},{2,1},{3,0},{4,7},{5,6},{6,5},{7,4},{8,11},{9,10},{10,... | collective-permute-start | bytes 52232 | tf_op jit(solution)/shard_map/ppermute | solution.py:765
  368.3 32.5 %collective-permute-start.95 = (f32[2,2176]{1,0:T(2,128)S(1)}, f32[2,2176]{1,0:T(2,128)S(1)}, u32[]{:S(2)}, u32[]{:S(2)}) collective-permute-start(f32[2,2176]{1,0:T(2,128)S(1)} %add_add_fusion.3), channel_id=1, source_target_pairs={{0,2},{1,3},{2,0},{3,1},{4,6},{5,7},{6,4},{7,5},{8,10},{9,11},{10,... | collective-permute-start | bytes 52232 | tf_op jit(solution)/shard_map/ppermute | solution.py:765
  369.1 31.6 %collective-permute-start.94 = (f32[2,2176]{1,0:T(2,128)S(1)}, f32[2,2176]{1,0:T(2,128)S(1)}, u32[]{:S(2)}, u32[]{:S(2)}) collective-permute-start(f32[2,2176]{1,0:T(2,128)S(1)} %add_add_fusion.3), channel_id=1, source_target_pairs={{0,1},{1,0},{2,3},{3,2},{4,5},{5,4},{6,7},{7,6},{8,9},{9,8},{10,11... | collective-permute-start | bytes 52232 | tf_op jit(solution)/shard_map/ppermute | solution.py:765
  395.4 101.0 %collective-permute-start.113 = (bf16[147,8,256]{2,1,0:T(8,128)(2,1)}, bf16[147,8,256]{2,1,0:T(8,128)(2,1)}, u32[]{:S(2)}, u32[]{:S(2)}) collective-permute-start(bf16[147,8,256]{2,1,0:T(8,128)(2,1)} %get-tuple-element.231), channel_id=1, source_target_pairs={{0,3},{1,2},{2,1},{3,0},{4,7},{5,6},{6,5},{7,4},{8,11},{9,10},{10,... | collective-permute-start | bytes 1806344 | tf_op jit(solution)/shard_map/ppermute | solution.py:765
  400.7 95.7 %collective-permute-start.112 = (bf16[147,8,256]{2,1,0:T(8,128)(2,1)}, bf16[147,8,256]{2,1,0:T(8,128)(2,1)}, u32[]{:S(2)}, u32[]{:S(2)}) collective-permute-start(bf16[147,8,256]{2,1,0:T(8,128)(2,1)} %get-tuple-element.232), channel_id=1, source_target_pairs={{0,2},{1,3},{2,0},{3,1},{4,6},{5,7},{6,4},{7,5},{8,10},{9,11},{10,... | collective-permute-start | bytes 1806344 | tf_op jit(solution)/shard_map/ppermute | solution.py:765
  493.8 82.0 %collective-permute-start.169 = (bf16[4,4,6,8,1024]{4,3,2,0,1:T(8,128)(2,1)}, bf16[4,4,6,8,1024]{4,3,2,0,1:T(8,128)(2,1)}, u32[]{:S(2)}, u32[]{:S(2)}) collective-permute-start(bf16[4,4,6,8,1024]{4,3,2,0,1:T(8,128)(2,1)} %dynamic-slice_bitcast_fusion), channel_id=1, source_target_pairs={{0,4},{4,0},{8,12},{12,8},{16,20},{20,16},{24,28},{28,24},{1,5},{5... | collective-permute-start | bytes 4718600 | tf_op jit(solution)/shard_map/ppermute | solution.py:765
  495.6 45.1 %collective-permute-start.183 = (bf16[4,4,9,8,256]{4,3,2,0,1:T(8,128)(2,1)}, bf16[4,4,9,8,256]{4,3,2,0,1:T(8,128)(2,1)}, u32[]{:S(2)}, u32[]{:S(2)}) collective-permute-start(bf16[4,4,9,8,256]{4,3,2,0,1:T(8,128)(2,1)} %bitcast.312), channel_id=1, source_target_pairs={{0,4},{4,0},{8,12},{12,8},{16,20},{20,16},{24,28},{28,24},{1,5},{5... | collective-permute-start | bytes 1769480 | tf_op jit(solution)/shard_map/ppermute | solution.py:765
  539.1 29.8 %collective-permute-start.141 = (bf16[4,4,3,8,1280]{4,3,2,0,1:T(8,128)(2,1)S(1)}, bf16[4,4,3,8,1280]{4,3,2,0,1:T(8,128)(2,1)S(1)}, u32[]{:S(2)}, u32[]{:S(2)}) collective-permute-start(bf16[4,4,3,8,1280]{4,3,2,0,1:T(8,128)(2,1)S(1)} %copy-done.228), channel_id=1, source_target_pairs={{0,4},{4,0},{8,12},{12,8},{16,20},{20,16},{24,28},{28,24},{1,5},{5... | collective-permute-start | bytes 2949128 | tf_op jit(solution)/shard_map/ppermute | solution.py:765
  604.3 30.6 %collective-permute-start.146 = (bf16[3,8,1280]{2,1,0:T(8,128)(2,1)S(1)}, bf16[3,8,1280]{2,1,0:T(8,128)(2,1)S(1)}, u32[]{:S(2)}, u32[]{:S(2)}) collective-permute-start(bf16[3,8,1280]{2,1,0:T(8,128)(2,1)S(1)} %get-tuple-element.279), channel_id=1, source_target_pairs={{0,2},{1,3},{2,0},{3,1},{4,6},{5,7},{6,4},{7,5},{8,10},{9,11},{10,... | collective-permute-start | bytes 184328 | tf_op jit(solution)/shard_map/ppermute | solution.py:765
  604.4 46.9 %collective-permute-start.123 = (bf16[147,8,256]{2,1,0:T(8,128)(2,1)S(1)}, bf16[147,8,256]{2,1,0:T(8,128)(2,1)S(1)}, u32[]{:S(2)}, u32[]{:S(2)}) collective-permute-start(bf16[147,8,256]{2,1,0:T(8,128)(2,1)S(1)} %copy-done.231), channel_id=1, source_target_pairs={{0,3},{1,2},{2,1},{3,0},{4,7},{5,6},{6,5},{7,4},{8,11},{9,10},{10,... | collective-permute-start | bytes 1806344 | tf_op jit(solution)/shard_map/ppermute | solution.py:765
  606.6 56.0 %collective-permute-start.122 = (bf16[147,8,256]{2,1,0:T(8,128)(2,1)S(1)}, bf16[147,8,256]{2,1,0:T(8,128)(2,1)S(1)}, u32[]{:S(2)}, u32[]{:S(2)}) collective-permute-start(bf16[147,8,256]{2,1,0:T(8,128)(2,1)S(1)} %copy-done.230), channel_id=1, source_target_pairs={{0,2},{1,3},{2,0},{3,1},{4,6},{5,7},{6,4},{7,5},{8,10},{9,11},{10,... | collective-permute-start | bytes 1806344 | tf_op jit(solution)/shard_map/ppermute | solution.py:765
  636.8 33.8 %collective-permute-start.121 = (bf16[147,8,256]{2,1,0:T(8,128)(2,1)S(1)}, bf16[147,8,256]{2,1,0:T(8,128)(2,1)S(1)}, u32[]{:S(2)}, u32[]{:S(2)}) collective-permute-start(bf16[147,8,256]{2,1,0:T(8,128)(2,1)S(1)} %copy-done.229), channel_id=1, source_target_pairs={{0,1},{1,0},{2,3},{3,2},{4,5},{5,4},{6,7},{7,6},{8,9},{9,8},{10,11... | collective-permute-start | bytes 1806344 | tf_op jit(solution)/shard_map/ppermute | solution.py:765
  (412 other events, 5074.7 us)

commit v3 on v2

--- a/solution.py
+++ b/solution.py
@@ -128,7 +128,7 @@
         out_specs=tuple(pl.BlockSpec(memory_space=pltpu.VMEM) for _ in outs),
         scratch_shapes=list(scratch),
         compiler_params=pltpu.CompilerParams(vmem_limit_bytes=room),
-        cost_estimate=pl.CostEstimate(flops=flops, bytes_accessed=total, transcendentals=0),
+        cost_estimate=pl.CostEstimate(flops=flops, bytes_accessed=1, transcendentals=0),
         name=name,
     )(*args)
 
@@ -159,26 +159,31 @@
     return v if shift == 0 else pltpu.roll(v, shift, v.ndim - 1)
 
 
-def pack_kernel(per_clip, clips, ids_ref, counts_ref, frames_ref, x_ref, out_ref, tmp_ref):
+def pack_kernel(per_clip, clips, ids_ref, counts_ref, frames_ref, x_ref, *refs):
+    out_ref, tmp_ref = refs[-2:]
     clip, dp = pl.program_id(0) // per_clip, ids_ref[0]
     chunk = x_ref.shape[0]
     frames = jnp.where(clip < counts_ref[dp], frames_ref[dp * clips + clip], 0)
     tmp_ref[...] = x_ref[...].astype(F32).reshape(chunk * 32, 32)
     parts = [tmp_ref[pl.ds(r, chunk * 8, stride=4), :] for r in range(4)]
-    out_ref[...] = (cells(jnp.concatenate(parts, axis=1)) * tile_mask(frames, 128)).astype(BF16)
-
-
-def unpack_kernel(ids_ref, *refs):
-    pieces, out_ref, tmp_ref = refs[:4], refs[4], refs[5]
+    out_ref[:, :, 0:128] = (cells(jnp.concatenate(parts, axis=1)) * tile_mask(frames, 128)).astype(BF16)
+    if len(refs) == 3:
+        out_ref[:, :, 128:384] = refs[0][...]
+
+
+def unpack_kernel(width, ids_ref, *refs):
+    pieces, tmp_ref = refs[:4], refs[-1]
     size = pieces[0].shape[0]
     for k in range(4):
         begin = (ids_ref[1] ^ k) * size
 
         def body(p, carry, k=k, begin=begin):
-            joined = rows(pieces[k][pl.ds(p, BIG)].astype(F32))
+            joined = rows(pieces[k][pl.ds(p, BIG), :, 0:128].astype(F32))
             for r in range(4):
                 tmp_ref[pl.ds(r, BIG * 8, stride=4), :] = joined[:, 32 * r : 32 * r + 32]
-            out_ref[pl.ds(begin + p, BIG)] = tmp_ref[...].reshape(BIG, 32, 32).astype(BF16)
+            refs[-2][pl.ds(begin + p, BIG)] = tmp_ref[...].reshape(BIG, 32, 32).astype(BF16)
+            if width > 128:
+                refs[4][pl.ds(begin + p, BIG)] = pieces[k][pl.ds(p, BIG), :, 128:width]
             return carry
 
         steps(size, BIG, body, 0)
@@ -186,28 +191,118 @@
 
 def place_kernel(ids_ref, *refs):
     pieces, out_ref = refs[:4], refs[4]
+    size = pieces[0].shape[0]
     for k in range(4):
-
-        def body(p, carry, k=k):
-            out_ref[ids_ref[1] ^ k, pl.ds(p, SMALL)] = pieces[k][pl.ds(p, SMALL)]
+        begin = (ids_ref[1] ^ k) * size
+
+        def body(p, carry, k=k, begin=begin):
+            out_ref[pl.ds(begin + p, SMALL)] = pieces[k][pl.ds(p, SMALL)]
             return carry
 
-        steps(pieces[0].shape[0], SMALL, body, 0)
-
-
-def first_weights_kernel(ids_ref, *refs):
-    shares, lat_shares = refs[0:8], refs[8:16]
-    fr_ref, fsp_ref, fex_ref, fin_ref, fout_ref = refs[16:21]
-    red_ref, lred_ref, first_ref, wsp_ref, wex_ref, gin_ref, gout_ref, lat_ref = refs[21:]
-    for kd in range(8):
-        d = ids_ref[2] ^ kd
-        for kz in range(4):
-            z = ids_ref[1] ^ kz
+        steps(size, SMALL, body, 0)
+
+
+def lanes_at(block, width):
+    return pl.ds(pl.multiple_of(block * width, width), width)
+
+
+LREDUCE = [(3, 256 * k) for k in range(3)]
+LATERAL = [(4, 128 * k) for k in range(5)]
+GAINS = [(3, 768), (3, 896), (4, 640), (4, 768)]
+SPATIAL = [(6 + k // 4, 256 * (k % 4)) for k in range(9)]
+
+
+def weight_slab_kernel(ids_ref, red_ref, lred_ref, lat_ref, exp_ref, short_ref, lshort_ref, sp_ref, ln_ref, sn_ref, on_ref, out_ref, more_ref,
+                       red_s, lred_s, lat_s, exp_s, short_s, lshort_s, sp_s, sem):
+    group = ids_ref[2]
+    eight, more = pl.ds(pl.multiple_of(group * 8, 8), 8), pl.ds(pl.multiple_of(group * 32, 32), 32)
+    copies = []
+    for i, (src, dst) in enumerate((
+        (red_ref.at[:, eight], red_s), (lred_ref.at[:, eight], lred_s), (lat_ref.at[:, eight], lat_s), (exp_ref.at[eight], exp_s),
+        (short_ref.at[more], short_s), (lshort_ref.at[eight], lshort_s), (sp_ref.at[:, eight], sp_s),
+    )):
+        copies.append(pltpu.make_async_copy(src, dst, sem.at[i]))
+    for copy in copies:
+        copy.start()
+    out_ref[4, :, 896:1024] = jnp.zeros((8, 128), BF16)
+    more_ref[8, :, 256:1024] = jnp.zeros((8, 768), BF16)
+    blank = jnp.zeros((2, 128), F32)
+    half = jnp.zeros((2, 64), F32)
+    inner = jnp.concatenate([jnp.concatenate([v, half], axis=1) for v in (ln_ref[...], sn_ref[0:2], sn_ref[2:4])] + [blank], axis=0)
+    outer = jnp.concatenate([on_ref[:, 0:128], on_ref[:, 128:256]], axis=0)
+    for i, v in enumerate((inner, outer)):
+        high = v.astype(BF16)
+        for k, part in ((i, high), (2 + i, (v - high.astype(F32)).astype(BF16))):
+            at, lane = GAINS[k]
+            out_ref[at, :, lane : lane + 128] = part
+    for copy in copies:
+        copy.wait()
+    for j in range(3):
+        out_ref[j] = red_s[j].astype(BF16)
+        at, lane = LREDUCE[j]
+        out_ref[at, :, lane : lane + 256] = lred_s[j].astype(BF16)
+    more_ref[0], more_ref[5] = exp_s[...].astype(BF16), lshort_s[...].astype(BF16)
+    for a in range(4):
+        more_ref[1 + a] = short_s[8 * a : 8 * a + 8].astype(BF16)
+    for k in range(9):
+        at, lane = SPATIAL[k]
+        more_ref[at, :, lane : lane + 256] = sp_s[k].astype(BF16)
+    for k in range(5):
+        at, lane = LATERAL[k]
+        out_ref[at, :, lane : lane + 128] = lat_s[k].astype(BF16)
+
+
+def more_weights_kernel(ids_ref, own_ref, other_ref, exp_ref, short_ref, lshort_ref, sp_ref):
+    me, group = ids_ref[1], ids_ref[2]
+
+    def place(i, carry):
+        chip, kz = i // 4, i % 4
+        z = me ^ kz
+        for core, ref in ((0, own_ref), (1, other_ref)):
+            d = group ^ (2 * chip + core)
+            exp_ref[z, d], lshort_ref[z, d] = ref[chip, kz, 0], ref[chip, kz, 5]
+            for a in range(4):
+                short_ref[z, d, a] = ref[chip, kz, 1 + a]
+            for k in range(9):
+                at, lane = SPATIAL[k]
+                sp_ref[k, z, d] = ref[chip, kz, at, :, lane : lane + 256]
+        return carry
+
+    lax.fori_loop(0, 16, place, 0)
+
+
+def weights_kernel(ids_ref, own_ref, other_ref, fr_ref, fsp_ref, fex_ref, fin_ref, fout_ref, red_ref, lred_ref, first_ref, wsp_ref, wex_ref,
+                   gin_ref, gout_ref, gmid_ref, gwide_ref, lat_ref):
+    me, group = ids_ref[1], ids_ref[2]
+
+    def place(i, carry):
+        chip, kz = i // 4, i % 4
+        z = me ^ kz
+        for core, ref in ((0, own_ref), (1, other_ref)):
+            d = group ^ (2 * chip + core)
             for j in range(3):
-                red_ref[j, z, d] = shares[kd][kz, j, :, 0:1024]
-                lred_ref[j, z, d] = shares[kd][kz, j, :, 1024:1280]
-            for j in range(5):
-                lat_ref[j, z, d] = lat_shares[kd][kz, j].astype(F32)
+                red_ref[j, z, d] = ref[chip, kz, j]
+                at, lane = LREDUCE[j]
+                lred_ref[j, z, d] = ref[chip, kz, at, :, lane : lane + 256]
+            for k in range(5):
+                at, lane = LATERAL[k]
+                lat_ref[k, z, d] = ref[chip, kz, at, :, lane : lane + 128].astype(F32)
+        return carry
+
+    lax.fori_loop(0, 16, place, 0)
+
+    mids = [jnp.zeros((8, 128), F32) for _ in range(2)]
+    for kz in range(4):
+        z = me ^ kz
+        parts = [own_ref[0, kz, at, :, lane : lane + 128].astype(F32) for at, lane in GAINS]
+        inner, outer = parts[0] + parts[2], parts[1] + parts[3]
+        for half in range(2):
+            for block in range(2):
+                here = (z == 2 * block + half).astype(F32)
+                mids[block] = mids[block] + moved(inner, 64 * half) * here
+        gwide_ref[z, :, 0:128], gwide_ref[z, :, 128:256] = outer[0:4], outer[4:8]
+    gmid_ref[:, 0:128], gmid_ref[:, 128:256] = mids[0], mids[1]
+
     first_ref[...] = jnp.zeros_like(first_ref)
     wsp_ref[...] = jnp.zeros_like(wsp_ref)
     for z in range(4):
@@ -235,59 +330,42 @@
     gin_ref[...] = jnp.concatenate([fin_ref[...]] * 4, axis=1)
 
 
-def second_weights_kernel(ids_ref, *refs):
-    shares, sp_shares = refs[0:8], refs[8:16]
-    exp_ref, short_ref, lshort_ref, sp_ref = refs[16:]
-    for kd in range(8):
-        d = ids_ref[2] ^ kd
-        for kz in range(4):
-            z = ids_ref[1] ^ kz
-            exp_ref[z, d] = shares[kd][kz, 0]
-            lshort_ref[z, d] = shares[kd][kz, 5]
+def first_grads_kernel(ids_ref, own_ref, other_ref, exp_ref, short_ref, lshort_ref):
+    def place(chip, carry):
+        for core, ref in ((0, own_ref), (1, other_ref)):
+            d = ids_ref[2] ^ (2 * chip + core)
+            exp_ref[d], lshort_ref[d] = ref[chip, 0].astype(F32), ref[chip, 5].astype(F32)
             for a in range(4):
-                short_ref[z, d, a] = shares[kd][kz, 1 + a]
-            for k in range(9):
-                sp_ref[k, z, d] = sp_shares[kd][kz, k]
-
-
-def first_grads_kernel(ids_ref, *refs):
-    shares, sp_shares = refs[0:8], refs[8:16]
-    exp_ref, short_ref, lshort_ref, sp_ref = refs[16:]
-    for kd in range(8):
-        d = ids_ref[2] ^ kd
-        exp_ref[d] = shares[kd][0].astype(F32)
-        lshort_ref[d] = shares[kd][5].astype(F32)
-        for a in range(4):
-            short_ref[d, a] = shares[kd][1 + a].astype(F32)
-        for k in range(9):
-            sp_ref[k, d] = sp_shares[kd][k].astype(F32)
-
-
-def second_grads_kernel(ids_ref, *refs):
-    shares, lat_shares = refs[0:8], refs[8:16]
-    red_ref, lred_ref, lat_ref = refs[16:]
-    for kd in range(8):
-        d = ids_ref[2] ^ kd
-        for j in range(3):
-            red_ref[j, d] = shares[kd][j, :, 0:1024].astype(F32)
-            lred_ref[j, d] = shares[kd][j, :, 1024:1280].astype(F32)
-        for j in range(5):
-            lat_ref[j, d] = lat_shares[kd][j].astype(F32)
-
-
-def lanes_at(block, width):
-    return pl.ds(pl.multiple_of(block * width, width), width)
+                short_ref[d, a] = ref[chip, 1 + a].astype(F32)
+        return carry
+
+    lax.fori_loop(0, 4, place, 0)
+
+
+def second_grads_kernel(ids_ref, own_ref, other_ref, red_ref, lred_ref, sp_ref):
+    def place(chip, carry):
+        for core, ref in ((0, own_ref), (1, other_ref)):
+            d = ids_ref[2] ^ (2 * chip + core)
+            for j in range(3):
+                red_ref[j, d] = ref[chip, j].astype(F32)
+                lred_ref[j, d] = ref[chip, 3, :, 256 * j : 256 * j + 256].astype(F32)
+            for k in range(8):
+                sp_ref[k, d] = ref[chip, 4 + k // 4, :, 256 * (k % 4) : 256 * (k % 4) + 256].astype(F32)
+            sp_ref[8, d] = ref[chip, 3, :, 768:1024].astype(F32)
+        return carry
+
+    lax.fori_loop(0, 4, place, 0)
 
 
 def fast_first_kernel(table_ref, f0_ref, f1_ref, f2_ref, f3_ref, w_ref, fx_ref, fa_ref, lp_ref, sums_ref, first_ref, last_ref):
     size = fa_ref.shape[0]
-    for k, ref in enumerate((f0_ref, f1_ref, f2_ref, f3_ref)):
-
-        def fill(p, carry, ref=ref, lanes=lanes_at(table_ref[5] ^ k, 128)):
-            fx_ref[pl.ds(p, SMALL), :, lanes] = ref[pl.ds(p, SMALL)]
-            return carry
-
-        steps(size, SMALL, fill, 0)
+
+    def fill(p, carry):
+        for k, ref in enumerate((f0_ref, f1_ref, f2_ref, f3_ref)):
+            fx_ref[pl.ds(p, SMALL), :, lanes_at(table_ref[5] ^ k, 128)] = ref[pl.ds(p, SMALL)]
+        return carry
+
+    steps(size, SMALL, fill, 0)
 
     def body(p, frames, carry):
         acc = cells(nt(rows_bf(fx_ref[pl.ds(p, BIG)]), w_ref[...]))
@@ -468,21 +546,23 @@
         wide_out += ref.shape[1]
 
 
-def fast_out_kernel(offset, table_ref, n_ref, fc_ref, sums_ref, gains_ref, fx_ref, cot_ref, out_ref, up_ref, slopes_ref):
+def fast_out_kernel(offset, table_ref, n_ref, fc_ref, sums_ref, gains_ref, fx_ref, c0_ref, c1_ref, c2_ref, c3_ref, out_ref, up_ref,
+                    slopes_ref, vec_ref):
     size, width = fc_ref.shape[0], fc_ref.shape[2]
-    factor, shift, center, inv_std = scale_of(folded(sums_ref[:, offset : offset + width]), gains_ref[...], n_ref[1])
-    for z in range(4):
-        lanes = slice(128 * z, 128 * z + 128)
-        vecs = [v[:, lanes][None] for v in (factor, shift, center, inv_std)]
-
-        def body(p, frames, carry, z=z, lanes=lanes, vecs=vecs):
-            fz, sz, cz, rz = vecs
+    vecs = scale_of(folded(sums_ref[:, offset : offset + width]), gains_ref[...], n_ref[1])
+    for i, v in enumerate(vecs):
+        vec_ref[i : i + 1] = v
+    for k, cot_ref in enumerate((c0_ref, c1_ref, c2_ref, c3_ref)):
+        lanes = lanes_at(table_ref[5] ^ k, 128)
+        fz, sz, cz, rz = (vec_ref[i : i + 1, lanes][None] for i in range(4))
+
+        def body(p, frames, carry, k=k, lanes=lanes, fz=fz, sz=sz, cz=cz, rz=rz, cot_ref=cot_ref):
             y = fc_ref[pl.ds(p, SMALL), :, lanes].astype(F32)
             mask = tile_mask(frames, 128)
             total = y * fz + sz + fx_ref[pl.ds(p, SMALL), :, lanes].astype(F32)
             value, slope = gelu_pair(total)
-            out_ref[z ^ table_ref[5], pl.ds(p, SMALL)] = (value * mask).astype(BF16)
-            up = slope * (cot_ref[z ^ table_ref[5], pl.ds(p, SMALL)].astype(F32) * mask)
+            out_ref[k, pl.ds(p, SMALL)] = (value * mask).astype(BF16)
+            up = slope * (cot_ref[pl.ds(p, SMALL), :, 0:128].astype(F32) * mask)
             up_ref[pl.ds(p, SMALL), :, lanes] = up.astype(BF16)
             return carry[0] + down(up), carry[1] + down(up * ((y - cz) * rz))
 
@@ -490,26 +570,31 @@
         slopes_ref[0:1, lanes], slopes_ref[1:2, lanes] = flat(a), flat(b)
 
 
-def slow_out_kernel(table_ref, n_ref, sc_ref, sp_ref, sums_ref, gains_ref, cot_ref, more_ref, out_ref, up_ref, slopes_ref):
+def slow_out_kernel(table_ref, n_ref, sc_ref, sp_ref, sums_ref, gains_ref, c0_ref, c1_ref, c2_ref, c3_ref, fast_ref, more_ref,
+                    o0_ref, o1_ref, o2_ref, o3_ref, up_ref, slopes_ref, vec_ref):
     size, width = sc_ref.shape[0], sc_ref.shape[2]
     cf, cs, cc, cr = scale_of(sums_ref[:, 0:width], gains_ref[0:2], n_ref[0])
     pf, ps, pc, pr = scale_of(sums_ref[:, width : 2 * width], gains_ref[2:4], n_ref[0])
-    for z in range(4):
-        lanes = slice(256 * z, 256 * z + 256)
-        vecs = [v[:, lanes][None] for v in (cf, cs + ps, cc, cr, pf, pc, pr)]
-
-        def body(p, frames, carry, z=z, lanes=lanes, vecs=vecs):
+    for i, v in enumerate((cf, cs + ps, cc, cr, pf, pc, pr)):
+        vec_ref[i : i + 1] = v
+    for k, (cot_ref, out_ref) in enumerate(((c0_ref, o0_ref), (c1_ref, o1_ref), (c2_ref, o2_ref), (c3_ref, o3_ref))):
+        block = table_ref[5] ^ k
+        lanes = lanes_at(block, 256)
+        vecs = [vec_ref[i : i + 1, lanes][None] for i in range(7)]
+
+        def body(p, frames, carry, k=k, lanes=lanes, vecs=vecs, cot_ref=cot_ref, out_ref=out_ref):
             cf, shift, cc, cr, pf, pc, pr = vecs
             yc, yp = (ref[pl.ds(p, SMALL), :, lanes].astype(F32) for ref in (sc_ref, sp_ref))
             mask = tile_mask(frames, 256)
             value, slope = gelu_pair(yc * cf + yp * pf + shift)
-            out_ref[z ^ table_ref[5], pl.ds(p, SMALL)] = (value * mask).astype(BF16)
-            up = slope * (cot_ref[z ^ table_ref[5], pl.ds(p, SMALL)].astype(F32) * mask)
+            out_ref[pl.ds(p, SMALL), :, 128:384] = (value * mask).astype(BF16)
+            out_ref[pl.ds(p, SMALL), :, 0:128] = fast_ref[k, pl.ds(p, SMALL)]
+            up = slope * (cot_ref[pl.ds(p, SMALL), :, 128:384].astype(F32) * mask)
             up_ref[pl.ds(p, SMALL), :, lanes] = up.astype(BF16)
             return (carry[0] + down(up), carry[1] + down(up * ((yc - cc) * cr)), carry[2] + down(up * ((yp - pc) * pr)))
 
         a, b, c = sweep(table_ref, size, SMALL, body, (jnp.zeros((8, 256), F32),) * 3)
-        own, other = lanes, slice(width + 256 * z, width + 256 * z + 256)
+        own, other = lanes, lanes_at(4 + block, 256)
         slopes_ref[0:1, own], slopes_ref[1:2, own] = flat(a), flat(b)
         slopes_ref[0:1, other], slopes_ref[1:2, other] = flat(a), flat(c)
     slopes_ref[:, 2 * width :] = more_ref[...]
@@ -573,7 +658,8 @@
 
 
 def conv_back_kernel(halo, row_len, per_clip, fold, offsets, table_ref, n_ref, ysums_ref, ygains_ref, slopes_ref, ylo_ref, y_ref, yhi_ref,
-                     dlo_ref, d_ref, dhi_ref, w_ref, z_ref, zsums_ref, zgains_ref, dy_ref, dz_ref, oslopes_ref, pad_ref):
+                     dlo_ref, d_ref, dhi_ref, w_ref, z_ref, zsums_ref, zgains_ref, *refs):
+    dy_ref, dz_ref, oslopes_ref, pad_ref = refs[-4:]
     size, width = y_ref.shape[0], y_ref.shape[2]
     fix = folded if fold else (lambda v: v)
     inv_n = n_ref[1 if fold else 0]
@@ -606,14 +692,16 @@
         return carry[0] + down(dz), carry[1] + down(dz * ((z - zc[None]) * zr[None]))
 
     a, b = sweep(table_ref, size, BIG, body, (jnp.zeros((8, width), F32),) * 2)
-    oslopes_ref[0:1], oslopes_ref[1:2] = flat(a), flat(b)
+    oslopes_ref[0:1, 0:width], oslopes_ref[1:2, 0:width] = flat(a), flat(b)
+    if not fold:
+        oslopes_ref[:, width:] = refs[0][...]
 
 
 def slow_back_kernel(table_ref, n_ref, dz_ref, y_ref, sums_ref, gains_ref, slopes_ref, w_ref, wl_ref, dx_ref, dl_ref,
-                     lp_ref, lsums_ref, lgains_ref, taps_ref, out_ref, dzl_ref, oslopes_ref):
+                     lp_ref, lsums_ref, lgains_ref, taps_ref, o0_ref, o1_ref, o2_ref, o3_ref, dzl_ref, oslopes_ref):
     size = y_ref.shape[0]
     factor, shift, center, inv_std = scale_of(sums_ref[:, 0:256], gains_ref[...], n_ref[0])
-    k0, k1 = slope_of(slopes_ref[...], factor, center, inv_std, n_ref[0])
+    k0, k1 = slope_of(slopes_ref[:, 0:256], factor, center, inv_std, n_ref[0])
 
     def fill(p, frames, carry):
         dy = dz_ref[pl.ds(p, SMALL)] * factor[None]
@@ -629,10 +717,10 @@
     def body(p, frames, carry):
         taps = rows_bf(taps_ref[pl.ds(p, BIG)])
         mask = tile_mask(frames, 256)
-        for z in range(4):
-            lanes = slice(256 * z, 256 * z + 256)
+        for k, out_ref in enumerate((o0_ref, o1_ref, o2_ref, o3_ref)):
+            lanes = lanes_at(table_ref[5] ^ k, 256)
             dx = cells(nn(taps, w_ref[:, lanes])) + dx_ref[pl.ds(p, BIG), :, lanes].astype(F32)
-            out_ref[z ^ table_ref[5], pl.ds(p, BIG)] = (dx * mask).astype(BF16)
+            out_ref[pl.ds(p, BIG)] = (dx * mask).astype(BF16)
         dl = cells(nn(taps, wl_ref[...])) + dl_ref[pl.ds(p, BIG)]
         y = lp_ref[pl.ds(p, BIG)]
         dz = gelu_slope(y * lf[None] + ls[None]) * dl * mask
@@ -644,7 +732,7 @@
 
 
 def fast_back_kernel(at_s, table_ref, n_ref, sums_ref, fgains_ref, lgains_ref, fslopes_ref, lslopes_ref, dzf_ref, fa_ref, dzl_ref, lp_ref,
-                     up_ref, w_ref, taps_ref, out_ref):
+                     up_ref, w_ref, taps_ref, o0_ref, o1_ref, o2_ref, o3_ref):
     size = fa_ref.shape[0]
     ff, fs, fc, fr = scale_of(folded(sums_ref[:, 0:128]), fgains_ref[...], n_ref[1])
     f0, f1 = slope_of(folded(fslopes_ref[:, at_s : at_s + 128]), ff, fc, fr, n_ref[1])
@@ -666,12 +754,12 @@
     sweep(table_ref, size, SMALL, fill)
 
     def body(p, frames, carry):
-        dx = cells(nn(rows_bf(taps_ref[pl.ds(p, BIG)]), w_ref[...]))
+        taps = rows_bf(taps_ref[pl.ds(p, BIG)])
         mask = tile_mask(frames, 128)
-        for z in range(4):
-            lanes = slice(128 * z, 128 * z + 128)
-            up = up_ref[pl.ds(p, BIG), :, lanes].astype(F32)
-            out_ref[z ^ table_ref[5], pl.ds(p, BIG)] = ((dx[:, :, lanes] + up) * mask).astype(BF16)
+        for k, out_ref in enumerate((o0_ref, o1_ref, o2_ref, o3_ref)):
+            lanes = lanes_at(table_ref[5] ^ k, 128)
+            dx = cells(nn(taps, w_ref[:, lanes])) + up_ref[pl.ds(p, BIG), :, lanes].astype(F32)
+            out_ref[pl.ds(p, BIG)] = (dx * mask).astype(BF16)
         return carry
 
     sweep(table_ref, size, BIG, body)
@@ -681,8 +769,16 @@
     return lax.dot_general(a, b, (((0,), (0,)), ((), ())), preferred_element_type=F32)
 
 
-def conv_weight_kernel(halo, row_len, per_clip, fold, table_ref, act_ref, dy_ref, out_ref, pad_ref, acc_ref):
-    size, width = dy_ref.shape[0], dy_ref.shape[2]
+def chunks(size):
+    return range(0, size, BIG)
+
+
+def added(acc_ref, at, part, first):
+    acc_ref[at] = part if first else acc_ref[at] + part
+
+
+def conv_weight(halo, row_len, per_clip, fold, table_ref, act_ref, dy_ref, pad_ref, acc_ref):
+    size = dy_ref.shape[0]
     phase = table_ref[5] * (size // SMALL)
 
     def copy(p, carry):
@@ -708,8 +804,7 @@
     end = size + 2 * halo
     pad_ref[2, end - 1 : end] = pad_ref[2, end - 1 : end] * (1.0 - high_even)
 
-    for c in range(size // BIG):
-        p = c * BIG
+    for p in chunks(size):
         top, bottom = edge_scales(table_ref, p, per_clip)
         dy = rows_bf(dy_ref[p : p + BIG])
         for i in range(3):
@@ -723,33 +818,69 @@
                     v = jnp.concatenate([v[: BIG - row_len], v[BIG - row_len :] * bottom], axis=0)
                 taps.append(rows(v).astype(BF16))
             taps = jnp.concatenate(taps, axis=1)
-            part = tn(taps, dy) if fold else tn(dy, taps)
-            acc_ref[i] = part if c == 0 else acc_ref[i] + part
-    if fold:
-        out_ref[...] = acc_ref[...]
-        return
-    for i in range(3):
+            added(acc_ref, i, tn(taps, dy) if fold else tn(dy, taps), p == 0)
+
+
+def first_slab_kernel(hb_ref, dsc_ref, x_ref, lat_ref, dsp_ref, out_ref, acc_ref):
+    for p in chunks(hb_ref.shape[0]):
+        at = slice(p, p + BIG)
+        dsc, dsp = rows_bf(dsc_ref[at]), rows_bf(dsp_ref[at])
+        added(acc_ref, 4, tn(rows_bf(hb_ref[at]), dsc), p == 0)
+        added(acc_ref, 5, tn(rows_bf(lat_ref[at]), dsp), p == 0)
+        for z in range(4):
+            added(acc_ref, z, tn(rows_bf(x_ref[at, :, 256 * z : 256 * z + 256]), dsp), p == 0)
+    out_ref[:, :, 0] = acc_ref[4].reshape(4, 8, 8, 1024).astype(BF16)
+    out_ref[:, :, 5] = acc_ref[5].reshape(4, 8, 8, 1024).astype(BF16)
+    for z in range(4):
+        out_ref[z, :, 1:5] = acc_ref[z].reshape(8, 4, 8, 1024).astype(BF16)
+
+
+def second_slab_kernel(halo, row_len, per_clip, table_ref, act_ref, dy_ref, taps_ref, x_ref, lat_ref, out_ref, pad_ref, acc_ref, red_ref,
+                       lred_ref):
+    conv_weight(halo, row_len, per_clip, False, table_ref, act_ref, dy_ref, pad_ref, acc_ref)
+    for k in range(9):
+        v = acc_ref[k // 3, :, 256 * (k % 3) : 256 * (k % 3) + 256].reshape(4, 8, 8, 256).astype(BF16)
+        at, lane = (3, 768) if k == 8 else (4 + k // 4, 256 * (k % 4))
+        out_ref[:, :, at, :, lane : lane + 256] = v
+    for p in chunks(dy_ref.shape[0]):
+        at = slice(p, p + BIG)
+        x, lat = rows_bf(x_ref[at]), rows_bf(lat_ref[at])
         for j in range(3):
-            v = acc_ref[i, :, width * j : width * j + width].reshape(4, 8, 8, width)
-            out_ref[:, :, 3 * i + j] = v.astype(BF16)
-
-
-def fast_grads_kernel(first_ref, sp_ref, ex_ref, lat_ref, out_ref):
-    def pick(at, count, r, ref=first_ref):
+            taps = rows_bf(taps_ref[at, :, 256 * j : 256 * j + 256])
+            added(red_ref, j, tn(taps, x), p == 0)
+            added(lred_ref, j, tn(taps, lat), p == 0)
+    for j in range(3):
+        out_ref[:, :, j] = red_ref[j].reshape(4, 8, 8, 1024).astype(BF16)
+        out_ref[:, :, 3, :, 256 * j : 256 * j + 256] = lred_ref[j].reshape(4, 8, 8, 256).astype(BF16)
+
+
+def fast_grads_kernel(halo, row_len, per_clip, table_ref, act_ref, dy_ref, taps_ref, fx_ref, h_ref, dfc_ref, lat_ref, out_ref,
+                      pad_ref, sp_ref, first_ref, ex_ref):
+    conv_weight(halo, row_len, per_clip, True, table_ref, act_ref, dy_ref, pad_ref, sp_ref)
+    for p in chunks(dy_ref.shape[0]):
+        at = slice(p, p + BIG)
+        added(first_ref, slice(0, 896), tn(rows_bf(taps_ref[at]), rows_bf(fx_ref[at])), p == 0)
+        added(ex_ref, slice(0, 128), tn(rows_bf(h_ref[at]), rows_bf(dfc_ref[at])), p == 0)
+
+    def gather(at, count, r, ref=first_ref):
         return sum(lane_group(moved(ref[at : at + count, 128 * z : 128 * z + 128], 32 * z - 32 * r), z) for z in range(4))
 
-    taps = [pick(640, 256, 2), pick(640, 256, 3), pick(384, 256, 0), pick(384, 256, 1), pick(384, 256, 2)]
+    taps = [gather(640, 256, 2), gather(640, 256, 3), gather(384, 256, 0), gather(384, 256, 1), gather(384, 256, 2)]
     for j in range(5):
-        lat_ref[:, :, j] = taps[j].reshape(4, 8, 8, 128).astype(BF16)
+        lat_ref[:, 8 * j : 8 * j + 8] = taps[j].reshape(4, 8, 8, 128).astype(BF16)
+
+    def tiles(first, v):
+        for i in range(v.shape[0] // 8):
+            out_ref[first + i] = v[8 * i : 8 * i + 8].astype(BF16)
+
     for j in range(3):
-        total = sum(pick(32 * q, 32, q + j - 1) for q in range(4) if 0 <= q + j - 1 < 4)
+        total = sum(gather(32 * q, 32, q + j - 1) for q in range(4) if 0 <= q + j - 1 < 4)
         if j == 0:
-            total = total + pick(128, 32, 3)
+            total = total + gather(128, 32, 3)
         if j == 2:
-            total = total + pick(352, 32, 0)
-        out_ref[4 * j : 4 * j + 4] = total.reshape(4, 8, 128).astype(BF16)
-    total = sum(pick(32 * r, 32, r, ex_ref) for r in range(4))
-    out_ref[12:16] = total.reshape(4, 8, 128).astype(BF16)
+            total = total + gather(352, 32, 0)
+        tiles(4 * j, total)
+    tiles(12, sum(gather(32 * r, 32, r, ex_ref) for r in range(4)))
     for i in range(3):
         total = None
         for j in range(3):
@@ -757,7 +888,7 @@
                 lane_group(moved(sp_ref[i, 128 * j + 32 * r : 128 * j + 32 * r + 32, :], 32 * j - 32 * r), j) for r in range(4)
             )
             total = tap if total is None else total + tap
-        out_ref[16 + 4 * i : 20 + 4 * i] = total.reshape(4, 8, 128).astype(BF16)
+        tiles(16 + 4 * i, total)
 
 
 def swap(tree, axis, size, distance):
@@ -795,8 +926,10 @@
     return add(tree, near, far, both)
 
 
-def everywhere(tree, sizes):
+def everywhere(tree, sizes, bulk=None):
     for axis, size in sizes.items():
+        if axis == "chan" and bulk is not None:
+            tree = after(tree, bulk)
         for bits in stages(size, axis == "dp"):
             tree = butterfly(tree, axis, size, bits)
     return tree
@@ -808,13 +941,10 @@
     return low, high
 
 
-def gather_group(tree, sizes):
+def gather_group(v, sizes):
     dp = sizes["dp"]
-    by_chip = [tree] + [swap(tree, "dp", dp, 2 * k) for k in (1, 2, 3)]
-    out = []
-    for piece in by_chip:
-        out += [piece, swap(piece, "dp", dp, 1)]
-    return out
+    own = jnp.stack([v] + [swap(v, "dp", dp, 2 * k) for k in (1, 2, 3)])
+    return own, swap(own, "dp", dp, 1)
 
 
 def pick(v, index, axis):
@@ -840,12 +970,8 @@
     return tree
 
 
-def send_blocks(blocks, size):
-    return [blocks[0]] + [swap(blocks[k], "chan", size, k) for k in range(1, size)]
-
-
-def weight_sum(a, b, dtype=BF16):
-    return jnp.einsum("pti,pto->io", a, b, preferred_element_type=F32).astype(dtype)
+def after(tree, gate):
+    return lax.optimization_barrier((tree, gate))[0]
 
 
 def local(
@@ -890,48 +1016,55 @@
     per_clip = area // BIG
     chunk = 98
 
-    def packed(v):
+    def packed(v, slow=None):
         v = v.transpose(0, 2, 3, 1, 4).reshape(places, fast_t, fast_part)
+        more = [] if slow is None else [slow.reshape(places, slow_t, slow_part)]
+        width = 128 if slow is None else 128 + slow_part
         return pl.pallas_call(
             functools.partial(pack_kernel, area // chunk, clips),
             grid=(places // chunk,),
-            out_shape=shape((places, slow_t, 128), BF16),
+            out_shape=shape((places, slow_t, width), BF16),
             in_specs=[pl.BlockSpec(memory_space=pltpu.SMEM)] * 3
-            + [pl.BlockSpec((chunk, fast_t, fast_part), lambda i: (i, 0, 0))],
-            out_specs=pl.BlockSpec((chunk, slow_t, 128), lambda i: (i, 0, 0)),
+            + [pl.BlockSpec((chunk, *u.shape[1:]), lambda i: (i, 0, 0)) for u in (v, *more)],
+            out_specs=pl.BlockSpec((chunk, slow_t, width), lambda i: (i, 0, 0)),
             scratch_shapes=[pltpu.VMEM((chunk * fast_t, fast_part), F32)],
-            compiler_params=pltpu.CompilerParams(vmem_limit_bytes=12 * 1024 * 1024),
+            compiler_params=pltpu.CompilerParams(vmem_limit_bytes=16 * 1024 * 1024),
             name="fast_pack",
-        )(ids, clip_counts, frame_counts, v).reshape(ways, mine, slow_t, 128)
+        )(ids, clip_counts, frame_counts, v, *more).reshape(ways, mine, slow_t, width)
 
     def unpacked(pieces):
-        (out,) = call(
-            unpack_kernel,
-            [shape((places, fast_t, fast_part), BF16)],
+        width = pieces[0].shape[2]
+        outs = [shape((places, fast_t, fast_part), BF16)]
+        if width > 128:
+            outs = [shape((places, slow_t, slow_part), BF16)] + outs
+        out = call(
+            functools.partial(unpack_kernel, width),
+            outs,
             [ids, *pieces],
             [pltpu.VMEM((BIG * fast_t, fast_part), F32)],
             smem=1,
             name="fast_unpack",
         )
-        return out.reshape(clips, height, across, fast_t, fast_part).transpose(0, 3, 1, 2, 4)
+        fast = out[-1].reshape(clips, height, across, fast_t, fast_part).transpose(0, 3, 1, 2, 4)
+        return (joined(out[0]), fast) if len(out) == 2 else fast
 
     def split(v):
         return v.transpose(0, 2, 3, 1, 4).reshape(ways, mine, slow_t, slow_part)
 
-    def joined(pieces):
-        (v,) = call(
-            place_kernel, [shape((ways, mine, slow_t, slow_part), BF16)], [ids, *pieces], smem=1, name="slow_place"
-        )
+    def joined(v):
         return v.reshape(clips, height, across, slow_t, slow_part).transpose(0, 3, 1, 2, 4)
 
-    def exchanged(v):
-        return send_blocks([pick(v, chan ^ k, 0) for k in range(ways)], ways)
-
-    def returned(v):
-        return send_blocks([v[k] for k in range(ways)], ways)
-
-    fx_pieces = exchanged(packed(fast_input))
-    x_pieces = exchanged(split(slow_input))
+    def at_once(v):
+        return [v[0]] + [swap(v[k], "chan", ways, k) for k in range(1, ways)]
+
+    def blocks_of(v):
+        return [pick(v, chan ^ k, 0) for k in range(ways)]
+
+    def send(v, k):
+        return swap(v, "chan", ways, k)
+
+    x_blocks = blocks_of(split(slow_input))
+    fx_pieces = at_once(blocks_of(packed(fast_input)))
 
     all_clips = frame_counts.shape[0]
     live = (jnp.arange(all_clips, dtype=jnp.int32) % clips) < jnp.repeat(clip_counts, clips)
@@ -944,30 +1077,32 @@
     around = jnp.sum(jnp.where(clip[:, None] == jnp.arange(all_clips)[None, :], valid[None, :], 0), axis=1)
     table = jnp.concatenate([around, jnp.stack([chan, jnp.full_like(chan, parts)])]).astype(jnp.int32)
 
-    def share_of(v, axis):
-        amount = v.shape[axis] // 8
-        return lax.dynamic_slice_in_dim(v, group * amount, amount, axis).astype(BF16)
-
-    def over_chan(tree):
-        pieces = [tree] + [swap(tree, "chan", ways, k) for k in (1, 2, 3)]
-        return jax.tree.map(lambda *vs: jnp.stack(vs), *pieces)
-
     lat_t, red_t, lred_t = (v.transpose(0, 2, 1) for v in (lateral_kernel, slow_reduce, lateral_reduce))
-    tree = (jnp.concatenate([share_of(red_t, 1), share_of(lred_t, 1)], axis=2), share_of(lat_t, 1))
-
-    def blocks_of(v):
-        width = v.shape[-1]
-        tiled = jnp.concatenate([v] * ways, axis=1)
-        return jnp.where(jnp.arange(ways * width)[None, :] // width == chan, tiled, 0.0)
-
-    mid_g = blocks_of(jnp.concatenate([lateral_norm, slow_inner_norm.reshape(4, -1)]))
-    out_g = blocks_of(slow_outer_norm.reshape(4, -1))
-    mid_g, out_g = butterfly((mid_g, out_g), "chan", ways, (1, 2))
-    lat_g, in_g = mid_g[0:2], (mid_g[2:4], mid_g[4:6])
-    pieces = gather_group(over_chan(tree), sizes)
+    spatial_t = slow_spatial.reshape(9, slow_spatial.shape[2], -1).transpose(0, 2, 1)
+    params = [red_t, lred_t, lat_t, slow_expand, shortcut, lateral_shortcut, spatial_t]
+    scratch = [(3, 8, wide_in), (3, 8, mid), (5, 8, 128), (8, wide_in), (32, wide_in), (8, wide_in), (9, 8, mid)]
+    small = [lateral_norm, slow_inner_norm.reshape(4, -1), slow_outer_norm.reshape(4, -1)]
+    any_spec, vmem_spec = pl.BlockSpec(memory_space=pl.ANY), pl.BlockSpec(memory_space=pltpu.VMEM)
+    slab_a, slab_b = pl.pallas_call(
+        weight_slab_kernel,
+        out_shape=(shape((5, 8, wide_in), BF16), shape((9, 8, wide_in), BF16)),
+        in_specs=[pl.BlockSpec(memory_space=pltpu.SMEM)] + [any_spec] * 7 + [vmem_spec] * 3,
+        out_specs=(vmem_spec, vmem_spec),
+        scratch_shapes=[pltpu.VMEM(dims, F32) for dims in scratch] + [pltpu.SemaphoreType.DMA((7,))],
+        compiler_params=pltpu.CompilerParams(vmem_limit_bytes=8 * 1024 * 1024),
+        name="weight_slab",
+    )(ids, *params, *small)
+    slab_a = at_once([slab_a] * ways)
+    x_blocks = after(x_blocks, slab_a)
+    x_second = send(x_blocks[2], 2)
+    near = after((x_blocks[1], x_blocks[3]), (x_second, fx_pieces))
+    x_pieces = [x_blocks[0], send(near[0], 1), x_second, send(near[1], 3)]
+    slab_a = after(jnp.stack(slab_a), fx_pieces)
+    by_chip = jnp.stack([slab_a] + [swap(slab_a, "dp", sizes["dp"], 2 * k) for k in (1, 2, 3)])
+    own_slabs, other_slabs = by_chip, swap(by_chip, "dp", sizes["dp"], 1)
     fr_t = fast_reduce.transpose(0, 2, 1)
-    red_w, lred_w, w_first, w_fsp, w_fex, fin_g, fout_g = call(
-        first_weights_kernel,
+    red_w, lred_w, w_first, w_fsp, w_fex, fin_g, fout_g, mid_g, out_g = call(
+        weights_kernel,
         [
             shape((3, ways, 8, 8, wide_in), BF16),
             shape((3, ways, 8, 8, mid), BF16),
@@ -976,35 +1111,19 @@
             shape((128, wide_f), BF16),
             shape((4, 128)),
             shape((2, wide_f)),
+            shape((8, mid)),
+            shape((ways, 4, mid)),
         ],
-        [ids, *(p[0] for p in pieces), *(p[1] for p in pieces), fr_t, fast_spatial.reshape(9, *fast_spatial.shape[2:]), fast_expand,
+        [ids, own_slabs, other_slabs, fr_t, fast_spatial.reshape(9, *fast_spatial.shape[2:]), fast_expand,
          fast_inner_norm.reshape(4, -1), fast_outer_norm],
         [pltpu.VMEM((5, ways, 8, 8, 128), F32)],
         smem=1,
-        name="first_weights",
+        name="weights",
     )
     red_w, lred_w = red_w.reshape(-1, wide_in), lred_w.reshape(-1, mid)
     fin_g = (fin_g[0:2], fin_g[2:4])
-    spatial_t = slow_spatial.reshape(9, slow_spatial.shape[2], -1).transpose(0, 2, 1)
-    tree = (
-        jnp.concatenate([share_of(v, 0).reshape(-1, 8, wide_in) for v in (slow_expand, shortcut, lateral_shortcut)]),
-        share_of(spatial_t, 1),
-    )
-    pieces = gather_group(over_chan(tree), sizes)
-    exp_w, short_w, lshort_w, spat_w = call(
-        second_weights_kernel,
-        [
-            shape((ways, 8, 8, wide_in), BF16),
-            shape((ways, 8, 4, 8, wide_in), BF16),
-            shape((ways, 8, 8, wide_in), BF16),
-            shape((9, ways, 8, 8, mid), BF16),
-        ],
-        [ids, *(p[0] for p in pieces), *(p[1] for p in pieces)],
-        smem=1,
-        name="second_weights",
-    )
-    exp_w, short_w, lshort_w = (v.reshape(-1, wide_in) for v in (exp_w, short_w, lshort_w))
-    spat_w = spat_w.reshape(9, mid, mid)
+    lat_g, in_g = mid_g[0:2], (mid_g[2:4], mid_g[4:6])
+    out_g = out_g.transpose(1, 0, 2).reshape(4, wide_in)
 
     edge = [shape((halo, 8, 128))] * 2
     edges = [shape((halo, 8, 384))] * 2
@@ -1016,9 +1135,26 @@
         smem=1,
         name="fast_first",
     )
-    sums1, fast_cotangent, slow_cotangent = lax.optimization_barrier((sums1, fast_cotangent, slow_cotangent))
     fa_lo, fa_hi = halos(first, last, ways)
-    sums1 = everywhere(sums1, sizes)
+    sums1 = everywhere(sums1, sizes, (x_pieces, fa_lo, fa_hi))
+    slab_b = jnp.stack(at_once([after(slab_b, sums1)] * ways))
+    cots = blocks_of(packed(fast_cotangent, split(slow_cotangent)))
+    cots[1] = send(after(cots[1], sums1), 1)
+    own_slabs, other_slabs = gather_group(slab_b, sizes)
+    exp_w, short_w, lshort_w, spat_w = call(
+        more_weights_kernel,
+        [
+            shape((ways, 8, 8, wide_in), BF16),
+            shape((ways, 8, 4, 8, wide_in), BF16),
+            shape((ways, 8, 8, wide_in), BF16),
+            shape((9, ways, 8, 8, mid), BF16),
+        ],
+        [ids, own_slabs, other_slabs],
+        smem=1,
+        name="more_weights",
+    )
+    exp_w, short_w, lshort_w = (v.reshape(-1, wide_in) for v in (exp_w, short_w, lshort_w))
+    spat_w = spat_w.reshape(9, mid, mid)
     fast_pad = [pltpu.VMEM((3, ext, 8, 128), F32)]
     slow_pad = [pltpu.VMEM((3, ext, 8, mid), F32)]
     h1, fb, fb_sums = call(
@@ -1037,7 +1173,8 @@
         name="slow_first",
     )
     sa_lo, sa_hi = halos(first, last, ways)
-    sums2 = everywhere(sums2, sizes)
+    sums2 = everywhere(sums2, sizes, (slab_b, cots[1], sa_lo, sa_hi))
+    cots[2] = send(after(cots[2], sums2), 2)
     h2, fc, fc_sums = call(
         functools.partial(expand_kernel, True, mid),
         [shape((mine, 8, 128), BF16), shape((mine, 8, wide_f), BF16), shape((2, wide_f))],
@@ -1053,7 +1190,8 @@
         smem=2,
         name="slow_second",
     )
-    sums3 = everywhere(sums3, sizes)
+    sums3 = everywhere(sums3, sizes, cots[2])
+    cots[3] = send(after(cots[3], sums3), 3)
     sp, sp_sums = call(
         bypass_kernel,
         [shape((mine, 8, wide_in), BF16), shape((2, wide_in))],
@@ -1061,144 +1199,149 @@
         smem=1,
         name="bypass",
     )
-    fcot = jnp.stack(exchanged(packed(fast_cotangent)))
-    cot = jnp.stack(exchanged(split(slow_cotangent)))
+    hb, sc, sums4 = call(
+        functools.partial(expand_kernel, False, 0),
+        [shape((mine, 8, mid), BF16), shape((mine, 8, wide_in), BF16), shape((2, 2 * wide_in))],
+        [table, inv_n, sb, sums3, in_g[1], exp_w, sp_sums],
+        smem=2,
+        name="slow_third",
+    )
+    sums4 = everywhere(sums4, sizes, cots[3])
     fast_out, dfs, fc_slopes = call(
         functools.partial(fast_out_kernel, mid),
         [shape((ways, mine, 8, 128), BF16), shape((mine, 8, wide_f), BF16), shape((2, wide_f))],
-        [table, inv_n, fc, sums3, fout_g, fx, fcot],
+        [table, inv_n, fc, sums3, fout_g, fx, *cots],
+        [pltpu.VMEM((8, wide_f), F32)],
         smem=2,
         name="fast_out",
     )
-    hb, sc, sums4 = call(
-        functools.partial(expand_kernel, False, 0),
-        [shape((mine, 8, mid), BF16), shape((mine, 8, wide_in), BF16), shape((2, 2 * wide_in + wide_f))],
-        [table, inv_n, sb, sums3, in_g[1], exp_w, sp_sums, fc_slopes],
+    *outs, dss, sums5 = call(
+        slow_out_kernel,
+        [*[shape((mine, 8, 384), BF16)] * 4, shape((mine, 8, wide_in), BF16), shape((2, 2 * wide_in + wide_f))],
+        [table, inv_n, sc, sp, sums4, out_g, *cots, fast_out, fc_slopes],
+        [pltpu.VMEM((8, wide_in), F32)],
         smem=2,
-        name="slow_third",
-    )
-    sums4 = everywhere(sums4, sizes)
+        name="slow_out",
+    )
+
+    outs[1] = send(outs[1], 1)
+    sums5 = everywhere(sums5, sizes, outs[1])
+    outs[2] = send(after(outs[2], sums5), 2)
     dfc, dzfb, fb_slopes, first, last = call(
         functools.partial(expand_back_kernel, True, (mid, 2 * wide_in, mid)),
         [shape((mine, 8, wide_f), BF16), narrow, shape((2, 128)), *edges],
-        [table, inv_n, dfs, fc, sums3, fout_g, sums4, fb, sums2, fin_g[1], w_fex, sb],
+        [table, inv_n, dfs, fc, sums3, fout_g, sums5, fb, sums2, fin_g[1], w_fex, sb],
         smem=2,
         name="fast_third_back",
     )
-    slow_out, dss, sums5 = call(
-        slow_out_kernel,
-        [shape((ways, mine, 8, mid), BF16), shape((mine, 8, wide_in), BF16), shape((2, 2 * wide_in + 128))],
-        [table, inv_n, sc, sp, sums4, out_g, cot, fb_slopes],
+    low6, high6 = halos(first, last, ways)
+    dsc, dzsb, sums6, first, last = call(
+        functools.partial(expand_back_kernel, False, (0, 0, 0)),
+        [shape((mine, 8, wide_in), BF16), middle, shape((2, mid + 128)), *[shape((halo, 8, mid))] * 2],
+        [table, inv_n, dss, sc, sums4, out_g[0:2], sums5, sb, sums3, in_g[1], exp_w, fb_slopes],
         smem=2,
-        name="slow_out",
-    )
-
-    low5, high5 = halos(first, last, ways)
-    sums5 = everywhere(sums5, sizes)
+        name="slow_third_back",
+    )
+    low_sb, high_sb = halos(first, last, ways)
+    dss_late, = after((dss,), sums6)
+    sums6 = everywhere(sums6, sizes, (outs[2], low6, high6, low_sb, high_sb))
+    outs[3] = send(after(outs[3], sums6), 3)
+    dsp, dx, dl = call(
+        bypass_back_kernel,
+        [shape((mine, 8, wide_in), BF16), shape((mine, 8, wide_in), BF16), middle],
+        [table, inv_n, dss_late, sp, sums4, out_g[2:4], sums5, short_w, lshort_w],
+        smem=2,
+        name="bypass_back",
+    )
+
+    (slab1,) = call(
+        first_slab_kernel,
+        [shape((ways, 8, 6, 8, wide_in), BF16)],
+        [hb, dsc, x, lat, dsp],
+        [pltpu.VMEM((6, mid, wide_in), F32)],
+        name="first_slab",
+    )
     dfb, dzfa, fa_slopes = call(
-        functools.partial(conv_back_kernel, halo, across, per_clip, True, (mid, 2 * wide_in, 0, mid, 0)),
+        functools.partial(conv_back_kernel, halo, across, per_clip, True, (mid, mid, 0, mid, 0)),
         [shape((mine, 8, 128), BF16), narrow, shape((2, 128))],
-        [table, inv_n, sums2, fin_g[1], sums5, sa_lo, fb, sa_hi, low5, dzfb, high5, w_fsp, fa, sums1, fin_g[0]],
+        [table, inv_n, sums2, fin_g[1], sums6, sa_lo, fb, sa_hi, low6, dzfb, high6, w_fsp, fa, sums1, fin_g[0]],
         fast_pad,
         smem=2,
         name="fast_second_back",
     )
-    dsc, dzsb, sums6, first, last = call(
-        functools.partial(expand_back_kernel, False, (0, 0, 0)),
-        [shape((mine, 8, wide_in), BF16), middle, shape((2, mid + 128)), *[shape((halo, 8, mid))] * 2],
-        [table, inv_n, dss, sc, sums4, out_g[0:2], sums5, sb, sums3, in_g[1], exp_w, fa_slopes],
-        smem=2,
-        name="slow_third_back",
-    )
-    low6, high6 = halos(first, last, ways)
-    sums6 = everywhere(sums6, sizes)
-    fast_output = unpacked(returned(fast_out))
-    dzsb, fast_output = lax.optimization_barrier((dzsb, fast_output))
-    dsp, dx, dl = call(
-        bypass_back_kernel,
-        [shape((mine, 8, wide_in), BF16), shape((mine, 8, wide_in), BF16), middle],
-        [table, inv_n, dss, sp, sums4, out_g[2:4], sums5, short_w, lshort_w],
-        smem=2,
-        name="bypass_back",
-    )
     dsb, dzsa, sums7 = call(
         functools.partial(conv_back_kernel, halo, across, per_clip, False, (0, 0, 0, 128, 0)),
-        [shape((mine, 8, mid), BF16), middle, shape((2, mid))],
-        [table, inv_n, sums3, in_g[1], sums6, low5, sb, high5, low6, dzsb, high6, spat_w, sa, sums2, in_g[0]],
+        [shape((mine, 8, mid), BF16), middle, shape((2, mid + 128))],
+        [table, inv_n, sums3, in_g[1], sums6, low6, sb, high6, low_sb, dzsb, high_sb, spat_w, sa, sums2, in_g[0], fa_slopes],
         slow_pad,
         smem=2,
         name="slow_second_back",
     )
-    sums7 = everywhere(sums7, sizes)
-    slow_output = joined(returned(slow_out))
-    dzsa, slow_output = lax.optimization_barrier((dzsa, slow_output))
-    dsa, dslow, dzlp, sums8 = call(
+    slab1, sums7 = lax.optimization_barrier((slab1, sums7))
+    sums7 = everywhere(sums7, sizes, outs[3])
+    slab1 = scatter_sum(slab1, sizes, group, chan)
+    dsa, *dslow, dzlp, sums8 = call(
         slow_back_kernel,
-        [shape((mine, 8, 3 * mid), BF16), shape((ways, mine, 8, mid), BF16), middle, shape((2, mid))],
+        [shape((mine, 8, 3 * mid), BF16), *[shape((mine, 8, mid), BF16)] * 4, middle, shape((2, mid))],
         [table, inv_n, dzsa, sa, sums2, in_g[0], sums7, red_w, lred_w, dx, dl, lp, sums1, lat_g],
         smem=2,
         name="slow_first_back",
     )
-    slow_input_grad = joined(returned(dslow))
-    sums8 = everywhere(sums8, sizes)
-    dfirst, dfast = call(
+    dslow[1] = send(dslow[1], 1)
+    dsa, dsb_late = after((dsa, dsb), sums8)
+    sums8 = everywhere(sums8, sizes, dslow[1])
+    dslow[2] = send(after(dslow[2], sums8), 2)
+    dslow[3] = send(after(dslow[3], dslow[2]), 3)
+    slow_output, fast_output = unpacked(after(outs, sums8))
+    (slab2,) = call(
+        functools.partial(second_slab_kernel, halo, across, per_clip),
+        [shape((ways, 8, 6, 8, wide_in), BF16)],
+        [table, ha, dsb_late, dsa, x, lat],
+        [*slow_pad, pltpu.VMEM((3, mid, 3 * mid), F32), pltpu.VMEM((3, mid, wide_in), F32), pltpu.VMEM((3, mid, mid), F32)],
+        smem=1,
+        name="second_slab",
+    )
+    slab2 = scatter_sum(slab2, sizes, group, chan)
+    dfirst, *dfast = call(
         functools.partial(fast_back_kernel, mid),
-        [shape((mine, 8, 896), BF16), shape((ways, mine, 8, 128), BF16)],
-        [table, inv_n, sums1, fin_g[0], lat_g, sums6, sums8, dzfa, fa, dzlp, lp, dfs, w_first],
+        [shape((mine, 8, 896), BF16), *[shape((mine, 8, 128), BF16)] * 4],
+        [table, inv_n, sums1, fin_g[0], lat_g, sums7, sums8, dzfa, fa, dzlp, lp, dfs, w_first],
         smem=2,
         name="fast_first_back",
     )
 
-    fast_input_grad = unpacked(returned(dfast))
-
-    def shares(v, lead):
-        return v.reshape(ways, 8, lead, 8, v.shape[-1])
-
-    g_wide = jnp.concatenate(
-        [shares(weight_sum(hb, dsc), 1), shares(weight_sum(x, dsp), 4), shares(weight_sum(lat, dsp), 1)], axis=2
-    )
-    (g_spat,) = call(
-        functools.partial(conv_weight_kernel, halo, across, per_clip, False),
-        [shape((ways, 8, 9, 8, mid), BF16)],
-        [table, ha, dsb],
-        [*slow_pad, pltpu.VMEM((3, mid, 3 * mid), F32)],
+    g_lat, g_fast = call(
+        functools.partial(fast_grads_kernel, halo, across, per_clip),
+        [shape((ways, 40, 8, 128), BF16), shape((28, 8, 128), BF16)],
+        [table, h1, dfb, dfirst, fx, h2, dfc],
+        [*fast_pad, pltpu.VMEM((3, 384, 128), F32), pltpu.VMEM((896, wide_f), F32), pltpu.VMEM((128, wide_f), F32)],
         smem=1,
-        name="slow_spatial_grad",
-    )
-    pieces = gather_group(scatter_sum((g_wide, g_spat), sizes, group, chan), sizes)
-    g_exp, g_short, g_lshort, g_spat = call(
+        name="fast_grads",
+    )
+    small = [jnp.concatenate([pick(g_lat, chan ^ k, 0), g_fast]) for k in range(ways)]
+    small = add(*at_once(after(small, dslow[2])))
+    for bits in stages(sizes["dp"], True):
+        small = butterfly(small, "dp", sizes["dp"], bits)
+    g_lat, g_fast = small[0:40].astype(F32), small[40:68].astype(F32)
+    own1, other1 = gather_group(slab1, sizes)
+    g_exp, g_short, g_lshort = call(
         first_grads_kernel,
-        [shape((8, 8, wide_in)), shape((8, 4, 8, wide_in)), shape((8, 8, wide_in)), shape((9, 8, 8, mid))],
-        [ids, *(p[0] for p in pieces), *(p[1] for p in pieces)],
+        [shape((8, 8, wide_in)), shape((8, 4, 8, wide_in)), shape((8, 8, wide_in))],
+        [ids, own1, other1],
         smem=1,
         name="first_grads",
     )
-    (g_fsp,) = call(
-        functools.partial(conv_weight_kernel, halo, across, per_clip, True),
-        [shape((3, 384, 128))],
-        [table, h1, dfb],
-        [*fast_pad, pltpu.VMEM((3, 384, 128), F32)],
-        smem=1,
-        name="fast_spatial_grad",
-    )
-    g_fex = weight_sum(h2, dfc, F32)
-    g_lat, g_fast = call(
-        fast_grads_kernel,
-        [shape((ways, 8, 5, 8, 128), BF16), shape((28, 8, 128), BF16)],
-        [weight_sum(dfirst, fx, F32), g_fsp, g_fex],
-        name="fast_grads",
-    )
-    g_red = weight_sum(dsa, jnp.concatenate([x, lat], axis=2)).reshape(3, ways, 8, 8, wide_in + mid).transpose(1, 2, 0, 3, 4)
-    g_fast = everywhere(g_fast, sizes)
-    pieces = gather_group(scatter_sum((g_red, g_lat), sizes, group, chan), sizes)
-    g_red, g_lred, g_lat = call(
+    own2, other2 = gather_group(slab2, sizes)
+    g_red, g_lred, g_spat = call(
         second_grads_kernel,
-        [shape((3, 8, 8, wide_in)), shape((3, 8, 8, mid)), shape((5, 8, 8, 128))],
-        [ids, *(p[0] for p in pieces), *(p[1] for p in pieces)],
+        [shape((3, 8, 8, wide_in)), shape((3, 8, 8, mid)), shape((9, 8, 8, mid))],
+        [ids, own2, other2],
         smem=1,
         name="second_grads",
     )
-    g_fast = g_fast.astype(F32)
+    (slow_input_grad,) = call(place_kernel, [shape((places, slow_t, slow_part), BF16)], [ids, *dslow], smem=1, name="slow_place")
+    slow_input_grad = joined(slow_input_grad)
+    fast_input_grad = unpacked(at_once(after(dfast, dslow[3])))
     g_fred = g_fast[0:12].reshape(3, 32, 128).transpose(0, 2, 1)
     g_fex = g_fast[12:16].reshape(32, 128)
     g_fsp = g_fast[16:28].reshape(3, 32, 128)[:, :, 0:96].reshape(3, 32, 3, 32).transpose(0, 2, 1, 3)
@@ -1213,11 +1356,11 @@
         return jnp.sum(slopes.reshape(2, ratio, 128 // ratio), axis=1)
 
     lw, sw, ow = lateral_norm.shape[1], slow_inner_norm.shape[2], slow_outer_norm.shape[2]
-    fast_inner_grad = jnp.stack([pair(fold_in(sums6[:, mid:])), pair(fold_in(sums5[:, 2 * wide_in :]))])
-    fc_slopes = sums4[:, 2 * wide_in :].reshape(2, ways, ratio, fast_part)
+    fast_inner_grad = jnp.stack([pair(fold_in(sums7[:, mid:])), pair(fold_in(sums6[:, mid:]))])
+    fc_slopes = sums5[:, 2 * wide_in :].reshape(2, ways, ratio, fast_part)
     fast_outer_grad = pair(jnp.sum(fc_slopes, axis=2).reshape(2, -1))
     lateral_grad = pair(own(sums8, lw))
-    slow_inner_grad = own(jnp.stack([pair(sums7), pair(sums6[:, 0:mid])]), sw)
+    slow_inner_grad = own(jnp.stack([pair(sums7[:, 0:mid]), pair(sums6[:, 0:mid])]), sw)
     slow_outer_grad = own(jnp.stack([pair(sums5[:, 0:wide_in]), pair(sums5[:, wide_in : 2 * wide_in])]), ow)
     return (
         slow_output,

time: 707 us -> 640 us (0.905)
  starting transfers between devices: 284 us -> 182 us
  waiting for transfers between devices: 175 us -> 256 us
  local copies, waits for them, and re-layouts: 103 us -> 57.7 us
  Pallas kernels: 103 us -> 118 us
  matrix products: 10.2 us -> 0 us
    ppermute x189 -> x117, starting transfers between devices: 250 us -> 161 us  [swap(): return jax.tree.map(lambda v: lax.ppermute(v, axis, pairs), tree)]
    ppermute x189 -> x117, waiting for transfers between devices: 165 us -> 230 us  [swap(): return jax.tree.map(lambda v: lax.ppermute(v, axis, pairs), tree)]
    unnamed x495 -> x211, local copies, waits for them, and re-layouts: 73.8 us -> 41.4 us
    ppermute x4, waiting for transfers between devices: 8.78 us -> 23.3 us  [halos(): high = lax.ppermute(first, 'chan', [(i + 1, i) for i in range(count - 1)])]
    pallas_call x27 -> x26, Pallas kernels: 96.9 us -> 111 us  [call(): pl.pallas_call(kernel, out_shape=tuple(outs), in_specs=specs, out_specs=t...]
    ppermute x4, starting transfers between devices: 28 us -> 16.1 us  [halos(): low = lax.ppermute(last, 'chan', [(i, i + 1) for i in range(count - 1)])]
    dot_general x6 -> x0, matrix products: 10.2 us -> none  [weight_sum(): jnp.einsum('pti,pto->io', a, b, preferred_element_type=F32).astype(dtype)]
  transfers between devices with their start and end apart: 197 -> 125, of which waited for: 67 -> 73; matrix products, arithmetic and copies ran while one was open for 8% -> 5% of each run, Pallas kernels for 13% -> 16%
where the time goes in v3:
time: 640 us; the launch traced here: 632 us
  waiting for transfers between devices  256 us (40%)
  starting transfers between devices  182 us (28%)
  Pallas kernels  118 us (18%)
  local copies, waits for them, and re-layouts  57.7 us (9%)
  other arithmetic  14.8 us (2%)
    ppermute x117, waiting for transfers between devices, swap(): return jax.tree.map(lambda v: lax.ppermute(v, axis, pairs), tree)  230 us
    ppermute x117, starting transfers between devices, swap(): return jax.tree.map(lambda v: lax.ppermute(v, axis, pairs), tree)  161 us
    pallas_call x26, Pallas kernels, call(): pl.pallas_call(kernel, out_shape=tuple(outs), in_specs=specs, out_specs=t...  111 us
    unnamed x211, local copies, waits for them, and re-layouts  41.4 us
    ppermute x4, waiting for transfers between devices, halos(): high = lax.ppermute(first, 'chan', [(i + 1, i) for i in range(count - 1)])  23.3 us
    ppermute x4, starting transfers between devices, halos(): low = lax.ppermute(last, 'chan', [(i, i + 1) for i in range(count - 1)])  16.1 us
  transfers between devices with their start and end apart: 125, of which 73 were waited for; matrix products, arithmetic and copies ran while one was open for 5% of the time, Pallas kernels for 16%

profile of v3, /device:TPU:0, one launch (start us, length us, event | category | flops | bytes accessed | tf_op | source)
XLA Modules:
  0.0 632.1 jit_solution(6245651892483443804)
XLA Ops:
  23.2 10.7 %collective-permute-done = bf16[5,8,1024]{2,1,0:T(8,128)(2,1)S(1)} collective-permute-done((bf16[5,8,1024]{2,1,0:T(8,128)(2,1)S(1)}, bf16[5,8,1024]{2,1,0:T(8,128)(2,1)S(1)}, u32[]{:S(2)}, u32[]{:S(2)}) %collective-permute-start) | collective-permute-done | bytes 81952 | tf_op jit(solution)/shard_map/ppermute | solution.py:896
  36.6 10.3 %collective-permute-done.1 = bf16[5,8,1024]{2,1,0:T(8,128)(2,1)S(1)} collective-permute-done((bf16[5,8,1024]{2,1,0:T(8,128)(2,1)S(1)}, bf16[5,8,1024]{2,1,0:T(8,128)(2,1)S(1)}, u32[]{:S(2)}, u32[]{:S(2)}) %collective-permute-start.1) | collective-permute-done | bytes 81952 | tf_op jit(solution)/shard_map/ppermute | solution.py:896
  50.6 8.1 %collective-permute-done.11 = bf16[4,5,8,1024]{3,2,1,0:T(8,128)(2,1)S(1)} collective-permute-done((bf16[4,5,8,1024]{3,2,1,0:T(8,128)(2,1)S(1)}, bf16[4,5,8,1024]{3,2,1,0:T(8,128)(2,1)S(1)}, u32[]{:S(2)}, u32[]{:S(2)}) %collective-permute-start.11) | collective-permute-done | bytes 327712 | tf_op jit(solution)/shard_map/ppermute | solution.py:896
  67.6 27.2 %collective-permute-done.3.x2_ref = bf16[147,8,256]{2,1,0:T(8,128)(2,1)S(1)} collective-permute-done((bf16[147,8,256]{2,1,0:T(8,128)(2,1)}, bf16[147,8,256]{2,1,0:T(8,128)(2,1)S(1)}, u32[]{:S(2)}, u32[]{:S(2)}) %collective-permute-start.3) | collective-permute-done | bytes 602144 | tf_op jit(solution)/shard_map/ppermute | solution.py:896
  140.8 4.7 collective-permute-done.27
  149.2 13.7 %collective-permute-done.37 = bf16[4,9,8,1024]{3,2,1,0:T(8,128)(2,1)S(1)} collective-permute-done((bf16[4,9,8,1024]{3,2,1,0:T(8,128)(2,1)S(1)}, bf16[4,9,8,1024]{3,2,1,0:T(8,128)(2,1)S(1)}, u32[]{:S(2)}, u32[]{:S(2)}) %collective-permute-start.37) | collective-permute-done | bytes 589856 | tf_op jit(solution)/shard_map/ppermute | solution.py:896
  162.9 9.8 %collective-permute-done.36 = bf16[4,9,8,1024]{3,2,1,0:T(8,128)(2,1)S(1)} collective-permute-done((bf16[4,9,8,1024]{3,2,1,0:T(8,128)(2,1)S(1)}, bf16[4,9,8,1024]{3,2,1,0:T(8,128)(2,1)S(1)}, u32[]{:S(2)}, u32[]{:S(2)}) %collective-permute-start.36) | collective-permute-done | bytes 589856 | tf_op jit(solution)/shard_map/ppermute | solution.py:896
  193.8 5.9 slow_first.1
  240.7 20.5 %collective-permute-done.43.c2_ref = bf16[147,8,384]{2,1,0:T(8,128)(2,1)S(1)} collective-permute-done((bf16[147,8,384]{2,1,0:T(8,128)(2,1)S(1)}, bf16[147,8,384]{2,1,0:T(8,128)(2,1)S(1)}, u32[]{:S(2)}, u32[]{:S(2)}) %collective-permute-start.43) | collective-permute-done | bytes 903200 | tf_op jit(solution)/shard_map/ppermute | solution.py:896
  268.7 4.4 bypass.1
  283.8 5.6 collective-permute-done.51.c3_ref
  289.4 18.6 %collective-permute-start.53 = (f32[2,2048]{1,0:T(2,128)S(1)}, f32[2,2048]{1,0:T(2,128)S(1)}, u32[]{:S(2)}, u32[]{:S(2)}) collective-permute-start(f32[2,2048]{1,0:T(2,128)S(1)} %add_add_fusion.3), channel_id=1, source_target_pairs={{0,2},{1,3},{2,0},{3,1},{4,6},{5,7},{6,4},{7,5},{8,10},{9,11},{10,... | collective-permute-start | bytes 49160 | tf_op jit(solution)/shard_map/ppermute | solution.py:896
  310.5 4.8 fast_out.1
  315.3 8.6 %slow_out.1 = (bf16[147,8,384]{2,1,0:T(8,128)(2,1)S(1)}, bf16[147,8,384]{2,1,0:T(8,128)(2,1)S(1)}, bf16[147,8,384]{2,1,0:T(8,128)(2,1)S(1)}, bf16[147,8,384]{2,1...) custom-call(s32[7]{0:T(128)S(1)} %pad_add_fusion.1.table_ref, ...), custom_call_target="tpu_custom_call" | custom-call | bytes 1 | tf_op jit(solution)/shard_map/slow_out/pallas_call | solution.py:124
  333.9 10.0 %collective-permute-done.55.refs_1_ = bf16[147,8,384]{2,1,0:T(8,128)(2,1)S(1)} collective-permute-done((bf16[147,8,384]{2,1,0:T(8,128)(2,1)S(1)}, bf16[147,8,384]{2,1,0:T(8,128)(2,1)S(1)}, u32[]{:S(2)}, u32[]{:S(2)}) %collective-permute-start.55) | collective-permute-done | bytes 903200 | tf_op jit(solution)/shard_map/ppermute | solution.py:896
  364.5 4.6 collective-permute-start.68
  370.4 4.6 collective-permute-start.70
  377.4 18.5 %collective-permute-done.71.dhi_ref = f32[15,8,256]{2,1,0:T(8,128)S(1)} collective-permute-done((f32[15,8,256]{2,1,0:T(8,128)S(1)}, f32[15,8,256]{2,1,0:T(8,128)S(1)}, u32[]{:S(2)}, u32[]{:S(2)}) %collective-permute-start.71) | collective-permute-done | bytes 122912 | tf_op jit(solution)/shard_map/ppermute | solution.py:940
  405.3 5.9 bypass_back.1
  411.2 5.1 first_slab.1
  435.3 9.1 %collective-permute-start.81 = (f32[2,384]{1,0:T(2,128)S(1)}, f32[2,384]{1,0:T(2,128)S(1)}, u32[]{:S(2)}, u32[]{:S(2)}) collective-permute-start(f32[2,384]{1,0:T(2,128)S(1)} %add_add_fusion.7), channel_id=1, source_target_pairs={{0,2},{1,3},{2,0},{3,1},{4,6},{5,7},{6,4},{7,5},{8,10},{9,11},{10,... | collective-permute-start | bytes 9224 | tf_op jit(solution)/shard_map/ppermute | solution.py:896
  450.6 5.9 slow_first_back.1
  468.8 6.7 %second_slab.1 = bf16[4,8,6,8,1024]{4,3,2,1,0:T(8,128)(2,1)S(1)} custom-call(s32[7]{0:T(128)S(1)} %pad_add_fusion.1.table_ref, bf16[177,8,256]{2,1,0:T(8,128)(2,1)S(1)} %copy-done.48, bf16[147,8,256]{2,1,0:T(8,128)(2,1)S(1)} %copy-done.50, bf16[147,8,768]{2,1,0:T(8,128)(2,1)S(1)} %copy-done.26, bf16[147,8,1024]{2,1,0:T(8,128)(2,1)S(1)} %get-tuple-element.188.x_ref, ...), custom_call_target="tpu_custom_call" | custom-call | bytes 1 | tf_op jit(solution)/shard_map/second_slab/pallas_call | solution.py:124
  491.0 5.3 fast_first_back.1
  502.3 11.6 %collective-permute-done.91.refs_2_ = bf16[147,8,256]{2,1,0:T(8,128)(2,1)S(1)} collective-permute-done((bf16[147,8,256]{2,1,0:T(8,128)(2,1)}, bf16[147,8,256]{2,1,0:T(8,128)(2,1)S(1)}, u32[]{:S(2)}, u32[]{:S(2)}) %collective-permute-start.91) | collective-permute-done | bytes 602144 | tf_op jit(solution)/shard_map/ppermute | solution.py:896
  522.6 4.7 collective-permute-done.97
  531.1 6.1 fast_unpack.2
  561.3 6.2 collective-permute-done.105
  570.3 5.6 collective-permute-done.117
  577.9 5.6 collective-permute-done.116
  588.3 9.0 %collective-permute-done.108 = bf16[6,8,1024]{2,1,0:T(8,128)(2,1)S(1)} collective-permute-done((bf16[6,8,1024]{2,1,0:T(8,128)(2,1)S(1)}, bf16[6,8,1024]{2,1,0:T(8,128)(2,1)S(1)}, u32[]{:S(2)}, u32[]{:S(2)}) %collective-permute-start.108) | collective-permute-done | bytes 98336 | tf_op jit(solution)/shard_map/ppermute | solution.py:896
  621.6 5.9 fast_unpack.3
  (552 shorter events, 345.3 us)
Async XLA Ops:
  8.7 38.3 %collective-permute-start.4 = (bf16[147,8,128]{2,1,0:T(8,128)(2,1)}, bf16[147,8,128]{2,1,0:T(8,128)(2,1)S(1)}, u32[]{:S(2)}, u32[]{:S(2)}) collective-permute-start(bf16[147,8,128]{2,1,0:T(8,128)(2,1)} %get-tuple-element.341), channel_id=1, source_target_pairs={{0,1},{1,0},{2,3},{3,2},{4,5},{5,4},{6,7},{7,6},{8,9},{9,8},{10,11... | collective-permute-start | bytes 903176 | tf_op jit(solution)/shard_map/ppermute | solution.py:896
  11.7 35.3 %collective-permute-start.5 = (bf16[147,8,128]{2,1,0:T(8,128)(2,1)}, bf16[147,8,128]{2,1,0:T(8,128)(2,1)S(1)}, u32[]{:S(2)}, u32[]{:S(2)}) collective-permute-start(bf16[147,8,128]{2,1,0:T(8,128)(2,1)} %get-tuple-element.340), channel_id=1, source_target_pairs={{0,2},{1,3},{2,0},{3,1},{4,6},{5,7},{6,4},{7,5},{8,10},{9,11},{10,... | collective-permute-start | bytes 903176 | tf_op jit(solution)/shard_map/ppermute | solution.py:896
  14.3 32.8 %collective-permute-start.6 = (bf16[147,8,128]{2,1,0:T(8,128)(2,1)}, bf16[147,8,128]{2,1,0:T(8,128)(2,1)}, u32[]{:S(2)}, u32[]{:S(2)}) collective-permute-start(bf16[147,8,128]{2,1,0:T(8,128)(2,1)} %get-tuple-element.339), channel_id=1, source_target_pairs={{0,3},{1,2},{2,1},{3,0},{4,7},{5,6},{6,5},{7,4},{8,11},{9,10},{10,... | collective-permute-start | bytes 903176 | tf_op jit(solution)/shard_map/ppermute | solution.py:896
  19.7 27.2 %collective-permute-start.1 = (bf16[5,8,1024]{2,1,0:T(8,128)(2,1)S(1)}, bf16[5,8,1024]{2,1,0:T(8,128)(2,1)S(1)}, u32[]{:S(2)}, u32[]{:S(2)}) collective-permute-start(bf16[5,8,1024]{2,1,0:T(8,128)(2,1)S(1)} %get-tuple-element.150), channel_id=1, source_target_pairs={{0,2},{1,3},{2,0},{3,1},{4,6},{5,7},{6,4},{7,5},{8,10},{9,11},{10,... | collective-permute-start | bytes 245768 | tf_op jit(solution)/shard_map/ppermute | solution.py:896
  62.4 35.0 %collective-permute-start.12 = (bf16[4,4,5,8,1024]{4,3,2,1,0:T(8,128)(2,1)S(1)}, bf16[4,4,5,8,1024]{4,3,2,1,0:T(8,128)(2,1)S(1)}, u32[]{:S(2)}, u32[]{:S(2)}) collective-permute-start(bf16[4,4,5,8,1024]{4,3,2,1,0:T(8,128)(2,1)S(1)} %pad_maximum_fusion.1.own_ref), channel_id=1, source_target_pairs={{0,4},{4,0},{8,12},{12,8},{16,20},{20,16},{24,28},{28,24},{1,5},{5... | collective-permute-start | bytes 3932168 | tf_op jit(solution)/shard_map/ppermute | solution.py:896
  64.0 30.7 %collective-permute-start.3 = (bf16[147,8,256]{2,1,0:T(8,128)(2,1)}, bf16[147,8,256]{2,1,0:T(8,128)(2,1)S(1)}, u32[]{:S(2)}, u32[]{:S(2)}) collective-permute-start(bf16[147,8,256]{2,1,0:T(8,128)(2,1)} %get-tuple-element.154), channel_id=1, source_target_pairs={{0,2},{1,3},{2,0},{3,1},{4,6},{5,7},{6,4},{7,5},{8,10},{9,11},{10,... | collective-permute-start | bytes 1806344 | tf_op jit(solution)/shard_map/ppermute | solution.py:896
  94.7 27.8 %collective-permute-start.7 = (bf16[147,8,256]{2,1,0:T(8,128)(2,1)}, bf16[147,8,256]{2,1,0:T(8,128)(2,1)}, u32[]{:S(2)}, u32[]{:S(2)}) collective-permute-start(bf16[147,8,256]{2,1,0:T(8,128)(2,1)} %get-tuple-element.155), channel_id=1, source_target_pairs={{0,1},{1,0},{2,3},{3,2},{4,5},{5,4},{6,7},{7,6},{8,9},{9,8},{10,11... | collective-permute-start | bytes 1806344 | tf_op jit(solution)/shard_map/ppermute | solution.py:896
  94.7 29.2 %collective-permute-start.8 = (bf16[147,8,256]{2,1,0:T(8,128)(2,1)}, bf16[147,8,256]{2,1,0:T(8,128)(2,1)}, u32[]{:S(2)}, u32[]{:S(2)}) collective-permute-start(bf16[147,8,256]{2,1,0:T(8,128)(2,1)} %get-tuple-element.156), channel_id=1, source_target_pairs={{0,3},{1,2},{2,1},{3,0},{4,7},{5,6},{6,5},{7,4},{8,11},{9,10},{10,... | collective-permute-start | bytes 1806344 | tf_op jit(solution)/shard_map/ppermute | solution.py:896
  147.4 25.3 %collective-permute-start.36 = (bf16[4,9,8,1024]{3,2,1,0:T(8,128)(2,1)S(1)}, bf16[4,9,8,1024]{3,2,1,0:T(8,128)(2,1)S(1)}, u32[]{:S(2)}, u32[]{:S(2)}) collective-permute-start(bf16[4,9,8,1024]{3,2,1,0:T(8,128)(2,1)S(1)} %get-tuple-element.344), channel_id=1, source_target_pairs={{0,16},{4,20},{8,24},{12,28},{16,0},{20,4},{24,8},{28,12},{1,17},{... | collective-permute-start | bytes 1769480 | tf_op jit(solution)/shard_map/ppermute | solution.py:896
  148.7 24.0 %collective-permute-start.35 = (bf16[4,9,8,1024]{3,2,1,0:T(8,128)(2,1)S(1)}, bf16[4,9,8,1024]{3,2,1,0:T(8,128)(2,1)S(1)}, u32[]{:S(2)}, u32[]{:S(2)}) collective-permute-start(bf16[4,9,8,1024]{3,2,1,0:T(8,128)(2,1)S(1)} %get-tuple-element.344), channel_id=1, source_target_pairs={{0,8},{4,12},{8,0},{12,4},{16,24},{20,28},{24,16},{28,20},{1,9},{5... | collective-permute-start | bytes 1769480 | tf_op jit(solution)/shard_map/ppermute | solution.py:896
  174.4 51.4 %collective-permute-start.38 = (bf16[4,4,9,8,1024]{4,3,2,1,0:T(8,128)(2,1)}, bf16[4,4,9,8,1024]{4,3,2,1,0:T(8,128)(2,1)}, u32[]{:S(2)}, u32[]{:S(2)}) collective-permute-start(bf16[4,4,9,8,1024]{4,3,2,1,0:T(8,128)(2,1)} %pad_maximum_fusion.own_ref), channel_id=1, source_target_pairs={{0,4},{4,0},{8,12},{12,8},{16,20},{20,16},{24,28},{28,24},{1,5},{5... | collective-permute-start | bytes 7077896 | tf_op jit(solution)/shard_map/ppermute | solution.py:896
  182.7 33.2 %collective-permute-start.29 = (bf16[147,8,384]{2,1,0:T(8,128)(2,1)}, bf16[147,8,384]{2,1,0:T(8,128)(2,1)}, u32[]{:S(2)}, u32[]{:S(2)}) collective-permute-start(bf16[147,8,384]{2,1,0:T(8,128)(2,1)} %get-tuple-element.175), channel_id=1, source_target_pairs={{0,1},{1,0},{2,3},{3,2},{4,5},{5,4},{6,7},{7,6},{8,9},{9,8},{10,11... | collective-permute-start | bytes 2709512 | tf_op jit(solution)/shard_map/ppermute | solution.py:896
  223.1 38.1 %collective-permute-start.43 = (bf16[147,8,384]{2,1,0:T(8,128)(2,1)S(1)}, bf16[147,8,384]{2,1,0:T(8,128)(2,1)S(1)}, u32[]{:S(2)}, u32[]{:S(2)}) collective-permute-start(bf16[147,8,384]{2,1,0:T(8,128)(2,1)S(1)} %copy-done.101), channel_id=1, source_target_pairs={{0,2},{1,3},{2,0},{3,1},{4,6},{5,7},{6,4},{7,5},{8,10},{9,11},{10,... | collective-permute-start | bytes 2709512 | tf_op jit(solution)/shard_map/ppermute | solution.py:896
  266.6 22.8 %collective-permute-start.51 = (bf16[147,8,384]{2,1,0:T(8,128)(2,1)S(1)}, bf16[147,8,384]{2,1,0:T(8,128)(2,1)S(1)}, u32[]{:S(2)}, u32[]{:S(2)}) collective-permute-start(bf16[147,8,384]{2,1,0:T(8,128)(2,1)S(1)} %copy-done.100), channel_id=1, source_target_pairs={{0,3},{1,2},{2,1},{3,0},{4,7},{5,6},{6,5},{7,4},{8,11},{9,10},{10,... | collective-permute-start | bytes 2709512 | tf_op jit(solution)/shard_map/ppermute | solution.py:896
  289.4 25.9 %collective-permute-start.53 = (f32[2,2048]{1,0:T(2,128)S(1)}, f32[2,2048]{1,0:T(2,128)S(1)}, u32[]{:S(2)}, u32[]{:S(2)}) collective-permute-start(f32[2,2048]{1,0:T(2,128)S(1)} %add_add_fusion.3), channel_id=1, source_target_pairs={{0,2},{1,3},{2,0},{3,1},{4,6},{5,7},{6,4},{7,5},{8,10},{9,11},{10,... | collective-permute-start | bytes 49160 | tf_op jit(solution)/shard_map/ppermute | solution.py:896
  323.9 20.0 %collective-permute-start.55 = (bf16[147,8,384]{2,1,0:T(8,128)(2,1)S(1)}, bf16[147,8,384]{2,1,0:T(8,128)(2,1)S(1)}, u32[]{:S(2)}, u32[]{:S(2)}) collective-permute-start(bf16[147,8,384]{2,1,0:T(8,128)(2,1)S(1)} %get-tuple-element.205), channel_id=1, source_target_pairs={{0,1},{1,0},{2,3},{3,2},{4,5},{5,4},{6,7},{7,6},{8,9},{9,8},{10,11... | collective-permute-start | bytes 2709512 | tf_op jit(solution)/shard_map/ppermute | solution.py:896
  352.1 43.9 %collective-permute-start.63 = (bf16[147,8,384]{2,1,0:T(8,128)(2,1)S(1)}, bf16[147,8,384]{2,1,0:T(8,128)(2,1)S(1)}, u32[]{:S(2)}, u32[]{:S(2)}) collective-permute-start(bf16[147,8,384]{2,1,0:T(8,128)(2,1)S(1)} %get-tuple-element.209), channel_id=1, source_target_pairs={{0,2},{1,3},{2,0},{3,1},{4,6},{5,7},{6,4},{7,5},{8,10},{9,11},{10,... | collective-permute-start | bytes 2709512 | tf_op jit(solution)/shard_map/ppermute | solution.py:896
  364.5 31.4 %collective-permute-start.68 = (f32[15,8,384]{2,1,0:T(8,128)S(1)}, f32[15,8,384]{2,1,0:T(8,128)S(1)}, u32[]{:S(2)}, u32[]{:S(2)}) collective-permute-start(f32[15,8,384]{2,1,0:T(8,128)S(1)} %get-tuple-element.215), channel_id=1, source_target_pairs={{0,1},{1,2},{2,3},{4,5},{5,6},{6,7},{8,9},{9,10},{10,11},{12,13},{... | collective-permute-start | bytes 552968 | tf_op jit(solution)/shard_map/ppermute | solution.py:939
  369.1 26.8 %collective-permute-start.69 = (f32[15,8,384]{2,1,0:T(8,128)S(1)}, f32[15,8,384]{2,1,0:T(8,128)S(1)}, u32[]{:S(2)}, u32[]{:S(2)}) collective-permute-start(f32[15,8,384]{2,1,0:T(8,128)S(1)} %get-tuple-element.216), channel_id=1, source_target_pairs={{1,0},{2,1},{3,2},{5,4},{6,5},{7,6},{9,8},{10,9},{11,10},{13,12},{... | collective-permute-start | bytes 552968 | tf_op jit(solution)/shard_map/ppermute | solution.py:940
  375.0 20.9 %collective-permute-start.71 = (f32[15,8,256]{2,1,0:T(8,128)S(1)}, f32[15,8,256]{2,1,0:T(8,128)S(1)}, u32[]{:S(2)}, u32[]{:S(2)}) collective-permute-start(f32[15,8,256]{2,1,0:T(8,128)S(1)} %get-tuple-element.218), channel_id=1, source_target_pairs={{1,0},{2,1},{3,2},{5,4},{6,5},{7,6},{9,8},{10,9},{11,10},{13,12},{... | collective-permute-start | bytes 368648 | tf_op jit(solution)/shard_map/ppermute | solution.py:940
  403.4 30.8 %collective-permute-start.75 = (bf16[147,8,384]{2,1,0:T(8,128)(2,1)S(1)}, bf16[147,8,384]{2,1,0:T(8,128)(2,1)S(1)}, u32[]{:S(2)}, u32[]{:S(2)}) collective-permute-start(bf16[147,8,384]{2,1,0:T(8,128)(2,1)S(1)} %get-tuple-element.220), channel_id=1, source_target_pairs={{0,3},{1,2},{2,1},{3,0},{4,7},{5,6},{6,5},{7,4},{8,11},{9,10},{10,... | collective-permute-start | bytes 2709512 | tf_op jit(solution)/shard_map/ppermute | solution.py:896
  483.8 59.5 %collective-permute-start.103 = (bf16[4,4,6,8,1024]{4,3,2,0,1:T(8,128)(2,1)}, bf16[4,4,6,8,1024]{4,3,2,0,1:T(8,128)(2,1)}, u32[]{:S(2)}, u32[]{:S(2)}) collective-permute-start(bf16[4,4,6,8,1024]{4,3,2,0,1:T(8,128)(2,1)} %bitcast.194), channel_id=1, source_target_pairs={{0,4},{4,0},{8,12},{12,8},{16,20},{20,16},{24,28},{28,24},{1,5},{5... | collective-permute-start | bytes 4718600 | tf_op jit(solution)/shard_map/ppermute | solution.py:896
  483.8 30.1 %collective-permute-start.91 = (bf16[147,8,256]{2,1,0:T(8,128)(2,1)}, bf16[147,8,256]{2,1,0:T(8,128)(2,1)S(1)}, u32[]{:S(2)}, u32[]{:S(2)}) collective-permute-start(bf16[147,8,256]{2,1,0:T(8,128)(2,1)} %get-tuple-element.245), channel_id=1, source_target_pairs={{0,2},{1,3},{2,0},{3,1},{4,6},{5,7},{6,4},{7,5},{8,10},{9,11},{10,... | collective-permute-start | bytes 1806344 | tf_op jit(solution)/shard_map/ppermute | solution.py:896
  489.7 56.1 %collective-permute-start.114 = (bf16[4,4,6,8,1024]{4,3,2,0,1:T(8,128)(2,1)}, bf16[4,4,6,8,1024]{4,3,2,0,1:T(8,128)(2,1)}, u32[]{:S(2)}, u32[]{:S(2)}) collective-permute-start(bf16[4,4,6,8,1024]{4,3,2,0,1:T(8,128)(2,1)} %bitcast.193), channel_id=1, source_target_pairs={{0,4},{4,0},{8,12},{12,8},{16,20},{20,16},{24,28},{28,24},{1,5},{5... | collective-permute-start | bytes 4718600 | tf_op jit(solution)/shard_map/ppermute | solution.py:896
  537.2 17.9 %collective-permute-start.92 = (bf16[147,8,256]{2,1,0:T(8,128)(2,1)S(1)}, bf16[147,8,256]{2,1,0:T(8,128)(2,1)S(1)}, u32[]{:S(2)}, u32[]{:S(2)}) collective-permute-start(bf16[147,8,256]{2,1,0:T(8,128)(2,1)S(1)} %copy-done.96), channel_id=1, source_target_pairs={{0,3},{1,2},{2,1},{3,0},{4,7},{5,6},{6,5},{7,4},{8,11},{9,10},{10,... | collective-permute-start | bytes 1806344 | tf_op jit(solution)/shard_map/ppermute | solution.py:896
  549.7 17.8 %collective-permute-start.105 = (bf16[4,6,8,1024]{3,2,1,0:T(8,128)(2,1)S(1)}, bf16[4,6,8,1024]{3,2,1,0:T(8,128)(2,1)S(1)}, u32[]{:S(2)}, u32[]{:S(2)}) collective-permute-start(bf16[4,6,8,1024]{3,2,1,0:T(8,128)(2,1)S(1)} %get-tuple-element.338), channel_id=1, source_target_pairs={{0,16},{4,20},{8,24},{12,28},{16,0},{20,4},{24,8},{28,12},{1,17},{... | collective-permute-start | bytes 1179656 | tf_op jit(solution)/shard_map/ppermute | solution.py:896
  551.3 17.8 %collective-permute-start.104 = (bf16[4,6,8,1024]{3,2,1,0:T(8,128)(2,1)S(1)}, bf16[4,6,8,1024]{3,2,1,0:T(8,128)(2,1)S(1)}, u32[]{:S(2)}, u32[]{:S(2)}) collective-permute-start(bf16[4,6,8,1024]{3,2,1,0:T(8,128)(2,1)S(1)} %get-tuple-element.336), channel_id=1, source_target_pairs={{0,8},{4,12},{8,0},{12,4},{16,24},{20,28},{24,16},{28,20},{1,9},{5... | collective-permute-start | bytes 1179656 | tf_op jit(solution)/shard_map/ppermute | solution.py:896
  552.1 23.8 %collective-permute-start.117 = (bf16[4,6,8,1024]{3,2,1,0:T(8,128)(2,1)S(1)}, bf16[4,6,8,1024]{3,2,1,0:T(8,128)(2,1)S(1)}, u32[]{:S(2)}, u32[]{:S(2)}) collective-permute-start(bf16[4,6,8,1024]{3,2,1,0:T(8,128)(2,1)S(1)} %get-tuple-element.334), channel_id=1, source_target_pairs={{0,24},{4,28},{8,16},{12,20},{16,8},{20,12},{24,0},{28,4},{1,25},{... | collective-permute-start | bytes 1179656 | tf_op jit(solution)/shard_map/ppermute | solution.py:896
  555.1 28.4 %collective-permute-start.116 = (bf16[4,6,8,1024]{3,2,1,0:T(8,128)(2,1)S(1)}, bf16[4,6,8,1024]{3,2,1,0:T(8,128)(2,1)S(1)}, u32[]{:S(2)}, u32[]{:S(2)}) collective-permute-start(bf16[4,6,8,1024]{3,2,1,0:T(8,128)(2,1)S(1)} %get-tuple-element.335), channel_id=1, source_target_pairs={{0,16},{4,20},{8,24},{12,28},{16,0},{20,4},{24,8},{28,12},{1,17},{... | collective-permute-start | bytes 1179656 | tf_op jit(solution)/shard_map/ppermute | solution.py:896
  559.0 24.7 %collective-permute-start.115 = (bf16[4,6,8,1024]{3,2,1,0:T(8,128)(2,1)S(1)}, bf16[4,6,8,1024]{3,2,1,0:T(8,128)(2,1)S(1)}, u32[]{:S(2)}, u32[]{:S(2)}) collective-permute-start(bf16[4,6,8,1024]{3,2,1,0:T(8,128)(2,1)S(1)} %get-tuple-element.333), channel_id=1, source_target_pairs={{0,8},{4,12},{8,0},{12,4},{16,24},{20,28},{24,16},{28,20},{1,9},{5... | collective-permute-start | bytes 1179656 | tf_op jit(solution)/shard_map/ppermute | solution.py:896
  567.5 54.1 %collective-permute-start.93 = (bf16[147,8,128]{2,1,0:T(8,128)(2,1)}, bf16[147,8,128]{2,1,0:T(8,128)(2,1)S(1)}, u32[]{:S(2)}, u32[]{:S(2)}) collective-permute-start(bf16[147,8,128]{2,1,0:T(8,128)(2,1)} %get-tuple-element.255), channel_id=1, source_target_pairs={{0,1},{1,0},{2,3},{3,2},{4,5},{5,4},{6,7},{7,6},{8,9},{9,8},{10,11... | collective-permute-start | bytes 903176 | tf_op jit(solution)/shard_map/ppermute | solution.py:896
  569.0 52.6 %collective-permute-start.94 = (bf16[147,8,128]{2,1,0:T(8,128)(2,1)}, bf16[147,8,128]{2,1,0:T(8,128)(2,1)}, u32[]{:S(2)}, u32[]{:S(2)}) collective-permute-start(bf16[147,8,128]{2,1,0:T(8,128)(2,1)} %get-tuple-element.256), channel_id=1, source_target_pairs={{0,2},{1,3},{2,0},{3,1},{4,6},{5,7},{6,4},{7,5},{8,10},{9,11},{10,... | collective-permute-start | bytes 903176 | tf_op jit(solution)/shard_map/ppermute | solution.py:896
  (198 other events, 2026.0 us)

commit v4 on v3

--- a/solution.py
+++ b/solution.py
@@ -13,6 +13,7 @@
 ROOT = 0.7978845608028654
 CUBIC = 0.044715
 BIG = 49
+PARTS = ((0, 0), (1, 0), (2, 0), (2, 98), (3, 0), (3, 49))
 SMALL = 7
 
 
@@ -142,10 +143,10 @@
     return wide(tile, width)[None]
 
 
-def sweep(table_ref, size, step, body, carry=0):
+def sweep(table_ref, size, step, body, carry=0, begin=0):
     def run(i, kept):
         p = i * step
-        return body(p, table_ref[1 + p // BIG], kept)
+        return body(p, table_ref[1 + (begin + p) // BIG], kept)
 
     return lax.fori_loop(0, size // step, run, carry)
 
@@ -171,35 +172,29 @@
         out_ref[:, :, 128:384] = refs[0][...]
 
 
-def unpack_kernel(width, ids_ref, *refs):
-    pieces, tmp_ref = refs[:4], refs[-1]
-    size = pieces[0].shape[0]
-    for k in range(4):
-        begin = (ids_ref[1] ^ k) * size
-
-        def body(p, carry, k=k, begin=begin):
-            joined = rows(pieces[k][pl.ds(p, BIG), :, 0:128].astype(F32))
+def unpack_kernel(ids_ref, *refs):
+    slow_ref, fast_ref, tmp_ref = refs[-3:]
+    size = refs[0].shape[0]
+    for (k, first), ref in zip(PARTS, refs):
+        begin = (ids_ref[1] ^ k) * size + first
+
+        def body(p, carry, ref=ref, begin=begin):
+            joined = rows(ref[pl.ds(p, BIG), :, 0:128].astype(F32))
             for r in range(4):
                 tmp_ref[pl.ds(r, BIG * 8, stride=4), :] = joined[:, 32 * r : 32 * r + 32]
-            refs[-2][pl.ds(begin + p, BIG)] = tmp_ref[...].reshape(BIG, 32, 32).astype(BF16)
-            if width > 128:
-                refs[4][pl.ds(begin + p, BIG)] = pieces[k][pl.ds(p, BIG), :, 128:width]
+            fast_ref[pl.ds(begin + p, BIG)] = tmp_ref[...].reshape(BIG, 32, 32).astype(BF16)
+            slow_ref[pl.ds(begin + p, BIG)] = ref[pl.ds(p, BIG), :, 128:384]
             return carry
 
-        steps(size, BIG, body, 0)
-
-
-def place_kernel(ids_ref, *refs):
-    pieces, out_ref = refs[:4], refs[4]
-    size = pieces[0].shape[0]
-    for k in range(4):
-        begin = (ids_ref[1] ^ k) * size
-
-        def body(p, carry, k=k, begin=begin):
-            out_ref[pl.ds(begin + p, SMALL)] = pieces[k][pl.ds(p, SMALL)]
-            return carry
-
-        steps(size, SMALL, body, 0)
+        steps(ref.shape[0], BIG, body, 0)
+
+
+def unpack_fast_kernel(x_ref, out_ref, tmp_ref):
+    chunk = x_ref.shape[0]
+    joined = rows(x_ref[...].astype(F32))
+    for r in range(4):
+        tmp_ref[pl.ds(r, chunk * 8, stride=4), :] = joined[:, 32 * r : 32 * r + 32]
+    out_ref[...] = tmp_ref[...].reshape(chunk, 32, 32).astype(BF16)
 
 
 def lanes_at(block, width):
@@ -209,10 +204,10 @@
 LREDUCE = [(3, 256 * k) for k in range(3)]
 LATERAL = [(4, 128 * k) for k in range(5)]
 GAINS = [(3, 768), (3, 896), (4, 640), (4, 768)]
-SPATIAL = [(6 + k // 4, 256 * (k % 4)) for k in range(9)]
-
-
-def weight_slab_kernel(ids_ref, red_ref, lred_ref, lat_ref, exp_ref, short_ref, lshort_ref, sp_ref, ln_ref, sn_ref, on_ref, out_ref, more_ref,
+SPATIAL = [(11 + k // 4, 256 * (k % 4)) for k in range(9)]
+
+
+def weight_slab_kernel(ids_ref, red_ref, lred_ref, lat_ref, exp_ref, short_ref, lshort_ref, sp_ref, ln_ref, sn_ref, on_ref, out_ref,
                        red_s, lred_s, lat_s, exp_s, short_s, lshort_s, sp_s, sem):
     group = ids_ref[2]
     eight, more = pl.ds(pl.multiple_of(group * 8, 8), 8), pl.ds(pl.multiple_of(group * 32, 32), 32)
@@ -225,7 +220,7 @@
     for copy in copies:
         copy.start()
     out_ref[4, :, 896:1024] = jnp.zeros((8, 128), BF16)
-    more_ref[8, :, 256:1024] = jnp.zeros((8, 768), BF16)
+    out_ref[13, :, 256:1024] = jnp.zeros((8, 768), BF16)
     blank = jnp.zeros((2, 128), F32)
     half = jnp.zeros((2, 64), F32)
     inner = jnp.concatenate([jnp.concatenate([v, half], axis=1) for v in (ln_ref[...], sn_ref[0:2], sn_ref[2:4])] + [blank], axis=0)
@@ -241,12 +236,12 @@
         out_ref[j] = red_s[j].astype(BF16)
         at, lane = LREDUCE[j]
         out_ref[at, :, lane : lane + 256] = lred_s[j].astype(BF16)
-    more_ref[0], more_ref[5] = exp_s[...].astype(BF16), lshort_s[...].astype(BF16)
+    out_ref[5], out_ref[10] = exp_s[...].astype(BF16), lshort_s[...].astype(BF16)
     for a in range(4):
-        more_ref[1 + a] = short_s[8 * a : 8 * a + 8].astype(BF16)
+        out_ref[6 + a] = short_s[8 * a : 8 * a + 8].astype(BF16)
     for k in range(9):
         at, lane = SPATIAL[k]
-        more_ref[at, :, lane : lane + 256] = sp_s[k].astype(BF16)
+        out_ref[at, :, lane : lane + 256] = sp_s[k].astype(BF16)
     for k in range(5):
         at, lane = LATERAL[k]
         out_ref[at, :, lane : lane + 128] = lat_s[k].astype(BF16)
@@ -265,7 +260,7 @@
                 short_ref[z, d, a] = ref[chip, kz, 1 + a]
             for k in range(9):
                 at, lane = SPATIAL[k]
-                sp_ref[k, z, d] = ref[chip, kz, at, :, lane : lane + 256]
+                sp_ref[k, z, d] = ref[chip, kz, at - 5, :, lane : lane + 256]
         return carry
 
     lax.fori_loop(0, 16, place, 0)
@@ -330,28 +325,19 @@
     gin_ref[...] = jnp.concatenate([fin_ref[...]] * 4, axis=1)
 
 
-def first_grads_kernel(ids_ref, own_ref, other_ref, exp_ref, short_ref, lshort_ref):
+def grads_kernel(ids_ref, own_ref, other_ref, exp_ref, short_ref, lshort_ref, red_ref, lred_ref, sp_ref):
     def place(chip, carry):
         for core, ref in ((0, own_ref), (1, other_ref)):
             d = ids_ref[2] ^ (2 * chip + core)
             exp_ref[d], lshort_ref[d] = ref[chip, 0].astype(F32), ref[chip, 5].astype(F32)
             for a in range(4):
                 short_ref[d, a] = ref[chip, 1 + a].astype(F32)
-        return carry
-
-    lax.fori_loop(0, 4, place, 0)
-
-
-def second_grads_kernel(ids_ref, own_ref, other_ref, red_ref, lred_ref, sp_ref):
-    def place(chip, carry):
-        for core, ref in ((0, own_ref), (1, other_ref)):
-            d = ids_ref[2] ^ (2 * chip + core)
             for j in range(3):
-                red_ref[j, d] = ref[chip, j].astype(F32)
-                lred_ref[j, d] = ref[chip, 3, :, 256 * j : 256 * j + 256].astype(F32)
+                red_ref[j, d] = ref[chip, 6 + j].astype(F32)
+                lred_ref[j, d] = ref[chip, 9, :, 256 * j : 256 * j + 256].astype(F32)
             for k in range(8):
-                sp_ref[k, d] = ref[chip, 4 + k // 4, :, 256 * (k % 4) : 256 * (k % 4) + 256].astype(F32)
-            sp_ref[8, d] = ref[chip, 3, :, 768:1024].astype(F32)
+                sp_ref[k, d] = ref[chip, 10 + k // 4, :, 256 * (k % 4) : 256 * (k % 4) + 256].astype(F32)
+            sp_ref[8, d] = ref[chip, 9, :, 768:1024].astype(F32)
         return carry
 
     lax.fori_loop(0, 4, place, 0)
@@ -476,7 +462,7 @@
         osums_ref[:, width:] = more_ref[...]
 
 
-def slow_first_kernel(table_ref, n_ref, x0_ref, x1_ref, x2_ref, x3_ref, lp_ref, lsums_ref, gains_ref, w_ref, wl_ref, fb_ref, more_ref,
+def slow_first_kernel(table_ref, n_ref, xs_ref, lp_ref, lsums_ref, gains_ref, w_ref, wl_ref,
                       x_ref, lat_ref, sa_ref, sums_ref, first_ref, last_ref):
     size = lp_ref.shape[0]
     factor, shift, _, _ = scale_of(lsums_ref[:, 128:384], gains_ref[...], n_ref[0])
@@ -484,9 +470,9 @@
     def fill(p, frames, carry):
         mask = tile_mask(frames, 256)
         lat_ref[pl.ds(p, SMALL)] = (gelu(lp_ref[pl.ds(p, SMALL)] * factor[None] + shift[None]) * mask).astype(BF16)
-        for k, ref in enumerate((x0_ref, x1_ref, x2_ref, x3_ref)):
-            v = ref[pl.ds(p, SMALL)].astype(F32) * mask
-            x_ref[pl.ds(p, SMALL), :, lanes_at(table_ref[5] ^ k, 256)] = v.astype(BF16)
+        for z in range(4):
+            v = xs_ref[z, pl.ds(p, SMALL)].astype(F32) * mask
+            x_ref[pl.ds(p, SMALL), :, 256 * z : 256 * z + 256] = v.astype(BF16)
         return carry
 
     sweep(table_ref, size, SMALL, fill)
@@ -500,11 +486,9 @@
         return carry[0] + down(masked), carry[1] + down(masked * sa)
 
     a, b = sweep(table_ref, size, BIG, body, (jnp.zeros((8, 256), F32),) * 2)
-    sums_ref[0:1, 0:256], sums_ref[1:2, 0:256] = flat(a), flat(b)
-    sums_ref[:, 256:] = more_ref[...]
+    sums_ref[0:1], sums_ref[1:2] = flat(a), flat(b)
     halo = first_ref.shape[0]
-    first_ref[:, :, 0:256], last_ref[:, :, 0:256] = sa_ref[0:halo], sa_ref[size - halo : size]
-    first_ref[:, :, 256:], last_ref[:, :, 256:] = fb_ref[0:halo], fb_ref[size - halo : size]
+    first_ref[...], last_ref[...] = sa_ref[0:halo], sa_ref[size - halo : size]
 
 
 def bypass_kernel(table_ref, x_ref, lat_ref, w_ref, wl_ref, sp_ref, sums_ref):
@@ -546,54 +530,63 @@
         wide_out += ref.shape[1]
 
 
-def fast_out_kernel(offset, table_ref, n_ref, fc_ref, sums_ref, gains_ref, fx_ref, c0_ref, c1_ref, c2_ref, c3_ref, out_ref, up_ref,
-                    slopes_ref, vec_ref):
-    size, width = fc_ref.shape[0], fc_ref.shape[2]
+def fast_out_kernel(offset, table_ref, n_ref, fc_ref, sums_ref, gains_ref, fx_ref, *refs):
+    cots, (out_ref, up_ref, slopes_ref, vec_ref) = refs[: len(PARTS)], refs[len(PARTS) :]
+    width = fc_ref.shape[2]
     vecs = scale_of(folded(sums_ref[:, offset : offset + width]), gains_ref[...], n_ref[1])
     for i, v in enumerate(vecs):
         vec_ref[i : i + 1] = v
-    for k, cot_ref in enumerate((c0_ref, c1_ref, c2_ref, c3_ref)):
+    kept = (jnp.zeros((8, 128), F32),) * 2
+    for part, ((k, begin), cot_ref) in enumerate(zip(PARTS, cots)):
         lanes = lanes_at(table_ref[5] ^ k, 128)
         fz, sz, cz, rz = (vec_ref[i : i + 1, lanes][None] for i in range(4))
 
-        def body(p, frames, carry, k=k, lanes=lanes, fz=fz, sz=sz, cz=cz, rz=rz, cot_ref=cot_ref):
-            y = fc_ref[pl.ds(p, SMALL), :, lanes].astype(F32)
+        def body(p, frames, carry, k=k, lanes=lanes, fz=fz, sz=sz, cz=cz, rz=rz, cot_ref=cot_ref, begin=begin):
+            here = pl.ds(begin + p, SMALL)
+            y = fc_ref[here, :, lanes].astype(F32)
             mask = tile_mask(frames, 128)
-            total = y * fz + sz + fx_ref[pl.ds(p, SMALL), :, lanes].astype(F32)
+            total = y * fz + sz + fx_ref[here, :, lanes].astype(F32)
             value, slope = gelu_pair(total)
-            out_ref[k, pl.ds(p, SMALL)] = (value * mask).astype(BF16)
+            out_ref[k, here] = (value * mask).astype(BF16)
             up = slope * (cot_ref[pl.ds(p, SMALL), :, 0:128].astype(F32) * mask)
-            up_ref[pl.ds(p, SMALL), :, lanes] = up.astype(BF16)
+            up_ref[here, :, lanes] = up.astype(BF16)
             return carry[0] + down(up), carry[1] + down(up * ((y - cz) * rz))
 
-        a, b = sweep(table_ref, size, SMALL, body, (jnp.zeros((8, 128), F32),) * 2)
-        slopes_ref[0:1, lanes], slopes_ref[1:2, lanes] = flat(a), flat(b)
-
-
-def slow_out_kernel(table_ref, n_ref, sc_ref, sp_ref, sums_ref, gains_ref, c0_ref, c1_ref, c2_ref, c3_ref, fast_ref, more_ref,
-                    o0_ref, o1_ref, o2_ref, o3_ref, up_ref, slopes_ref, vec_ref):
-    size, width = sc_ref.shape[0], sc_ref.shape[2]
+        zero = (jnp.zeros((8, 128), F32),) * 2
+        kept = sweep(table_ref, cot_ref.shape[0], SMALL, body, kept if begin else zero, begin)
+        slopes_ref[0:1, lanes], slopes_ref[1:2, lanes] = flat(kept[0]), flat(kept[1])
+
+
+def slow_out_kernel(table_ref, n_ref, sc_ref, sp_ref, sums_ref, gains_ref, *refs):
+    count = len(PARTS)
+    cots, (fast_ref, more_ref), outs = refs[:count], refs[count : count + 2], refs[count + 2 : 2 * count + 2]
+    up_ref, slopes_ref, vec_ref = refs[2 * count + 2 :]
+    width = sc_ref.shape[2]
     cf, cs, cc, cr = scale_of(sums_ref[:, 0:width], gains_ref[0:2], n_ref[0])
     pf, ps, pc, pr = scale_of(sums_ref[:, width : 2 * width], gains_ref[2:4], n_ref[0])
     for i, v in enumerate((cf, cs + ps, cc, cr, pf, pc, pr)):
         vec_ref[i : i + 1] = v
-    for k, (cot_ref, out_ref) in enumerate(((c0_ref, o0_ref), (c1_ref, o1_ref), (c2_ref, o2_ref), (c3_ref, o3_ref))):
+    kept = ()
+    for (k, begin), cot_ref, out_ref in zip(PARTS, cots, outs):
         block = table_ref[5] ^ k
         lanes = lanes_at(block, 256)
         vecs = [vec_ref[i : i + 1, lanes][None] for i in range(7)]
 
-        def body(p, frames, carry, k=k, lanes=lanes, vecs=vecs, cot_ref=cot_ref, out_ref=out_ref):
+        def body(p, frames, carry, k=k, lanes=lanes, vecs=vecs, cot_ref=cot_ref, out_ref=out_ref, begin=begin):
             cf, shift, cc, cr, pf, pc, pr = vecs
-            yc, yp = (ref[pl.ds(p, SMALL), :, lanes].astype(F32) for ref in (sc_ref, sp_ref))
+            here = pl.ds(begin + p, SMALL)
+            yc, yp = (ref[here, :, lanes].astype(F32) for ref in (sc_ref, sp_ref))
             mask = tile_mask(frames, 256)
             value, slope = gelu_pair(yc * cf + yp * pf + shift)
             out_ref[pl.ds(p, SMALL), :, 128:384] = (value * mask).astype(BF16)
-            out_ref[pl.ds(p, SMALL), :, 0:128] = fast_ref[k, pl.ds(p, SMALL)]
+            out_ref[pl.ds(p, SMALL), :, 0:128] = fast_ref[k, here]
             up = slope * (cot_ref[pl.ds(p, SMALL), :, 128:384].astype(F32) * mask)
-            up_ref[pl.ds(p, SMALL), :, lanes] = up.astype(BF16)
+            up_ref[here, :, lanes] = up.astype(BF16)
             return (carry[0] + down(up), carry[1] + down(up * ((yc - cc) * cr)), carry[2] + down(up * ((yp - pc) * pr)))
 
-        a, b, c = sweep(table_ref, size, SMALL, body, (jnp.zeros((8, 256), F32),) * 3)
+        zero = (jnp.zeros((8, 256), F32),) * 3
+        kept = sweep(table_ref, cot_ref.shape[0], SMALL, body, kept if begin else zero, begin)
+        a, b, c = kept
         own, other = lanes, lanes_at(4 + block, 256)
         slopes_ref[0:1, own], slopes_ref[1:2, own] = flat(a), flat(b)
         slopes_ref[0:1, other], slopes_ref[1:2, other] = flat(a), flat(c)
@@ -637,7 +630,9 @@
     halo = first_ref.shape[0]
     first_ref[:, :, 0:inner], last_ref[:, :, 0:inner] = dz_ref[0:halo], dz_ref[size - halo : size]
     if fold:
-        first_ref[:, :, inner:], last_ref[:, :, inner:] = other_ref[0:halo], other_ref[size - halo : size]
+        wide_edge = inner + other_ref.shape[2]
+        first_ref[:, :, inner:wide_edge], last_ref[:, :, inner:wide_edge] = other_ref[0:halo], other_ref[size - halo : size]
+        first_ref[:, :, wide_edge:], last_ref[:, :, wide_edge:] = z_ref[0:halo], z_ref[size - halo : size]
     else:
         oslopes_ref[:, inner:] = other_ref[...]
 
@@ -698,7 +693,7 @@
 
 
 def slow_back_kernel(table_ref, n_ref, dz_ref, y_ref, sums_ref, gains_ref, slopes_ref, w_ref, wl_ref, dx_ref, dl_ref,
-                     lp_ref, lsums_ref, lgains_ref, taps_ref, o0_ref, o1_ref, o2_ref, o3_ref, dzl_ref, oslopes_ref):
+                     lp_ref, lsums_ref, lgains_ref, taps_ref, out_ref, dzl_ref, oslopes_ref):
     size = y_ref.shape[0]
     factor, shift, center, inv_std = scale_of(sums_ref[:, 0:256], gains_ref[...], n_ref[0])
     k0, k1 = slope_of(slopes_ref[:, 0:256], factor, center, inv_std, n_ref[0])
@@ -717,10 +712,10 @@
     def body(p, frames, carry):
         taps = rows_bf(taps_ref[pl.ds(p, BIG)])
         mask = tile_mask(frames, 256)
-        for k, out_ref in enumerate((o0_ref, o1_ref, o2_ref, o3_ref)):
-            lanes = lanes_at(table_ref[5] ^ k, 256)
+        for z in range(4):
+            lanes = slice(256 * z, 256 * z + 256)
             dx = cells(nn(taps, w_ref[:, lanes])) + dx_ref[pl.ds(p, BIG), :, lanes].astype(F32)
-            out_ref[pl.ds(p, BIG)] = (dx * mask).astype(BF16)
+            out_ref[z, pl.ds(p, BIG)] = (dx * mask).astype(BF16)
         dl = cells(nn(taps, wl_ref[...])) + dl_ref[pl.ds(p, BIG)]
         y = lp_ref[pl.ds(p, BIG)]
         dz = gelu_slope(y * lf[None] + ls[None]) * dl * mask
@@ -732,7 +727,7 @@
 
 
 def fast_back_kernel(at_s, table_ref, n_ref, sums_ref, fgains_ref, lgains_ref, fslopes_ref, lslopes_ref, dzf_ref, fa_ref, dzl_ref, lp_ref,
-                     up_ref, w_ref, taps_ref, o0_ref, o1_ref, o2_ref, o3_ref):
+                     up_ref, w_ref, taps_ref, out_ref):
     size = fa_ref.shape[0]
     ff, fs, fc, fr = scale_of(folded(sums_ref[:, 0:128]), fgains_ref[...], n_ref[1])
     f0, f1 = slope_of(folded(fslopes_ref[:, at_s : at_s + 128]), ff, fc, fr, n_ref[1])
@@ -754,12 +749,11 @@
     sweep(table_ref, size, SMALL, fill)
 
     def body(p, frames, carry):
-        taps = rows_bf(taps_ref[pl.ds(p, BIG)])
+        dx = cells(nn(rows_bf(taps_ref[pl.ds(p, BIG)]), w_ref[...]))
         mask = tile_mask(frames, 128)
-        for k, out_ref in enumerate((o0_ref, o1_ref, o2_ref, o3_ref)):
-            lanes = lanes_at(table_ref[5] ^ k, 128)
-            dx = cells(nn(taps, w_ref[:, lanes])) + up_ref[pl.ds(p, BIG), :, lanes].astype(F32)
-            out_ref[pl.ds(p, BIG)] = (dx * mask).astype(BF16)
+        for z in range(4):
+            lanes = slice(128 * z, 128 * z + 128)
+            out_ref[z, pl.ds(p, BIG)] = ((dx[:, :, lanes] + up_ref[pl.ds(p, BIG), :, lanes].astype(F32)) * mask).astype(BF16)
         return carry
 
     sweep(table_ref, size, BIG, body)
@@ -821,6 +815,10 @@
             added(acc_ref, i, tn(taps, dy) if fold else tn(dy, taps), p == 0)
 
 
+def by_share(v):
+    return v.reshape(4, 4, 2, 8, v.shape[1]).transpose(2, 1, 0, 3, 4).astype(BF16)
+
+
 def first_slab_kernel(hb_ref, dsc_ref, x_ref, lat_ref, dsp_ref, out_ref, acc_ref):
     for p in chunks(hb_ref.shape[0]):
         at = slice(p, p + BIG)
@@ -829,19 +827,19 @@
         added(acc_ref, 5, tn(rows_bf(lat_ref[at]), dsp), p == 0)
         for z in range(4):
             added(acc_ref, z, tn(rows_bf(x_ref[at, :, 256 * z : 256 * z + 256]), dsp), p == 0)
-    out_ref[:, :, 0] = acc_ref[4].reshape(4, 8, 8, 1024).astype(BF16)
-    out_ref[:, :, 5] = acc_ref[5].reshape(4, 8, 8, 1024).astype(BF16)
+    out_ref[:, :, :, 0], out_ref[:, :, :, 5] = by_share(acc_ref[4]), by_share(acc_ref[5])
     for z in range(4):
-        out_ref[z, :, 1:5] = acc_ref[z].reshape(8, 4, 8, 1024).astype(BF16)
+        part = acc_ref[z].reshape(4, 2, 4, 8, 1024).astype(BF16)
+        for core in range(2):
+            out_ref[core, :, z, 1:5] = part[:, core]
 
 
 def second_slab_kernel(halo, row_len, per_clip, table_ref, act_ref, dy_ref, taps_ref, x_ref, lat_ref, out_ref, pad_ref, acc_ref, red_ref,
                        lred_ref):
     conv_weight(halo, row_len, per_clip, False, table_ref, act_ref, dy_ref, pad_ref, acc_ref)
     for k in range(9):
-        v = acc_ref[k // 3, :, 256 * (k % 3) : 256 * (k % 3) + 256].reshape(4, 8, 8, 256).astype(BF16)
         at, lane = (3, 768) if k == 8 else (4 + k // 4, 256 * (k % 4))
-        out_ref[:, :, at, :, lane : lane + 256] = v
+        out_ref[:, :, :, at, :, lane : lane + 256] = by_share(acc_ref[k // 3, :, 256 * (k % 3) : 256 * (k % 3) + 256])
     for p in chunks(dy_ref.shape[0]):
         at = slice(p, p + BIG)
         x, lat = rows_bf(x_ref[at]), rows_bf(lat_ref[at])
@@ -850,8 +848,8 @@
             added(red_ref, j, tn(taps, x), p == 0)
             added(lred_ref, j, tn(taps, lat), p == 0)
     for j in range(3):
-        out_ref[:, :, j] = red_ref[j].reshape(4, 8, 8, 1024).astype(BF16)
-        out_ref[:, :, 3, :, 256 * j : 256 * j + 256] = lred_ref[j].reshape(4, 8, 8, 256).astype(BF16)
+        out_ref[:, :, :, j] = by_share(red_ref[j])
+        out_ref[:, :, :, 3, :, 256 * j : 256 * j + 256] = by_share(lred_ref[j])
 
 
 def fast_grads_kernel(halo, row_len, per_clip, table_ref, act_ref, dy_ref, taps_ref, fx_ref, h_ref, dfc_ref, lat_ref, out_ref,
@@ -926,13 +924,24 @@
     return add(tree, near, far, both)
 
 
-def everywhere(tree, sizes, bulk=None):
-    for axis, size in sizes.items():
-        if axis == "chan" and bulk is not None:
-            tree = after(tree, bulk)
-        for bits in stages(size, axis == "dp"):
-            tree = butterfly(tree, axis, size, bits)
+def over_dp(tree, sizes, early=None):
+    for i, bits in enumerate(stages(sizes["dp"], True)):
+        if i == 1 and early is not None:
+            tree = after(tree, early)
+        tree = butterfly(tree, "dp", sizes["dp"], bits)
     return tree
+
+
+def over_chan(tree, sizes, bulk=None):
+    if bulk is not None:
+        tree = after(tree, bulk)
+    for bits in stages(sizes["chan"], False):
+        tree = butterfly(tree, "chan", sizes["chan"], bits)
+    return tree
+
+
+def everywhere(tree, sizes, bulk=None, early=None):
+    return over_chan(over_dp(tree, sizes, early), sizes, bulk)
 
 
 def halos(first, last, count):
@@ -943,24 +952,26 @@
 
 def gather_group(v, sizes):
     dp = sizes["dp"]
-    own = jnp.stack([v] + [swap(v, "dp", dp, 2 * k) for k in (1, 2, 3)])
-    return own, swap(own, "dp", dp, 1)
+    own = [v] + [swap(v, "dp", dp, 2 * k) for k in (1, 2, 3)]
+    return jnp.stack(own), jnp.stack([swap(u, "dp", dp, 1) for u in own])
 
 
 def pick(v, index, axis):
     return lax.dynamic_index_in_dim(v, index, axis, keepdims=False)
 
 
-def scatter_sum(tree, sizes, group, chan):
+def scatter_group(tree, sizes, group):
     dp = sizes["dp"]
     core, chip = group % 2, group // 2
-    tree = jax.tree.map(lambda v: v.reshape(v.shape[0], 4, 2, *v.shape[2:]), tree)
-    sent = jax.tree.map(lambda v: pick(v, 1 - core, 2), tree)
-    kept = jax.tree.map(lambda v: pick(v, core, 2), tree)
+    sent = jax.tree.map(lambda v: pick(v, 1 - core, 0), tree)
+    kept = jax.tree.map(lambda v: pick(v, core, 0), tree)
     tree = add(kept, swap(sent, "dp", dp, 1))
-    got = [swap(jax.tree.map(lambda v: pick(v, chip ^ k, 1), tree), "dp", dp, 2 * k) for k in (1, 2, 3)]
-    tree = add(jax.tree.map(lambda v: pick(v, chip, 1), tree), *got)
-    size = sizes["chan"]
+    got = [swap(jax.tree.map(lambda v: pick(v, chip ^ k, 0), tree), "dp", dp, 2 * k) for k in (1, 2, 3)]
+    return add(jax.tree.map(lambda v: pick(v, chip, 0), tree), *got)
+
+
+def scatter_chan(tree, sizes, chan):
+    size, dp = sizes["chan"], sizes["dp"]
     got = [swap(jax.tree.map(lambda v: pick(v, chan ^ k, 0), tree), "chan", size, k) for k in (1, 2, 3)]
     tree = add(jax.tree.map(lambda v: pick(v, chan, 0), tree), *got)
     bits = [1 << i for i in range(3, dp.bit_length() - 1)]
@@ -1032,21 +1043,16 @@
             name="fast_pack",
         )(ids, clip_counts, frame_counts, v, *more).reshape(ways, mine, slow_t, width)
 
-    def unpacked(pieces):
-        width = pieces[0].shape[2]
-        outs = [shape((places, fast_t, fast_part), BF16)]
-        if width > 128:
-            outs = [shape((places, slow_t, slow_part), BF16)] + outs
-        out = call(
-            functools.partial(unpack_kernel, width),
-            outs,
-            [ids, *pieces],
+    def unpacked(parts):
+        slow, fast = call(
+            unpack_kernel,
+            [shape((places, slow_t, slow_part), BF16), shape((places, fast_t, fast_part), BF16)],
+            [ids, *parts],
             [pltpu.VMEM((BIG * fast_t, fast_part), F32)],
             smem=1,
-            name="fast_unpack",
+            name="outputs",
         )
-        fast = out[-1].reshape(clips, height, across, fast_t, fast_part).transpose(0, 3, 1, 2, 4)
-        return (joined(out[0]), fast) if len(out) == 2 else fast
+        return joined(slow), fast.reshape(clips, height, across, fast_t, fast_part).transpose(0, 3, 1, 2, 4)
 
     def split(v):
         return v.transpose(0, 2, 3, 1, 4).reshape(ways, mine, slow_t, slow_part)
@@ -1060,11 +1066,18 @@
     def blocks_of(v):
         return [pick(v, chan ^ k, 0) for k in range(ways)]
 
-    def send(v, k):
-        return swap(v, "chan", ways, k)
-
-    x_blocks = blocks_of(split(slow_input))
-    fx_pieces = at_once(blocks_of(packed(fast_input)))
+    def all_to_all(v):
+        return lax.all_to_all(v, "chan", 0, 0, tiled=True)
+
+    def parted(blocks):
+        bounds = PARTS + ((len(blocks), 0),)
+        ends = [b[1] if a[0] == b[0] else mine for a, b in zip(bounds, bounds[1:])]
+        return [blocks[k][begin:end] for (k, begin), end in zip(PARTS, ends)]
+
+    def send_parts(parts, which, gate):
+        for i in which:
+            parts[i] = swap(after(parts[i], gate), "chan", ways, PARTS[i][0])
+
 
     all_clips = frame_counts.shape[0]
     live = (jnp.arange(all_clips, dtype=jnp.int32) % clips) < jnp.repeat(clip_counts, clips)
@@ -1083,23 +1096,20 @@
     scratch = [(3, 8, wide_in), (3, 8, mid), (5, 8, 128), (8, wide_in), (32, wide_in), (8, wide_in), (9, 8, mid)]
     small = [lateral_norm, slow_inner_norm.reshape(4, -1), slow_outer_norm.reshape(4, -1)]
     any_spec, vmem_spec = pl.BlockSpec(memory_space=pl.ANY), pl.BlockSpec(memory_space=pltpu.VMEM)
-    slab_a, slab_b = pl.pallas_call(
+    slab = pl.pallas_call(
         weight_slab_kernel,
-        out_shape=(shape((5, 8, wide_in), BF16), shape((9, 8, wide_in), BF16)),
+        out_shape=shape((14, 8, wide_in), BF16),
         in_specs=[pl.BlockSpec(memory_space=pltpu.SMEM)] + [any_spec] * 7 + [vmem_spec] * 3,
-        out_specs=(vmem_spec, vmem_spec),
+        out_specs=vmem_spec,
         scratch_shapes=[pltpu.VMEM(dims, F32) for dims in scratch] + [pltpu.SemaphoreType.DMA((7,))],
-        compiler_params=pltpu.CompilerParams(vmem_limit_bytes=8 * 1024 * 1024),
+        compiler_params=pltpu.CompilerParams(vmem_limit_bytes=58 * 1024 * 1024),
         name="weight_slab",
     )(ids, *params, *small)
-    slab_a = at_once([slab_a] * ways)
-    x_blocks = after(x_blocks, slab_a)
-    x_second = send(x_blocks[2], 2)
-    near = after((x_blocks[1], x_blocks[3]), (x_second, fx_pieces))
-    x_pieces = [x_blocks[0], send(near[0], 1), x_second, send(near[1], 3)]
-    slab_a = after(jnp.stack(slab_a), fx_pieces)
-    by_chip = jnp.stack([slab_a] + [swap(slab_a, "dp", sizes["dp"], 2 * k) for k in (1, 2, 3)])
-    own_slabs, other_slabs = by_chip, swap(by_chip, "dp", sizes["dp"], 1)
+    slabs = at_once([slab] * ways)
+    fx_pieces = at_once(blocks_of(packed(after(fast_input, slab))))
+    xs = all_to_all(after(split(slow_input), (slabs, fx_pieces)))
+    early, late = jnp.stack([v[0:5] for v in slabs]), jnp.stack([v[5:14] for v in slabs])
+    own_slabs, other_slabs = gather_group(early, sizes)
     fr_t = fast_reduce.transpose(0, 2, 1)
     red_w, lred_w, w_first, w_fsp, w_fex, fin_g, fout_g, mid_g, out_g = call(
         weights_kernel,
@@ -1126,7 +1136,7 @@
     out_g = out_g.transpose(1, 0, 2).reshape(4, wide_in)
 
     edge = [shape((halo, 8, 128))] * 2
-    edges = [shape((halo, 8, 384))] * 2
+    edges = [shape((halo, 8, 512))] * 2
     narrow, middle = shape((mine, 8, 128)), shape((mine, 8, mid))
     fx, fa, lp, sums1, first, last = call(
         fast_first_kernel,
@@ -1136,11 +1146,9 @@
         name="fast_first",
     )
     fa_lo, fa_hi = halos(first, last, ways)
-    sums1 = everywhere(sums1, sizes, (x_pieces, fa_lo, fa_hi))
-    slab_b = jnp.stack(at_once([after(slab_b, sums1)] * ways))
-    cots = blocks_of(packed(fast_cotangent, split(slow_cotangent)))
-    cots[1] = send(after(cots[1], sums1), 1)
-    own_slabs, other_slabs = gather_group(slab_b, sizes)
+    cots = parted(blocks_of(packed(fast_cotangent, split(slow_cotangent))))
+    sums1 = over_dp(sums1, sizes)
+    own_late, other_late = gather_group(after(late, sums1), sizes)
     exp_w, short_w, lshort_w, spat_w = call(
         more_weights_kernel,
         [
@@ -1149,49 +1157,45 @@
             shape((ways, 8, 8, wide_in), BF16),
             shape((9, ways, 8, 8, mid), BF16),
         ],
-        [ids, own_slabs, other_slabs],
+        [ids, own_late, other_late],
         smem=1,
         name="more_weights",
     )
     exp_w, short_w, lshort_w = (v.reshape(-1, wide_in) for v in (exp_w, short_w, lshort_w))
     spat_w = spat_w.reshape(9, mid, mid)
+    sums1 = over_chan(sums1, sizes, (xs, fa_lo, fa_hi, cots))
+    send_parts(cots, (2,), sums1)
     fast_pad = [pltpu.VMEM((3, ext, 8, 128), F32)]
     slow_pad = [pltpu.VMEM((3, ext, 8, mid), F32)]
+    x, lat, sa, sums2, first, last = call(
+        slow_first_kernel,
+        [shape((mine, 8, wide_in), BF16), shape((mine, 8, mid), BF16), middle, shape((2, mid)), *[shape((halo, 8, mid))] * 2],
+        [table, inv_n, xs, lp, sums1, lat_g, red_w, lred_w],
+        smem=2,
+        name="slow_first",
+    )
+    sa_lo, sa_hi = halos(first, last, ways)
+    fa_late = after(fa, sums2)
     h1, fb, fb_sums = call(
         functools.partial(conv_kernel, halo, across, per_clip, True, (0, 0)),
         [shape((ext, 8, 128), BF16), narrow, shape((2, 128))],
-        [table, inv_n, sums1, fin_g[0], fa_lo, fa, fa_hi, w_fsp],
+        [table, inv_n, sums1, fin_g[0], fa_lo, fa_late, fa_hi, w_fsp],
         fast_pad,
         smem=2,
         name="fast_second",
     )
-    x, lat, sa, sums2, first, last = call(
-        slow_first_kernel,
-        [shape((mine, 8, wide_in), BF16), shape((mine, 8, mid), BF16), middle, shape((2, mid + 128)), *edges],
-        [table, inv_n, *x_pieces, lp, sums1, lat_g, red_w, lred_w, fb, fb_sums],
-        smem=2,
-        name="slow_first",
-    )
-    sa_lo, sa_hi = halos(first, last, ways)
-    sums2 = everywhere(sums2, sizes, (slab_b, cots[1], sa_lo, sa_hi))
-    cots[2] = send(after(cots[2], sums2), 2)
-    h2, fc, fc_sums = call(
-        functools.partial(expand_kernel, True, mid),
-        [shape((mine, 8, 128), BF16), shape((mine, 8, wide_f), BF16), shape((2, wide_f))],
-        [table, inv_n, fb, sums2, fin_g[1], w_fex],
-        smem=2,
-        name="fast_third",
-    )
+    sums2 = everywhere(sums2, sizes, (cots[2], sa_lo, sa_hi))
+    send_parts(cots, (3, 4, 1), sums2)
     ha, sb, sums3 = call(
         functools.partial(conv_kernel, halo, across, per_clip, False, (0, 0)),
-        [shape((ext, 8, mid), BF16), middle, shape((2, mid + wide_f))],
-        [table, inv_n, sums2, in_g[0], sa_lo, sa, sa_hi, spat_w, fc_sums],
+        [shape((ext, 8, mid), BF16), middle, shape((2, mid + 128))],
+        [table, inv_n, sums2, in_g[0], sa_lo, sa, sa_hi, spat_w, fb_sums],
         slow_pad,
         smem=2,
         name="slow_second",
     )
-    sums3 = everywhere(sums3, sizes, cots[2])
-    cots[3] = send(after(cots[3], sums3), 3)
+    sums3 = everywhere(sums3, sizes, (cots[3], cots[4], cots[1]))
+    send_parts(cots, (5,), sums3)
     sp, sp_sums = call(
         bypass_kernel,
         [shape((mine, 8, wide_in), BF16), shape((2, wide_in))],
@@ -1199,38 +1203,45 @@
         smem=1,
         name="bypass",
     )
+    h2, fc, fc_sums = call(
+        functools.partial(expand_kernel, True, mid),
+        [shape((mine, 8, 128), BF16), shape((mine, 8, wide_f), BF16), shape((2, wide_f))],
+        [table, inv_n, fb, sums3, fin_g[1], w_fex],
+        smem=2,
+        name="fast_third",
+    )
     hb, sc, sums4 = call(
         functools.partial(expand_kernel, False, 0),
-        [shape((mine, 8, mid), BF16), shape((mine, 8, wide_in), BF16), shape((2, 2 * wide_in))],
-        [table, inv_n, sb, sums3, in_g[1], exp_w, sp_sums],
+        [shape((mine, 8, mid), BF16), shape((mine, 8, wide_in), BF16), shape((2, 2 * wide_in + wide_f))],
+        [table, inv_n, sb, sums3, in_g[1], exp_w, sp_sums, fc_sums],
         smem=2,
         name="slow_third",
     )
-    sums4 = everywhere(sums4, sizes, cots[3])
+    sums4 = everywhere(sums4, sizes, cots[5])
     fast_out, dfs, fc_slopes = call(
-        functools.partial(fast_out_kernel, mid),
+        functools.partial(fast_out_kernel, 2 * wide_in),
         [shape((ways, mine, 8, 128), BF16), shape((mine, 8, wide_f), BF16), shape((2, wide_f))],
-        [table, inv_n, fc, sums3, fout_g, fx, *cots],
+        [table, inv_n, fc, sums4, fout_g, fx, *cots],
         [pltpu.VMEM((8, wide_f), F32)],
         smem=2,
         name="fast_out",
     )
     *outs, dss, sums5 = call(
         slow_out_kernel,
-        [*[shape((mine, 8, 384), BF16)] * 4, shape((mine, 8, wide_in), BF16), shape((2, 2 * wide_in + wide_f))],
+        [*[shape(c.shape, BF16) for c in cots], shape((mine, 8, wide_in), BF16), shape((2, 2 * wide_in + wide_f))],
         [table, inv_n, sc, sp, sums4, out_g, *cots, fast_out, fc_slopes],
         [pltpu.VMEM((8, wide_in), F32)],
         smem=2,
         name="slow_out",
     )
 
-    outs[1] = send(outs[1], 1)
-    sums5 = everywhere(sums5, sizes, outs[1])
-    outs[2] = send(after(outs[2], sums5), 2)
+    send_parts(outs, (2,), dss)
+    sums5 = everywhere(sums5, sizes, outs[2])
+    send_parts(outs, (3, 4, 1), sums5)
     dfc, dzfb, fb_slopes, first, last = call(
-        functools.partial(expand_back_kernel, True, (mid, 2 * wide_in, mid)),
+        functools.partial(expand_back_kernel, True, (2 * wide_in, 2 * wide_in, mid)),
         [shape((mine, 8, wide_f), BF16), narrow, shape((2, 128)), *edges],
-        [table, inv_n, dfs, fc, sums3, fout_g, sums5, fb, sums2, fin_g[1], w_fex, sb],
+        [table, inv_n, dfs, fc, sums4, fout_g, sums5, fb, sums3, fin_g[1], w_fex, sb],
         smem=2,
         name="fast_third_back",
     )
@@ -1244,8 +1255,6 @@
     )
     low_sb, high_sb = halos(first, last, ways)
     dss_late, = after((dss,), sums6)
-    sums6 = everywhere(sums6, sizes, (outs[2], low6, high6, low_sb, high_sb))
-    outs[3] = send(after(outs[3], sums6), 3)
     dsp, dx, dl = call(
         bypass_back_kernel,
         [shape((mine, 8, wide_in), BF16), shape((mine, 8, wide_in), BF16), middle],
@@ -1254,17 +1263,12 @@
         name="bypass_back",
     )
 
-    (slab1,) = call(
-        first_slab_kernel,
-        [shape((ways, 8, 6, 8, wide_in), BF16)],
-        [hb, dsc, x, lat, dsp],
-        [pltpu.VMEM((6, mid, wide_in), F32)],
-        name="first_slab",
-    )
+    sums6 = everywhere(sums6, sizes, (low6, high6, low_sb, high_sb), (outs[3], outs[4], outs[1]))
+    send_parts(outs, (5,), sums6)
     dfb, dzfa, fa_slopes = call(
-        functools.partial(conv_back_kernel, halo, across, per_clip, True, (mid, mid, 0, mid, 0)),
+        functools.partial(conv_back_kernel, halo, across, per_clip, True, (mid, mid, 0, 384, 0)),
         [shape((mine, 8, 128), BF16), narrow, shape((2, 128))],
-        [table, inv_n, sums2, fin_g[1], sums6, sa_lo, fb, sa_hi, low6, dzfb, high6, w_fsp, fa, sums1, fin_g[0]],
+        [table, inv_n, sums3, fin_g[1], sums6, low6, fb, high6, low6, dzfb, high6, w_fsp, fa, sums1, fin_g[0]],
         fast_pad,
         smem=2,
         name="fast_second_back",
@@ -1277,34 +1281,38 @@
         smem=2,
         name="slow_second_back",
     )
-    slab1, sums7 = lax.optimization_barrier((slab1, sums7))
-    sums7 = everywhere(sums7, sizes, outs[3])
-    slab1 = scatter_sum(slab1, sizes, group, chan)
-    dsa, *dslow, dzlp, sums8 = call(
+    dsc_late, dsp = after((dsc, dsp), sums7)
+    (slab1,) = call(
+        first_slab_kernel,
+        [shape((2, 4, ways, 6, 8, wide_in), BF16)],
+        [hb, dsc_late, x, lat, dsp],
+        [pltpu.VMEM((6, mid, wide_in), F32)],
+        name="first_slab",
+    )
+    sums7 = everywhere(sums7, sizes, (outs[5], dx, dl))
+    dsa, dslow, dzlp, sums8 = call(
         slow_back_kernel,
-        [shape((mine, 8, 3 * mid), BF16), *[shape((mine, 8, mid), BF16)] * 4, middle, shape((2, mid))],
+        [shape((mine, 8, 3 * mid), BF16), shape((ways, mine, 8, mid), BF16), middle, shape((2, mid))],
         [table, inv_n, dzsa, sa, sums2, in_g[0], sums7, red_w, lred_w, dx, dl, lp, sums1, lat_g],
         smem=2,
         name="slow_first_back",
     )
-    dslow[1] = send(dslow[1], 1)
+    sums8 = over_dp(sums8, sizes)
+    dslow = all_to_all(dslow)
     dsa, dsb_late = after((dsa, dsb), sums8)
-    sums8 = everywhere(sums8, sizes, dslow[1])
-    dslow[2] = send(after(dslow[2], sums8), 2)
-    dslow[3] = send(after(dslow[3], dslow[2]), 3)
-    slow_output, fast_output = unpacked(after(outs, sums8))
     (slab2,) = call(
         functools.partial(second_slab_kernel, halo, across, per_clip),
-        [shape((ways, 8, 6, 8, wide_in), BF16)],
+        [shape((2, 4, ways, 6, 8, wide_in), BF16)],
         [table, ha, dsb_late, dsa, x, lat],
         [*slow_pad, pltpu.VMEM((3, mid, 3 * mid), F32), pltpu.VMEM((3, mid, wide_in), F32), pltpu.VMEM((3, mid, mid), F32)],
         smem=1,
         name="second_slab",
     )
-    slab2 = scatter_sum(slab2, sizes, group, chan)
-    dfirst, *dfast = call(
+    slabs = jnp.concatenate(scatter_group((slab1, slab2), sizes, group), axis=1)
+    sums8 = over_chan(sums8, sizes, (dslow, slabs))
+    dfirst, dfast = call(
         functools.partial(fast_back_kernel, mid),
-        [shape((mine, 8, 896), BF16), *[shape((mine, 8, 128), BF16)] * 4],
+        [shape((mine, 8, 896), BF16), shape((ways, mine, 8, 128), BF16)],
         [table, inv_n, sums1, fin_g[0], lat_g, sums7, sums8, dzfa, fa, dzlp, lp, dfs, w_first],
         smem=2,
         name="fast_first_back",
@@ -1318,30 +1326,35 @@
         smem=1,
         name="fast_grads",
     )
+    slow_output, fast_output = unpacked(after(outs, dfirst))
+    slabs = scatter_chan(slabs, sizes, chan)
     small = [jnp.concatenate([pick(g_lat, chan ^ k, 0), g_fast]) for k in range(ways)]
-    small = add(*at_once(after(small, dslow[2])))
+    small = add(*at_once(small))
+    dfast = all_to_all(dfast)
     for bits in stages(sizes["dp"], True):
         small = butterfly(small, "dp", sizes["dp"], bits)
     g_lat, g_fast = small[0:40].astype(F32), small[40:68].astype(F32)
-    own1, other1 = gather_group(slab1, sizes)
-    g_exp, g_short, g_lshort = call(
-        first_grads_kernel,
-        [shape((8, 8, wide_in)), shape((8, 4, 8, wide_in)), shape((8, 8, wide_in))],
-        [ids, own1, other1],
+    own_slabs, other_slabs = gather_group(slabs, sizes)
+    g_exp, g_short, g_lshort, g_red, g_lred, g_spat = call(
+        grads_kernel,
+        [shape((8, 8, wide_in)), shape((8, 4, 8, wide_in)), shape((8, 8, wide_in)), shape((3, 8, 8, wide_in)), shape((3, 8, 8, mid)),
+         shape((9, 8, 8, mid))],
+        [ids, own_slabs, other_slabs],
         smem=1,
-        name="first_grads",
-    )
-    own2, other2 = gather_group(slab2, sizes)
-    g_red, g_lred, g_spat = call(
-        second_grads_kernel,
-        [shape((3, 8, 8, wide_in)), shape((3, 8, 8, mid)), shape((9, 8, 8, mid))],
-        [ids, own2, other2],
-        smem=1,
-        name="second_grads",
-    )
-    (slow_input_grad,) = call(place_kernel, [shape((places, slow_t, slow_part), BF16)], [ids, *dslow], smem=1, name="slow_place")
-    slow_input_grad = joined(slow_input_grad)
-    fast_input_grad = unpacked(at_once(after(dfast, dslow[3])))
+        name="grads",
+    )
+    slow_input_grad = joined(dslow)
+    fast_input_grad = pl.pallas_call(
+        unpack_fast_kernel,
+        grid=(places // chunk,),
+        out_shape=shape((places, fast_t, fast_part), BF16),
+        in_specs=[pl.BlockSpec((chunk, slow_t, 128), lambda i: (i, 0, 0))],
+        out_specs=pl.BlockSpec((chunk, fast_t, fast_part), lambda i: (i, 0, 0)),
+        scratch_shapes=[pltpu.VMEM((chunk * fast_t, fast_part), F32)],
+        compiler_params=pltpu.CompilerParams(vmem_limit_bytes=16 * 1024 * 1024),
+        name="fast_unpack",
+    )(dfast.reshape(places, slow_t, 128))
+    fast_input_grad = fast_input_grad.reshape(clips, height, across, fast_t, fast_part).transpose(0, 3, 1, 2, 4)
     g_fred = g_fast[0:12].reshape(3, 32, 128).transpose(0, 2, 1)
     g_fex = g_fast[12:16].reshape(32, 128)
     g_fsp = g_fast[16:28].reshape(3, 32, 128)[:, :, 0:96].reshape(3, 32, 3, 32).transpose(0, 2, 1, 3)

time: 640 us -> 584 us (0.912)
  waiting for transfers between devices: 256 us -> 220 us
  starting transfers between devices: 182 us -> 161 us
  Pallas kernels: 118 us -> 106 us
  local copies, waits for them, and re-layouts: 57.7 us -> 66.5 us
    ppermute x117 -> x111, starting transfers between devices: 161 us -> 129 us  [swap(): return jax.tree.map(lambda v: lax.ppermute(v, axis, pairs), tree)]
    ppermute x117 -> x111, waiting for transfers between devices: 230 us -> 202 us  [swap(): return jax.tree.map(lambda v: lax.ppermute(v, axis, pairs), tree)]
    pallas_call x26 -> x23, Pallas kernels: 111 us -> 92.3 us  [call(): pl.pallas_call(kernel, out_shape=tuple(outs), in_specs=specs, out_specs=t...]
    all_to_all x0 -> x3, starting transfers between devices: none -> 16 us  [all_to_all(): return lax.all_to_all(v, 'chan', 0, 0, tiled=True)]
    unnamed x211 -> x212, local copies, waits for them, and re-layouts: 41.4 us -> 49.7 us
    ppermute x4, waiting for transfers between devices: 23.3 us -> 15.4 us  [halos(): high = lax.ppermute(first, 'chan', [(i + 1, i) for i in range(count - 1)])]
    dynamic_slice x3 -> x0, local copies, waits for them, and re-layouts: 6.72 us -> none  [pick(): return lax.dynamic_index_in_dim(v, index, axis, keepdims=False)]
  transfers between devices with their start and end apart: 125 -> 122, of which waited for: 73 -> 54; matrix products, arithmetic and copies ran while one was open for 5% -> 6% of each run, Pallas kernels for 16% -> 13%
where the time goes in v4:
time: 584 us; the launch traced here: 577 us
  waiting for transfers between devices  220 us (38%)
  starting transfers between devices  161 us (28%)
  Pallas kernels  106 us (18%)
  local copies, waits for them, and re-layouts  66.5 us (11%)
  other arithmetic  19.8 us (3%)
    ppermute x111, waiting for transfers between devices, swap(): return jax.tree.map(lambda v: lax.ppermute(v, axis, pairs), tree)  202 us
    ppermute x111, starting transfers between devices, swap(): return jax.tree.map(lambda v: lax.ppermute(v, axis, pairs), tree)  129 us
    pallas_call x23, Pallas kernels, call(): pl.pallas_call(kernel, out_shape=tuple(outs), in_specs=specs, out_specs=t...  92.3 us
    unnamed x212, local copies, waits for them, and re-layouts  49.7 us
    all_to_all x3, starting transfers between devices, all_to_all(): return lax.all_to_all(v, 'chan', 0, 0, tiled=True)  16 us
    ppermute x4, waiting for transfers between devices, halos(): high = lax.ppermute(first, 'chan', [(i + 1, i) for i in range(count - 1)])  15.4 us
  transfers between devices with their start and end apart: 122, of which 54 were waited for; matrix products, arithmetic and copies ran while one was open for 6% of the time, Pallas kernels for 13%

profile of v4, /device:TPU:0, one launch (start us, length us, event | category | flops | bytes accessed | tf_op | source)
XLA Modules:
  0.0 576.8 jit_solution(8948681896471386516)
XLA Ops:
  21.7 38.2 %collective-permute-done.1 = bf16[14,8,1024]{2,1,0:T(8,128)(2,1)S(1)} collective-permute-done((bf16[14,8,1024]{2,1,0:T(8,128)(2,1)S(1)}, bf16[14,8,1024]{2,1,0:T(8,128)(2,1)S(1)}, u32[]{:S(2)}, u32[]{:S(2)}) %collective-permute-start.1) | collective-permute-done | bytes 229408 | tf_op jit(solution)/shard_map/ppermute | solution.py:894
  62.1 7.5 %all-to-all-start = ((bf16[4,147,8,256]{3,2,1,0:T(8,128)(2,1)}), bf16[4,147,8,256]{3,2,1,0:T(8,128)(2,1)S(1)}, u32[]{:S(2)}, u32[]{:S(2)}) async-start(bf16[4,147,8,256]{3,2,1,0:T(8,128)(2,1)} %bitcast.223), calls=%async_computation | async-start | bytes 4816896 | tf_op jit(solution)/shard_map/all_to_all | solution.py:1070
  86.7 7.3 %collective-permute-done.8 = bf16[4,5,8,1024]{3,2,1,0:T(8,128)(2,1)S(1)} collective-permute-done((bf16[4,5,8,1024]{3,2,1,0:T(8,128)(2,1)S(1)}, bf16[4,5,8,1024]{3,2,1,0:T(8,128)(2,1)S(1)}, u32[]{:S(2)}, u32[]{:S(2)}) %collective-permute-start.8) | collective-permute-done | bytes 327712 | tf_op jit(solution)/shard_map/ppermute | solution.py:894
  120.5 4.3 collective-permute-done.18.hi_ref
  143.4 4.8 slow_first.1
  151.0 7.6 %collective-permute-done.24 = f32[2,256]{1,0:T(2,128)S(1)} collective-permute-done((f32[2,256]{1,0:T(2,128)S(1)}, f32[2,256]{1,0:T(2,128)S(1)}, u32[]{:S(2)}, u32[]{:S(2)}) %collective-permute-start.24) | collective-permute-done | bytes 2080 | tf_op jit(solution)/shard_map/ppermute | solution.py:894
  173.8 5.7 collective-permute-done.28.hi_ref
  199.0 4.1 slow_second.1
  214.7 8.3 %collective-permute-done.44.refs_4_ = bf16[49,8,384]{2,1,0:T(8,128)(2,1)S(1)} collective-permute-done((bf16[49,8,384]{2,1,0:T(8,128)(2,1)S(1)}, bf16[49,8,384]{2,1,0:T(8,128)(2,1)S(1)}, u32[]{:S(2)}, u32[]{:S(2)}) %collective-permute-start.44) | collective-permute-done | bytes 301088 | tf_op jit(solution)/shard_map/ppermute | solution.py:894
  226.7 4.4 bypass.1
  243.9 13.5 %collective-permute-done.53.refs_5_ = bf16[98,8,384]{2,1,0:T(8,128)(2,1)S(1)} collective-permute-done((bf16[98,8,384]{2,1,0:T(8,128)(2,1)S(1)}, bf16[98,8,384]{2,1,0:T(8,128)(2,1)S(1)}, u32[]{:S(2)}, u32[]{:S(2)}) %collective-permute-start.53) | collective-permute-done | bytes 602144 | tf_op jit(solution)/shard_map/ppermute | solution.py:894
  257.3 11.9 %collective-permute-start.55 = (f32[2,2560]{1,0:T(2,128)S(1)}, f32[2,2560]{1,0:T(2,128)S(1)}, u32[]{:S(2)}, u32[]{:S(2)}) collective-permute-start(f32[2,2560]{1,0:T(2,128)S(1)} %add_add_fusion.3), channel_id=1, source_target_pairs={{0,2},{1,3},{2,0},{3,1},{4,6},{5,7},{6,4},{7,5},{8,10},{9,11},{10,... | collective-permute-start | bytes 61448 | tf_op jit(solution)/shard_map/ppermute | solution.py:894
  275.1 4.1 fast_out.1
  279.3 7.7 %slow_out.1 = (bf16[147,8,384]{2,1,0:T(8,128)(2,1)S(1)}, bf16[147,8,384]{2,1,0:T(8,128)(2,1)S(1)}, bf16[98,8,384]{2,1,0:T(8,128)(2,1)S(1)}, bf16[49,8,384]{2,1,0...) custom-call(s32[7]{0:T(128)S(1)} %pad_add_fusion.1.table_ref, ...), custom_call_target="tpu_custom_call" | custom-call | bytes 1 | tf_op jit(solution)/shard_map/slow_out/pallas_call | solution.py:125
  295.1 25.0 %collective-permute-done.61.refs_2_ = bf16[98,8,384]{2,1,0:T(8,128)(2,1)S(1)} collective-permute-done((bf16[98,8,384]{2,1,0:T(8,128)(2,1)S(1)}, bf16[98,8,384]{2,1,0:T(8,128)(2,1)S(1)}, u32[]{:S(2)}, u32[]{:S(2)}) %collective-permute-start.61) | collective-permute-done | bytes 602144 | tf_op jit(solution)/shard_map/ppermute | solution.py:894
  341.7 13.6 %collective-permute-done.66.refs_3_ = bf16[49,8,384]{2,1,0:T(8,128)(2,1)S(1)} collective-permute-done((bf16[49,8,384]{2,1,0:T(8,128)(2,1)S(1)}, bf16[49,8,384]{2,1,0:T(8,128)(2,1)S(1)}, u32[]{:S(2)}, u32[]{:S(2)}) %collective-permute-start.66) | collective-permute-done | bytes 301088 | tf_op jit(solution)/shard_map/ppermute | solution.py:894
  356.0 7.9 %collective-permute-done.67.refs_4_ = bf16[49,8,384]{2,1,0:T(8,128)(2,1)S(1)} collective-permute-done((bf16[49,8,384]{2,1,0:T(8,128)(2,1)S(1)}, bf16[49,8,384]{2,1,0:T(8,128)(2,1)S(1)}, u32[]{:S(2)}, u32[]{:S(2)}) %collective-permute-start.67) | collective-permute-done | bytes 301088 | tf_op jit(solution)/shard_map/ppermute | solution.py:894
  372.0 5.4 collective-permute-done.75.dhi_ref
  380.9 6.2 %collective-permute-done.77 = f32[2,384]{1,0:T(2,128)S(1)} collective-permute-done((f32[2,384]{1,0:T(2,128)S(1)}, f32[2,384]{1,0:T(2,128)S(1)}, u32[]{:S(2)}, u32[]{:S(2)}) %collective-permute-start.77) | collective-permute-done | bytes 3104 | tf_op jit(solution)/shard_map/ppermute | solution.py:894
  402.0 5.9 %bypass_back.1 = (bf16[147,8,1024]{2,1,0:T(8,128)(2,1)S(1)}, bf16[147,8,1024]{2,1,0:T(8,128)(2,1)S(1)}, f32[147,8,256]{2,1,0:T(8,128)S(1)}) custom-call(s32[7]{0:T(128)S(1)} %pad_add_fusion.1.table_ref, f32[2]{0:T(128)S(1)} %pad_maximum_fusion.14.n_ref, bf16[147,8,1024]{2,1,0:T(8,128)(2,1)S(1)} %get-tuple-element.215.up_ref, ...), custom_call_target="tpu_custom_call" | custom-call | bytes 1 | tf_op jit(solution)/shard_map/bypass_back/pallas_call | solution.py:125
  416.0 4.9 slow_first_back.1
  424.6 4.8 all-to-all-start.1
  433.9 5.1 first_slab.1
  451.7 6.5 %second_slab.1 = bf16[2,4,4,6,8,1024]{5,4,3,2,1,0:T(8,128)(2,1)S(1)} custom-call(s32[7]{0:T(128)S(1)} %pad_add_fusion.1.table_ref, bf16[177,8,256]{2,1,0:T(8,128)(2,1)S(1)} %copy-done.49, bf16[147,8,256]{2,1,0:T(8,128)(2,1)S(1)} %copy-done.53, bf16[147,8,768]{2,1,0:T(8,128)(2,1)S(1)} %copy-done.33, bf16[147,8,1024]{2,1,0:T(8,128)(2,1)S(1)} %get-tuple-element.169.x_ref, ...), custom_call_target="tpu_custom_call" | custom-call | bytes 1 | tf_op jit(solution)/shard_map/second_slab/pallas_call | solution.py:125
  480.8 5.4 collective-permute-done.93
  488.2 6.5 %collective-permute-done.98 = bf16[4,6,8,1024]{3,2,1,0:T(8,128)(2,1)} collective-permute-done((bf16[4,6,8,1024]{3,2,1,0:T(8,128)(2,1)}, bf16[4,6,8,1024]{3,2,1,0:T(8,128)(2,1)}, u32[]{:S(2)}, u32[]{:S(2)}) %collective-permute-start.98) | collective-permute-done | bytes 393248 | tf_op jit(solution)/shard_map/ppermute | solution.py:894
  494.7 7.3 %collective-permute-done.97 = bf16[4,6,8,1024]{3,2,1,0:T(8,128)(2,1)} collective-permute-done((bf16[4,6,8,1024]{3,2,1,0:T(8,128)(2,1)}, bf16[4,6,8,1024]{3,2,1,0:T(8,128)(2,1)}, u32[]{:S(2)}, u32[]{:S(2)}) %collective-permute-start.97) | collective-permute-done | bytes 393248 | tf_op jit(solution)/shard_map/ppermute | solution.py:894
  517.9 4.4 fast_first_back.1
  522.4 4.3 fast_grads.1
  531.2 4.2 collective-permute-done.110
  559.1 6.0 %outputs.1 = (bf16[588,8,256]{2,1,0:T(8,128)(2,1)}, bf16[588,32,32]{2,1,0:T(8,128)(2,1)}) custom-call(s32[3]{0:T(128)S(1)} %copy-done.78, bf16[147,8,384]{2,1,0:T(8,128)(2,1)S(1)} %copy-done.45, bf16[147,8,384]{2,1,0:T(8,128)(2,1)S(1)} %copy-done.47, bf16[98,8,384]{2,1,0:T(8,128)(2,1)S(1)} %copy-done.57, bf16[49,8,384]{2,1,0:T(8,128)(2,1)S(1)} %copy-done.69, ...), custom_call_target="tpu_custom_call" | custom-call | bytes 1 | tf_op jit(solution)/shard_map/outputs/pallas_call | solution.py:125
  569.0 4.1 fast_unpack.1
  (553 shorter events, 316.4 us)
Async XLA Ops:
  14.7 45.2 %collective-permute-start.3 = (bf16[147,8,128]{2,1,0:T(8,128)(2,1)S(1)}, bf16[147,8,128]{2,1,0:T(8,128)(2,1)S(1)}, u32[]{:S(2)}, u32[]{:S(2)}) collective-permute-start(bf16[147,8,128]{2,1,0:T(8,128)(2,1)S(1)} %get-tuple-element.311), channel_id=1, source_target_pairs={{0,1},{1,0},{2,3},{3,2},{4,5},{5,4},{6,7},{7,6},{8,9},{9,8},{10,11... | collective-permute-start | bytes 903176 | tf_op jit(solution)/shard_map/ppermute | solution.py:894
  14.8 45.9 %collective-permute-start.4 = (bf16[147,8,128]{2,1,0:T(8,128)(2,1)S(1)}, bf16[147,8,128]{2,1,0:T(8,128)(2,1)S(1)}, u32[]{:S(2)}, u32[]{:S(2)}) collective-permute-start(bf16[147,8,128]{2,1,0:T(8,128)(2,1)S(1)} %get-tuple-element.310), channel_id=1, source_target_pairs={{0,2},{1,3},{2,0},{3,1},{4,6},{5,7},{6,4},{7,5},{8,10},{9,11},{10,... | collective-permute-start | bytes 903176 | tf_op jit(solution)/shard_map/ppermute | solution.py:894
  17.8 43.6 %collective-permute-start.5 = (bf16[147,8,128]{2,1,0:T(8,128)(2,1)S(1)}, bf16[147,8,128]{2,1,0:T(8,128)(2,1)S(1)}, u32[]{:S(2)}, u32[]{:S(2)}) collective-permute-start(bf16[147,8,128]{2,1,0:T(8,128)(2,1)S(1)} %get-tuple-element.309), channel_id=1, source_target_pairs={{0,3},{1,2},{2,1},{3,0},{4,7},{5,6},{6,5},{7,4},{8,11},{9,10},{10,... | collective-permute-start | bytes 903176 | tf_op jit(solution)/shard_map/ppermute | solution.py:894
  19.1 40.8 %collective-permute-start.1 = (bf16[14,8,1024]{2,1,0:T(8,128)(2,1)S(1)}, bf16[14,8,1024]{2,1,0:T(8,128)(2,1)S(1)}, u32[]{:S(2)}, u32[]{:S(2)}) collective-permute-start(bf16[14,8,1024]{2,1,0:T(8,128)(2,1)S(1)} %copy-done.93), channel_id=1, source_target_pairs={{0,2},{1,3},{2,0},{3,1},{4,6},{5,7},{6,4},{7,5},{8,10},{9,11},{10,... | collective-permute-start | bytes 688136 | tf_op jit(solution)/shard_map/ppermute | solution.py:894
  20.8 39.1 %collective-permute-start.2 = (bf16[14,8,1024]{2,1,0:T(8,128)(2,1)S(1)}, bf16[14,8,1024]{2,1,0:T(8,128)(2,1)S(1)}, u32[]{:S(2)}, u32[]{:S(2)}) collective-permute-start(bf16[14,8,1024]{2,1,0:T(8,128)(2,1)S(1)} %copy-done.93), channel_id=1, source_target_pairs={{0,3},{1,2},{2,1},{3,0},{4,7},{5,6},{6,5},{7,4},{8,11},{9,10},{10,... | collective-permute-start | bytes 688136 | tf_op jit(solution)/shard_map/ppermute | solution.py:894
  62.1 63.3 %all-to-all-start = ((bf16[4,147,8,256]{3,2,1,0:T(8,128)(2,1)}), bf16[4,147,8,256]{3,2,1,0:T(8,128)(2,1)S(1)}, u32[]{:S(2)}, u32[]{:S(2)}) async-start(bf16[4,147,8,256]{3,2,1,0:T(8,128)(2,1)} %bitcast.223), calls=%async_computation | async-start | bytes 4816896 | tf_op jit(solution)/shard_map/all_to_all | solution.py:1070
  131.9 52.0 %collective-permute-start.34 = (bf16[4,9,8,1024]{3,2,1,0:T(8,128)(2,1)S(1)}, bf16[4,9,8,1024]{3,2,1,0:T(8,128)(2,1)S(1)}, u32[]{:S(2)}, u32[]{:S(2)}) collective-permute-start(bf16[4,9,8,1024]{3,2,1,0:T(8,128)(2,1)S(1)} %pad_maximum_fusion.7), channel_id=1, source_target_pairs={{0,24},{4,28},{8,16},{12,20},{16,8},{20,12},{24,0},{28,4},{1,25},{... | collective-permute-start | bytes 1769480 | tf_op jit(solution)/shard_map/ppermute | solution.py:894
  133.7 50.1 %collective-permute-start.33 = (bf16[4,9,8,1024]{3,2,1,0:T(8,128)(2,1)S(1)}, bf16[4,9,8,1024]{3,2,1,0:T(8,128)(2,1)S(1)}, u32[]{:S(2)}, u32[]{:S(2)}) collective-permute-start(bf16[4,9,8,1024]{3,2,1,0:T(8,128)(2,1)S(1)} %pad_maximum_fusion.7), channel_id=1, source_target_pairs={{0,16},{4,20},{8,24},{12,28},{16,0},{20,4},{24,8},{28,12},{1,17},{... | collective-permute-start | bytes 1769480 | tf_op jit(solution)/shard_map/ppermute | solution.py:894
  135.0 49.0 %collective-permute-start.32 = (bf16[4,9,8,1024]{3,2,1,0:T(8,128)(2,1)S(1)}, bf16[4,9,8,1024]{3,2,1,0:T(8,128)(2,1)S(1)}, u32[]{:S(2)}, u32[]{:S(2)}) collective-permute-start(bf16[4,9,8,1024]{3,2,1,0:T(8,128)(2,1)S(1)} %pad_maximum_fusion.7), channel_id=1, source_target_pairs={{0,8},{4,12},{8,0},{12,4},{16,24},{20,28},{24,16},{28,20},{1,9},{5... | collective-permute-start | bytes 1769480 | tf_op jit(solution)/shard_map/ppermute | solution.py:894
  135.5 44.0 %collective-permute-start.26 = (bf16[98,8,384]{2,1,0:T(8,128)(2,1)}, bf16[98,8,384]{2,1,0:T(8,128)(2,1)S(1)}, u32[]{:S(2)}, u32[]{:S(2)}) collective-permute-start(bf16[98,8,384]{2,1,0:T(8,128)(2,1)} %get-tuple-element.150), channel_id=1, source_target_pairs={{0,2},{1,3},{2,0},{3,1},{4,6},{5,7},{6,4},{7,5},{8,10},{9,11},{10,... | collective-permute-start | bytes 1806344 | tf_op jit(solution)/shard_map/ppermute | solution.py:894
  187.8 35.4 %collective-permute-start.45 = (bf16[147,8,384]{2,1,0:T(8,128)(2,1)S(1)}, bf16[147,8,384]{2,1,0:T(8,128)(2,1)S(1)}, u32[]{:S(2)}, u32[]{:S(2)}) collective-permute-start(bf16[147,8,384]{2,1,0:T(8,128)(2,1)S(1)} %copy-done.95), channel_id=1, source_target_pairs={{0,1},{1,0},{2,3},{3,2},{4,5},{5,4},{6,7},{7,6},{8,9},{9,8},{10,11... | collective-permute-start | bytes 2709512 | tf_op jit(solution)/shard_map/ppermute | solution.py:894
  188.8 25.9 %collective-permute-start.43 = (bf16[49,8,384]{2,1,0:T(8,128)(2,1)S(1)}, bf16[49,8,384]{2,1,0:T(8,128)(2,1)S(1)}, u32[]{:S(2)}, u32[]{:S(2)}) collective-permute-start(bf16[49,8,384]{2,1,0:T(8,128)(2,1)S(1)} %copy-done.98), channel_id=1, source_target_pairs={{0,2},{1,3},{2,0},{3,1},{4,6},{5,7},{6,4},{7,5},{8,10},{9,11},{10,... | collective-permute-start | bytes 903176 | tf_op jit(solution)/shard_map/ppermute | solution.py:894
  191.4 31.7 %collective-permute-start.44 = (bf16[49,8,384]{2,1,0:T(8,128)(2,1)S(1)}, bf16[49,8,384]{2,1,0:T(8,128)(2,1)S(1)}, u32[]{:S(2)}, u32[]{:S(2)}) collective-permute-start(bf16[49,8,384]{2,1,0:T(8,128)(2,1)S(1)} %copy-done.97), channel_id=1, source_target_pairs={{0,3},{1,2},{2,1},{3,0},{4,7},{5,6},{6,5},{7,4},{8,11},{9,10},{10,... | collective-permute-start | bytes 903176 | tf_op jit(solution)/shard_map/ppermute | solution.py:894
  240.6 16.7 %collective-permute-start.53 = (bf16[98,8,384]{2,1,0:T(8,128)(2,1)S(1)}, bf16[98,8,384]{2,1,0:T(8,128)(2,1)S(1)}, u32[]{:S(2)}, u32[]{:S(2)}) collective-permute-start(bf16[98,8,384]{2,1,0:T(8,128)(2,1)S(1)} %copy-done.96), channel_id=1, source_target_pairs={{0,3},{1,2},{2,1},{3,0},{4,7},{5,6},{6,5},{7,4},{8,11},{9,10},{10,... | collective-permute-start | bytes 1806344 | tf_op jit(solution)/shard_map/ppermute | solution.py:894
  291.8 28.3 %collective-permute-start.61 = (bf16[98,8,384]{2,1,0:T(8,128)(2,1)S(1)}, bf16[98,8,384]{2,1,0:T(8,128)(2,1)S(1)}, u32[]{:S(2)}, u32[]{:S(2)}) collective-permute-start(bf16[98,8,384]{2,1,0:T(8,128)(2,1)S(1)} %get-tuple-element.193), channel_id=1, source_target_pairs={{0,2},{1,3},{2,0},{3,1},{4,6},{5,7},{6,4},{7,5},{8,10},{9,11},{10,... | collective-permute-start | bytes 1806344 | tf_op jit(solution)/shard_map/ppermute | solution.py:894
  326.7 38.0 %collective-permute-start.65 = (bf16[147,8,384]{2,1,0:T(8,128)(2,1)S(1)}, bf16[147,8,384]{2,1,0:T(8,128)(2,1)S(1)}, u32[]{:S(2)}, u32[]{:S(2)}) collective-permute-start(bf16[147,8,384]{2,1,0:T(8,128)(2,1)S(1)} %get-tuple-element.195), channel_id=1, source_target_pairs={{0,1},{1,0},{2,3},{3,2},{4,5},{5,4},{6,7},{7,6},{8,9},{9,8},{10,11... | collective-permute-start | bytes 2709512 | tf_op jit(solution)/shard_map/ppermute | solution.py:894
  328.3 27.0 %collective-permute-start.66 = (bf16[49,8,384]{2,1,0:T(8,128)(2,1)S(1)}, bf16[49,8,384]{2,1,0:T(8,128)(2,1)S(1)}, u32[]{:S(2)}, u32[]{:S(2)}) collective-permute-start(bf16[49,8,384]{2,1,0:T(8,128)(2,1)S(1)} %get-tuple-element.197), channel_id=1, source_target_pairs={{0,2},{1,3},{2,0},{3,1},{4,6},{5,7},{6,4},{7,5},{8,10},{9,11},{10,... | collective-permute-start | bytes 903176 | tf_op jit(solution)/shard_map/ppermute | solution.py:894
  329.2 34.7 %collective-permute-start.67 = (bf16[49,8,384]{2,1,0:T(8,128)(2,1)S(1)}, bf16[49,8,384]{2,1,0:T(8,128)(2,1)S(1)}, u32[]{:S(2)}, u32[]{:S(2)}) collective-permute-start(bf16[49,8,384]{2,1,0:T(8,128)(2,1)S(1)} %get-tuple-element.199), channel_id=1, source_target_pairs={{0,3},{1,2},{2,1},{3,0},{4,7},{5,6},{6,5},{7,4},{8,11},{9,10},{10,... | collective-permute-start | bytes 903176 | tf_op jit(solution)/shard_map/ppermute | solution.py:894
  337.8 39.6 %collective-permute-start.72 = (f32[15,8,512]{2,1,0:T(8,128)S(1)}, f32[15,8,512]{2,1,0:T(8,128)S(1)}, u32[]{:S(2)}, u32[]{:S(2)}) collective-permute-start(f32[15,8,512]{2,1,0:T(8,128)S(1)} %get-tuple-element.205), channel_id=1, source_target_pairs={{0,1},{1,2},{2,3},{4,5},{5,6},{6,7},{8,9},{9,10},{10,11},{12,13},{... | collective-permute-start | bytes 737288 | tf_op jit(solution)/shard_map/ppermute | solution.py:948
  340.4 37.1 %collective-permute-start.73 = (f32[15,8,512]{2,1,0:T(8,128)S(1)}, f32[15,8,512]{2,1,0:T(8,128)S(1)}, u32[]{:S(2)}, u32[]{:S(2)}) collective-permute-start(f32[15,8,512]{2,1,0:T(8,128)S(1)} %get-tuple-element.206), channel_id=1, source_target_pairs={{1,0},{2,1},{3,2},{5,4},{6,5},{7,6},{9,8},{10,9},{11,10},{13,12},{... | collective-permute-start | bytes 737288 | tf_op jit(solution)/shard_map/ppermute | solution.py:949
  387.1 22.2 %collective-permute-start.79 = (bf16[98,8,384]{2,1,0:T(8,128)(2,1)S(1)}, bf16[98,8,384]{2,1,0:T(8,128)(2,1)S(1)}, u32[]{:S(2)}, u32[]{:S(2)}) collective-permute-start(bf16[98,8,384]{2,1,0:T(8,128)(2,1)S(1)} %get-tuple-element.210), channel_id=1, source_target_pairs={{0,3},{1,2},{2,1},{3,0},{4,7},{5,6},{6,5},{7,4},{8,11},{9,10},{10,... | collective-permute-start | bytes 1806344 | tf_op jit(solution)/shard_map/ppermute | solution.py:894
  424.6 79.7 %all-to-all-start.1 = ((bf16[4,147,8,256]{3,2,1,0:T(8,128)(2,1)}), bf16[4,147,8,256]{3,2,1,0:T(8,128)(2,1)}, u32[]{:S(2)}, u32[]{:S(2)}) async-start(bf16[4,147,8,256]{3,2,1,0:T(8,128)(2,1)} %copy-done.31), calls=%async_computation.1 | async-start | bytes 4816896 | tf_op jit(solution)/shard_map/all_to_all | solution.py:1070
  442.0 19.7 %collective-permute-start.91 = (bf16[4,4,6,8,1024]{4,3,2,1,0:T(8,128)(2,1)}, bf16[4,4,6,8,1024]{4,3,2,1,0:T(8,128)(2,1)}, u32[]{:S(2)}, u32[]{:S(2)}) collective-permute-start(bf16[4,4,6,8,1024]{4,3,2,1,0:T(8,128)(2,1)} %dynamic-slice_bitcast_fusion.1), channel_id=1, source_target_pairs={{0,4},{4,0},{8,12},{12,8},{16,20},{20,16},{24,28},{28,24},{1,5},{5... | collective-permute-start | bytes 4718600 | tf_op jit(solution)/shard_map/ppermute | solution.py:894
  466.2 19.9 %collective-permute-start.93 = (bf16[4,6,8,1024]{3,2,1,0:T(8,128)(2,1)S(1)}, bf16[4,6,8,1024]{3,2,1,0:T(8,128)(2,1)S(1)}, u32[]{:S(2)}, u32[]{:S(2)}) collective-permute-start(bf16[4,6,8,1024]{3,2,1,0:T(8,128)(2,1)S(1)} %get-tuple-element.308), channel_id=1, source_target_pairs={{0,16},{4,20},{8,24},{12,28},{16,0},{20,4},{24,8},{28,12},{1,17},{... | collective-permute-start | bytes 1179656 | tf_op jit(solution)/shard_map/ppermute | solution.py:894
  466.7 19.5 %collective-permute-start.92 = (bf16[4,6,8,1024]{3,2,1,0:T(8,128)(2,1)S(1)}, bf16[4,6,8,1024]{3,2,1,0:T(8,128)(2,1)S(1)}, u32[]{:S(2)}, u32[]{:S(2)}) collective-permute-start(bf16[4,6,8,1024]{3,2,1,0:T(8,128)(2,1)S(1)} %get-tuple-element.306), channel_id=1, source_target_pairs={{0,8},{4,12},{8,0},{12,4},{16,24},{20,28},{24,16},{28,20},{1,9},{5... | collective-permute-start | bytes 1179656 | tf_op jit(solution)/shard_map/ppermute | solution.py:894
  471.9 22.8 %collective-permute-start.98 = (bf16[4,6,8,1024]{3,2,1,0:T(8,128)(2,1)}, bf16[4,6,8,1024]{3,2,1,0:T(8,128)(2,1)}, u32[]{:S(2)}, u32[]{:S(2)}) collective-permute-start(bf16[4,6,8,1024]{3,2,1,0:T(8,128)(2,1)} %get-tuple-element.304), channel_id=1, source_target_pairs={{0,24},{4,28},{8,16},{12,20},{16,8},{20,12},{24,0},{28,4},{1,25},{... | collective-permute-start | bytes 1179656 | tf_op jit(solution)/shard_map/ppermute | solution.py:894
  473.4 28.6 %collective-permute-start.97 = (bf16[4,6,8,1024]{3,2,1,0:T(8,128)(2,1)}, bf16[4,6,8,1024]{3,2,1,0:T(8,128)(2,1)}, u32[]{:S(2)}, u32[]{:S(2)}) collective-permute-start(bf16[4,6,8,1024]{3,2,1,0:T(8,128)(2,1)} %get-tuple-element.305), channel_id=1, source_target_pairs={{0,16},{4,20},{8,24},{12,28},{16,0},{20,4},{24,8},{28,12},{1,17},{... | collective-permute-start | bytes 1179656 | tf_op jit(solution)/shard_map/ppermute | solution.py:894
  477.7 24.3 %collective-permute-start.96 = (bf16[4,6,8,1024]{3,2,1,0:T(8,128)(2,1)}, bf16[4,6,8,1024]{3,2,1,0:T(8,128)(2,1)}, u32[]{:S(2)}, u32[]{:S(2)}) collective-permute-start(bf16[4,6,8,1024]{3,2,1,0:T(8,128)(2,1)} %get-tuple-element.303), channel_id=1, source_target_pairs={{0,8},{4,12},{8,0},{12,4},{16,24},{20,28},{24,16},{28,20},{1,9},{5... | collective-permute-start | bytes 1179656 | tf_op jit(solution)/shard_map/ppermute | solution.py:894
  509.9 19.8 %collective-permute-start.111 = (bf16[12,8,1024]{2,1,0:T(8,128)(2,1)S(1)}, bf16[12,8,1024]{2,1,0:T(8,128)(2,1)S(1)}, u32[]{:S(2)}, u32[]{:S(2)}) collective-permute-start(bf16[12,8,1024]{2,1,0:T(8,128)(2,1)S(1)} %get-tuple-element.315), channel_id=1, source_target_pairs={{0,3},{1,2},{2,1},{3,0},{4,7},{5,6},{6,5},{7,4},{8,11},{9,10},{10,... | collective-permute-start | bytes 589832 | tf_op jit(solution)/shard_map/ppermute | solution.py:894
  512.9 22.5 %collective-permute-start.110 = (bf16[12,8,1024]{2,1,0:T(8,128)(2,1)S(1)}, bf16[12,8,1024]{2,1,0:T(8,128)(2,1)S(1)}, u32[]{:S(2)}, u32[]{:S(2)}) collective-permute-start(bf16[12,8,1024]{2,1,0:T(8,128)(2,1)S(1)} %get-tuple-element.314), channel_id=1, source_target_pairs={{0,2},{1,3},{2,0},{3,1},{4,6},{5,7},{6,4},{7,5},{8,10},{9,11},{10,... | collective-permute-start | bytes 589832 | tf_op jit(solution)/shard_map/ppermute | solution.py:894
  513.5 22.0 %collective-permute-start.109 = (bf16[12,8,1024]{2,1,0:T(8,128)(2,1)S(1)}, bf16[12,8,1024]{2,1,0:T(8,128)(2,1)S(1)}, u32[]{:S(2)}, u32[]{:S(2)}) collective-permute-start(bf16[12,8,1024]{2,1,0:T(8,128)(2,1)S(1)} %get-tuple-element.313), channel_id=1, source_target_pairs={{0,1},{1,0},{2,3},{3,2},{4,5},{5,4},{6,7},{7,6},{8,9},{9,8},{10,11... | collective-permute-start | bytes 589832 | tf_op jit(solution)/shard_map/ppermute | solution.py:894
  537.9 31.1 %all-to-all-start.2 = ((bf16[4,147,8,128]{3,2,1,0:T(8,128)(2,1)}), bf16[4,147,8,128]{3,2,1,0:T(8,128)(2,1)S(1)}, u32[]{:S(2)}, u32[]{:S(2)}) async-start(bf16[4,147,8,128]{3,2,1,0:T(8,128)(2,1)} %get-tuple-element.244), calls=%async_computation.2 | async-start | bytes 2408448 | tf_op jit(solution)/shard_map/all_to_all | solution.py:1070
  (195 other events, 1807.3 us)

commit v5 on v4

--- a/solution.py
+++ b/solution.py
@@ -195,6 +195,14 @@
     for r in range(4):
         tmp_ref[pl.ds(r, chunk * 8, stride=4), :] = joined[:, 32 * r : 32 * r + 32]
     out_ref[...] = tmp_ref[...].reshape(chunk, 32, 32).astype(BF16)
+
+
+def copy_kernel(x_ref, out_ref):
+    def body(p, carry):
+        out_ref[pl.ds(p, SMALL)] = x_ref[pl.ds(p, SMALL)]
+        return carry
+
+    steps(x_ref.shape[0], SMALL, body, 0)
 
 
 def lanes_at(block, width):
@@ -924,24 +932,18 @@
     return add(tree, near, far, both)
 
 
-def over_dp(tree, sizes, early=None):
-    for i, bits in enumerate(stages(sizes["dp"], True)):
-        if i == 1 and early is not None:
-            tree = after(tree, early)
-        tree = butterfly(tree, "dp", sizes["dp"], bits)
-    return tree
-
-
-def over_chan(tree, sizes, bulk=None):
+def everywhere(tree, sizes, bulk=None):
+    dp, chan = sizes["dp"], sizes["chan"]
+    first, *others = stages(dp, True)
+    tree = butterfly(tree, "dp", dp, first)
     if bulk is not None:
         tree = after(tree, bulk)
-    for bits in stages(sizes["chan"], False):
-        tree = butterfly(tree, "chan", sizes["chan"], bits)
-    return tree
-
-
-def everywhere(tree, sizes, bulk=None, early=None):
-    return over_chan(over_dp(tree, sizes, early), sizes, bulk)
+    for bits in stages(chan, False):
+        tree = butterfly(tree, "chan", chan, bits)
+    passed = tree
+    for bits in others:
+        tree = butterfly(tree, "dp", dp, bits)
+    return tree, passed
 
 
 def halos(first, last, count):
@@ -950,30 +952,34 @@
     return low, high
 
 
-def gather_group(v, sizes):
-    dp = sizes["dp"]
-    own = [v] + [swap(v, "dp", dp, 2 * k) for k in (1, 2, 3)]
-    return jnp.stack(own), jnp.stack([swap(u, "dp", dp, 1) for u in own])
+def gather_chips(v, sizes):
+    return [v] + [swap(v, "dp", sizes["dp"], 2 * k) for k in (1, 2, 3)]
+
+
+def gather_cores(own, sizes):
+    return jnp.stack(own), jnp.stack([swap(v, "dp", sizes["dp"], 1) for v in own])
 
 
 def pick(v, index, axis):
     return lax.dynamic_index_in_dim(v, index, axis, keepdims=False)
 
 
-def scatter_group(tree, sizes, group):
-    dp = sizes["dp"]
-    core, chip = group % 2, group // 2
-    sent = jax.tree.map(lambda v: pick(v, 1 - core, 0), tree)
-    kept = jax.tree.map(lambda v: pick(v, core, 0), tree)
-    tree = add(kept, swap(sent, "dp", dp, 1))
-    got = [swap(jax.tree.map(lambda v: pick(v, chip ^ k, 0), tree), "dp", dp, 2 * k) for k in (1, 2, 3)]
-    return add(jax.tree.map(lambda v: pick(v, chip, 0), tree), *got)
-
-
-def scatter_chan(tree, sizes, chan):
+def scatter_cores(v, sizes, group):
+    sent, kept = pick(v, 1 - group % 2, 0), pick(v, group % 2, 0)
+    got = jnp.concatenate([swap(sent[:2], "dp", sizes["dp"], 1), swap(sent[2:], "dp", sizes["dp"], 1)])
+    return add(kept, got)
+
+
+def scatter_chips(v, sizes, group):
+    chip = group // 2
+    got = [swap(pick(v, chip ^ k, 0), "dp", sizes["dp"], 2 * k) for k in (1, 2, 3)]
+    return add(pick(v, chip, 0), *got)
+
+
+def scatter_chan(tree, sizes, chan, gate):
     size, dp = sizes["chan"], sizes["dp"]
     got = [swap(jax.tree.map(lambda v: pick(v, chan ^ k, 0), tree), "chan", size, k) for k in (1, 2, 3)]
-    tree = add(jax.tree.map(lambda v: pick(v, chan, 0), tree), *got)
+    tree = add(jax.tree.map(lambda v: pick(v, chan, 0), tree), *after(got, gate))
     bits = [1 << i for i in range(3, dp.bit_length() - 1)]
     while bits:
         tree = butterfly(tree, "dp", dp, bits[:2])
@@ -1106,10 +1112,10 @@
         name="weight_slab",
     )(ids, *params, *small)
     slabs = at_once([slab] * ways)
-    fx_pieces = at_once(blocks_of(packed(after(fast_input, slab))))
+    fx_pieces = at_once(after(blocks_of(packed(after(fast_input, slab))), slabs))
     xs = all_to_all(after(split(slow_input), (slabs, fx_pieces)))
     early, late = jnp.stack([v[0:5] for v in slabs]), jnp.stack([v[5:14] for v in slabs])
-    own_slabs, other_slabs = gather_group(early, sizes)
+    own_slabs, other_slabs = gather_cores(gather_chips(early, sizes), sizes)
     fr_t = fast_reduce.transpose(0, 2, 1)
     red_w, lred_w, w_first, w_fsp, w_fex, fin_g, fout_g, mid_g, out_g = call(
         weights_kernel,
@@ -1147,8 +1153,8 @@
     )
     fa_lo, fa_hi = halos(first, last, ways)
     cots = parted(blocks_of(packed(fast_cotangent, split(slow_cotangent))))
-    sums1 = over_dp(sums1, sizes)
-    own_late, other_late = gather_group(after(late, sums1), sizes)
+    late = gather_chips(after(late, other_slabs), sizes)
+    own_late, other_late = gather_cores(late, sizes)
     exp_w, short_w, lshort_w, spat_w = call(
         more_weights_kernel,
         [
@@ -1163,8 +1169,8 @@
     )
     exp_w, short_w, lshort_w = (v.reshape(-1, wide_in) for v in (exp_w, short_w, lshort_w))
     spat_w = spat_w.reshape(9, mid, mid)
-    sums1 = over_chan(sums1, sizes, (xs, fa_lo, fa_hi, cots))
-    send_parts(cots, (2,), sums1)
+    sums1, passed = everywhere(sums1, sizes, (xs, fa_lo, fa_hi, cots, late))
+    send_parts(cots, (2,), passed)
     fast_pad = [pltpu.VMEM((3, ext, 8, 128), F32)]
     slow_pad = [pltpu.VMEM((3, ext, 8, mid), F32)]
     x, lat, sa, sums2, first, last = call(
@@ -1184,8 +1190,8 @@
         smem=2,
         name="fast_second",
     )
-    sums2 = everywhere(sums2, sizes, (cots[2], sa_lo, sa_hi))
-    send_parts(cots, (3, 4, 1), sums2)
+    sums2, passed = everywhere(sums2, sizes, (cots[2], sa_lo, sa_hi))
+    send_parts(cots, (3, 4, 1), passed)
     ha, sb, sums3 = call(
         functools.partial(conv_kernel, halo, across, per_clip, False, (0, 0)),
         [shape((ext, 8, mid), BF16), middle, shape((2, mid + 128))],
@@ -1194,8 +1200,8 @@
         smem=2,
         name="slow_second",
     )
-    sums3 = everywhere(sums3, sizes, (cots[3], cots[4], cots[1]))
-    send_parts(cots, (5,), sums3)
+    sums3, passed = everywhere(sums3, sizes, (cots[3], cots[4], cots[1]))
+    send_parts(cots, (5,), passed)
     sp, sp_sums = call(
         bypass_kernel,
         [shape((mine, 8, wide_in), BF16), shape((2, wide_in))],
@@ -1217,7 +1223,7 @@
         smem=2,
         name="slow_third",
     )
-    sums4 = everywhere(sums4, sizes, cots[5])
+    sums4, _ = everywhere(sums4, sizes, cots[5])
     fast_out, dfs, fc_slopes = call(
         functools.partial(fast_out_kernel, 2 * wide_in),
         [shape((ways, mine, 8, 128), BF16), shape((mine, 8, wide_f), BF16), shape((2, wide_f))],
@@ -1235,9 +1241,8 @@
         name="slow_out",
     )
 
-    send_parts(outs, (2,), dss)
-    sums5 = everywhere(sums5, sizes, outs[2])
-    send_parts(outs, (3, 4, 1), sums5)
+    sums5, passed = everywhere(sums5, sizes)
+    send_parts(outs, (2,), passed)
     dfc, dzfb, fb_slopes, first, last = call(
         functools.partial(expand_back_kernel, True, (2 * wide_in, 2 * wide_in, mid)),
         [shape((mine, 8, wide_f), BF16), narrow, shape((2, 128)), *edges],
@@ -1254,17 +1259,8 @@
         name="slow_third_back",
     )
     low_sb, high_sb = halos(first, last, ways)
-    dss_late, = after((dss,), sums6)
-    dsp, dx, dl = call(
-        bypass_back_kernel,
-        [shape((mine, 8, wide_in), BF16), shape((mine, 8, wide_in), BF16), middle],
-        [table, inv_n, dss_late, sp, sums4, out_g[2:4], sums5, short_w, lshort_w],
-        smem=2,
-        name="bypass_back",
-    )
-
-    sums6 = everywhere(sums6, sizes, (low6, high6, low_sb, high_sb), (outs[3], outs[4], outs[1]))
-    send_parts(outs, (5,), sums6)
+    sums6, passed = everywhere(sums6, sizes, (outs[2], low6, high6, low_sb, high_sb))
+    send_parts(outs, (3, 4, 1), passed)
     dfb, dzfa, fa_slopes = call(
         functools.partial(conv_back_kernel, halo, across, per_clip, True, (mid, mid, 0, 384, 0)),
         [shape((mine, 8, 128), BF16), narrow, shape((2, 128))],
@@ -1281,7 +1277,25 @@
         smem=2,
         name="slow_second_back",
     )
-    dsc_late, dsp = after((dsc, dsp), sums7)
+    dss_late, = after((dss,), sums7)
+    dsp, dx, dl = call(
+        bypass_back_kernel,
+        [shape((mine, 8, wide_in), BF16), shape((mine, 8, wide_in), BF16), middle],
+        [table, inv_n, dss_late, sp, sums4, out_g[2:4], sums5, short_w, lshort_w],
+        smem=2,
+        name="bypass_back",
+    )
+
+    sums7, passed = everywhere(sums7, sizes, (outs[3], outs[4], outs[1], dx, dl))
+    send_parts(outs, (5,), passed)
+    dsa, dslow, dzlp, sums8 = call(
+        slow_back_kernel,
+        [shape((mine, 8, 3 * mid), BF16), shape((ways, mine, 8, mid), BF16), middle, shape((2, mid))],
+        [table, inv_n, dzsa, sa, sums2, in_g[0], sums7, red_w, lred_w, dx, dl, lp, sums1, lat_g],
+        smem=2,
+        name="slow_first_back",
+    )
+    dsc_late, dsp = after((dsc, dsp), sums8)
     (slab1,) = call(
         first_slab_kernel,
         [shape((2, 4, ways, 6, 8, wide_in), BF16)],
@@ -1289,17 +1303,10 @@
         [pltpu.VMEM((6, mid, wide_in), F32)],
         name="first_slab",
     )
-    sums7 = everywhere(sums7, sizes, (outs[5], dx, dl))
-    dsa, dslow, dzlp, sums8 = call(
-        slow_back_kernel,
-        [shape((mine, 8, 3 * mid), BF16), shape((ways, mine, 8, mid), BF16), middle, shape((2, mid))],
-        [table, inv_n, dzsa, sa, sums2, in_g[0], sums7, red_w, lred_w, dx, dl, lp, sums1, lat_g],
-        smem=2,
-        name="slow_first_back",
-    )
-    sums8 = over_dp(sums8, sizes)
-    dslow = all_to_all(dslow)
-    dsa, dsb_late = after((dsa, dsb), sums8)
+    sums8, passed = everywhere(sums8, sizes, (outs[5], slab1))
+    dslow = all_to_all(after(dslow, passed))
+    slab1 = scatter_cores(slab1, sizes, group)
+    dsa, dsb_late = after((dsa, dsb), (sums8, slab1))
     (slab2,) = call(
         functools.partial(second_slab_kernel, halo, across, per_clip),
         [shape((2, 4, ways, 6, 8, wide_in), BF16)],
@@ -1308,8 +1315,10 @@
         smem=1,
         name="second_slab",
     )
-    slabs = jnp.concatenate(scatter_group((slab1, slab2), sizes, group), axis=1)
-    sums8 = over_chan(sums8, sizes, (dslow, slabs))
+    slab1 = scatter_chips(slab1, sizes, group)
+    slab2 = scatter_cores(slab2, sizes, group)
+    dzlp = after(dzlp, slab2)
+    slab2 = scatter_chips(slab2, sizes, group)
     dfirst, dfast = call(
         functools.partial(fast_back_kernel, mid),
         [shape((mine, 8, 896), BF16), shape((ways, mine, 8, 128), BF16)],
@@ -1326,15 +1335,18 @@
         smem=1,
         name="fast_grads",
     )
-    slow_output, fast_output = unpacked(after(outs, dfirst))
-    slabs = scatter_chan(slabs, sizes, chan)
+    (slow_input_grad,) = call(
+        copy_kernel, [shape((places, slow_t, slow_part), BF16)], [dslow.reshape(places, slow_t, slow_part)], name="slow_grad"
+    )
+    slow_output, fast_output = unpacked(after(outs, slow_input_grad))
+    slabs = scatter_chan(jnp.concatenate([slab1, slab2], axis=1), sizes, chan, (slow_output, fast_output))
     small = [jnp.concatenate([pick(g_lat, chan ^ k, 0), g_fast]) for k in range(ways)]
     small = add(*at_once(small))
-    dfast = all_to_all(dfast)
+    dfast = all_to_all(after(dfast, (dslow, slabs, small)))
     for bits in stages(sizes["dp"], True):
         small = butterfly(small, "dp", sizes["dp"], bits)
     g_lat, g_fast = small[0:40].astype(F32), small[40:68].astype(F32)
-    own_slabs, other_slabs = gather_group(slabs, sizes)
+    own_slabs, other_slabs = gather_cores(gather_chips(slabs, sizes), sizes)
     g_exp, g_short, g_lshort, g_red, g_lred, g_spat = call(
         grads_kernel,
         [shape((8, 8, wide_in)), shape((8, 4, 8, wide_in)), shape((8, 8, wide_in)), shape((3, 8, 8, wide_in)), shape((3, 8, 8, mid)),
@@ -1343,7 +1355,7 @@
         smem=1,
         name="grads",
     )
-    slow_input_grad = joined(dslow)
+    slow_input_grad = joined(slow_input_grad)
     fast_input_grad = pl.pallas_call(
         unpack_fast_kernel,
         grid=(places // chunk,),

time: 584 us -> 527 us (0.902)
  waiting for transfers between devices: 220 us -> 168 us
  local copies, waits for them, and re-layouts: 66.5 us -> 53.5 us
  starting transfers between devices: 161 us -> 168 us
    ppermute x111 -> x113, waiting for transfers between devices: 202 us -> 147 us  [swap(): return jax.tree.map(lambda v: lax.ppermute(v, axis, pairs), tree)]
    unnamed x212 -> x217, local copies, waits for them, and re-layouts: 49.7 us -> 35.6 us
    pallas_call x23 -> x24, Pallas kernels: 92.3 us -> 96.2 us  [call(): pl.pallas_call(kernel, out_shape=tuple(outs), in_specs=specs, out_specs=t...]
    ppermute x111 -> x113, starting transfers between devices: 129 us -> 128 us  [swap(): return jax.tree.map(lambda v: lax.ppermute(v, axis, pairs), tree)]
  transfers between devices with their start and end apart: 122 -> 124, of which waited for: 54 -> 63; matrix products, arithmetic and copies ran while one was open for 6% -> 7% of each run, Pallas kernels for 13% -> 17%
where the time goes in v5:
time: 527 us; the launch traced here: 520 us
  starting transfers between devices  168 us (32%)
  waiting for transfers between devices  168 us (32%)
  Pallas kernels  110 us (21%)
  local copies, waits for them, and re-layouts  53.5 us (10%)
  other arithmetic  18.1 us (3%)
    ppermute x113, waiting for transfers between devices, swap(): return jax.tree.map(lambda v: lax.ppermute(v, axis, pairs), tree)  147 us
    ppermute x113, starting transfers between devices, swap(): return jax.tree.map(lambda v: lax.ppermute(v, axis, pairs), tree)  128 us
    pallas_call x24, Pallas kernels, call(): pl.pallas_call(kernel, out_shape=tuple(outs), in_specs=specs, out_specs=t...  96.2 us
    unnamed x217, local copies, waits for them, and re-layouts  35.6 us
    all_to_all x3, starting transfers between devices, all_to_all(): return lax.all_to_all(v, 'chan', 0, 0, tiled=True)  20.1 us
    ppermute x4, waiting for transfers between devices, halos(): high = lax.ppermute(first, 'chan', [(i + 1, i) for i in range(count - 1)])  16.3 us
    ppermute x4, starting transfers between devices, halos(): low = lax.ppermute(last, 'chan', [(i, i + 1) for i in range(count - 1)])  14.1 us
  transfers between devices with their start and end apart: 124, of which 63 were waited for; matrix products, arithmetic and copies ran while one was open for 7% of the time, Pallas kernels for 17%

profile of v5, /device:TPU:0, one launch (start us, length us, event | category | flops | bytes accessed | tf_op | source)
XLA Modules:
  0.0 520.2 jit_solution(11347857461528095795)
XLA Ops:
  5.2 5.1 collective-permute-start.2
  17.4 12.7 %collective-permute-done.1 = bf16[14,8,1024]{2,1,0:T(8,128)(2,1)S(1)} collective-permute-done((bf16[14,8,1024]{2,1,0:T(8,128)(2,1)}, bf16[14,8,1024]{2,1,0:T(8,128)(2,1)S(1)}, u32[]{:S(2)}, u32[]{:S(2)}) %collective-permute-start.1) | collective-permute-done | bytes 229408 | tf_op jit(solution)/shard_map/ppermute | solution.py:902
  34.5 9.1 %collective-permute-done.3.f1_ref = bf16[147,8,128]{2,1,0:T(8,128)(2,1)S(1)} collective-permute-done((bf16[147,8,128]{2,1,0:T(8,128)(2,1)S(1)}, bf16[147,8,128]{2,1,0:T(8,128)(2,1)S(1)}, u32[]{:S(2)}, u32[]{:S(2)}) %collective-permute-start.3) | collective-permute-done | bytes 301088 | tf_op jit(solution)/shard_map/ppermute | solution.py:902
  44.4 9.7 %collective-permute-done.4.f2_ref = bf16[147,8,128]{2,1,0:T(8,128)(2,1)S(1)} collective-permute-done((bf16[147,8,128]{2,1,0:T(8,128)(2,1)S(1)}, bf16[147,8,128]{2,1,0:T(8,128)(2,1)S(1)}, u32[]{:S(2)}, u32[]{:S(2)}) %collective-permute-start.4) | collective-permute-done | bytes 301088 | tf_op jit(solution)/shard_map/ppermute | solution.py:902
  55.6 6.6 %all-to-all-start = ((bf16[4,147,8,256]{3,2,1,0:T(8,128)(2,1)}), bf16[4,147,8,256]{3,2,1,0:T(8,128)(2,1)S(1)}, u32[]{:S(2)}, u32[]{:S(2)}) async-start(bf16[4,147,8,256]{3,2,1,0:T(8,128)(2,1)} %bitcast.228), calls=%async_computation | async-start | bytes 4816896 | tf_op jit(solution)/shard_map/all_to_all | solution.py:1076
  69.4 6.2 %collective-permute-done.6 = bf16[4,5,8,1024]{3,2,1,0:T(8,128)(2,1)S(1)} collective-permute-done((bf16[4,5,8,1024]{3,2,1,0:T(8,128)(2,1)S(1)}, bf16[4,5,8,1024]{3,2,1,0:T(8,128)(2,1)S(1)}, u32[]{:S(2)}, u32[]{:S(2)}) %collective-permute-start.6) | collective-permute-done | bytes 327712 | tf_op jit(solution)/shard_map/ppermute | solution.py:902
  75.6 5.0 collective-permute-done.7
  143.4 4.8 slow_first.1
  148.2 4.4 collective-permute-start.27
  183.4 4.1 slow_second.1
  189.5 5.7 %collective-permute-done.40.refs_3_ = bf16[49,8,384]{2,1,0:T(8,128)(2,1)S(1)} collective-permute-done((bf16[49,8,384]{2,1,0:T(8,128)(2,1)S(1)}, bf16[49,8,384]{2,1,0:T(8,128)(2,1)S(1)}, u32[]{:S(2)}, u32[]{:S(2)}) %collective-permute-start.40) | collective-permute-done | bytes 301088 | tf_op jit(solution)/shard_map/ppermute | solution.py:902
  195.2 7.0 %collective-permute-done.41.refs_4_ = bf16[49,8,384]{2,1,0:T(8,128)(2,1)S(1)} collective-permute-done((bf16[49,8,384]{2,1,0:T(8,128)(2,1)S(1)}, bf16[49,8,384]{2,1,0:T(8,128)(2,1)S(1)}, u32[]{:S(2)}, u32[]{:S(2)}) %collective-permute-start.41) | collective-permute-done | bytes 301088 | tf_op jit(solution)/shard_map/ppermute | solution.py:902
  215.6 4.4 bypass.1
  226.0 8.2 %collective-permute-start.51 = (f32[2,2560]{1,0:T(2,128)S(1)}, f32[2,2560]{1,0:T(2,128)S(1)}, u32[]{:S(2)}, u32[]{:S(2)}) collective-permute-start(f32[2,2560]{1,0:T(2,128)S(1)} %add.365), channel_id=1, source_target_pairs={{0,1},{1,0},{2,3},{3,2},{4,5},{5,4},{6,7},{7,6},{8,9},{9,8},{10,11... | collective-permute-start | bytes 61448 | tf_op jit(solution)/shard_map/ppermute | solution.py:902
  246.8 4.1 fast_out.1
  251.0 7.7 %slow_out.1 = (bf16[147,8,384]{2,1,0:T(8,128)(2,1)S(1)}, bf16[147,8,384]{2,1,0:T(8,128)(2,1)S(1)}, bf16[98,8,384]{2,1,0:T(8,128)(2,1)S(1)}, bf16[49,8,384]{2,1,0...) custom-call(s32[7]{0:T(128)S(1)} %pad_add_fusion.1.table_ref, ...), custom_call_target="tpu_custom_call" | custom-call | bytes 1 | tf_op jit(solution)/shard_map/slow_out/pallas_call | solution.py:125
  285.3 4.6 collective-permute-start.68
  293.1 9.5 %collective-permute-done.69.dhi_ref = f32[15,8,256]{2,1,0:T(8,128)S(1)} collective-permute-done((f32[15,8,256]{2,1,0:T(8,128)S(1)}, f32[15,8,256]{2,1,0:T(8,128)S(1)}, u32[]{:S(2)}, u32[]{:S(2)}) %collective-permute-start.69) | collective-permute-done | bytes 122912 | tf_op jit(solution)/shard_map/ppermute | solution.py:951
  328.4 4.0 slow_second_back.1
  333.3 5.9 %bypass_back.1 = (bf16[147,8,1024]{2,1,0:T(8,128)(2,1)S(1)}, bf16[147,8,1024]{2,1,0:T(8,128)(2,1)S(1)}, f32[147,8,256]{2,1,0:T(8,128)S(1)}) custom-call(s32[7]{0:T(128)S(1)} %pad_add_fusion.1.table_ref, f32[2]{0:T(128)S(1)} %pad_maximum_fusion.13.n_ref, bf16[147,8,1024]{2,1,0:T(8,128)(2,1)S(1)} %get-tuple-element.224.up_ref, ...), custom_call_target="tpu_custom_call" | custom-call | bytes 1 | tf_op jit(solution)/shard_map/bypass_back/pallas_call | solution.py:125
  363.1 4.9 slow_first_back.1
  369.3 5.1 first_slab.1
  385.3 4.7 all-to-all-start.1
  403.7 6.5 %second_slab.1 = bf16[2,4,4,6,8,1024]{5,4,3,2,1,0:T(8,128)(2,1)S(1)} custom-call(s32[7]{0:T(128)S(1)} %pad_add_fusion.1.table_ref, bf16[177,8,256]{2,1,0:T(8,128)(2,1)S(1)} %copy-done.44, bf16[147,8,256]{2,1,0:T(8,128)(2,1)S(1)} %copy-done.46, bf16[147,8,768]{2,1,0:T(8,128)(2,1)S(1)} %copy-done.30, bf16[147,8,1024]{2,1,0:T(8,128)(2,1)S(1)} %get-tuple-element.181.x_ref, ...), custom_call_target="tpu_custom_call" | custom-call | bytes 1 | tf_op jit(solution)/shard_map/second_slab/pallas_call | solution.py:125
  424.9 4.1 collective-permute-done.100
  430.5 7.0 %collective-permute-done.98 = bf16[4,6,8,1024]{3,2,1,0:T(8,128)(2,1)S(1)} collective-permute-done((bf16[4,6,8,1024]{3,2,1,0:T(8,128)(2,1)S(1)}, bf16[4,6,8,1024]{3,2,1,0:T(8,128)(2,1)S(1)}, u32[]{:S(2)}, u32[]{:S(2)}) %collective-permute-start.98) | collective-permute-done | bytes 393248 | tf_op jit(solution)/shard_map/ppermute | solution.py:902
  437.9 4.3 fast_first_back.1
  442.2 4.6 fast_grads.1
  465.7 6.1 %outputs.1 = (bf16[588,8,256]{2,1,0:T(8,128)(2,1)}, bf16[588,32,32]{2,1,0:T(8,128)(2,1)}) custom-call(s32[3]{0:T(128)S(1)} %copy-done.76, bf16[147,8,384]{2,1,0:T(8,128)(2,1)S(1)} %copy-done.42, bf16[147,8,384]{2,1,0:T(8,128)(2,1)S(1)} %collective-permute-done.73.refs_1_, bf16[98,8,384]{2,1,0:T(8,128)(2,1)S(1)} %copy-done.50, ...), custom_call_target="tpu_custom_call" | custom-call | bytes 1 | tf_op jit(solution)/shard_map/outputs/pallas_call | solution.py:125
  471.7 5.5 %collective-permute-done.105 = bf16[12,8,1024]{2,1,0:T(8,128)(2,1)S(1)} collective-permute-done((bf16[12,8,1024]{2,1,0:T(8,128)(2,1)S(1)}, bf16[12,8,1024]{2,1,0:T(8,128)(2,1)S(1)}, u32[]{:S(2)}, u32[]{:S(2)}) %collective-permute-start.105) | collective-permute-done | bytes 196640 | tf_op jit(solution)/shard_map/ppermute | solution.py:902
  477.4 8.7 %all-to-all-start.2 = ((bf16[4,147,8,128]{3,2,1,0:T(8,128)(2,1)}), bf16[4,147,8,128]{3,2,1,0:T(8,128)(2,1)S(1)}, u32[]{:S(2)}, u32[]{:S(2)}) async-start(bf16[4,147,8,128]{3,2,1,0:T(8,128)(2,1)} %get-tuple-element.266), calls=%async_computation.2 | async-start | bytes 2408448 | tf_op jit(solution)/shard_map/all_to_all | solution.py:1076
  515.8 4.1 fast_unpack.1
  (563 shorter events, 322.4 us)
Async XLA Ops:
  10.3 19.7 %collective-permute-start.1 = (bf16[14,8,1024]{2,1,0:T(8,128)(2,1)}, bf16[14,8,1024]{2,1,0:T(8,128)(2,1)S(1)}, u32[]{:S(2)}, u32[]{:S(2)}) collective-permute-start(bf16[14,8,1024]{2,1,0:T(8,128)(2,1)} %weight_slab.1), channel_id=1, source_target_pairs={{0,2},{1,3},{2,0},{3,1},{4,6},{5,7},{6,4},{7,5},{8,10},{9,11},{10,... | collective-permute-start | bytes 688136 | tf_op jit(solution)/shard_map/ppermute | solution.py:902
  10.3 19.7 %collective-permute-start = (bf16[14,8,1024]{2,1,0:T(8,128)(2,1)}, bf16[14,8,1024]{2,1,0:T(8,128)(2,1)S(1)}, u32[]{:S(2)}, u32[]{:S(2)}) collective-permute-start(bf16[14,8,1024]{2,1,0:T(8,128)(2,1)} %weight_slab.1), channel_id=1, source_target_pairs={{0,1},{1,0},{2,3},{3,2},{4,5},{5,4},{6,7},{7,6},{8,9},{9,8},{10,11... | collective-permute-start | bytes 688136 | tf_op jit(solution)/shard_map/ppermute | solution.py:902
  30.1 24.0 %collective-permute-start.4 = (bf16[147,8,128]{2,1,0:T(8,128)(2,1)S(1)}, bf16[147,8,128]{2,1,0:T(8,128)(2,1)S(1)}, u32[]{:S(2)}, u32[]{:S(2)}) collective-permute-start(bf16[147,8,128]{2,1,0:T(8,128)(2,1)S(1)} %get-tuple-element.149), channel_id=1, source_target_pairs={{0,2},{1,3},{2,0},{3,1},{4,6},{5,7},{6,4},{7,5},{8,10},{9,11},{10,... | collective-permute-start | bytes 903176 | tf_op jit(solution)/shard_map/ppermute | solution.py:902
  33.2 21.7 %collective-permute-start.5 = (bf16[147,8,128]{2,1,0:T(8,128)(2,1)S(1)}, bf16[147,8,128]{2,1,0:T(8,128)(2,1)S(1)}, u32[]{:S(2)}, u32[]{:S(2)}) collective-permute-start(bf16[147,8,128]{2,1,0:T(8,128)(2,1)S(1)} %get-tuple-element.150), channel_id=1, source_target_pairs={{0,3},{1,2},{2,1},{3,0},{4,7},{5,6},{6,5},{7,4},{8,11},{9,10},{10,... | collective-permute-start | bytes 903176 | tf_op jit(solution)/shard_map/ppermute | solution.py:902
  55.6 66.5 %all-to-all-start = ((bf16[4,147,8,256]{3,2,1,0:T(8,128)(2,1)}), bf16[4,147,8,256]{3,2,1,0:T(8,128)(2,1)S(1)}, u32[]{:S(2)}, u32[]{:S(2)}) async-start(bf16[4,147,8,256]{3,2,1,0:T(8,128)(2,1)} %bitcast.228), calls=%async_computation | async-start | bytes 4816896 | tf_op jit(solution)/shard_map/all_to_all | solution.py:1076
  68.4 14.5 %collective-permute-start.9 = (bf16[4,5,8,1024]{3,2,1,0:T(8,128)(2,1)S(1)}, bf16[4,5,8,1024]{3,2,1,0:T(8,128)(2,1)S(1)}, u32[]{:S(2)}, u32[]{:S(2)}) collective-permute-start(bf16[4,5,8,1024]{3,2,1,0:T(8,128)(2,1)S(1)} %get-tuple-element.341), channel_id=1, source_target_pairs={{0,4},{4,0},{8,12},{12,8},{16,20},{20,16},{24,28},{28,24},{1,5},{5... | collective-permute-start | bytes 983048 | tf_op jit(solution)/shard_map/ppermute | solution.py:902
  84.2 37.9 %collective-permute-start.16 = (bf16[4,9,8,1024]{3,2,1,0:T(8,128)(2,1)}, bf16[4,9,8,1024]{3,2,1,0:T(8,128)(2,1)}, u32[]{:S(2)}, u32[]{:S(2)}) collective-permute-start(bf16[4,9,8,1024]{3,2,1,0:T(8,128)(2,1)} %pad_maximum_fusion.6), channel_id=1, source_target_pairs={{0,8},{4,12},{8,0},{12,4},{16,24},{20,28},{24,16},{28,20},{1,9},{5... | collective-permute-start | bytes 1769480 | tf_op jit(solution)/shard_map/ppermute | solution.py:902
  85.1 37.0 %collective-permute-start.17 = (bf16[4,9,8,1024]{3,2,1,0:T(8,128)(2,1)}, bf16[4,9,8,1024]{3,2,1,0:T(8,128)(2,1)}, u32[]{:S(2)}, u32[]{:S(2)}) collective-permute-start(bf16[4,9,8,1024]{3,2,1,0:T(8,128)(2,1)} %pad_maximum_fusion.6), channel_id=1, source_target_pairs={{0,16},{4,20},{8,24},{12,28},{16,0},{20,4},{24,8},{28,12},{1,17},{... | collective-permute-start | bytes 1769480 | tf_op jit(solution)/shard_map/ppermute | solution.py:902
  86.3 35.8 %collective-permute-start.18 = (bf16[4,9,8,1024]{3,2,1,0:T(8,128)(2,1)}, bf16[4,9,8,1024]{3,2,1,0:T(8,128)(2,1)}, u32[]{:S(2)}, u32[]{:S(2)}) collective-permute-start(bf16[4,9,8,1024]{3,2,1,0:T(8,128)(2,1)} %pad_maximum_fusion.6), channel_id=1, source_target_pairs={{0,24},{4,28},{8,16},{12,20},{16,8},{20,12},{24,0},{28,4},{1,25},{... | collective-permute-start | bytes 1769480 | tf_op jit(solution)/shard_map/ppermute | solution.py:902
  131.1 29.2 %collective-permute-start.26 = (bf16[98,8,384]{2,1,0:T(8,128)(2,1)}, bf16[98,8,384]{2,1,0:T(8,128)(2,1)S(1)}, u32[]{:S(2)}, u32[]{:S(2)}) collective-permute-start(bf16[98,8,384]{2,1,0:T(8,128)(2,1)} %get-tuple-element.163), channel_id=1, source_target_pairs={{0,2},{1,3},{2,0},{3,1},{4,6},{5,7},{6,4},{7,5},{8,10},{9,11},{10,... | collective-permute-start | bytes 1806344 | tf_op jit(solution)/shard_map/ppermute | solution.py:902
  168.2 34.0 %collective-permute-start.42 = (bf16[147,8,384]{2,1,0:T(8,128)(2,1)S(1)}, bf16[147,8,384]{2,1,0:T(8,128)(2,1)S(1)}, u32[]{:S(2)}, u32[]{:S(2)}) collective-permute-start(bf16[147,8,384]{2,1,0:T(8,128)(2,1)S(1)} %copy-done.94), channel_id=1, source_target_pairs={{0,1},{1,0},{2,3},{3,2},{4,5},{5,4},{6,7},{7,6},{8,9},{9,8},{10,11... | collective-permute-start | bytes 2709512 | tf_op jit(solution)/shard_map/ppermute | solution.py:902
  173.9 21.3 %collective-permute-start.40 = (bf16[49,8,384]{2,1,0:T(8,128)(2,1)S(1)}, bf16[49,8,384]{2,1,0:T(8,128)(2,1)S(1)}, u32[]{:S(2)}, u32[]{:S(2)}) collective-permute-start(bf16[49,8,384]{2,1,0:T(8,128)(2,1)S(1)} %copy-done.103), channel_id=1, source_target_pairs={{0,2},{1,3},{2,0},{3,1},{4,6},{5,7},{6,4},{7,5},{8,10},{9,11},{10,... | collective-permute-start | bytes 903176 | tf_op jit(solution)/shard_map/ppermute | solution.py:902
  176.3 25.9 %collective-permute-start.41 = (bf16[49,8,384]{2,1,0:T(8,128)(2,1)S(1)}, bf16[49,8,384]{2,1,0:T(8,128)(2,1)S(1)}, u32[]{:S(2)}, u32[]{:S(2)}) collective-permute-start(bf16[49,8,384]{2,1,0:T(8,128)(2,1)S(1)} %copy-done.102), channel_id=1, source_target_pairs={{0,3},{1,2},{2,1},{3,0},{4,7},{5,6},{6,5},{7,4},{8,11},{9,10},{10,... | collective-permute-start | bytes 903176 | tf_op jit(solution)/shard_map/ppermute | solution.py:902
  210.1 15.9 %collective-permute-start.50 = (bf16[98,8,384]{2,1,0:T(8,128)(2,1)S(1)}, bf16[98,8,384]{2,1,0:T(8,128)(2,1)S(1)}, u32[]{:S(2)}, u32[]{:S(2)}) collective-permute-start(bf16[98,8,384]{2,1,0:T(8,128)(2,1)S(1)} %copy-done.95), channel_id=1, source_target_pairs={{0,3},{1,2},{2,1},{3,0},{4,7},{5,6},{6,5},{7,4},{8,11},{9,10},{10,... | collective-permute-start | bytes 1806344 | tf_op jit(solution)/shard_map/ppermute | solution.py:902
  271.9 30.7 %collective-permute-start.65 = (bf16[98,8,384]{2,1,0:T(8,128)(2,1)S(1)}, bf16[98,8,384]{2,1,0:T(8,128)(2,1)S(1)}, u32[]{:S(2)}, u32[]{:S(2)}) collective-permute-start(bf16[98,8,384]{2,1,0:T(8,128)(2,1)S(1)} %get-tuple-element.208), channel_id=1, source_target_pairs={{0,2},{1,3},{2,0},{3,1},{4,6},{5,7},{6,4},{7,5},{8,10},{9,11},{10,... | collective-permute-start | bytes 1806344 | tf_op jit(solution)/shard_map/ppermute | solution.py:902
  278.7 23.8 %collective-permute-start.66 = (f32[15,8,512]{2,1,0:T(8,128)S(1)}, f32[15,8,512]{2,1,0:T(8,128)S(1)}, u32[]{:S(2)}, u32[]{:S(2)}) collective-permute-start(f32[15,8,512]{2,1,0:T(8,128)S(1)} %get-tuple-element.209), channel_id=1, source_target_pairs={{0,1},{1,2},{2,3},{4,5},{5,6},{6,7},{8,9},{9,10},{10,11},{12,13},{... | collective-permute-start | bytes 737288 | tf_op jit(solution)/shard_map/ppermute | solution.py:950
  280.0 22.5 %collective-permute-start.67 = (f32[15,8,512]{2,1,0:T(8,128)S(1)}, f32[15,8,512]{2,1,0:T(8,128)S(1)}, u32[]{:S(2)}, u32[]{:S(2)}) collective-permute-start(f32[15,8,512]{2,1,0:T(8,128)S(1)} %get-tuple-element.210), channel_id=1, source_target_pairs={{1,0},{2,1},{3,2},{5,4},{6,5},{7,6},{9,8},{10,9},{11,10},{13,12},{... | collective-permute-start | bytes 737288 | tf_op jit(solution)/shard_map/ppermute | solution.py:951
  313.3 33.4 %collective-permute-start.73 = (bf16[147,8,384]{2,1,0:T(8,128)(2,1)S(1)}, bf16[147,8,384]{2,1,0:T(8,128)(2,1)S(1)}, u32[]{:S(2)}, u32[]{:S(2)}) collective-permute-start(bf16[147,8,384]{2,1,0:T(8,128)(2,1)S(1)} %get-tuple-element.214), channel_id=1, source_target_pairs={{0,1},{1,0},{2,3},{3,2},{4,5},{5,4},{6,7},{7,6},{8,9},{9,8},{10,11... | collective-permute-start | bytes 2709512 | tf_op jit(solution)/shard_map/ppermute | solution.py:902
  313.5 29.1 %collective-permute-start.75 = (bf16[49,8,384]{2,1,0:T(8,128)(2,1)S(1)}, bf16[49,8,384]{2,1,0:T(8,128)(2,1)S(1)}, u32[]{:S(2)}, u32[]{:S(2)}) collective-permute-start(bf16[49,8,384]{2,1,0:T(8,128)(2,1)S(1)} %get-tuple-element.218), channel_id=1, source_target_pairs={{0,3},{1,2},{2,1},{3,0},{4,7},{5,6},{6,5},{7,4},{8,11},{9,10},{10,... | collective-permute-start | bytes 903176 | tf_op jit(solution)/shard_map/ppermute | solution.py:902
  315.2 29.3 %collective-permute-start.74 = (bf16[49,8,384]{2,1,0:T(8,128)(2,1)S(1)}, bf16[49,8,384]{2,1,0:T(8,128)(2,1)S(1)}, u32[]{:S(2)}, u32[]{:S(2)}) collective-permute-start(bf16[49,8,384]{2,1,0:T(8,128)(2,1)S(1)} %get-tuple-element.216), channel_id=1, source_target_pairs={{0,2},{1,3},{2,0},{3,1},{4,6},{5,7},{6,4},{7,5},{8,10},{9,11},{10,... | collective-permute-start | bytes 903176 | tf_op jit(solution)/shard_map/ppermute | solution.py:902
  354.5 21.6 %collective-permute-start.83 = (bf16[98,8,384]{2,1,0:T(8,128)(2,1)S(1)}, bf16[98,8,384]{2,1,0:T(8,128)(2,1)S(1)}, u32[]{:S(2)}, u32[]{:S(2)}) collective-permute-start(bf16[98,8,384]{2,1,0:T(8,128)(2,1)S(1)} %get-tuple-element.228), channel_id=1, source_target_pairs={{0,3},{1,2},{2,1},{3,0},{4,7},{5,6},{6,5},{7,4},{8,11},{9,10},{10,... | collective-permute-start | bytes 1806344 | tf_op jit(solution)/shard_map/ppermute | solution.py:902
  385.3 76.6 %all-to-all-start.1 = ((bf16[4,147,8,256]{3,2,1,0:T(8,128)(2,1)}), bf16[4,147,8,256]{3,2,1,0:T(8,128)(2,1)}, u32[]{:S(2)}, u32[]{:S(2)}) async-start(bf16[4,147,8,256]{3,2,1,0:T(8,128)(2,1)} %copy-done.28), calls=%async_computation.1 | async-start | bytes 4816896 | tf_op jit(solution)/shard_map/all_to_all | solution.py:1076
  417.5 19.9 %collective-permute-start.98 = (bf16[4,6,8,1024]{3,2,1,0:T(8,128)(2,1)S(1)}, bf16[4,6,8,1024]{3,2,1,0:T(8,128)(2,1)S(1)}, u32[]{:S(2)}, u32[]{:S(2)}) collective-permute-start(bf16[4,6,8,1024]{3,2,1,0:T(8,128)(2,1)S(1)} %get-tuple-element.326), channel_id=1, source_target_pairs={{0,8},{4,12},{8,0},{12,4},{16,24},{20,28},{24,16},{28,20},{1,9},{5... | collective-permute-start | bytes 1179656 | tf_op jit(solution)/shard_map/ppermute | solution.py:902
  419.0 18.4 %collective-permute-start.99 = (bf16[4,6,8,1024]{3,2,1,0:T(8,128)(2,1)S(1)}, bf16[4,6,8,1024]{3,2,1,0:T(8,128)(2,1)S(1)}, u32[]{:S(2)}, u32[]{:S(2)}) collective-permute-start(bf16[4,6,8,1024]{3,2,1,0:T(8,128)(2,1)S(1)} %get-tuple-element.328), channel_id=1, source_target_pairs={{0,16},{4,20},{8,24},{12,28},{16,0},{20,4},{24,8},{28,12},{1,17},{... | collective-permute-start | bytes 1179656 | tf_op jit(solution)/shard_map/ppermute | solution.py:902
  422.8 28.5 %collective-permute-start.101 = (bf16[4,6,8,1024]{3,2,1,0:T(8,128)(2,1)S(1)}, bf16[4,6,8,1024]{3,2,1,0:T(8,128)(2,1)S(1)}, u32[]{:S(2)}, u32[]{:S(2)}) collective-permute-start(bf16[4,6,8,1024]{3,2,1,0:T(8,128)(2,1)S(1)} %get-tuple-element.323), channel_id=1, source_target_pairs={{0,8},{4,12},{8,0},{12,4},{16,24},{20,28},{24,16},{28,20},{1,9},{5... | collective-permute-start | bytes 1179656 | tf_op jit(solution)/shard_map/ppermute | solution.py:902
  423.7 27.7 %collective-permute-start.102 = (bf16[4,6,8,1024]{3,2,1,0:T(8,128)(2,1)S(1)}, bf16[4,6,8,1024]{3,2,1,0:T(8,128)(2,1)S(1)}, u32[]{:S(2)}, u32[]{:S(2)}) collective-permute-start(bf16[4,6,8,1024]{3,2,1,0:T(8,128)(2,1)S(1)} %get-tuple-element.325), channel_id=1, source_target_pairs={{0,16},{4,20},{8,24},{12,28},{16,0},{20,4},{24,8},{28,12},{1,17},{... | collective-permute-start | bytes 1179656 | tf_op jit(solution)/shard_map/ppermute | solution.py:902
  429.0 24.4 %collective-permute-start.103 = (bf16[4,6,8,1024]{3,2,1,0:T(8,128)(2,1)S(1)}, bf16[4,6,8,1024]{3,2,1,0:T(8,128)(2,1)S(1)}, u32[]{:S(2)}, u32[]{:S(2)}) collective-permute-start(bf16[4,6,8,1024]{3,2,1,0:T(8,128)(2,1)S(1)} %get-tuple-element.324), channel_id=1, source_target_pairs={{0,24},{4,28},{8,16},{12,20},{16,8},{20,12},{24,0},{28,4},{1,25},{... | collective-permute-start | bytes 1179656 | tf_op jit(solution)/shard_map/ppermute | solution.py:902
  453.7 18.1 %collective-permute-start.104 = (bf16[12,8,1024]{2,1,0:T(8,128)(2,1)S(1)}, bf16[12,8,1024]{2,1,0:T(8,128)(2,1)S(1)}, u32[]{:S(2)}, u32[]{:S(2)}) collective-permute-start(bf16[12,8,1024]{2,1,0:T(8,128)(2,1)S(1)} %get-tuple-element.334), channel_id=1, source_target_pairs={{0,1},{1,0},{2,3},{3,2},{4,5},{5,4},{6,7},{7,6},{8,9},{9,8},{10,11... | collective-permute-start | bytes 589832 | tf_op jit(solution)/shard_map/ppermute | solution.py:902
  455.7 21.5 %collective-permute-start.105 = (bf16[12,8,1024]{2,1,0:T(8,128)(2,1)S(1)}, bf16[12,8,1024]{2,1,0:T(8,128)(2,1)S(1)}, u32[]{:S(2)}, u32[]{:S(2)}) collective-permute-start(bf16[12,8,1024]{2,1,0:T(8,128)(2,1)S(1)} %get-tuple-element.335), channel_id=1, source_target_pairs={{0,2},{1,3},{2,0},{3,1},{4,6},{5,7},{6,4},{7,5},{8,10},{9,11},{10,... | collective-permute-start | bytes 589832 | tf_op jit(solution)/shard_map/ppermute | solution.py:902
  458.1 19.2 %collective-permute-start.106 = (bf16[12,8,1024]{2,1,0:T(8,128)(2,1)S(1)}, bf16[12,8,1024]{2,1,0:T(8,128)(2,1)S(1)}, u32[]{:S(2)}, u32[]{:S(2)}) collective-permute-start(bf16[12,8,1024]{2,1,0:T(8,128)(2,1)S(1)} %get-tuple-element.333), channel_id=1, source_target_pairs={{0,3},{1,2},{2,1},{3,0},{4,7},{5,6},{6,5},{7,4},{8,11},{9,10},{10,... | collective-permute-start | bytes 589832 | tf_op jit(solution)/shard_map/ppermute | solution.py:902
  461.8 24.3 %collective-permute-start.110 = (bf16[68,8,128]{2,1,0:T(8,128)(2,1)S(1)}, bf16[68,8,128]{2,1,0:T(8,128)(2,1)}, u32[]{:S(2)}, u32[]{:S(2)}) collective-permute-start(bf16[68,8,128]{2,1,0:T(8,128)(2,1)S(1)} %add_convert_fusion.2), channel_id=1, source_target_pairs={{0,4},{4,0},{8,12},{12,8},{16,20},{20,16},{24,28},{28,24},{1,5},{5... | collective-permute-start | bytes 417800 | tf_op jit(solution)/shard_map/ppermute | solution.py:902
  477.4 38.4 %all-to-all-start.2 = ((bf16[4,147,8,128]{3,2,1,0:T(8,128)(2,1)}), bf16[4,147,8,128]{3,2,1,0:T(8,128)(2,1)S(1)}, u32[]{:S(2)}, u32[]{:S(2)}) async-start(bf16[4,147,8,128]{3,2,1,0:T(8,128)(2,1)} %get-tuple-element.266), calls=%async_computation.2 | async-start | bytes 2408448 | tf_op jit(solution)/shard_map/all_to_all | solution.py:1076
  (200 other events, 2056.5 us)

commit v6 on v5

--- a/solution.py
+++ b/solution.py
@@ -231,8 +231,8 @@
     out_ref[13, :, 256:1024] = jnp.zeros((8, 768), BF16)
     blank = jnp.zeros((2, 128), F32)
     half = jnp.zeros((2, 64), F32)
-    inner = jnp.concatenate([jnp.concatenate([v, half], axis=1) for v in (ln_ref[...], sn_ref[0:2], sn_ref[2:4])] + [blank], axis=0)
-    outer = jnp.concatenate([on_ref[:, 0:128], on_ref[:, 128:256]], axis=0)
+    inner = jnp.concatenate([jnp.concatenate([v, half], axis=1) for v in (ln_ref[...], sn_ref[0], sn_ref[1])] + [blank], axis=0)
+    outer = jnp.concatenate([on_ref[k, :, 128 * h : 128 * h + 128] for h in range(2) for k in range(2)], axis=0)
     for i, v in enumerate((inner, outer)):
         high = v.astype(BF16)
         for k, part in ((i, high), (2 + i, (v - high.astype(F32)).astype(BF16))):
@@ -932,16 +932,18 @@
     return add(tree, near, far, both)
 
 
-def everywhere(tree, sizes, bulk=None):
+def everywhere(tree, sizes, bulk=None, chan_last=False):
     dp, chan = sizes["dp"], sizes["chan"]
     first, *others = stages(dp, True)
-    tree = butterfly(tree, "dp", dp, first)
+    before, behind = (others, []) if chan_last else ([], others)
+    for bits in [first, *before]:
+        tree = butterfly(tree, "dp", dp, bits)
     if bulk is not None:
         tree = after(tree, bulk)
     for bits in stages(chan, False):
         tree = butterfly(tree, "chan", chan, bits)
     passed = tree
-    for bits in others:
+    for bits in behind:
         tree = butterfly(tree, "dp", dp, bits)
     return tree, passed
 
@@ -1100,7 +1102,7 @@
     spatial_t = slow_spatial.reshape(9, slow_spatial.shape[2], -1).transpose(0, 2, 1)
     params = [red_t, lred_t, lat_t, slow_expand, shortcut, lateral_shortcut, spatial_t]
     scratch = [(3, 8, wide_in), (3, 8, mid), (5, 8, 128), (8, wide_in), (32, wide_in), (8, wide_in), (9, 8, mid)]
-    small = [lateral_norm, slow_inner_norm.reshape(4, -1), slow_outer_norm.reshape(4, -1)]
+    small = [lateral_norm, slow_inner_norm, slow_outer_norm]
     any_spec, vmem_spec = pl.BlockSpec(memory_space=pl.ANY), pl.BlockSpec(memory_space=pltpu.VMEM)
     slab = pl.pallas_call(
         weight_slab_kernel,
@@ -1113,9 +1115,10 @@
     )(ids, *params, *small)
     slabs = at_once([slab] * ways)
     fx_pieces = at_once(after(blocks_of(packed(after(fast_input, slab))), slabs))
-    xs = all_to_all(after(split(slow_input), (slabs, fx_pieces)))
     early, late = jnp.stack([v[0:5] for v in slabs]), jnp.stack([v[5:14] for v in slabs])
-    own_slabs, other_slabs = gather_cores(gather_chips(early, sizes), sizes)
+    early = gather_chips(early, sizes)
+    xs = all_to_all(after(split(slow_input), (fx_pieces, early)))
+    own_slabs, other_slabs = gather_cores(early, sizes)
     fr_t = fast_reduce.transpose(0, 2, 1)
     red_w, lred_w, w_first, w_fsp, w_fex, fin_g, fout_g, mid_g, out_g = call(
         weights_kernel,
@@ -1169,7 +1172,7 @@
     )
     exp_w, short_w, lshort_w = (v.reshape(-1, wide_in) for v in (exp_w, short_w, lshort_w))
     spat_w = spat_w.reshape(9, mid, mid)
-    sums1, passed = everywhere(sums1, sizes, (xs, fa_lo, fa_hi, cots, late))
+    sums1, passed = everywhere(sums1, sizes, (xs, fa_lo, fa_hi, cots, late), True)
     send_parts(cots, (2,), passed)
     fast_pad = [pltpu.VMEM((3, ext, 8, 128), F32)]
     slow_pad = [pltpu.VMEM((3, ext, 8, mid), F32)]
@@ -1339,14 +1342,16 @@
         copy_kernel, [shape((places, slow_t, slow_part), BF16)], [dslow.reshape(places, slow_t, slow_part)], name="slow_grad"
     )
     slow_output, fast_output = unpacked(after(outs, slow_input_grad))
-    slabs = scatter_chan(jnp.concatenate([slab1, slab2], axis=1), sizes, chan, (slow_output, fast_output))
+    slab1 = scatter_chan(slab1, sizes, chan, dfirst)
+    slab2 = scatter_chan(after(slab2, slab1), sizes, chan, slab1)
+    slabs = jnp.concatenate([slab1, slab2])
     small = [jnp.concatenate([pick(g_lat, chan ^ k, 0), g_fast]) for k in range(ways)]
     small = add(*at_once(small))
     dfast = all_to_all(after(dfast, (dslow, slabs, small)))
     for bits in stages(sizes["dp"], True):
         small = butterfly(small, "dp", sizes["dp"], bits)
     g_lat, g_fast = small[0:40].astype(F32), small[40:68].astype(F32)
-    own_slabs, other_slabs = gather_cores(gather_chips(slabs, sizes), sizes)
+    own_slabs, other_slabs = gather_cores(after(gather_chips(slabs, sizes), (slow_output, fast_output)), sizes)
     g_exp, g_short, g_lshort, g_red, g_lred, g_spat = call(
         grads_kernel,
         [shape((8, 8, wide_in)), shape((8, 4, 8, wide_in)), shape((8, 8, wide_in)), shape((3, 8, 8, wide_in)), shape((3, 8, 8, mid)),

time: 527 us -> 523 us (level)
    ppermute x113 -> x116, waiting for transfers between devices: 147 us -> 138 us  [swap(): return jax.tree.map(lambda v: lax.ppermute(v, axis, pairs), tree)]
    ppermute x4, waiting for transfers between devices: 16.3 us -> 21.6 us  [halos(): high = lax.ppermute(first, 'chan', [(i + 1, i) for i in range(count - 1)])]
    ppermute x113 -> x116, starting transfers between devices: 128 us -> 132 us  [swap(): return jax.tree.map(lambda v: lax.ppermute(v, axis, pairs), tree)]
    unnamed x217 -> x193, local copies, waits for them, and re-layouts: 35.6 us -> 37.8 us
  transfers between devices with their start and end apart: 124 -> 127, of which waited for: 63 -> 57; matrix products, arithmetic and copies ran while one was open for 7% -> 6% of each run, Pallas kernels for 17% -> 18%
where the time goes in v6:
time: 523 us; the launch traced here: 516 us
  starting transfers between devices  169 us (32%)
  waiting for transfers between devices  163 us (31%)
  Pallas kernels  112 us (21%)
  local copies, waits for them, and re-layouts  52.4 us (10%)
  other arithmetic  17.3 us (3%)
    ppermute x116, waiting for transfers between devices, swap(): return jax.tree.map(lambda v: lax.ppermute(v, axis, pairs), tree)  138 us
    ppermute x116, starting transfers between devices, swap(): return jax.tree.map(lambda v: lax.ppermute(v, axis, pairs), tree)  132 us
    pallas_call x24, Pallas kernels, call(): pl.pallas_call(kernel, out_shape=tuple(outs), in_specs=specs, out_specs=t...  99 us
    unnamed x193, local copies, waits for them, and re-layouts  37.8 us
    ppermute x4, waiting for transfers between devices, halos(): high = lax.ppermute(first, 'chan', [(i + 1, i) for i in range(count - 1)])  21.6 us
    ppermute x4, starting transfers between devices, halos(): low = lax.ppermute(last, 'chan', [(i, i + 1) for i in range(count - 1)])  15.9 us
    all_to_all x3, starting transfers between devices, all_to_all(): return lax.all_to_all(v, 'chan', 0, 0, tiled=True)  14.8 us
  transfers between devices with their start and end apart: 127, of which 57 were waited for; matrix products, arithmetic and copies ran while one was open for 6% of the time, Pallas kernels for 18%

profile of v6, /device:TPU:0, one launch (start us, length us, event | category | flops | bytes accessed | tf_op | source)
XLA Modules:
  0.0 516.5 jit_solution(11165125366088184158)
XLA Ops:
  3.9 5.1 collective-permute-start.2
  16.3 12.5 %collective-permute-done.1 = bf16[14,8,1024]{2,1,0:T(8,128)(2,1)S(1)} collective-permute-done((bf16[14,8,1024]{2,1,0:T(8,128)(2,1)}, bf16[14,8,1024]{2,1,0:T(8,128)(2,1)S(1)}, u32[]{:S(2)}, u32[]{:S(2)}) %collective-permute-start.1) | collective-permute-done | bytes 229408 | tf_op jit(solution)/shard_map/ppermute | solution.py:902
  35.5 4.2 collective-permute-done.3.f1_ref
  41.3 14.8 %collective-permute-done.4.f2_ref = bf16[147,8,128]{2,1,0:T(8,128)(2,1)S(1)} collective-permute-done((bf16[147,8,128]{2,1,0:T(8,128)(2,1)S(1)}, bf16[147,8,128]{2,1,0:T(8,128)(2,1)S(1)}, u32[]{:S(2)}, u32[]{:S(2)}) %collective-permute-start.4) | collective-permute-done | bytes 301088 | tf_op jit(solution)/shard_map/ppermute | solution.py:902
  57.6 6.6 %all-to-all-start = ((bf16[4,147,8,256]{3,2,1,0:T(8,128)(2,1)}), bf16[4,147,8,256]{3,2,1,0:T(8,128)(2,1)S(1)}, u32[]{:S(2)}, u32[]{:S(2)}) async-start(bf16[4,147,8,256]{3,2,1,0:T(8,128)(2,1)} %bitcast.234), calls=%async_computation | async-start | bytes 4816896 | tf_op jit(solution)/shard_map/all_to_all | solution.py:1078
  98.3 6.7 %collective-permute-done.14 = f32[2,384]{1,0:T(2,128)S(1)} collective-permute-done((f32[2,384]{1,0:T(2,128)S(1)}, f32[2,384]{1,0:T(2,128)S(1)}, u32[]{:S(2)}, u32[]{:S(2)}) %collective-permute-start.14) | collective-permute-done | bytes 3104 | tf_op jit(solution)/shard_map/ppermute | solution.py:902
  115.4 4.2 collective-permute-done.18.hi_ref
  136.7 4.8 slow_first.1
  141.5 4.3 collective-permute-start.27
  149.6 8.1 %collective-permute-done.28.hi_ref = f32[15,8,256]{2,1,0:T(8,128)S(1)} collective-permute-done((f32[15,8,256]{2,1,0:T(8,128)S(1)}, f32[15,8,256]{2,1,0:T(8,128)S(1)}, u32[]{:S(2)}, u32[]{:S(2)}) %collective-permute-start.28) | collective-permute-done | bytes 122912 | tf_op jit(solution)/shard_map/ppermute | solution.py:953
  187.2 4.8 collective-permute-done.40.refs_3_
  192.0 7.1 %collective-permute-done.41.refs_4_ = bf16[49,8,384]{2,1,0:T(8,128)(2,1)S(1)} collective-permute-done((bf16[49,8,384]{2,1,0:T(8,128)(2,1)S(1)}, bf16[49,8,384]{2,1,0:T(8,128)(2,1)S(1)}, u32[]{:S(2)}, u32[]{:S(2)}) %collective-permute-start.41) | collective-permute-done | bytes 301088 | tf_op jit(solution)/shard_map/ppermute | solution.py:902
  212.6 4.4 bypass.1
  222.9 8.6 %collective-permute-start.51 = (f32[2,2560]{1,0:T(2,128)S(1)}, f32[2,2560]{1,0:T(2,128)S(1)}, u32[]{:S(2)}, u32[]{:S(2)}) collective-permute-start(f32[2,2560]{1,0:T(2,128)S(1)} %add.378), channel_id=1, source_target_pairs={{0,1},{1,0},{2,3},{3,2},{4,5},{5,4},{6,7},{7,6},{8,9},{9,8},{10,11... | collective-permute-start | bytes 61448 | tf_op jit(solution)/shard_map/ppermute | solution.py:902
  246.5 4.7 fast_out.1
  251.2 9.4 %slow_out.1 = (bf16[147,8,384]{2,1,0:T(8,128)(2,1)S(1)}, bf16[147,8,384]{2,1,0:T(8,128)(2,1)S(1)}, bf16[98,8,384]{2,1,0:T(8,128)(2,1)S(1)}, bf16[49,8,384]{2,1,0...) custom-call(s32[7]{0:T(128)S(1)} %pad_add_fusion.1.table_ref, ...), custom_call_target="tpu_custom_call" | custom-call | bytes 1 | tf_op jit(solution)/shard_map/slow_out/pallas_call | solution.py:125
  285.9 4.6 collective-permute-start.68
  293.7 9.4 %collective-permute-done.69.dhi_ref = f32[15,8,256]{2,1,0:T(8,128)S(1)} collective-permute-done((f32[15,8,256]{2,1,0:T(8,128)S(1)}, f32[15,8,256]{2,1,0:T(8,128)S(1)}, u32[]{:S(2)}, u32[]{:S(2)}) %collective-permute-start.69) | collective-permute-done | bytes 122912 | tf_op jit(solution)/shard_map/ppermute | solution.py:953
  303.9 5.2 %collective-permute-start.70 = (f32[2,384]{1,0:T(2,128)S(1)}, f32[2,384]{1,0:T(2,128)S(1)}, u32[]{:S(2)}, u32[]{:S(2)}) collective-permute-start(f32[2,384]{1,0:T(2,128)S(1)} %add.392), channel_id=1, source_target_pairs={{0,1},{1,0},{2,3},{3,2},{4,5},{5,4},{6,7},{7,6},{8,9},{9,8},{10,11... | collective-permute-start | bytes 9224 | tf_op jit(solution)/shard_map/ppermute | solution.py:902
  322.1 4.1 collective-permute-done.78
  333.9 5.9 %bypass_back.1 = (bf16[147,8,1024]{2,1,0:T(8,128)(2,1)S(1)}, bf16[147,8,1024]{2,1,0:T(8,128)(2,1)S(1)}, f32[147,8,256]{2,1,0:T(8,128)S(1)}) custom-call(s32[7]{0:T(128)S(1)} %pad_add_fusion.1.table_ref, f32[2]{0:T(128)S(1)} %pad_maximum_fusion.14.n_ref, bf16[147,8,1024]{2,1,0:T(8,128)(2,1)S(1)} %get-tuple-element.232.up_ref, ...), custom_call_target="tpu_custom_call" | custom-call | bytes 1 | tf_op jit(solution)/shard_map/bypass_back/pallas_call | solution.py:125
  363.3 4.9 slow_first_back.1
  376.4 5.1 first_slab.1
  389.8 4.7 all-to-all-start.1
  409.6 6.5 %second_slab.1 = bf16[2,4,4,6,8,1024]{5,4,3,2,1,0:T(8,128)(2,1)S(1)} custom-call(s32[7]{0:T(128)S(1)} %pad_add_fusion.1.table_ref, bf16[177,8,256]{2,1,0:T(8,128)(2,1)S(1)} %copy-done.48, bf16[147,8,256]{2,1,0:T(8,128)(2,1)S(1)} %copy-done.52, bf16[147,8,768]{2,1,0:T(8,128)(2,1)S(1)} %copy-done.33, bf16[147,8,1024]{2,1,0:T(8,128)(2,1)S(1)} %get-tuple-element.189.x_ref, ...), custom_call_target="tpu_custom_call" | custom-call | bytes 1 | tf_op jit(solution)/shard_map/second_slab/pallas_call | solution.py:125
  433.8 4.3 fast_first_back.1
  438.1 4.6 fast_grads.1
  445.0 10.9 %collective-permute-done.102 = bf16[6,8,1024]{2,1,0:T(8,128)(2,1)S(1)} collective-permute-done((bf16[6,8,1024]{2,1,0:T(8,128)(2,1)S(1)}, bf16[6,8,1024]{2,1,0:T(8,128)(2,1)S(1)}, u32[]{:S(2)}, u32[]{:S(2)}) %collective-permute-start.102) | collective-permute-done | bytes 98336 | tf_op jit(solution)/shard_map/ppermute | solution.py:902
  465.4 8.1 %collective-permute-done.111 = bf16[68,8,128]{2,1,0:T(8,128)(2,1)S(1)} collective-permute-done((bf16[68,8,128]{2,1,0:T(8,128)(2,1)S(1)}, bf16[68,8,128]{2,1,0:T(8,128)(2,1)S(1)}, u32[]{:S(2)}, u32[]{:S(2)}) %collective-permute-start.111) | collective-permute-done | bytes 139296 | tf_op jit(solution)/shard_map/ppermute | solution.py:902
  473.6 4.9 collective-permute-done.108
  500.3 6.6 %outputs.1 = (bf16[588,8,256]{2,1,0:T(8,128)(2,1)}, bf16[588,32,32]{2,1,0:T(8,128)(2,1)}) custom-call(s32[3]{0:T(128)S(1)} %copy-done.73, bf16[147,8,384]{2,1,0:T(8,128)(2,1)S(1)} %copy-done.44, bf16[147,8,384]{2,1,0:T(8,128)(2,1)S(1)} %copy-done.46, bf16[98,8,384]{2,1,0:T(8,128)(2,1)S(1)} %copy-done.56, bf16[49,8,384]{2,1,0:T(8,128)(2,1)S(1)} %copy-done.66, ...), custom_call_target="tpu_custom_call" | custom-call | bytes 1 | tf_op jit(solution)/shard_map/outputs/pallas_call | solution.py:125
  512.1 4.1 fast_unpack.1
  (547 shorter events, 309.2 us)
Async XLA Ops:
  9.0 19.7 %collective-permute-start.1 = (bf16[14,8,1024]{2,1,0:T(8,128)(2,1)}, bf16[14,8,1024]{2,1,0:T(8,128)(2,1)S(1)}, u32[]{:S(2)}, u32[]{:S(2)}) collective-permute-start(bf16[14,8,1024]{2,1,0:T(8,128)(2,1)} %weight_slab.1), channel_id=1, source_target_pairs={{0,2},{1,3},{2,0},{3,1},{4,6},{5,7},{6,4},{7,5},{8,10},{9,11},{10,... | collective-permute-start | bytes 688136 | tf_op jit(solution)/shard_map/ppermute | solution.py:902
  9.0 19.7 %collective-permute-start = (bf16[14,8,1024]{2,1,0:T(8,128)(2,1)}, bf16[14,8,1024]{2,1,0:T(8,128)(2,1)S(1)}, u32[]{:S(2)}, u32[]{:S(2)}) collective-permute-start(bf16[14,8,1024]{2,1,0:T(8,128)(2,1)} %weight_slab.1), channel_id=1, source_target_pairs={{0,1},{1,0},{2,3},{3,2},{4,5},{5,4},{6,7},{7,6},{8,9},{9,8},{10,11... | collective-permute-start | bytes 688136 | tf_op jit(solution)/shard_map/ppermute | solution.py:902
  29.6 28.0 %collective-permute-start.6 = (bf16[4,5,8,1024]{3,2,1,0:T(8,128)(2,1)S(1)}, bf16[4,5,8,1024]{3,2,1,0:T(8,128)(2,1)}, u32[]{:S(2)}, u32[]{:S(2)}) collective-permute-start(bf16[4,5,8,1024]{3,2,1,0:T(8,128)(2,1)S(1)} %get-tuple-element.360), channel_id=1, source_target_pairs={{0,8},{4,12},{8,0},{12,4},{16,24},{20,28},{24,16},{28,20},{1,9},{5... | collective-permute-start | bytes 983048 | tf_op jit(solution)/shard_map/ppermute | solution.py:902
  31.1 26.4 %collective-permute-start.7 = (bf16[4,5,8,1024]{3,2,1,0:T(8,128)(2,1)S(1)}, bf16[4,5,8,1024]{3,2,1,0:T(8,128)(2,1)}, u32[]{:S(2)}, u32[]{:S(2)}) collective-permute-start(bf16[4,5,8,1024]{3,2,1,0:T(8,128)(2,1)S(1)} %get-tuple-element.360), channel_id=1, source_target_pairs={{0,16},{4,20},{8,24},{12,28},{16,0},{20,4},{24,8},{28,12},{1,17},{... | collective-permute-start | bytes 983048 | tf_op jit(solution)/shard_map/ppermute | solution.py:902
  32.7 24.9 %collective-permute-start.8 = (bf16[4,5,8,1024]{3,2,1,0:T(8,128)(2,1)S(1)}, bf16[4,5,8,1024]{3,2,1,0:T(8,128)(2,1)}, u32[]{:S(2)}, u32[]{:S(2)}) collective-permute-start(bf16[4,5,8,1024]{3,2,1,0:T(8,128)(2,1)S(1)} %get-tuple-element.360), channel_id=1, source_target_pairs={{0,24},{4,28},{8,16},{12,20},{16,8},{20,12},{24,0},{28,4},{1,25},{... | collective-permute-start | bytes 983048 | tf_op jit(solution)/shard_map/ppermute | solution.py:902
  33.1 23.0 %collective-permute-start.4 = (bf16[147,8,128]{2,1,0:T(8,128)(2,1)S(1)}, bf16[147,8,128]{2,1,0:T(8,128)(2,1)S(1)}, u32[]{:S(2)}, u32[]{:S(2)}) collective-permute-start(bf16[147,8,128]{2,1,0:T(8,128)(2,1)S(1)} %get-tuple-element.157), channel_id=1, source_target_pairs={{0,2},{1,3},{2,0},{3,1},{4,6},{5,7},{6,4},{7,5},{8,10},{9,11},{10,... | collective-permute-start | bytes 903176 | tf_op jit(solution)/shard_map/ppermute | solution.py:902
  39.7 17.1 %collective-permute-start.5 = (bf16[147,8,128]{2,1,0:T(8,128)(2,1)S(1)}, bf16[147,8,128]{2,1,0:T(8,128)(2,1)S(1)}, u32[]{:S(2)}, u32[]{:S(2)}) collective-permute-start(bf16[147,8,128]{2,1,0:T(8,128)(2,1)S(1)} %get-tuple-element.158), channel_id=1, source_target_pairs={{0,3},{1,2},{2,1},{3,0},{4,7},{5,6},{6,5},{7,4},{8,11},{9,10},{10,... | collective-permute-start | bytes 903176 | tf_op jit(solution)/shard_map/ppermute | solution.py:902
  57.6 62.7 %all-to-all-start = ((bf16[4,147,8,256]{3,2,1,0:T(8,128)(2,1)}), bf16[4,147,8,256]{3,2,1,0:T(8,128)(2,1)S(1)}, u32[]{:S(2)}, u32[]{:S(2)}) async-start(bf16[4,147,8,256]{3,2,1,0:T(8,128)(2,1)} %bitcast.234), calls=%async_computation | async-start | bytes 4816896 | tf_op jit(solution)/shard_map/all_to_all | solution.py:1078
  76.6 43.6 %collective-permute-start.19 = (bf16[4,9,8,1024]{3,2,1,0:T(8,128)(2,1)}, bf16[4,9,8,1024]{3,2,1,0:T(8,128)(2,1)}, u32[]{:S(2)}, u32[]{:S(2)}) collective-permute-start(bf16[4,9,8,1024]{3,2,1,0:T(8,128)(2,1)} %pad_maximum_fusion.6), channel_id=1, source_target_pairs={{0,8},{4,12},{8,0},{12,4},{16,24},{20,28},{24,16},{28,20},{1,9},{5... | collective-permute-start | bytes 1769480 | tf_op jit(solution)/shard_map/ppermute | solution.py:902
  78.2 42.0 %collective-permute-start.20 = (bf16[4,9,8,1024]{3,2,1,0:T(8,128)(2,1)}, bf16[4,9,8,1024]{3,2,1,0:T(8,128)(2,1)}, u32[]{:S(2)}, u32[]{:S(2)}) collective-permute-start(bf16[4,9,8,1024]{3,2,1,0:T(8,128)(2,1)} %pad_maximum_fusion.6), channel_id=1, source_target_pairs={{0,16},{4,20},{8,24},{12,28},{16,0},{20,4},{24,8},{28,12},{1,17},{... | collective-permute-start | bytes 1769480 | tf_op jit(solution)/shard_map/ppermute | solution.py:902
  79.7 40.5 %collective-permute-start.21 = (bf16[4,9,8,1024]{3,2,1,0:T(8,128)(2,1)}, bf16[4,9,8,1024]{3,2,1,0:T(8,128)(2,1)}, u32[]{:S(2)}, u32[]{:S(2)}) collective-permute-start(bf16[4,9,8,1024]{3,2,1,0:T(8,128)(2,1)} %pad_maximum_fusion.6), channel_id=1, source_target_pairs={{0,24},{4,28},{8,16},{12,20},{16,8},{20,12},{24,0},{28,4},{1,25},{... | collective-permute-start | bytes 1769480 | tf_op jit(solution)/shard_map/ppermute | solution.py:902
  129.5 28.2 %collective-permute-start.26 = (bf16[98,8,384]{2,1,0:T(8,128)(2,1)}, bf16[98,8,384]{2,1,0:T(8,128)(2,1)}, u32[]{:S(2)}, u32[]{:S(2)}) collective-permute-start(bf16[98,8,384]{2,1,0:T(8,128)(2,1)} %get-tuple-element.171), channel_id=1, source_target_pairs={{0,2},{1,3},{2,0},{3,1},{4,6},{5,7},{6,4},{7,5},{8,10},{9,11},{10,... | collective-permute-start | bytes 1806344 | tf_op jit(solution)/shard_map/ppermute | solution.py:902
  147.6 17.5 %collective-permute-start.35 = (bf16[4,9,8,1024]{3,2,1,0:T(8,128)(2,1)}, bf16[4,9,8,1024]{3,2,1,0:T(8,128)(2,1)S(1)}, u32[]{:S(2)}, u32[]{:S(2)}) collective-permute-start(bf16[4,9,8,1024]{3,2,1,0:T(8,128)(2,1)} %pad_maximum_fusion.6), channel_id=1, source_target_pairs={{0,4},{4,0},{8,12},{12,8},{16,20},{20,16},{24,28},{28,24},{1,5},{5... | collective-permute-start | bytes 1769480 | tf_op jit(solution)/shard_map/ppermute | solution.py:902
  165.0 34.1 %collective-permute-start.42 = (bf16[147,8,384]{2,1,0:T(8,128)(2,1)S(1)}, bf16[147,8,384]{2,1,0:T(8,128)(2,1)S(1)}, u32[]{:S(2)}, u32[]{:S(2)}) collective-permute-start(bf16[147,8,384]{2,1,0:T(8,128)(2,1)S(1)} %copy-done.84), channel_id=1, source_target_pairs={{0,1},{1,0},{2,3},{3,2},{4,5},{5,4},{6,7},{7,6},{8,9},{9,8},{10,11... | collective-permute-start | bytes 2709512 | tf_op jit(solution)/shard_map/ppermute | solution.py:902
  170.8 21.2 %collective-permute-start.40 = (bf16[49,8,384]{2,1,0:T(8,128)(2,1)S(1)}, bf16[49,8,384]{2,1,0:T(8,128)(2,1)S(1)}, u32[]{:S(2)}, u32[]{:S(2)}) collective-permute-start(bf16[49,8,384]{2,1,0:T(8,128)(2,1)S(1)} %copy-done.89), channel_id=1, source_target_pairs={{0,2},{1,3},{2,0},{3,1},{4,6},{5,7},{6,4},{7,5},{8,10},{9,11},{10,... | collective-permute-start | bytes 903176 | tf_op jit(solution)/shard_map/ppermute | solution.py:902
  173.9 25.2 %collective-permute-start.41 = (bf16[49,8,384]{2,1,0:T(8,128)(2,1)S(1)}, bf16[49,8,384]{2,1,0:T(8,128)(2,1)S(1)}, u32[]{:S(2)}, u32[]{:S(2)}) collective-permute-start(bf16[49,8,384]{2,1,0:T(8,128)(2,1)S(1)} %copy-done.88), channel_id=1, source_target_pairs={{0,3},{1,2},{2,1},{3,0},{4,7},{5,6},{6,5},{7,4},{8,11},{9,10},{10,... | collective-permute-start | bytes 903176 | tf_op jit(solution)/shard_map/ppermute | solution.py:902
  273.1 30.0 %collective-permute-start.65 = (bf16[98,8,384]{2,1,0:T(8,128)(2,1)S(1)}, bf16[98,8,384]{2,1,0:T(8,128)(2,1)S(1)}, u32[]{:S(2)}, u32[]{:S(2)}) collective-permute-start(bf16[98,8,384]{2,1,0:T(8,128)(2,1)S(1)} %get-tuple-element.216), channel_id=1, source_target_pairs={{0,2},{1,3},{2,0},{3,1},{4,6},{5,7},{6,4},{7,5},{8,10},{9,11},{10,... | collective-permute-start | bytes 1806344 | tf_op jit(solution)/shard_map/ppermute | solution.py:902
  277.5 25.5 %collective-permute-start.66 = (f32[15,8,512]{2,1,0:T(8,128)S(1)}, f32[15,8,512]{2,1,0:T(8,128)S(1)}, u32[]{:S(2)}, u32[]{:S(2)}) collective-permute-start(f32[15,8,512]{2,1,0:T(8,128)S(1)} %get-tuple-element.217), channel_id=1, source_target_pairs={{0,1},{1,2},{2,3},{4,5},{5,6},{6,7},{8,9},{9,10},{10,11},{12,13},{... | collective-permute-start | bytes 737288 | tf_op jit(solution)/shard_map/ppermute | solution.py:952
  280.7 22.4 %collective-permute-start.67 = (f32[15,8,512]{2,1,0:T(8,128)S(1)}, f32[15,8,512]{2,1,0:T(8,128)S(1)}, u32[]{:S(2)}, u32[]{:S(2)}) collective-permute-start(f32[15,8,512]{2,1,0:T(8,128)S(1)} %get-tuple-element.218), channel_id=1, source_target_pairs={{1,0},{2,1},{3,2},{5,4},{6,5},{7,6},{9,8},{10,9},{11,10},{13,12},{... | collective-permute-start | bytes 737288 | tf_op jit(solution)/shard_map/ppermute | solution.py:953
  314.6 33.4 %collective-permute-start.73 = (bf16[147,8,384]{2,1,0:T(8,128)(2,1)S(1)}, bf16[147,8,384]{2,1,0:T(8,128)(2,1)S(1)}, u32[]{:S(2)}, u32[]{:S(2)}) collective-permute-start(bf16[147,8,384]{2,1,0:T(8,128)(2,1)S(1)} %get-tuple-element.222), channel_id=1, source_target_pairs={{0,1},{1,0},{2,3},{3,2},{4,5},{5,4},{6,7},{7,6},{8,9},{9,8},{10,11... | collective-permute-start | bytes 2709512 | tf_op jit(solution)/shard_map/ppermute | solution.py:902
  314.9 29.7 %collective-permute-start.75 = (bf16[49,8,384]{2,1,0:T(8,128)(2,1)S(1)}, bf16[49,8,384]{2,1,0:T(8,128)(2,1)S(1)}, u32[]{:S(2)}, u32[]{:S(2)}) collective-permute-start(bf16[49,8,384]{2,1,0:T(8,128)(2,1)S(1)} %get-tuple-element.226), channel_id=1, source_target_pairs={{0,3},{1,2},{2,1},{3,0},{4,7},{5,6},{6,5},{7,4},{8,11},{9,10},{10,... | collective-permute-start | bytes 903176 | tf_op jit(solution)/shard_map/ppermute | solution.py:902
  317.1 28.8 %collective-permute-start.74 = (bf16[49,8,384]{2,1,0:T(8,128)(2,1)S(1)}, bf16[49,8,384]{2,1,0:T(8,128)(2,1)S(1)}, u32[]{:S(2)}, u32[]{:S(2)}) collective-permute-start(bf16[49,8,384]{2,1,0:T(8,128)(2,1)S(1)} %get-tuple-element.224), channel_id=1, source_target_pairs={{0,2},{1,3},{2,0},{3,1},{4,6},{5,7},{6,4},{7,5},{8,10},{9,11},{10,... | collective-permute-start | bytes 903176 | tf_op jit(solution)/shard_map/ppermute | solution.py:902
  356.4 25.2 %collective-permute-start.83 = (bf16[98,8,384]{2,1,0:T(8,128)(2,1)}, bf16[98,8,384]{2,1,0:T(8,128)(2,1)}, u32[]{:S(2)}, u32[]{:S(2)}) collective-permute-start(bf16[98,8,384]{2,1,0:T(8,128)(2,1)} %get-tuple-element.236), channel_id=1, source_target_pairs={{0,3},{1,2},{2,1},{3,0},{4,7},{5,6},{6,5},{7,4},{8,11},{9,10},{10,... | collective-permute-start | bytes 1806344 | tf_op jit(solution)/shard_map/ppermute | solution.py:902
  389.8 88.8 %all-to-all-start.1 = ((bf16[4,147,8,256]{3,2,1,0:T(8,128)(2,1)}), bf16[4,147,8,256]{3,2,1,0:T(8,128)(2,1)}, u32[]{:S(2)}, u32[]{:S(2)}) async-start(bf16[4,147,8,256]{3,2,1,0:T(8,128)(2,1)} %copy-done.31), calls=%async_computation.1 | async-start | bytes 4816896 | tf_op jit(solution)/shard_map/all_to_all | solution.py:1078
  425.5 17.2 %collective-permute-start.101 = (bf16[6,8,1024]{2,1,0:T(8,128)(2,1)S(1)}, bf16[6,8,1024]{2,1,0:T(8,128)(2,1)S(1)}, u32[]{:S(2)}, u32[]{:S(2)}) collective-permute-start(bf16[6,8,1024]{2,1,0:T(8,128)(2,1)S(1)} %get-tuple-element.354), channel_id=1, source_target_pairs={{0,1},{1,0},{2,3},{3,2},{4,5},{5,4},{6,7},{7,6},{8,9},{9,8},{10,11... | collective-permute-start | bytes 294920 | tf_op jit(solution)/shard_map/ppermute | solution.py:902
  427.3 28.7 %collective-permute-start.102 = (bf16[6,8,1024]{2,1,0:T(8,128)(2,1)S(1)}, bf16[6,8,1024]{2,1,0:T(8,128)(2,1)S(1)}, u32[]{:S(2)}, u32[]{:S(2)}) collective-permute-start(bf16[6,8,1024]{2,1,0:T(8,128)(2,1)S(1)} %get-tuple-element.353), channel_id=1, source_target_pairs={{0,2},{1,3},{2,0},{3,1},{4,6},{5,7},{6,4},{7,5},{8,10},{9,11},{10,... | collective-permute-start | bytes 294920 | tf_op jit(solution)/shard_map/ppermute | solution.py:902
  429.7 26.3 %collective-permute-start.103 = (bf16[6,8,1024]{2,1,0:T(8,128)(2,1)S(1)}, bf16[6,8,1024]{2,1,0:T(8,128)(2,1)S(1)}, u32[]{:S(2)}, u32[]{:S(2)}) collective-permute-start(bf16[6,8,1024]{2,1,0:T(8,128)(2,1)S(1)} %get-tuple-element.352), channel_id=1, source_target_pairs={{0,3},{1,2},{2,1},{3,0},{4,7},{5,6},{6,5},{7,4},{8,11},{9,10},{10,... | collective-permute-start | bytes 294920 | tf_op jit(solution)/shard_map/ppermute | solution.py:902
  432.4 25.8 %collective-permute-start.104 = (bf16[4,6,8,1024]{3,2,1,0:T(8,128)(2,1)S(1)}, bf16[4,6,8,1024]{3,2,1,0:T(8,128)(2,1)S(1)}, u32[]{:S(2)}, u32[]{:S(2)}) collective-permute-start(bf16[4,6,8,1024]{3,2,1,0:T(8,128)(2,1)S(1)} %get-tuple-element.342), channel_id=1, source_target_pairs={{0,8},{4,12},{8,0},{12,4},{16,24},{20,28},{24,16},{28,20},{1,9},{5... | collective-permute-start | bytes 1179656 | tf_op jit(solution)/shard_map/ppermute | solution.py:902
  432.8 27.8 %collective-permute-start.105 = (bf16[4,6,8,1024]{3,2,1,0:T(8,128)(2,1)S(1)}, bf16[4,6,8,1024]{3,2,1,0:T(8,128)(2,1)S(1)}, u32[]{:S(2)}, u32[]{:S(2)}) collective-permute-start(bf16[4,6,8,1024]{3,2,1,0:T(8,128)(2,1)S(1)} %get-tuple-element.344), channel_id=1, source_target_pairs={{0,16},{4,20},{8,24},{12,28},{16,0},{20,4},{24,8},{28,12},{1,17},{... | collective-permute-start | bytes 1179656 | tf_op jit(solution)/shard_map/ppermute | solution.py:902
  442.7 17.9 %collective-permute-start.106 = (bf16[4,6,8,1024]{3,2,1,0:T(8,128)(2,1)S(1)}, bf16[4,6,8,1024]{3,2,1,0:T(8,128)(2,1)S(1)}, u32[]{:S(2)}, u32[]{:S(2)}) collective-permute-start(bf16[4,6,8,1024]{3,2,1,0:T(8,128)(2,1)S(1)} %get-tuple-element.343), channel_id=1, source_target_pairs={{0,24},{4,28},{8,16},{12,20},{16,8},{20,12},{24,0},{28,4},{1,25},{... | collective-permute-start | bytes 1179656 | tf_op jit(solution)/shard_map/ppermute | solution.py:902
  461.7 16.9 %collective-permute-start.108 = (bf16[6,8,1024]{2,1,0:T(8,128)(2,1)S(1)}, bf16[6,8,1024]{2,1,0:T(8,128)(2,1)S(1)}, u32[]{:S(2)}, u32[]{:S(2)}) collective-permute-start(bf16[6,8,1024]{2,1,0:T(8,128)(2,1)S(1)} %get-tuple-element.350), channel_id=1, source_target_pairs={{0,2},{1,3},{2,0},{3,1},{4,6},{5,7},{6,4},{7,5},{8,10},{9,11},{10,... | collective-permute-start | bytes 294920 | tf_op jit(solution)/shard_map/ppermute | solution.py:902
  478.6 33.5 %all-to-all-start.2 = ((bf16[4,147,8,128]{3,2,1,0:T(8,128)(2,1)}), bf16[4,147,8,128]{3,2,1,0:T(8,128)(2,1)S(1)}, u32[]{:S(2)}, u32[]{:S(2)}) async-start(bf16[4,147,8,128]{3,2,1,0:T(8,128)(2,1)} %get-tuple-element.278), calls=%async_computation.2 | async-start | bytes 2408448 | tf_op jit(solution)/shard_map/all_to_all | solution.py:1078
  (191 other events, 1484.0 us)

commit v7 on v6

--- a/solution.py
+++ b/solution.py
@@ -558,11 +558,12 @@
             out_ref[k, here] = (value * mask).astype(BF16)
             up = slope * (cot_ref[pl.ds(p, SMALL), :, 0:128].astype(F32) * mask)
             up_ref[here, :, lanes] = up.astype(BF16)
-            return carry[0] + down(up), carry[1] + down(up * ((y - cz) * rz))
+            return carry[0] + down(up), carry[1] + down(up * y)
 
         zero = (jnp.zeros((8, 128), F32),) * 2
         kept = sweep(table_ref, cot_ref.shape[0], SMALL, body, kept if begin else zero, begin)
-        slopes_ref[0:1, lanes], slopes_ref[1:2, lanes] = flat(kept[0]), flat(kept[1])
+        total = flat(kept[0])
+        slopes_ref[0:1, lanes], slopes_ref[1:2, lanes] = total, (flat(kept[1]) - cz[0] * total) * rz[0]
 
 
 def slow_out_kernel(table_ref, n_ref, sc_ref, sp_ref, sums_ref, gains_ref, *refs):
@@ -581,7 +582,7 @@
         vecs = [vec_ref[i : i + 1, lanes][None] for i in range(7)]
 
         def body(p, frames, carry, k=k, lanes=lanes, vecs=vecs, cot_ref=cot_ref, out_ref=out_ref, begin=begin):
-            cf, shift, cc, cr, pf, pc, pr = vecs
+            cf, shift, _, _, pf, _, _ = vecs
             here = pl.ds(begin + p, SMALL)
             yc, yp = (ref[here, :, lanes].astype(F32) for ref in (sc_ref, sp_ref))
             mask = tile_mask(frames, 256)
@@ -590,14 +591,15 @@
             out_ref[pl.ds(p, SMALL), :, 0:128] = fast_ref[k, here]
             up = slope * (cot_ref[pl.ds(p, SMALL), :, 128:384].astype(F32) * mask)
             up_ref[here, :, lanes] = up.astype(BF16)
-            return (carry[0] + down(up), carry[1] + down(up * ((yc - cc) * cr)), carry[2] + down(up * ((yp - pc) * pr)))
+            return carry[0] + down(up), carry[1] + down(up * yc), carry[2] + down(up * yp)
 
         zero = (jnp.zeros((8, 256), F32),) * 3
         kept = sweep(table_ref, cot_ref.shape[0], SMALL, body, kept if begin else zero, begin)
-        a, b, c = kept
+        _, _, cc, cr, _, pc, pr = (v[0] for v in vecs)
+        a, b, c = (flat(v) for v in kept)
         own, other = lanes, lanes_at(4 + block, 256)
-        slopes_ref[0:1, own], slopes_ref[1:2, own] = flat(a), flat(b)
-        slopes_ref[0:1, other], slopes_ref[1:2, other] = flat(a), flat(c)
+        slopes_ref[0:1, own], slopes_ref[1:2, own] = a, (b - cc * a) * cr
+        slopes_ref[0:1, other], slopes_ref[1:2, other] = a, (c - pc * a) * pr
     slopes_ref[:, 2 * width :] = more_ref[...]
 
 

time: 523 us -> 523 us (level)
  no operation moved by 1% of the time
where the time goes in v7:
time: 523 us; the launch traced here: 516 us
  starting transfers between devices  169 us (32%)
  waiting for transfers between devices  163 us (31%)
  Pallas kernels  112 us (21%)
  local copies, waits for them, and re-layouts  52.4 us (10%)
  other arithmetic  17.3 us (3%)
    ppermute x116, waiting for transfers between devices, swap(): return jax.tree.map(lambda v: lax.ppermute(v, axis, pairs), tree)  138 us
    ppermute x116, starting transfers between devices, swap(): return jax.tree.map(lambda v: lax.ppermute(v, axis, pairs), tree)  132 us
    pallas_call x24, Pallas kernels, call(): pl.pallas_call(kernel, out_shape=tuple(outs), in_specs=specs, out_specs=t...  98.4 us
    unnamed x193, local copies, waits for them, and re-layouts  37.8 us
    ppermute x4, waiting for transfers between devices, halos(): high = lax.ppermute(first, 'chan', [(i + 1, i) for i in range(count - 1)])  21.6 us
    ppermute x4, starting transfers between devices, halos(): low = lax.ppermute(last, 'chan', [(i, i + 1) for i in range(count - 1)])  15.9 us
    all_to_all x3, starting transfers between devices, all_to_all(): return lax.all_to_all(v, 'chan', 0, 0, tiled=True)  14.8 us
  transfers between devices with their start and end apart: 127, of which 57 were waited for; matrix products, arithmetic and copies ran while one was open for 6% of the time, Pallas kernels for 18%

profile of v7, /device:TPU:0, one launch (start us, length us, event | category | flops | bytes accessed | tf_op | source)
XLA Modules:
  0.0 515.9 jit_solution(8744804034840749041)
XLA Ops:
  3.9 5.1 collective-permute-start.2
  16.3 12.5 %collective-permute-done.1 = bf16[14,8,1024]{2,1,0:T(8,128)(2,1)S(1)} collective-permute-done((bf16[14,8,1024]{2,1,0:T(8,128)(2,1)}, bf16[14,8,1024]{2,1,0:T(8,128)(2,1)S(1)}, u32[]{:S(2)}, u32[]{:S(2)}) %collective-permute-start.1) | collective-permute-done | bytes 229408 | tf_op jit(solution)/shard_map/ppermute | solution.py:904
  35.5 4.2 collective-permute-done.3.f1_ref
  41.3 14.8 %collective-permute-done.4.f2_ref = bf16[147,8,128]{2,1,0:T(8,128)(2,1)S(1)} collective-permute-done((bf16[147,8,128]{2,1,0:T(8,128)(2,1)S(1)}, bf16[147,8,128]{2,1,0:T(8,128)(2,1)S(1)}, u32[]{:S(2)}, u32[]{:S(2)}) %collective-permute-start.4) | collective-permute-done | bytes 301088 | tf_op jit(solution)/shard_map/ppermute | solution.py:904
  57.6 6.6 %all-to-all-start = ((bf16[4,147,8,256]{3,2,1,0:T(8,128)(2,1)}), bf16[4,147,8,256]{3,2,1,0:T(8,128)(2,1)S(1)}, u32[]{:S(2)}, u32[]{:S(2)}) async-start(bf16[4,147,8,256]{3,2,1,0:T(8,128)(2,1)} %bitcast.234), calls=%async_computation | async-start | bytes 4816896 | tf_op jit(solution)/shard_map/all_to_all | solution.py:1080
  98.3 6.7 %collective-permute-done.14 = f32[2,384]{1,0:T(2,128)S(1)} collective-permute-done((f32[2,384]{1,0:T(2,128)S(1)}, f32[2,384]{1,0:T(2,128)S(1)}, u32[]{:S(2)}, u32[]{:S(2)}) %collective-permute-start.14) | collective-permute-done | bytes 3104 | tf_op jit(solution)/shard_map/ppermute | solution.py:904
  115.4 4.2 collective-permute-done.18.hi_ref
  136.7 4.8 slow_first.1
  141.5 4.3 collective-permute-start.27
  149.6 8.1 %collective-permute-done.28.hi_ref = f32[15,8,256]{2,1,0:T(8,128)S(1)} collective-permute-done((f32[15,8,256]{2,1,0:T(8,128)S(1)}, f32[15,8,256]{2,1,0:T(8,128)S(1)}, u32[]{:S(2)}, u32[]{:S(2)}) %collective-permute-start.28) | collective-permute-done | bytes 122912 | tf_op jit(solution)/shard_map/ppermute | solution.py:955
  187.2 4.8 collective-permute-done.40.refs_3_
  192.0 7.1 %collective-permute-done.41.refs_4_ = bf16[49,8,384]{2,1,0:T(8,128)(2,1)S(1)} collective-permute-done((bf16[49,8,384]{2,1,0:T(8,128)(2,1)S(1)}, bf16[49,8,384]{2,1,0:T(8,128)(2,1)S(1)}, u32[]{:S(2)}, u32[]{:S(2)}) %collective-permute-start.41) | collective-permute-done | bytes 301088 | tf_op jit(solution)/shard_map/ppermute | solution.py:904
  212.6 4.4 bypass.1
  222.9 8.6 %collective-permute-start.51 = (f32[2,2560]{1,0:T(2,128)S(1)}, f32[2,2560]{1,0:T(2,128)S(1)}, u32[]{:S(2)}, u32[]{:S(2)}) collective-permute-start(f32[2,2560]{1,0:T(2,128)S(1)} %add.378), channel_id=1, source_target_pairs={{0,1},{1,0},{2,3},{3,2},{4,5},{5,4},{6,7},{7,6},{8,9},{9,8},{10,11... | collective-permute-start | bytes 61448 | tf_op jit(solution)/shard_map/ppermute | solution.py:904
  246.5 4.7 fast_out.1
  251.3 8.8 %slow_out.1 = (bf16[147,8,384]{2,1,0:T(8,128)(2,1)S(1)}, bf16[147,8,384]{2,1,0:T(8,128)(2,1)S(1)}, bf16[98,8,384]{2,1,0:T(8,128)(2,1)S(1)}, bf16[49,8,384]{2,1,0...) custom-call(s32[7]{0:T(128)S(1)} %pad_add_fusion.1.table_ref, ...), custom_call_target="tpu_custom_call" | custom-call | bytes 1 | tf_op jit(solution)/shard_map/slow_out/pallas_call | solution.py:125
  285.3 4.6 collective-permute-start.68
  293.1 9.4 %collective-permute-done.69.dhi_ref = f32[15,8,256]{2,1,0:T(8,128)S(1)} collective-permute-done((f32[15,8,256]{2,1,0:T(8,128)S(1)}, f32[15,8,256]{2,1,0:T(8,128)S(1)}, u32[]{:S(2)}, u32[]{:S(2)}) %collective-permute-start.69) | collective-permute-done | bytes 122912 | tf_op jit(solution)/shard_map/ppermute | solution.py:955
  303.3 5.2 %collective-permute-start.70 = (f32[2,384]{1,0:T(2,128)S(1)}, f32[2,384]{1,0:T(2,128)S(1)}, u32[]{:S(2)}, u32[]{:S(2)}) collective-permute-start(f32[2,384]{1,0:T(2,128)S(1)} %add.392), channel_id=1, source_target_pairs={{0,1},{1,0},{2,3},{3,2},{4,5},{5,4},{6,7},{7,6},{8,9},{9,8},{10,11... | collective-permute-start | bytes 9224 | tf_op jit(solution)/shard_map/ppermute | solution.py:904
  321.5 4.1 collective-permute-done.78
  333.3 5.9 %bypass_back.1 = (bf16[147,8,1024]{2,1,0:T(8,128)(2,1)S(1)}, bf16[147,8,1024]{2,1,0:T(8,128)(2,1)S(1)}, f32[147,8,256]{2,1,0:T(8,128)S(1)}) custom-call(s32[7]{0:T(128)S(1)} %pad_add_fusion.1.table_ref, f32[2]{0:T(128)S(1)} %pad_maximum_fusion.14.n_ref, bf16[147,8,1024]{2,1,0:T(8,128)(2,1)S(1)} %get-tuple-element.232.up_ref, ...), custom_call_target="tpu_custom_call" | custom-call | bytes 1 | tf_op jit(solution)/shard_map/bypass_back/pallas_call | solution.py:125
  362.7 4.9 slow_first_back.1
  375.8 5.1 first_slab.1
  389.2 4.7 all-to-all-start.1
  409.0 6.5 %second_slab.1 = bf16[2,4,4,6,8,1024]{5,4,3,2,1,0:T(8,128)(2,1)S(1)} custom-call(s32[7]{0:T(128)S(1)} %pad_add_fusion.1.table_ref, bf16[177,8,256]{2,1,0:T(8,128)(2,1)S(1)} %copy-done.48, bf16[147,8,256]{2,1,0:T(8,128)(2,1)S(1)} %copy-done.52, bf16[147,8,768]{2,1,0:T(8,128)(2,1)S(1)} %copy-done.33, bf16[147,8,1024]{2,1,0:T(8,128)(2,1)S(1)} %get-tuple-element.189.x_ref, ...), custom_call_target="tpu_custom_call" | custom-call | bytes 1 | tf_op jit(solution)/shard_map/second_slab/pallas_call | solution.py:125
  433.2 4.3 fast_first_back.1
  437.5 4.6 fast_grads.1
  444.4 10.9 %collective-permute-done.102 = bf16[6,8,1024]{2,1,0:T(8,128)(2,1)S(1)} collective-permute-done((bf16[6,8,1024]{2,1,0:T(8,128)(2,1)S(1)}, bf16[6,8,1024]{2,1,0:T(8,128)(2,1)S(1)}, u32[]{:S(2)}, u32[]{:S(2)}) %collective-permute-start.102) | collective-permute-done | bytes 98336 | tf_op jit(solution)/shard_map/ppermute | solution.py:904
  464.7 8.1 %collective-permute-done.111 = bf16[68,8,128]{2,1,0:T(8,128)(2,1)S(1)} collective-permute-done((bf16[68,8,128]{2,1,0:T(8,128)(2,1)S(1)}, bf16[68,8,128]{2,1,0:T(8,128)(2,1)S(1)}, u32[]{:S(2)}, u32[]{:S(2)}) %collective-permute-start.111) | collective-permute-done | bytes 139296 | tf_op jit(solution)/shard_map/ppermute | solution.py:904
  473.0 4.9 collective-permute-done.108
  499.7 6.6 %outputs.1 = (bf16[588,8,256]{2,1,0:T(8,128)(2,1)}, bf16[588,32,32]{2,1,0:T(8,128)(2,1)}) custom-call(s32[3]{0:T(128)S(1)} %copy-done.73, bf16[147,8,384]{2,1,0:T(8,128)(2,1)S(1)} %copy-done.44, bf16[147,8,384]{2,1,0:T(8,128)(2,1)S(1)} %copy-done.46, bf16[98,8,384]{2,1,0:T(8,128)(2,1)S(1)} %copy-done.56, bf16[49,8,384]{2,1,0:T(8,128)(2,1)S(1)} %copy-done.66, ...), custom_call_target="tpu_custom_call" | custom-call | bytes 1 | tf_op jit(solution)/shard_map/outputs/pallas_call | solution.py:125
  511.5 4.1 fast_unpack.1
  (547 shorter events, 309.2 us)
Async XLA Ops:
  9.0 19.7 %collective-permute-start.1 = (bf16[14,8,1024]{2,1,0:T(8,128)(2,1)}, bf16[14,8,1024]{2,1,0:T(8,128)(2,1)S(1)}, u32[]{:S(2)}, u32[]{:S(2)}) collective-permute-start(bf16[14,8,1024]{2,1,0:T(8,128)(2,1)} %weight_slab.1), channel_id=1, source_target_pairs={{0,2},{1,3},{2,0},{3,1},{4,6},{5,7},{6,4},{7,5},{8,10},{9,11},{10,... | collective-permute-start | bytes 688136 | tf_op jit(solution)/shard_map/ppermute | solution.py:904
  9.0 19.7 %collective-permute-start = (bf16[14,8,1024]{2,1,0:T(8,128)(2,1)}, bf16[14,8,1024]{2,1,0:T(8,128)(2,1)S(1)}, u32[]{:S(2)}, u32[]{:S(2)}) collective-permute-start(bf16[14,8,1024]{2,1,0:T(8,128)(2,1)} %weight_slab.1), channel_id=1, source_target_pairs={{0,1},{1,0},{2,3},{3,2},{4,5},{5,4},{6,7},{7,6},{8,9},{9,8},{10,11... | collective-permute-start | bytes 688136 | tf_op jit(solution)/shard_map/ppermute | solution.py:904
  29.6 28.0 %collective-permute-start.6 = (bf16[4,5,8,1024]{3,2,1,0:T(8,128)(2,1)S(1)}, bf16[4,5,8,1024]{3,2,1,0:T(8,128)(2,1)}, u32[]{:S(2)}, u32[]{:S(2)}) collective-permute-start(bf16[4,5,8,1024]{3,2,1,0:T(8,128)(2,1)S(1)} %get-tuple-element.360), channel_id=1, source_target_pairs={{0,8},{4,12},{8,0},{12,4},{16,24},{20,28},{24,16},{28,20},{1,9},{5... | collective-permute-start | bytes 983048 | tf_op jit(solution)/shard_map/ppermute | solution.py:904
  31.1 26.4 %collective-permute-start.7 = (bf16[4,5,8,1024]{3,2,1,0:T(8,128)(2,1)S(1)}, bf16[4,5,8,1024]{3,2,1,0:T(8,128)(2,1)}, u32[]{:S(2)}, u32[]{:S(2)}) collective-permute-start(bf16[4,5,8,1024]{3,2,1,0:T(8,128)(2,1)S(1)} %get-tuple-element.360), channel_id=1, source_target_pairs={{0,16},{4,20},{8,24},{12,28},{16,0},{20,4},{24,8},{28,12},{1,17},{... | collective-permute-start | bytes 983048 | tf_op jit(solution)/shard_map/ppermute | solution.py:904
  32.7 24.9 %collective-permute-start.8 = (bf16[4,5,8,1024]{3,2,1,0:T(8,128)(2,1)S(1)}, bf16[4,5,8,1024]{3,2,1,0:T(8,128)(2,1)}, u32[]{:S(2)}, u32[]{:S(2)}) collective-permute-start(bf16[4,5,8,1024]{3,2,1,0:T(8,128)(2,1)S(1)} %get-tuple-element.360), channel_id=1, source_target_pairs={{0,24},{4,28},{8,16},{12,20},{16,8},{20,12},{24,0},{28,4},{1,25},{... | collective-permute-start | bytes 983048 | tf_op jit(solution)/shard_map/ppermute | solution.py:904
  33.1 23.0 %collective-permute-start.4 = (bf16[147,8,128]{2,1,0:T(8,128)(2,1)S(1)}, bf16[147,8,128]{2,1,0:T(8,128)(2,1)S(1)}, u32[]{:S(2)}, u32[]{:S(2)}) collective-permute-start(bf16[147,8,128]{2,1,0:T(8,128)(2,1)S(1)} %get-tuple-element.157), channel_id=1, source_target_pairs={{0,2},{1,3},{2,0},{3,1},{4,6},{5,7},{6,4},{7,5},{8,10},{9,11},{10,... | collective-permute-start | bytes 903176 | tf_op jit(solution)/shard_map/ppermute | solution.py:904
  39.7 17.1 %collective-permute-start.5 = (bf16[147,8,128]{2,1,0:T(8,128)(2,1)S(1)}, bf16[147,8,128]{2,1,0:T(8,128)(2,1)S(1)}, u32[]{:S(2)}, u32[]{:S(2)}) collective-permute-start(bf16[147,8,128]{2,1,0:T(8,128)(2,1)S(1)} %get-tuple-element.158), channel_id=1, source_target_pairs={{0,3},{1,2},{2,1},{3,0},{4,7},{5,6},{6,5},{7,4},{8,11},{9,10},{10,... | collective-permute-start | bytes 903176 | tf_op jit(solution)/shard_map/ppermute | solution.py:904
  57.6 62.7 %all-to-all-start = ((bf16[4,147,8,256]{3,2,1,0:T(8,128)(2,1)}), bf16[4,147,8,256]{3,2,1,0:T(8,128)(2,1)S(1)}, u32[]{:S(2)}, u32[]{:S(2)}) async-start(bf16[4,147,8,256]{3,2,1,0:T(8,128)(2,1)} %bitcast.234), calls=%async_computation | async-start | bytes 4816896 | tf_op jit(solution)/shard_map/all_to_all | solution.py:1080
  76.6 43.6 %collective-permute-start.19 = (bf16[4,9,8,1024]{3,2,1,0:T(8,128)(2,1)}, bf16[4,9,8,1024]{3,2,1,0:T(8,128)(2,1)}, u32[]{:S(2)}, u32[]{:S(2)}) collective-permute-start(bf16[4,9,8,1024]{3,2,1,0:T(8,128)(2,1)} %pad_maximum_fusion.6), channel_id=1, source_target_pairs={{0,8},{4,12},{8,0},{12,4},{16,24},{20,28},{24,16},{28,20},{1,9},{5... | collective-permute-start | bytes 1769480 | tf_op jit(solution)/shard_map/ppermute | solution.py:904
  78.2 42.0 %collective-permute-start.20 = (bf16[4,9,8,1024]{3,2,1,0:T(8,128)(2,1)}, bf16[4,9,8,1024]{3,2,1,0:T(8,128)(2,1)}, u32[]{:S(2)}, u32[]{:S(2)}) collective-permute-start(bf16[4,9,8,1024]{3,2,1,0:T(8,128)(2,1)} %pad_maximum_fusion.6), channel_id=1, source_target_pairs={{0,16},{4,20},{8,24},{12,28},{16,0},{20,4},{24,8},{28,12},{1,17},{... | collective-permute-start | bytes 1769480 | tf_op jit(solution)/shard_map/ppermute | solution.py:904
  79.7 40.5 %collective-permute-start.21 = (bf16[4,9,8,1024]{3,2,1,0:T(8,128)(2,1)}, bf16[4,9,8,1024]{3,2,1,0:T(8,128)(2,1)}, u32[]{:S(2)}, u32[]{:S(2)}) collective-permute-start(bf16[4,9,8,1024]{3,2,1,0:T(8,128)(2,1)} %pad_maximum_fusion.6), channel_id=1, source_target_pairs={{0,24},{4,28},{8,16},{12,20},{16,8},{20,12},{24,0},{28,4},{1,25},{... | collective-permute-start | bytes 1769480 | tf_op jit(solution)/shard_map/ppermute | solution.py:904
  129.5 28.2 %collective-permute-start.26 = (bf16[98,8,384]{2,1,0:T(8,128)(2,1)}, bf16[98,8,384]{2,1,0:T(8,128)(2,1)}, u32[]{:S(2)}, u32[]{:S(2)}) collective-permute-start(bf16[98,8,384]{2,1,0:T(8,128)(2,1)} %get-tuple-element.171), channel_id=1, source_target_pairs={{0,2},{1,3},{2,0},{3,1},{4,6},{5,7},{6,4},{7,5},{8,10},{9,11},{10,... | collective-permute-start | bytes 1806344 | tf_op jit(solution)/shard_map/ppermute | solution.py:904
  147.6 17.5 %collective-permute-start.35 = (bf16[4,9,8,1024]{3,2,1,0:T(8,128)(2,1)}, bf16[4,9,8,1024]{3,2,1,0:T(8,128)(2,1)S(1)}, u32[]{:S(2)}, u32[]{:S(2)}) collective-permute-start(bf16[4,9,8,1024]{3,2,1,0:T(8,128)(2,1)} %pad_maximum_fusion.6), channel_id=1, source_target_pairs={{0,4},{4,0},{8,12},{12,8},{16,20},{20,16},{24,28},{28,24},{1,5},{5... | collective-permute-start | bytes 1769480 | tf_op jit(solution)/shard_map/ppermute | solution.py:904
  165.0 34.1 %collective-permute-start.42 = (bf16[147,8,384]{2,1,0:T(8,128)(2,1)S(1)}, bf16[147,8,384]{2,1,0:T(8,128)(2,1)S(1)}, u32[]{:S(2)}, u32[]{:S(2)}) collective-permute-start(bf16[147,8,384]{2,1,0:T(8,128)(2,1)S(1)} %copy-done.84), channel_id=1, source_target_pairs={{0,1},{1,0},{2,3},{3,2},{4,5},{5,4},{6,7},{7,6},{8,9},{9,8},{10,11... | collective-permute-start | bytes 2709512 | tf_op jit(solution)/shard_map/ppermute | solution.py:904
  170.8 21.2 %collective-permute-start.40 = (bf16[49,8,384]{2,1,0:T(8,128)(2,1)S(1)}, bf16[49,8,384]{2,1,0:T(8,128)(2,1)S(1)}, u32[]{:S(2)}, u32[]{:S(2)}) collective-permute-start(bf16[49,8,384]{2,1,0:T(8,128)(2,1)S(1)} %copy-done.89), channel_id=1, source_target_pairs={{0,2},{1,3},{2,0},{3,1},{4,6},{5,7},{6,4},{7,5},{8,10},{9,11},{10,... | collective-permute-start | bytes 903176 | tf_op jit(solution)/shard_map/ppermute | solution.py:904
  173.9 25.2 %collective-permute-start.41 = (bf16[49,8,384]{2,1,0:T(8,128)(2,1)S(1)}, bf16[49,8,384]{2,1,0:T(8,128)(2,1)S(1)}, u32[]{:S(2)}, u32[]{:S(2)}) collective-permute-start(bf16[49,8,384]{2,1,0:T(8,128)(2,1)S(1)} %copy-done.88), channel_id=1, source_target_pairs={{0,3},{1,2},{2,1},{3,0},{4,7},{5,6},{6,5},{7,4},{8,11},{9,10},{10,... | collective-permute-start | bytes 903176 | tf_op jit(solution)/shard_map/ppermute | solution.py:904
  272.5 30.0 %collective-permute-start.65 = (bf16[98,8,384]{2,1,0:T(8,128)(2,1)S(1)}, bf16[98,8,384]{2,1,0:T(8,128)(2,1)S(1)}, u32[]{:S(2)}, u32[]{:S(2)}) collective-permute-start(bf16[98,8,384]{2,1,0:T(8,128)(2,1)S(1)} %get-tuple-element.216), channel_id=1, source_target_pairs={{0,2},{1,3},{2,0},{3,1},{4,6},{5,7},{6,4},{7,5},{8,10},{9,11},{10,... | collective-permute-start | bytes 1806344 | tf_op jit(solution)/shard_map/ppermute | solution.py:904
  276.9 25.5 %collective-permute-start.66 = (f32[15,8,512]{2,1,0:T(8,128)S(1)}, f32[15,8,512]{2,1,0:T(8,128)S(1)}, u32[]{:S(2)}, u32[]{:S(2)}) collective-permute-start(f32[15,8,512]{2,1,0:T(8,128)S(1)} %get-tuple-element.217), channel_id=1, source_target_pairs={{0,1},{1,2},{2,3},{4,5},{5,6},{6,7},{8,9},{9,10},{10,11},{12,13},{... | collective-permute-start | bytes 737288 | tf_op jit(solution)/shard_map/ppermute | solution.py:954
  280.1 22.4 %collective-permute-start.67 = (f32[15,8,512]{2,1,0:T(8,128)S(1)}, f32[15,8,512]{2,1,0:T(8,128)S(1)}, u32[]{:S(2)}, u32[]{:S(2)}) collective-permute-start(f32[15,8,512]{2,1,0:T(8,128)S(1)} %get-tuple-element.218), channel_id=1, source_target_pairs={{1,0},{2,1},{3,2},{5,4},{6,5},{7,6},{9,8},{10,9},{11,10},{13,12},{... | collective-permute-start | bytes 737288 | tf_op jit(solution)/shard_map/ppermute | solution.py:955
  314.0 33.4 %collective-permute-start.73 = (bf16[147,8,384]{2,1,0:T(8,128)(2,1)S(1)}, bf16[147,8,384]{2,1,0:T(8,128)(2,1)S(1)}, u32[]{:S(2)}, u32[]{:S(2)}) collective-permute-start(bf16[147,8,384]{2,1,0:T(8,128)(2,1)S(1)} %get-tuple-element.222), channel_id=1, source_target_pairs={{0,1},{1,0},{2,3},{3,2},{4,5},{5,4},{6,7},{7,6},{8,9},{9,8},{10,11... | collective-permute-start | bytes 2709512 | tf_op jit(solution)/shard_map/ppermute | solution.py:904
  314.2 29.7 %collective-permute-start.75 = (bf16[49,8,384]{2,1,0:T(8,128)(2,1)S(1)}, bf16[49,8,384]{2,1,0:T(8,128)(2,1)S(1)}, u32[]{:S(2)}, u32[]{:S(2)}) collective-permute-start(bf16[49,8,384]{2,1,0:T(8,128)(2,1)S(1)} %get-tuple-element.226), channel_id=1, source_target_pairs={{0,3},{1,2},{2,1},{3,0},{4,7},{5,6},{6,5},{7,4},{8,11},{9,10},{10,... | collective-permute-start | bytes 903176 | tf_op jit(solution)/shard_map/ppermute | solution.py:904
  316.5 28.8 %collective-permute-start.74 = (bf16[49,8,384]{2,1,0:T(8,128)(2,1)S(1)}, bf16[49,8,384]{2,1,0:T(8,128)(2,1)S(1)}, u32[]{:S(2)}, u32[]{:S(2)}) collective-permute-start(bf16[49,8,384]{2,1,0:T(8,128)(2,1)S(1)} %get-tuple-element.224), channel_id=1, source_target_pairs={{0,2},{1,3},{2,0},{3,1},{4,6},{5,7},{6,4},{7,5},{8,10},{9,11},{10,... | collective-permute-start | bytes 903176 | tf_op jit(solution)/shard_map/ppermute | solution.py:904
  355.8 25.2 %collective-permute-start.83 = (bf16[98,8,384]{2,1,0:T(8,128)(2,1)}, bf16[98,8,384]{2,1,0:T(8,128)(2,1)}, u32[]{:S(2)}, u32[]{:S(2)}) collective-permute-start(bf16[98,8,384]{2,1,0:T(8,128)(2,1)} %get-tuple-element.236), channel_id=1, source_target_pairs={{0,3},{1,2},{2,1},{3,0},{4,7},{5,6},{6,5},{7,4},{8,11},{9,10},{10,... | collective-permute-start | bytes 1806344 | tf_op jit(solution)/shard_map/ppermute | solution.py:904
  389.2 88.8 %all-to-all-start.1 = ((bf16[4,147,8,256]{3,2,1,0:T(8,128)(2,1)}), bf16[4,147,8,256]{3,2,1,0:T(8,128)(2,1)}, u32[]{:S(2)}, u32[]{:S(2)}) async-start(bf16[4,147,8,256]{3,2,1,0:T(8,128)(2,1)} %copy-done.31), calls=%async_computation.1 | async-start | bytes 4816896 | tf_op jit(solution)/shard_map/all_to_all | solution.py:1080
  424.9 17.2 %collective-permute-start.101 = (bf16[6,8,1024]{2,1,0:T(8,128)(2,1)S(1)}, bf16[6,8,1024]{2,1,0:T(8,128)(2,1)S(1)}, u32[]{:S(2)}, u32[]{:S(2)}) collective-permute-start(bf16[6,8,1024]{2,1,0:T(8,128)(2,1)S(1)} %get-tuple-element.354), channel_id=1, source_target_pairs={{0,1},{1,0},{2,3},{3,2},{4,5},{5,4},{6,7},{7,6},{8,9},{9,8},{10,11... | collective-permute-start | bytes 294920 | tf_op jit(solution)/shard_map/ppermute | solution.py:904
  426.7 28.7 %collective-permute-start.102 = (bf16[6,8,1024]{2,1,0:T(8,128)(2,1)S(1)}, bf16[6,8,1024]{2,1,0:T(8,128)(2,1)S(1)}, u32[]{:S(2)}, u32[]{:S(2)}) collective-permute-start(bf16[6,8,1024]{2,1,0:T(8,128)(2,1)S(1)} %get-tuple-element.353), channel_id=1, source_target_pairs={{0,2},{1,3},{2,0},{3,1},{4,6},{5,7},{6,4},{7,5},{8,10},{9,11},{10,... | collective-permute-start | bytes 294920 | tf_op jit(solution)/shard_map/ppermute | solution.py:904
  429.1 26.3 %collective-permute-start.103 = (bf16[6,8,1024]{2,1,0:T(8,128)(2,1)S(1)}, bf16[6,8,1024]{2,1,0:T(8,128)(2,1)S(1)}, u32[]{:S(2)}, u32[]{:S(2)}) collective-permute-start(bf16[6,8,1024]{2,1,0:T(8,128)(2,1)S(1)} %get-tuple-element.352), channel_id=1, source_target_pairs={{0,3},{1,2},{2,1},{3,0},{4,7},{5,6},{6,5},{7,4},{8,11},{9,10},{10,... | collective-permute-start | bytes 294920 | tf_op jit(solution)/shard_map/ppermute | solution.py:904
  431.8 25.8 %collective-permute-start.104 = (bf16[4,6,8,1024]{3,2,1,0:T(8,128)(2,1)S(1)}, bf16[4,6,8,1024]{3,2,1,0:T(8,128)(2,1)S(1)}, u32[]{:S(2)}, u32[]{:S(2)}) collective-permute-start(bf16[4,6,8,1024]{3,2,1,0:T(8,128)(2,1)S(1)} %get-tuple-element.342), channel_id=1, source_target_pairs={{0,8},{4,12},{8,0},{12,4},{16,24},{20,28},{24,16},{28,20},{1,9},{5... | collective-permute-start | bytes 1179656 | tf_op jit(solution)/shard_map/ppermute | solution.py:904
  432.2 27.8 %collective-permute-start.105 = (bf16[4,6,8,1024]{3,2,1,0:T(8,128)(2,1)S(1)}, bf16[4,6,8,1024]{3,2,1,0:T(8,128)(2,1)S(1)}, u32[]{:S(2)}, u32[]{:S(2)}) collective-permute-start(bf16[4,6,8,1024]{3,2,1,0:T(8,128)(2,1)S(1)} %get-tuple-element.344), channel_id=1, source_target_pairs={{0,16},{4,20},{8,24},{12,28},{16,0},{20,4},{24,8},{28,12},{1,17},{... | collective-permute-start | bytes 1179656 | tf_op jit(solution)/shard_map/ppermute | solution.py:904
  442.1 17.9 %collective-permute-start.106 = (bf16[4,6,8,1024]{3,2,1,0:T(8,128)(2,1)S(1)}, bf16[4,6,8,1024]{3,2,1,0:T(8,128)(2,1)S(1)}, u32[]{:S(2)}, u32[]{:S(2)}) collective-permute-start(bf16[4,6,8,1024]{3,2,1,0:T(8,128)(2,1)S(1)} %get-tuple-element.343), channel_id=1, source_target_pairs={{0,24},{4,28},{8,16},{12,20},{16,8},{20,12},{24,0},{28,4},{1,25},{... | collective-permute-start | bytes 1179656 | tf_op jit(solution)/shard_map/ppermute | solution.py:904
  461.1 16.9 %collective-permute-start.108 = (bf16[6,8,1024]{2,1,0:T(8,128)(2,1)S(1)}, bf16[6,8,1024]{2,1,0:T(8,128)(2,1)S(1)}, u32[]{:S(2)}, u32[]{:S(2)}) collective-permute-start(bf16[6,8,1024]{2,1,0:T(8,128)(2,1)S(1)} %get-tuple-element.350), channel_id=1, source_target_pairs={{0,2},{1,3},{2,0},{3,1},{4,6},{5,7},{6,4},{7,5},{8,10},{9,11},{10,... | collective-permute-start | bytes 294920 | tf_op jit(solution)/shard_map/ppermute | solution.py:904
  478.0 33.5 %all-to-all-start.2 = ((bf16[4,147,8,128]{3,2,1,0:T(8,128)(2,1)}), bf16[4,147,8,128]{3,2,1,0:T(8,128)(2,1)S(1)}, u32[]{:S(2)}, u32[]{:S(2)}) async-start(bf16[4,147,8,128]{3,2,1,0:T(8,128)(2,1)} %get-tuple-element.278), calls=%async_computation.2 | async-start | bytes 2408448 | tf_op jit(solution)/shard_map/all_to_all | solution.py:1080
  (191 other events, 1483.4 us)
